TPU v7x, 32 devices: a whole 2x2x4 slice. The times are simulated.
32 devices in a mesh: ca: 4 (over y, core), fe: 8 (over z, x).
Axes of the slice: x: 2, y: 2, z: 4, core: 2. Of those that a mesh axis runs over, the one named last changes fastest.
Arguments:
- grain_ids: int32 [216, 65536], P(None, ('ca', 'fe')), may hold values from 0 to 4095
- euler_angles: float32 [3, 4096], replicated, may hold values from -3.140625 to 3.140625
- brick_active: int32 [65536], P(('ca', 'fe')), may hold values 0 or 1
- brick_owner: int32 [65536, 1], P(('ca', 'fe')), may hold values from 0 to 31, as said below
- brick_element: int32 [65536], P(('ca', 'fe')), may hold values from 0 to 224, as said below
- displacement: float32 [3, 32, 256], P(None, ('ca', 'fe')), may hold values from -0.3 to 0.3
- stress_old: float32 [6, 8, 7200], P(None, None, ('ca', 'fe')), may hold values from -3 to 3
- resistance: float32 [12, 8, 7200], P(None, None, ('ca', 'fe')), may hold values from 0.2 to 0.8
- quad_weights: int32 [8, 7200], P(None, ('ca', 'fe')), may hold values from 32768 to 98304
Outputs:
- stress_new: float32 [6, 8, 7200], P(None, None, ('ca', 'fe'))
- forces: float32 [3, 32, 256], P(None, ('ca', 'fe'))
Inputs may be any that keep to these rules, and one draw needn't show every extreme that they name: `brick_owner`: the bricks of one device name each owner at least 2048 / 64 times and at most 160 times; one owner is named exactly 160 times by the bricks of every device. `brick_element`: every element of every owner is named by at least one brick.
All inputs are finite; a program needn't handle non-finite values. No bound on the sum of `brick_active` on one device may be relied on, other than what follows from the above.
Results may differ from a plain program's by a relative error of at most 0.0002.
Values sent between devices are 32-bit elements; how exact they have to be, the bound alone decides.
No kernel may reach another device: no remote copies, remote signals or barrier semaphores. Data moves between devices by JAX's collectives and lax.ppermute only.
A program may use at most 448 MiB of HBM per device.

v0:
```python
import math

import jax
import jax.numpy as jnp
from jax import lax
from jax.sharding import PartitionSpec as P

GX = 15


SLIP_PLANES = [
    [value / math.sqrt(3.0) for value in row]
    for row in [[1, 1, 1]] * 3 + [[-1, 1, 1]] * 3 + [[1, -1, 1]] * 3 + [[1, 1, -1]] * 3
]
SLIP_DIRECTIONS = [
    [value / math.sqrt(2.0) for value in row]
    for row in [
        [0, 1, -1],
        [1, 0, -1],
        [1, -1, 0],
        [0, 1, -1],
        [1, 0, 1],
        [1, 1, 0],
        [0, 1, 1],
        [1, 0, -1],
        [1, 1, 0],
        [0, 1, 1],
        [1, 0, 1],
        [1, -1, 0],
    ]
]
LAMBDA_ELASTIC = 1.5
SHEAR_MODULUS = 1.0
RATE_STEP = 0.1
FIXED_POINT = 65536.0


def passed_along(block, axis, distance):
    devices = range(lax.axis_size(axis))
    route = [(i - distance, i) for i in devices if i - distance in devices]
    return lax.ppermute(block, axis, route)


def shape_gradients():
    grad_table = [[[0.0, 0.0, 0.0] for corner in range(8)] for quadrature in range(8)]
    point_offset = 1.0 / math.sqrt(3.0)
    for quadrature in range(8):
        natural = [
            (2 * (quadrature >> shift_bits & 1) - 1) * point_offset for shift_bits in (2, 1, 0)
        ]
        for corner in range(8):
            sign_list = [2 * (corner >> shift_bits & 1) - 1 for shift_bits in (2, 1, 0)]
            factors = [1.0 + sign_list[axis_id] * natural[axis_id] for axis_id in range(3)]
            for direction in range(3):
                others = 1.0
                for axis_id in range(3):
                    if axis_id != direction:
                        others = others * factors[axis_id]
                grad_table[quadrature][corner][direction] = (
                    2.0 * sign_list[direction] * others / 8.0
                )
    return grad_table


def rotation_table(euler_angles):
    cos_one, sin_one = (jnp.cos(euler_angles[0]), jnp.sin(euler_angles[0]))
    cos_mid, sin_mid = (jnp.cos(euler_angles[1]), jnp.sin(euler_angles[1]))
    cos_two, sin_two = (jnp.cos(euler_angles[2]), jnp.sin(euler_angles[2]))
    entries_list = [
        cos_one * cos_two - sin_one * sin_two * cos_mid,
        -cos_one * sin_two - sin_one * cos_two * cos_mid,
        sin_one * sin_mid,
        sin_one * cos_two + cos_one * sin_two * cos_mid,
        -sin_one * sin_two + cos_one * cos_two * cos_mid,
        -cos_one * sin_mid,
        sin_two * sin_mid,
        cos_two * sin_mid,
        cos_mid,
    ]
    return jnp.stack(entries_list)


def octant_sums(rotation, grain_ids):
    per_octant = grain_ids.shape[0] // 8
    pieces = []
    for octant in range(8):
        picked = jnp.take(
            rotation, grain_ids[octant * per_octant : (octant + 1) * per_octant], axis=1
        )
        pieces.append(jnp.sum(picked, axis=1))
    return jnp.concatenate(pieces, axis=0)


def corner_values(padded, layers):
    corners = []
    for corner in range(8):
        step_x, step_y, step_z = (corner >> 2 & 1, corner >> 1 & 1, corner & 1)
        block_values = padded[
            :, :, step_z : step_z + layers, step_y : step_y + GX, step_x : step_x + GX
        ]
        corners.append(block_values.reshape(3, -1))
    return jnp.stack(corners, axis=1)


def element_update(padded, layers, orient, stress_old, resistance, quad_weights):
    grad_table = jnp.asarray(shape_gradients(), dtype=jnp.float32)
    corners = corner_values(padded, layers)
    gradients = jnp.einsum("cne,qnd->cdqe", corners, grad_table, precision=lax.Precision.HIGHEST)
    strain = [
        gradients[0, 0],
        gradients[1, 1],
        gradients[2, 2],
        0.5 * (gradients[1, 2] + gradients[2, 1]),
        0.5 * (gradients[0, 2] + gradients[2, 0]),
        0.5 * (gradients[0, 1] + gradients[1, 0]),
    ]
    volume = strain[0] + strain[1] + strain[2]
    trial_stress = []
    for component in range(6):
        change = 2.0 * SHEAR_MODULUS * strain[component]
        if component < 3:
            change = change + LAMBDA_ELASTIC * volume
        trial_stress.append(stress_old[component] + change)
    frames = orient.reshape(8, 3, 3, -1)
    correction = [jnp.zeros_like(trial_stress[0]) for component in range(6)]
    for system in range(12):
        rotated_dir = [
            frames[:, row_index, 0] * float(SLIP_DIRECTIONS[system][0])
            + frames[:, row_index, 1] * float(SLIP_DIRECTIONS[system][1])
            + frames[:, row_index, 2] * float(SLIP_DIRECTIONS[system][2])
            for row_index in range(3)
        ]
        rotated_normal = [
            frames[:, row_index, 0] * float(SLIP_PLANES[system][0])
            + frames[:, row_index, 1] * float(SLIP_PLANES[system][1])
            + frames[:, row_index, 2] * float(SLIP_PLANES[system][2])
            for row_index in range(3)
        ]
        schmid = [
            rotated_dir[0] * rotated_normal[0],
            rotated_dir[1] * rotated_normal[1],
            rotated_dir[2] * rotated_normal[2],
            0.5 * (rotated_dir[1] * rotated_normal[2] + rotated_dir[2] * rotated_normal[1]),
            0.5 * (rotated_dir[0] * rotated_normal[2] + rotated_dir[2] * rotated_normal[0]),
            0.5 * (rotated_dir[0] * rotated_normal[1] + rotated_dir[1] * rotated_normal[0]),
        ]
        resolved = (
            trial_stress[0] * schmid[0]
            + trial_stress[1] * schmid[1]
            + trial_stress[2] * schmid[2]
            + 2.0
            * (
                trial_stress[3] * schmid[3]
                + trial_stress[4] * schmid[4]
                + trial_stress[5] * schmid[5]
            )
        )
        slip_ratio = resolved / resistance[system]
        slip_step = RATE_STEP * slip_ratio * jnp.abs(slip_ratio)
        correction = [
            correction[component] + slip_step * schmid[component] for component in range(6)
        ]
    updated = [
        trial_stress[component] - 2.0 * SHEAR_MODULUS * correction[component]
        for component in range(6)
    ]
    stress_new = jnp.stack(updated)
    tensor = jnp.stack(
        [
            jnp.stack([updated[0], updated[5], updated[4]]),
            jnp.stack([updated[5], updated[1], updated[3]]),
            jnp.stack([updated[4], updated[3], updated[2]]),
        ]
    )
    point_scale = quad_weights.astype(jnp.float32) * (1.0 / (FIXED_POINT * 8.0))
    element_forces = jnp.einsum(
        "cdqe,qnd->cne", tensor * point_scale, grad_table, precision=lax.Precision.HIGHEST
    )
    component_count = padded.shape[1]
    nodal = jnp.zeros((3, component_count, layers + 1, GX + 1, GX + 1), jnp.float32)
    for corner in range(8):
        step_x, step_y, step_z = (corner >> 2 & 1, corner >> 1 & 1, corner & 1)
        nodal = nodal.at[
            :, :, step_z : step_z + layers, step_y : step_y + GX, step_x : step_x + GX
        ].add(element_forces[:, corner].reshape(3, component_count, layers, GX, GX))
    return (stress_new, nodal)


def body(
    grain_ids,
    euler_angles,
    brick_active,
    brick_owner,
    brick_element,
    displacement,
    stress_old,
    resistance,
    quad_weights,
):
    groups = lax.axis_size("ca")
    members = lax.axis_size("fe")
    devices = groups * members
    bricks = grain_ids.shape[1]
    capacity = 5 * bricks // (2 * devices)
    elements = stress_old.shape[2]
    layers = displacement.shape[1]
    rotation = rotation_table(euler_angles)
    active = brick_active.astype(jnp.float32)
    octant_total = octant_sums(rotation, grain_ids) * active[None]
    owner = brick_owner[:, 0]
    onehot = (owner[:, None] == jnp.arange(devices, dtype=jnp.int32)[None]).astype(jnp.int32)
    earlier = jnp.sum(jnp.cumsum(onehot, axis=0) * onehot, axis=1) - 1
    position = owner * capacity + earlier
    send_values = jnp.zeros((72, devices * capacity), jnp.float32).at[:, position].set(octant_total)
    label_values = jnp.where(brick_active > 0, brick_element, -1).astype(jnp.float32)
    send_labels = (
        jnp.full((1, devices * capacity), -1.0, jnp.float32).at[:, position].set(label_values[None])
    )
    got_values, got_labels = (
        lax.all_to_all(
            send_values.reshape(72, devices, capacity),
            ("ca", "fe"),
            split_axis=1,
            concat_axis=1,
            tiled=True,
        ),
        lax.all_to_all(
            send_labels.reshape(1, devices, capacity),
            ("ca", "fe"),
            split_axis=1,
            concat_axis=1,
            tiled=True,
        ),
    )
    values = got_values.reshape(72, devices * capacity)
    labels = got_labels.reshape(devices * capacity).astype(jnp.int32)
    slot_index = jnp.where(labels >= 0, labels, elements)
    gathered = (
        jnp.zeros((72, elements + 1), jnp.float32).at[:, slot_index].add(values)[:, :elements]
    )
    counts = (
        jnp.zeros((elements + 1,), jnp.float32)
        .at[slot_index]
        .add((labels >= 0).astype(jnp.float32))[:elements]
    )
    orient = gathered / (8.0 * jnp.maximum(counts, 1.0))
    upper_layer = passed_along(displacement, "fe", -1)
    node_field = jnp.concatenate([displacement, upper_layer], axis=1).reshape(
        3, 1, layers + 1, GX + 1, GX + 1
    )
    stress_new, nodal = element_update(
        node_field, layers, orient, stress_old, resistance, quad_weights
    )
    nodal = nodal.reshape(3, layers + 1, (GX + 1) * (GX + 1))
    owned_forces = nodal[:, :layers]
    top_partial = nodal[:, layers:]
    from_below = passed_along(top_partial, "fe", 1)
    forces = owned_forces.at[:, :1].add(from_below)
    return (stress_new, forces)


def solution(mesh):
    placed = (
        P(None, ("ca", "fe")),
        P(),
        P(("ca", "fe")),
        P(("ca", "fe"), None),
        P(("ca", "fe")),
        P(None, ("ca", "fe"), None),
        P(None, None, ("ca", "fe")),
        P(None, None, ("ca", "fe")),
        P(None, ("ca", "fe")),
    )
    return jax.shard_map(
        body,
        mesh=mesh,
        in_specs=placed,
        out_specs=(P(None, None, ("ca", "fe")), P(None, ("ca", "fe"), None)),
        check_vma=False,
    )
```

profile of v0, /device:TPU:0, one launch (start us, length us, event | category | flops | bytes accessed | tf_op | source)
XLA Modules:
  0.0 1729.3 jit_solution(12503940195946216384)
XLA Ops:
  1.3 9.1 reduce-window.6
  13.5 8.1 scatter_custom_fusion
  22.3 7.4 all-to-all-start
  29.7 2.4 slice_cosine_fusion
  32.1 2.3 multiply_add_fusion.1
  34.4 2.9 compare_select_fusion
  37.3 3.1 compare_and_fusion
  43.3 182.1 %gather_fusion.6 = f32[55296,9]{1,0:T(8,128)} fusion(f32[9,4096]{0,1:T(8,128)S(1)} %copy.150, s32[55296]{0:T(1024)S(1)} %broadcast_clamp_fusion.1), kind=kCustom, calls=%fused_computation.6.clone | custom fusion | bytes 4202496 | tf_op jit(solution)/shard_map/jit(_take)/gather | solution.py:87
  225.4 182.0 %gather_fusion.7 = f32[55296,9]{1,0:T(8,128)} fusion(f32[9,4096]{0,1:T(8,128)S(1)} %copy.150, s32[55296]{0:T(1024)S(1)} %broadcast_clamp_fusion), kind=kCustom, calls=%fused_computation.7.clone | custom fusion | bytes 4202496 | tf_op jit(solution)/shard_map/jit(_take)/gather | solution.py:87
  408.4 182.0 %gather_fusion.4 = f32[55296,9]{1,0:T(8,128)} fusion(f32[9,4096]{0,1:T(8,128)S(1)} %copy.150, s32[55296]{0:T(1024)S(1)} %broadcast_clamp_fusion.3), kind=kCustom, calls=%fused_computation.4.clone | custom fusion | bytes 4202496 | tf_op jit(solution)/shard_map/jit(_take)/gather | solution.py:87
  591.4 182.0 %gather_fusion.5 = f32[55296,9]{1,0:T(8,128)} fusion(f32[9,4096]{0,1:T(8,128)S(1)} %copy.150, s32[55296]{0:T(1024)S(1)} %broadcast_clamp_fusion.2), kind=kCustom, calls=%fused_computation.5.clone | custom fusion | bytes 4202496 | tf_op jit(solution)/shard_map/jit(_take)/gather | solution.py:87
  774.5 182.0 %gather_fusion.2 = f32[55296,9]{1,0:T(8,128)} fusion(f32[9,4096]{0,1:T(8,128)S(1)} %copy.150, s32[55296]{0:T(1024)S(1)} %broadcast_clamp_fusion.5), kind=kCustom, calls=%fused_computation.2.clone | custom fusion | bytes 4202496 | tf_op jit(solution)/shard_map/jit(_take)/gather | solution.py:87
  956.6 182.1 %gather_fusion.3 = f32[55296,9]{1,0:T(8,128)} fusion(f32[9,4096]{0,1:T(8,128)S(1)} %copy.150, s32[55296]{0:T(1024)S(1)} %broadcast_clamp_fusion.4), kind=kCustom, calls=%fused_computation.3.clone | custom fusion | bytes 4202496 | tf_op jit(solution)/shard_map/jit(_take)/gather | solution.py:87
  1138.8 182.1 %gather_fusion = f32[55296,9]{1,0:T(8,128)} fusion(f32[9,4096]{0,1:T(8,128)S(1)} %copy.150, s32[55296]{0:T(1024)S(1)} %broadcast_clamp_fusion.7), kind=kCustom, calls=%fused_computation.clone | custom fusion | bytes 4202496 | tf_op jit(solution)/shard_map/jit(_take)/gather | solution.py:87
  1320.9 182.0 %gather_fusion.1 = f32[55296,9]{1,0:T(8,128)} fusion(f32[9,4096]{0,1:T(8,128)S(1)} %copy.150, s32[55296]{0:T(1024)S(1)} %broadcast_clamp_fusion.6), kind=kCustom, calls=%fused_computation.1.clone | custom fusion | bytes 4202496 | tf_op jit(solution)/shard_map/jit(_take)/gather | solution.py:87
  1503.0 21.0 %bitcast_reduce_fusion = (f32[9,2048]{0,1:T(8,128)S(1)}, f32[9,2048]{0,1:T(8,128)S(1)}) fusion(f32[27,2048,9]{2,1,0:T(8,128)} %bitcast.1213, pred[27,2048]{1,0:T(8,128)(4,1)S(1)} %copy-done.6, f32[27,2048,9]{2,1,0:T(8,128)} %bitcast.1212, pred[27,2048]{1,0:T(8,128)(4,1)S(1)} %copy-done.7), kind=kLoop, calls=%fused_computation.12 | loop fusion | flops 1953792 | bytes 4239360 | tf_op jit(solution)/shard_map/reduce_sum | solution.py:90
  1524.0 22.0 %bitcast_reduce_fusion.2 = (f32[9,2048]{0,1:T(8,128)S(1)}, f32[9,2048]{0,1:T(8,128)}) fusion(f32[27,2048,9]{2,1,0:T(8,128)} %bitcast.1215, pred[27,2048]{1,0:T(8,128)(4,1)S(1)} %copy-done.4, f32[27,2048,9]{2,1,0:T(8,128)} %bitcast.1214, pred[27,2048]{1,0:T(8,128)(4,1)S(1)} %copy-done.5), kind=kLoop, calls=%fused_computation.14 | loop fusion | flops 1953792 | bytes 4239360 | tf_op jit(solution)/shard_map/reduce_sum | solution.py:90
  1546.0 22.3 %bitcast_reduce_fusion.4 = (f32[9,2048]{0,1:T(8,128)}, f32[9,2048]{0,1:T(8,128)}) fusion(f32[27,2048,9]{2,1,0:T(8,128)} %bitcast.1218, pred[27,2048]{1,0:T(8,128)(4,1)S(1)} %copy-done.2, f32[27,2048,9]{2,1,0:T(8,128)} %bitcast.1216, pred[27,2048]{1,0:T(8,128)(4,1)S(1)} %copy-done.3), kind=kLoop, calls=%fused_computation.16 | loop fusion | flops 1953792 | bytes 4239360 | tf_op jit(solution)/shard_map/reduce_sum | solution.py:90
  1568.4 22.2 %bitcast_reduce_fusion.6 = (f32[9,2048]{0,1:T(8,128)}, f32[9,2048]{0,1:T(8,128)}) fusion(f32[27,2048,9]{2,1,0:T(8,128)} %bitcast.1219, pred[27,2048]{1,0:T(8,128)(4,1)S(1)} %copy-done, f32[27,2048,9]{2,1,0:T(8,128)} %bitcast.1217, pred[27,2048]{1,0:T(8,128)(4,1)S(1)} %copy-done.1), kind=kLoop, calls=%fused_computation.18 | loop fusion | flops 1953792 | bytes 4239360 | tf_op jit(solution)/shard_map/reduce_sum | solution.py:90
  1590.6 6.1 concatenate.37
  1596.7 7.9 scatter_custom_fusion.1
  1604.5 2.4 copy.158
  1607.0 5.8 all-to-all-start.1
  1614.1 13.3 collective-permute-done
  1630.5 35.8 %scatter_custom_fusion.3 = f32[226]{0:T(256)S(1)} fusion(s32[5120]{0:T(1024)S(1)} %bitcast.1229, f32[5120]{0:T(1024)S(1)} %reshape.4087, f32[]{:T(128)} %constant.341.clone.1), kind=kCustom, calls=%fused_computation.530 | custom fusion | flops 5120 | bytes 908 | tf_op jit(solution)/shard_map/scatter-add | solution.py:244
  1666.4 2.1 all-to-all-done.1
  1668.5 2.1 copy.159
  1670.6 2.9 reshape.4076
  1673.5 2.0 copy.160
  1675.5 32.1 %scatter_custom_fusion.2 = f32[72,226]{0,1:T(8,128)S(1)} fusion(s32[5120]{0:T(1024)S(1)} %bitcast.1230, f32[5120,72]{1,0:T(8,128)} %copy.160, f32[]{:T(128)} %constant.341.clone.1), kind=kCustom, calls=%fused_computation.66 | custom fusion | flops 368640 | bytes 65600 | tf_op jit(solution)/shard_map/scatter-add | solution.py:239
  1713.9 1.3 scatter-add.54
  1716.8 10.7 collective-permute-start.1
  (120 shorter events, 24.5 us)
Async XLA Ops:
  12.7 27.7 %copy-start.11 = (s32[2048,1]{0,1:T(1,128)}, s32[2048,1]{0,1:T(1,128)S(1)}, u32[]{:S(2)}) copy-start(s32[2048,1]{0,1:T(1,128)S(1)} %compare_select_fusion.10) | copy-start | bytes 24580
  22.3 1584.7 %all-to-all-start = ((f32[1,32,160]{2,0,1:T(1,128)}), f32[1,32,160]{2,0,1:T(1,128)}, u32[]{:S(2)}, u32[]{:S(2)}) async-start(f32[1,32,160]{2,0,1:T(1,128)} %reshape.3873), calls=%async_computation | async-start | bytes 65536 | tf_op jit(solution)/shard_map/all_to_all | solution.py:227
  956.6 546.4 %copy-start.6 = (pred[27,2048]{1,0:T(8,128)(4,1)S(1)}, pred[27,2048]{1,0:T(8,128)(4,1)}, u32[]{:S(2)}) copy-start(pred[27,2048]{1,0:T(8,128)(4,1)} %get-tuple-element.188) | copy-start | bytes 165892
  956.6 546.4 %copy-start.7 = (pred[27,2048]{1,0:T(8,128)(4,1)S(1)}, pred[27,2048]{1,0:T(8,128)(4,1)}, u32[]{:S(2)}) copy-start(pred[27,2048]{1,0:T(8,128)(4,1)} %get-tuple-element.189) | copy-start | bytes 165892
  1503.0 21.0 %copy-start.4 = (pred[27,2048]{1,0:T(8,128)(4,1)S(1)}, pred[27,2048]{1,0:T(8,128)(4,1)}, u32[]{:S(2)}) copy-start(pred[27,2048]{1,0:T(8,128)(4,1)} %get-tuple-element.190) | copy-start | bytes 165892
  1503.0 21.0 %copy-start.5 = (pred[27,2048]{1,0:T(8,128)(4,1)S(1)}, pred[27,2048]{1,0:T(8,128)(4,1)}, u32[]{:S(2)}) copy-start(pred[27,2048]{1,0:T(8,128)(4,1)} %get-tuple-element.191) | copy-start | bytes 165892
  1524.0 22.0 %copy-start.2 = (pred[27,2048]{1,0:T(8,128)(4,1)S(1)}, pred[27,2048]{1,0:T(8,128)(4,1)}, u32[]{:S(2)}) copy-start(pred[27,2048]{1,0:T(8,128)(4,1)} %get-tuple-element.192) | copy-start | bytes 165892
  1524.0 22.0 %copy-start.3 = (pred[27,2048]{1,0:T(8,128)(4,1)S(1)}, pred[27,2048]{1,0:T(8,128)(4,1)}, u32[]{:S(2)}) copy-start(pred[27,2048]{1,0:T(8,128)(4,1)} %get-tuple-element.193) | copy-start | bytes 165892
  1546.0 22.3 %copy-start = (pred[27,2048]{1,0:T(8,128)(4,1)S(1)}, pred[27,2048]{1,0:T(8,128)(4,1)}, u32[]{:S(2)}) copy-start(pred[27,2048]{1,0:T(8,128)(4,1)} %get-tuple-element.194) | copy-start | bytes 165892
  1546.0 22.3 %copy-start.1 = (pred[27,2048]{1,0:T(8,128)(4,1)S(1)}, pred[27,2048]{1,0:T(8,128)(4,1)}, u32[]{:S(2)}) copy-start(pred[27,2048]{1,0:T(8,128)(4,1)} %get-tuple-element.195) | copy-start | bytes 165892
  1568.3 44.4 %copy-start.13 = (f32[3,1,256]{2,1,0:T(1,128)S(1)}, f32[3,1,256]{2,1,0:T(1,128)}, u32[]{:S(2)}) copy-start(f32[3,1,256]{2,1,0:T(1,128)} %param.37) | copy-start | bytes 9220
  1568.3 45.7 %copy-start.12 = (s32[8,225]{1,0:T(8,128)S(1)}, s32[8,225]{1,0:T(8,128)}, u32[]{:S(2)}) copy-start(s32[8,225]{1,0:T(8,128)} %param.40) | copy-start | bytes 21604
  1568.3 60.0 %copy-start.9 = (f32[8,8,3,1]{1,0,2,3:T(8,128)S(1)}, f32[8,8,3,1]{1,0,2,3:T(8,128)}, u32[]{:S(2)}) copy-start(f32[8,8,3,1]{1,0,2,3:T(8,128)} %constant.366) | copy-start | bytes 2308
  1568.3 60.2 %copy-start.10 = (f32[6,8,225]{2,1,0:T(8,128)S(1)}, f32[6,8,225]{2,1,0:T(8,128)}, u32[]{:S(2)}) copy-start(f32[6,8,225]{2,1,0:T(8,128)} %param.38) | copy-start | bytes 129604
  1590.6 117.2 %copy-start.8 = (f32[12,8,225]{2,1,0:T(8,128)S(1)}, f32[12,8,225]{2,1,0:T(8,128)}, u32[]{:S(2)}) copy-start(f32[12,8,225]{2,1,0:T(8,128)} %param.39) | copy-start | bytes 259204
  1607.0 61.5 %all-to-all-start.1 = ((f32[72,32,160]{2,0,1:T(8,128)}), f32[72,32,160]{2,0,1:T(8,128)S(1)}, u32[]{:S(2)}, u32[]{:S(2)}) async-start(f32[72,32,160]{2,0,1:T(8,128)} %copy.158), calls=%async_computation.1 | async-start | bytes 4718592 | tf_op jit(solution)/shard_map/all_to_all | solution.py:220
  1612.8 14.6 collective-permute-start
  1708.3 21.0 %copy-start.14 = (f32[6,8,225]{2,1,0:T(8,128)}, f32[6,8,225]{2,1,0:T(8,128)S(1)}, u32[]{:S(2)}) copy-start(f32[6,8,225]{2,1,0:T(8,128)S(1)} %get-tuple-element.127) | copy-start | bytes 129604
  1716.8 12.0 collective-permute-start.1
where the time goes:
time: 1760 us; the launch traced here: 1730 us
  local copies, waits for them, and re-layouts  1500 us (85%)
  other arithmetic  190 us (11%)
  starting transfers between devices  25.1 us (1%)
    gather x8, local copies, waits for them, and re-layouts, octant_sums(): jnp.take(rotation, grain_ids[octant * per_octant:(octant + 1) * per_octan...  1460 us
    reduce_sum x4, other arithmetic, octant_sums(): pieces.append(jnp.sum(picked, axis=1))  87.5 us
    scatter-add x1, other arithmetic, body(): counts = jnp.zeros((elements + 1,), jnp.float32).at[slot_index].add((labe...  35.8 us
  transfers between devices with their start and end apart: 4, of which 3 were waited for; matrix products, arithmetic and copies ran while one was open for 93% of the time, Pallas kernels for 0%

commit v1 on v0

v1 whole, which is shorter than its diff:
```python
import functools
import math

import jax
import jax.numpy as jnp
from jax import lax
from jax.experimental import pallas as pl
from jax.experimental.pallas import tpu as pltpu
from jax.sharding import PartitionSpec as P

GX = 15
LANES = 128
COLUMNS = 256
ROWS = 80
QUANTUM = 32767.0

SLIP_PLANES = [
    [value / math.sqrt(3.0) for value in row]
    for row in [[1, 1, 1]] * 3 + [[-1, 1, 1]] * 3 + [[1, -1, 1]] * 3 + [[1, 1, -1]] * 3
]
SLIP_DIRECTIONS = [
    [value / math.sqrt(2.0) for value in row]
    for row in [
        [0, 1, -1],
        [1, 0, -1],
        [1, -1, 0],
        [0, 1, -1],
        [1, 0, 1],
        [1, 1, 0],
        [0, 1, 1],
        [1, 0, -1],
        [1, 1, 0],
        [0, 1, 1],
        [1, 0, 1],
        [1, -1, 0],
    ]
]
LAMBDA_ELASTIC = 1.5
SHEAR_MODULUS = 1.0
RATE_STEP = 0.1
FIXED_POINT = 65536.0


def passed_along(block, axis, distance):
    devices = range(lax.axis_size(axis))
    route = [(i - distance, i) for i in devices if i - distance in devices]
    return lax.ppermute(block, axis, route)


def shape_gradients():
    grad_table = [[[0.0, 0.0, 0.0] for corner in range(8)] for quadrature in range(8)]
    point_offset = 1.0 / math.sqrt(3.0)
    for quadrature in range(8):
        natural = [
            (2 * (quadrature >> shift_bits & 1) - 1) * point_offset for shift_bits in (2, 1, 0)
        ]
        for corner in range(8):
            sign_list = [2 * (corner >> shift_bits & 1) - 1 for shift_bits in (2, 1, 0)]
            factors = [1.0 + sign_list[axis_id] * natural[axis_id] for axis_id in range(3)]
            for direction in range(3):
                others = 1.0
                for axis_id in range(3):
                    if axis_id != direction:
                        others = others * factors[axis_id]
                grad_table[quadrature][corner][direction] = (
                    2.0 * sign_list[direction] * others / 8.0
                )
    return grad_table


def cos_sin(angle):
    square = angle * angle
    cosine = 1.0 / math.factorial(12)
    for power in (10, 8, 6, 4, 2, 0):
        cosine = cosine * square + (-1.0) ** (power // 2) / math.factorial(power)
    sine = 1.0 / math.factorial(13)
    for power in (11, 9, 7, 5, 3, 1):
        sine = sine * square + (-1.0) ** (power // 2) / math.factorial(power)
    return cosine, sine * angle


def quaternion_words(euler_ref):
    cos_one, sin_one = cos_sin(0.5 * euler_ref[0])
    cos_mid, sin_mid = cos_sin(0.5 * euler_ref[1])
    cos_two, sin_two = cos_sin(0.5 * euler_ref[2])
    quaternion = [
        cos_mid * (cos_one * cos_two - sin_one * sin_two),
        sin_mid * (cos_one * cos_two + sin_one * sin_two),
        sin_mid * (sin_one * cos_two - cos_one * sin_two),
        cos_mid * (sin_one * cos_two + cos_one * sin_two),
    ]
    whole = [jnp.round(value * QUANTUM).astype(jnp.int32) for value in quaternion]
    return [
        lax.shift_left(whole[0], 16) | (whole[1] & 0xFFFF),
        lax.shift_left(whole[2], 16) | (whole[3] & 0xFFFF),
    ]


def unpacked(word):
    upper = lax.shift_right_arithmetic(word, 16)
    lower = lax.shift_right_arithmetic(lax.shift_left(word, 16), 16)
    return upper.astype(jnp.float32), lower.astype(jnp.float32)


def looked_up(table_ref, first_row, rows, lane, bits):
    if rows == 1:
        row = jnp.broadcast_to(table_ref[pl.ds(first_row, 1), :], lane.shape)
        return jnp.take_along_axis(row, lane, axis=1, mode="promise_in_bounds")
    half = rows // 2
    level = half.bit_length() - 1
    low = looked_up(table_ref, first_row, half, lane, bits)
    high = looked_up(table_ref, first_row + half, half, lane, bits)
    return jnp.where(bits[level], high, low)


def handover_kernel(
    ids_ref, euler_ref, owner_ref, element_ref, out_ref, table_ref, tile_ref, split_ref, masked_ref
):
    per_octant = ids_ref.shape[0] // 8
    bricks = ids_ref.shape[1]
    table_rows = euler_ref.shape[1]
    owners = out_ref.shape[0]
    words = quaternion_words(euler_ref)
    table_ref[pl.ds(0, table_rows), :] = words[0]
    table_ref[pl.ds(table_rows, table_rows), :] = words[1]

    def tile_sums(tile, carry):
        lanes = pl.ds(pl.multiple_of(tile * LANES, LANES), LANES)
        tile_ref[...] = ids_ref[:, lanes]
        sums = [jnp.zeros((8, LANES), jnp.float32) for pair in range(10)]
        for cell in range(per_octant):
            ids = tile_ref[pl.ds(cell, 8, stride=per_octant), :]
            lane = ids & (LANES - 1)
            row = lax.shift_right_logical(ids, 7)
            bits = [(row & (1 << level)) != 0 for level in range(table_rows.bit_length() - 1)]
            w, x = unpacked(looked_up(table_ref, 0, table_rows, lane, bits))
            y, z = unpacked(looked_up(table_ref, table_rows, table_rows, lane, bits))
            products = [w * w, x * x, y * y, z * z, w * x, w * y, w * z, x * y, x * z, y * z]
            sums = [total + product for total, product in zip(sums, products)]
        scale = 1.0 / (QUANTUM * QUANTUM)
        ww, xx, yy, zz = [value * scale for value in sums[:4]]
        wx, wy, wz, xy, xz, yz = [value * (2.0 * scale) for value in sums[4:]]
        entries = [
            (ww - zz) + (xx - yy),
            xy - wz,
            xz + wy,
            xy + wz,
            (ww - zz) - (xx - yy),
            yz - wx,
            xz - wy,
            yz + wx,
            (ww + zz) - (xx + yy),
        ]
        stacked = jnp.concatenate(entries, axis=0)
        leading = stacked.astype(jnp.bfloat16)
        trailing = (stacked - leading.astype(jnp.float32)).astype(jnp.bfloat16)
        split_ref[:, lanes] = jnp.concatenate([leading, trailing], axis=0)
        return carry

    lax.fori_loop(0, bricks // LANES, tile_sums, 0)

    element = element_ref[...]
    column = lax.broadcasted_iota(jnp.int32, (COLUMNS, bricks), 0)
    chosen = (column == element).astype(jnp.bfloat16)
    split_rows = split_ref.shape[0]
    group = masked_ref.shape[0] // (split_rows + 16)

    def owner_group(step, carry):
        owner = owner_ref[...]
        for member in range(group):
            mask = (owner == step * group + member).astype(jnp.bfloat16)
            first = member * (split_rows + 16)
            masked_ref[pl.ds(first, split_rows), :] = split_ref[...] * mask
            masked_ref[pl.ds(first + split_rows, 16), :] = jnp.broadcast_to(mask, (16, bricks))
        product = lax.dot_general(
            masked_ref[...], chosen, (((1,), (1,)), ((), ())), preferred_element_type=jnp.float32
        )
        for member in range(group):
            first = member * (split_rows + 16)
            half = split_rows // 2
            out_ref[step * group + member, pl.ds(0, half), :] = (
                product[first : first + half] + product[first + half : first + split_rows]
            )
            out_ref[step * group + member, pl.ds(half, 8), :] = product[
                first + split_rows : first + split_rows + 8
            ]
        return carry

    lax.fori_loop(0, owners // group, owner_group, 0)


def handover(grain_ids, euler_angles, owner, element, owners):
    bricks = grain_ids.shape[1]
    table_rows = euler_angles.shape[1] // LANES
    group = 8
    return pl.pallas_call(
        handover_kernel,
        out_shape=jax.ShapeDtypeStruct((owners, ROWS, COLUMNS), jnp.float32),
        scratch_shapes=[
            pltpu.VMEM((2 * table_rows, LANES), jnp.int32),
            pltpu.VMEM((grain_ids.shape[0], LANES), jnp.int32),
            pltpu.VMEM((144, bricks), jnp.bfloat16),
            pltpu.VMEM((group * 160, bricks), jnp.bfloat16),
        ],
        compiler_params=pltpu.CompilerParams(vmem_limit_bytes=48 * 1024 * 1024),
        name="handover",
    )(grain_ids, euler_angles.reshape(3, table_rows, LANES), owner, element)


def three_parts(value):
    first = value.astype(jnp.bfloat16)
    rest = value - first.astype(jnp.float32)
    second = rest.astype(jnp.bfloat16)
    third = (rest - second.astype(jnp.float32)).astype(jnp.bfloat16)
    return first, second, third


def dot_selected(value, selector, contract):
    total = None
    for part in three_parts(value):
        term = lax.dot_general(
            part, selector, (((1,), (contract,)), ((), ())), preferred_element_type=jnp.float32
        )
        total = term if total is None else total + term
    return total


def update_kernel(
    gathered_ref,
    own_ref,
    upper_ref,
    stress_ref,
    resistance_ref,
    weights_ref,
    table_ref,
    stress_out_ref,
    nodal_ref,
):
    elements = stress_ref.shape[2]
    counts = gathered_ref[72:73, 0:elements]
    per_brick = 1.0 / (8.0 * jnp.maximum(counts, 1.0))
    frames = [gathered_ref[8 * k : 8 * k + 8, 0:elements] * per_brick for k in range(9)]

    node = lax.broadcasted_iota(jnp.int32, (COLUMNS, elements), 0)
    element = lax.broadcasted_iota(jnp.int32, (COLUMNS, elements), 1)
    base = element + element // GX
    selectors = [
        (node == base + (step_y * (GX + 1) + step_x)).astype(jnp.bfloat16)
        for step_x in range(2)
        for step_y in range(2)
    ]
    corner = lax.broadcasted_iota(jnp.int32, (24, 1), 0) & 7
    upper_corner = (corner & 1) == 1
    values = jnp.where(
        upper_corner,
        jnp.concatenate([jnp.broadcast_to(upper_ref[c], (8, COLUMNS)) for c in range(3)], axis=0),
        jnp.concatenate([jnp.broadcast_to(own_ref[c], (8, COLUMNS)) for c in range(3)], axis=0),
    )
    corners = jnp.zeros((24, elements), jnp.float32)
    for step in range(4):
        part = jnp.where(corner >> 1 == step, values, 0.0)
        corners = corners + dot_selected(part, selectors[step], 0)
    gradients = []
    for c in range(3):
        product = jnp.dot(
            table_ref[...],
            corners[8 * c : 8 * c + 8],
            precision=lax.Precision.HIGHEST,
            preferred_element_type=jnp.float32,
        )
        gradients.append([product[8 * d : 8 * d + 8] for d in range(3)])
    strain = [
        gradients[0][0],
        gradients[1][1],
        gradients[2][2],
        0.5 * (gradients[1][2] + gradients[2][1]),
        0.5 * (gradients[0][2] + gradients[2][0]),
        0.5 * (gradients[0][1] + gradients[1][0]),
    ]
    volume = strain[0] + strain[1] + strain[2]
    trial = []
    for component in range(6):
        change = 2.0 * SHEAR_MODULUS * strain[component]
        if component < 3:
            change = change + LAMBDA_ELASTIC * volume
        trial.append(stress_ref[component] + change)
    correction = [jnp.zeros_like(trial[0]) for component in range(6)]
    for system in range(12):
        rotated_dir = [
            sum(
                frames[3 * row + axis_id] * SLIP_DIRECTIONS[system][axis_id]
                for axis_id in range(3)
                if SLIP_DIRECTIONS[system][axis_id] != 0.0
            )
            for row in range(3)
        ]
        rotated_normal = [
            sum(frames[3 * row + axis_id] * SLIP_PLANES[system][axis_id] for axis_id in range(3))
            for row in range(3)
        ]
        schmid = [
            rotated_dir[0] * rotated_normal[0],
            rotated_dir[1] * rotated_normal[1],
            rotated_dir[2] * rotated_normal[2],
            0.5 * (rotated_dir[1] * rotated_normal[2] + rotated_dir[2] * rotated_normal[1]),
            0.5 * (rotated_dir[0] * rotated_normal[2] + rotated_dir[2] * rotated_normal[0]),
            0.5 * (rotated_dir[0] * rotated_normal[1] + rotated_dir[1] * rotated_normal[0]),
        ]
        resolved = (
            trial[0] * schmid[0]
            + trial[1] * schmid[1]
            + trial[2] * schmid[2]
            + 2.0 * (trial[3] * schmid[3] + trial[4] * schmid[4] + trial[5] * schmid[5])
        )
        slip_ratio = resolved / resistance_ref[system]
        slip_step = RATE_STEP * slip_ratio * jnp.abs(slip_ratio)
        correction = [
            correction[component] + slip_step * schmid[component] for component in range(6)
        ]
    updated = [
        trial[component] - 2.0 * SHEAR_MODULUS * correction[component] for component in range(6)
    ]
    for component in range(6):
        stress_out_ref[component] = updated[component]
    point_scale = weights_ref[...].astype(jnp.float32) * (1.0 / (FIXED_POINT * 8.0))
    scaled = [value * point_scale for value in updated]
    forces = []
    for rows in [(0, 5, 4), (5, 1, 3), (4, 3, 2)]:
        forces.append(
            lax.dot_general(
                table_ref[...],
                jnp.concatenate([scaled[row] for row in rows], axis=0),
                (((0,), (0,)), ((), ())),
                precision=lax.Precision.HIGHEST,
                preferred_element_type=jnp.float32,
            )
        )
    forces = jnp.concatenate(forces, axis=0)
    nodal = jnp.zeros((24, COLUMNS), jnp.float32)
    for step in range(4):
        part = jnp.where(corner >> 1 == step, forces, 0.0)
        nodal = nodal + dot_selected(part, selectors[step], 1)
    lower = jnp.where(upper_corner, 0.0, nodal)
    above = jnp.where(upper_corner, nodal, 0.0)
    for c in range(3):
        nodal_ref[0, c] = jnp.sum(lower[8 * c : 8 * c + 8], axis=0, keepdims=True)
        nodal_ref[1, c] = jnp.sum(above[8 * c : 8 * c + 8], axis=0, keepdims=True)


def element_update(gathered, own, upper, stress_old, resistance, quad_weights):
    grad_table = shape_gradients()
    table = jnp.asarray(
        [
            [grad_table[quadrature][corner][direction] for corner in range(8)]
            for direction in range(3)
            for quadrature in range(8)
        ],
        dtype=jnp.float32,
    )
    return pl.pallas_call(
        update_kernel,
        out_shape=(
            jax.ShapeDtypeStruct(stress_old.shape, jnp.float32),
            jax.ShapeDtypeStruct((2,) + own.shape, jnp.float32),
        ),
        compiler_params=pltpu.CompilerParams(vmem_limit_bytes=32 * 1024 * 1024),
        name="stress_update",
    )(gathered, own, upper, stress_old, resistance, quad_weights, table)


def body(
    grain_ids,
    euler_angles,
    brick_active,
    brick_owner,
    brick_element,
    displacement,
    stress_old,
    resistance,
    quad_weights,
):
    devices = lax.axis_size("ca") * lax.axis_size("fe")
    bricks = grain_ids.shape[1]
    upper_layer = passed_along(displacement, "fe", -1)
    owner = jnp.where(brick_active > 0, brick_owner[:, 0], -1).reshape(1, bricks)
    partial = handover(grain_ids, euler_angles, owner, brick_element.reshape(1, bricks), devices)
    gathered = lax.psum_scatter(partial, ("ca", "fe"), scatter_dimension=0)
    stress_new, nodal = element_update(
        gathered, displacement, upper_layer, stress_old, resistance, quad_weights
    )
    forces = nodal[0] + passed_along(nodal[1], "fe", 1)
    return (stress_new, forces)


def solution(mesh):
    placed = (
        P(None, ("ca", "fe")),
        P(),
        P(("ca", "fe")),
        P(("ca", "fe"), None),
        P(("ca", "fe")),
        P(None, ("ca", "fe"), None),
        P(None, None, ("ca", "fe")),
        P(None, None, ("ca", "fe")),
        P(None, ("ca", "fe")),
    )
    return jax.shard_map(
        body,
        mesh=mesh,
        in_specs=placed,
        out_specs=(P(None, None, ("ca", "fe")), P(None, ("ca", "fe"), None)),
        check_vma=False,
    )
```

time: 1760 us -> 208 us (0.12); the launches traced: 1730 us -> 207 us
  local copies, waits for them, and re-layouts: 1500 us -> 3.92 us
  other arithmetic: 190 us -> 1.3 us
  waiting for transfers between devices: 16.7 us -> 142 us
  Pallas kernels: 0 us -> 43.4 us
  starting transfers between devices: 25.1 us -> 2.62 us
    gather x8 -> x0, local copies, waits for them, and re-layouts: 1460 us -> none  [octant_sums(): jnp.take(rotation, grain_ids[octant * per_octant:(octant + 1) * per_octan...]
    reduce_scatter x0 -> x1, waiting for transfers between devices: none -> 136 us  [body(): gathered = lax.psum_scatter(partial, ('ca', 'fe'), scatter_dimension=0)]
    reduce_sum x5 -> x0, other arithmetic: 88.3 us -> none  [the longest x4 87.5 us: octant_sums(): pieces.append(jnp.sum(picked, axis=1))]
    scatter-add x2 -> x0, other arithmetic: 67.9 us -> none  [the longest x1 35.8 us: body(): counts = jnp.zeros((elements + 1,), jnp.float32).at[slot_index].add((labe...]
    pallas_call x0 -> x2, Pallas kernels: none -> 43.4 us  [the longest x1 41.7 us: handover(): pl.pallas_call(handover_kernel, out_shape=jax.ShapeDtypeStruct((owners, R...]
  transfers between devices with their start and end apart: 4 -> 3, of which waited for: 3 -> 3; matrix products, arithmetic and copies ran while one was open for 93% -> 0% of each run, Pallas kernels for 0% -> 0%
where the time goes in v1:
time: 208 us; the launch traced here: 207 us
  waiting for transfers between devices  142 us (68%)
  Pallas kernels  43.4 us (21%)
  between operations  14.1 us (7%)
  local copies, waits for them, and re-layouts  3.92 us (2%)
  starting transfers between devices  2.62 us (1%)
    reduce_scatter x1, waiting for transfers between devices, body(): gathered = lax.psum_scatter(partial, ('ca', 'fe'), scatter_dimension=0)  136 us
    pallas_call x1, Pallas kernels, handover(): pl.pallas_call(handover_kernel, out_shape=jax.ShapeDtypeStruct((owners, R...  41.7 us
    ppermute x2, waiting for transfers between devices, passed_along(): return lax.ppermute(block, axis, route)  6.42 us
  transfers between devices with their start and end apart: 3, of which 3 were waited for; matrix products, arithmetic and copies ran while one was open for 0% of the time, Pallas kernels for 0%

profile of v1, /device:TPU:0, one launch (start us, length us, event | category | flops | bytes accessed | tf_op | source)
XLA Modules:
  0.0 207.4 jit_solution(3519094908389706800)
XLA Ops:
  7.2 0.0 reduce-scatter.2.cloned.1.call-start
  7.2 0.8 copy.14
  8.1 0.7 compare_select_fusion
  8.8 0.0 copy-start
  8.8 1.5 copy-done
  10.2 0.0 copy-start.5
  10.2 0.7 copy-done.5
  10.9 0.0 copy-start.7
  10.9 0.0 copy-start.1
  10.9 0.0 copy-start.3
  11.0 0.0 copy-start.4
  11.0 0.0 copy-start.6
  11.0 41.7 %handover.1 = f32[32,80,256]{2,1,0:T(8,128)} custom-call(s32[216,2048]{1,0:T(8,128)S(1)} %copy-done, f32[3,32,128]{2,1,0:T(8,128)S(1)} %bitcast.12, s32[1,2048]{1,0:T(1,128)S(1)} %bitcast.14, s32[1,2048]{1,0:T(1,128)S(1)} %bitcast.15), custom_call_target="tpu_custom_call" | custom-call | tf_op jit(solution)/shard_map/handover/pallas_call | solution.py:196
  52.7 0.0 reduce-scatter.2.cloned.1.call-update
  52.7 0.0 copy-done.7
  52.7 1.3 collective-permute-start
  54.0 5.1 %collective-permute-done.upper_ref = f32[3,1,256]{2,1,0:T(1,128)S(1)} collective-permute-done((f32[3,1,256]{2,1,0:T(1,128)S(1)}, f32[3,1,256]{2,1,0:T(1,128)S(1)}, u32[]{:S(2)}, u32[]{:S(2)}) %collective-permute-start) | collective-permute-done | bytes 3104 | tf_op jit(solution)/shard_map/ppermute | solution.py:47
  59.1 135.7 %reduce-scatter.2.cloned.1.call-done = f32[1,80,256]{2,1,0:T(8,128)} async-done(((f32[32,80,256]{2,1,0:T(8,128)}), f32[1,80,256]{2,1,0:T(8,128)}) %reduce-scatter.2.cloned.1.call-update) | async-done | bytes 81936 | tf_op jit(solution)/shard_map/reduce_scatter | solution.py:387
  194.8 0.0 copy-done.1
  194.8 0.0 copy-done.3
  194.8 0.0 copy-done.4
  194.8 0.0 copy-done.6
  194.8 0.0 copy-start.2
  194.8 0.9 copy-done.2
  195.7 1.7 stress_update.1
  197.4 1.3 collective-permute-start.1
  198.7 1.3 collective-permute-done.1
  200.0 0.6 bitcast_add_fusion
  (1 shorter events, 0.0 us)
Async XLA Ops:
  7.2 187.6 %reduce-scatter.2.cloned.1.call-start = ((), (), s32[]{:S(2)}) async-start(), calls=%async_computation.1 | async-start | bytes 2703360 | tf_op jit(solution)/shard_map/reduce_scatter | solution.py:387
  8.8 1.5 copy-start
  10.2 0.7 copy-start.5
  10.9 41.8 %copy-start.7 = (f32[3,1,256]{2,1,0:T(1,128)S(1)}, f32[3,1,256]{2,1,0:T(1,128)}, u32[]{:S(2)}) copy-start(f32[3,1,256]{2,1,0:T(1,128)} %own_ref.1) | copy-start | bytes 9220
  10.9 183.9 %copy-start.1 = (f32[12,8,225]{2,1,0:T(8,128)S(1)}, f32[12,8,225]{2,1,0:T(8,128)}, u32[]{:S(2)}) copy-start(f32[12,8,225]{2,1,0:T(8,128)} %resistance_ref.1) | copy-start | bytes 259204
  10.9 183.9 %copy-start.3 = (f32[6,8,225]{2,1,0:T(8,128)S(1)}, f32[6,8,225]{2,1,0:T(8,128)}, u32[]{:S(2)}) copy-start(f32[6,8,225]{2,1,0:T(8,128)} %stress_ref.1) | copy-start | bytes 129604
  11.0 183.9 %copy-start.4 = (f32[24,8]{1,0:T(8,128)S(1)}, f32[24,8]{1,0:T(8,128)}, u32[]{:S(2)}) copy-start(f32[24,8]{1,0:T(8,128)} %constant.6.clone.table_ref) | copy-start | bytes 2308
  11.0 183.9 %copy-start.6 = (s32[8,225]{1,0:T(8,128)S(1)}, s32[8,225]{1,0:T(8,128)}, u32[]{:S(2)}) copy-start(s32[8,225]{1,0:T(8,128)} %weights_ref.1) | copy-start | bytes 21604
  52.7 6.4 %collective-permute-start = (f32[3,1,256]{2,1,0:T(1,128)S(1)}, f32[3,1,256]{2,1,0:T(1,128)S(1)}, u32[]{:S(2)}, u32[]{:S(2)}) collective-permute-start(f32[3,1,256]{2,1,0:T(1,128)S(1)} %copy-done.7), channel_id=1, source_target_pairs={{1,0},{2,1},{3,2},{4,3},{5,4},{6,5},{7,6},{9,8},{10,9},{11,10},{12... | collective-permute-start | bytes 9224 | tf_op jit(solution)/shard_map/ppermute | solution.py:47
  194.8 0.9 copy-start.2
  197.4 2.6 %collective-permute-start.1 = (f32[3,1,256]{2,1,0:T(1,128)S(1)}, f32[3,1,256]{2,1,0:T(1,128)S(1)}, u32[]{:S(2)}, u32[]{:S(2)}) collective-permute-start(f32[3,1,256]{2,1,0:T(1,128)S(1)} %slice_bitcast_fusion), channel_id=1, source_target_pairs={{0,1},{1,2},{2,3},{3,4},{4,5},{5,6},{6,7},{8,9},{9,10},{10,11},{11... | collective-permute-start | bytes 9224 | tf_op jit(solution)/shard_map/ppermute | solution.py:47
Sparse Core Ops, SparseCore 0:
  52.8 141.9 reduce-scatter.1

commit v2 on v1

--- a/solution.py
+++ b/solution.py
@@ -11,8 +11,10 @@
 GX = 15
 LANES = 128
 COLUMNS = 256
-ROWS = 80
-QUANTUM = 32767.0
+ROWS = 72
+COUNT_SPAN = 31
+SPARE = 11
+QUANTUM = float((1 << 20) - 1)
 
 SLIP_PLANES = [
     [value / math.sqrt(3.0) for value in row]
@@ -79,27 +81,37 @@
     return cosine, sine * angle
 
 
-def quaternion_words(euler_ref):
+def rotation_words(euler_ref):
     cos_one, sin_one = cos_sin(0.5 * euler_ref[0])
     cos_mid, sin_mid = cos_sin(0.5 * euler_ref[1])
     cos_two, sin_two = cos_sin(0.5 * euler_ref[2])
-    quaternion = [
-        cos_mid * (cos_one * cos_two - sin_one * sin_two),
-        sin_mid * (cos_one * cos_two + sin_one * sin_two),
-        sin_mid * (sin_one * cos_two - cos_one * sin_two),
-        cos_mid * (sin_one * cos_two + cos_one * sin_two),
-    ]
-    whole = [jnp.round(value * QUANTUM).astype(jnp.int32) for value in quaternion]
+    w = cos_mid * (cos_one * cos_two - sin_one * sin_two)
+    factor = jnp.where(w < 0.0, -QUANTUM, QUANTUM) / (1.0 + jnp.abs(w))
+    x = sin_mid * (cos_one * cos_two + sin_one * sin_two) * factor
+    y = sin_mid * (sin_one * cos_two - cos_one * sin_two) * factor
+    z = cos_mid * (sin_one * cos_two + cos_one * sin_two) * factor
+    x, y, z = [
+        jnp.clip(jnp.round(value), -QUANTUM, QUANTUM).astype(jnp.int32) for value in (x, y, z)
+    ]
+    low = (1 << SPARE) - 1
     return [
-        lax.shift_left(whole[0], 16) | (whole[1] & 0xFFFF),
-        lax.shift_left(whole[2], 16) | (whole[3] & 0xFFFF),
-    ]
-
-
-def unpacked(word):
-    upper = lax.shift_right_arithmetic(word, 16)
-    lower = lax.shift_right_arithmetic(lax.shift_left(word, 16), 16)
-    return upper.astype(jnp.float32), lower.astype(jnp.float32)
+        lax.shift_left(x, SPARE) | (lax.shift_right_arithmetic(z, SPARE) & low),
+        lax.shift_left(y, SPARE) | (z & low),
+    ]
+
+
+def rotation_products(first, second):
+    x = lax.shift_right_arithmetic(first, SPARE).astype(jnp.float32)
+    y = lax.shift_right_arithmetic(second, SPARE).astype(jnp.float32)
+    z = (
+        lax.shift_right_arithmetic(lax.shift_left(first, 32 - SPARE), 32 - 2 * SPARE)
+        | (second & ((1 << SPARE) - 1))
+    ).astype(jnp.float32)
+    square = x * x + y * y + z * z
+    scale = 2.0 / (1.0 + square * (1.0 / (QUANTUM * QUANTUM)))
+    w = scale - 1.0
+    x, y, z = x * scale, y * scale, z * scale
+    return [x * x, y * y, z * z, x * y, x * z, y * z, w * x, w * y, w * z]
 
 
 def looked_up(table_ref, first_row, rows, lane, bits):
@@ -113,98 +125,128 @@
     return jnp.where(bits[level], high, low)
 
 
+def count_row(element):
+    return lax.shift_right_logical(element * (65536 // COUNT_SPAN + 1), 16)
+
+
 def handover_kernel(
-    ids_ref, euler_ref, owner_ref, element_ref, out_ref, table_ref, tile_ref, split_ref, masked_ref
+    ids_ref,
+    euler_ref,
+    place_ref,
+    element_ref,
+    keep_ref,
+    send_ref,
+    table_ref,
+    tile_ref,
+    split_ref,
+    masked_ref,
 ):
     per_octant = ids_ref.shape[0] // 8
     bricks = ids_ref.shape[1]
     table_rows = euler_ref.shape[1]
-    owners = out_ref.shape[0]
-    words = quaternion_words(euler_ref)
+    half_places = keep_ref.shape[0]
+    words = rotation_words(euler_ref)
     table_ref[pl.ds(0, table_rows), :] = words[0]
     table_ref[pl.ds(table_rows, table_rows), :] = words[1]
 
     def tile_sums(tile, carry):
         lanes = pl.ds(pl.multiple_of(tile * LANES, LANES), LANES)
         tile_ref[...] = ids_ref[:, lanes]
-        sums = [jnp.zeros((8, LANES), jnp.float32) for pair in range(10)]
+        sums = [jnp.zeros((8, LANES), jnp.float32) for pair in range(9)]
         for cell in range(per_octant):
             ids = tile_ref[pl.ds(cell, 8, stride=per_octant), :]
             lane = ids & (LANES - 1)
             row = lax.shift_right_logical(ids, 7)
             bits = [(row & (1 << level)) != 0 for level in range(table_rows.bit_length() - 1)]
-            w, x = unpacked(looked_up(table_ref, 0, table_rows, lane, bits))
-            y, z = unpacked(looked_up(table_ref, table_rows, table_rows, lane, bits))
-            products = [w * w, x * x, y * y, z * z, w * x, w * y, w * z, x * y, x * z, y * z]
-            sums = [total + product for total, product in zip(sums, products)]
-        scale = 1.0 / (QUANTUM * QUANTUM)
-        ww, xx, yy, zz = [value * scale for value in sums[:4]]
-        wx, wy, wz, xy, xz, yz = [value * (2.0 * scale) for value in sums[4:]]
+            first = looked_up(table_ref, 0, table_rows, lane, bits)
+            second = looked_up(table_ref, table_rows, table_rows, lane, bits)
+            sums = [
+                total + product
+                for total, product in zip(sums, rotation_products(first, second))
+            ]
+        vector = 2.0 / (QUANTUM * QUANTUM)
+        xx, yy, zz, xy, xz, yz = [value * vector for value in sums[:6]]
+        wx, wy, wz = [value * (2.0 / QUANTUM) for value in sums[6:]]
         entries = [
-            (ww - zz) + (xx - yy),
+            per_octant - (yy + zz),
             xy - wz,
             xz + wy,
             xy + wz,
-            (ww - zz) - (xx - yy),
+            per_octant - (xx + zz),
             yz - wx,
             xz - wy,
             yz + wx,
-            (ww + zz) - (xx + yy),
+            per_octant - (xx + yy),
         ]
         stacked = jnp.concatenate(entries, axis=0)
         leading = stacked.astype(jnp.bfloat16)
         trailing = (stacked - leading.astype(jnp.float32)).astype(jnp.bfloat16)
-        split_ref[:, lanes] = jnp.concatenate([leading, trailing], axis=0)
+        split_ref[pl.ds(0, 2 * ROWS), lanes] = jnp.concatenate([leading, trailing], axis=0)
         return carry
 
     lax.fori_loop(0, bricks // LANES, tile_sums, 0)
 
     element = element_ref[...]
     column = lax.broadcasted_iota(jnp.int32, (COLUMNS, bricks), 0)
-    chosen = (column == element).astype(jnp.bfloat16)
+    row_of = count_row(element)
+    chosen = (
+        (column == element) | (column == element - row_of * COUNT_SPAN + (COLUMNS - COUNT_SPAN))
+    ).astype(jnp.bfloat16)
+    split_ref[pl.ds(2 * ROWS, 16), :] = (
+        lax.broadcasted_iota(jnp.int32, (16, bricks), 0) == row_of
+    ).astype(jnp.bfloat16)
     split_rows = split_ref.shape[0]
-    group = masked_ref.shape[0] // (split_rows + 16)
-
-    def owner_group(step, carry):
-        owner = owner_ref[...]
-        for member in range(group):
-            mask = (owner == step * group + member).astype(jnp.bfloat16)
-            first = member * (split_rows + 16)
-            masked_ref[pl.ds(first, split_rows), :] = split_ref[...] * mask
-            masked_ref[pl.ds(first + split_rows, 16), :] = jnp.broadcast_to(mask, (16, bricks))
-        product = lax.dot_general(
-            masked_ref[...], chosen, (((1,), (1,)), ((), ())), preferred_element_type=jnp.float32
-        )
-        for member in range(group):
-            first = member * (split_rows + 16)
-            half = split_rows // 2
-            out_ref[step * group + member, pl.ds(0, half), :] = (
-                product[first : first + half] + product[first + half : first + split_rows]
+    group = masked_ref.shape[0] // split_rows
+    in_counts = lax.broadcasted_iota(jnp.int32, (8, COLUMNS), 1) >= COLUMNS - COUNT_SPAN
+
+    for base, out_ref in ((0, keep_ref), (half_places, send_ref)):
+
+        def place_group(step, carry):
+            place = place_ref[...] - base
+            for member in range(group):
+                mask = (place == step * group + member).astype(jnp.bfloat16)
+                masked_ref[pl.ds(member * split_rows, split_rows), :] = split_ref[...] * mask
+            product = lax.dot_general(
+                masked_ref[...],
+                chosen,
+                (((1,), (1,)), ((), ())),
+                preferred_element_type=jnp.float32,
             )
-            out_ref[step * group + member, pl.ds(half, 8), :] = product[
-                first + split_rows : first + split_rows + 8
-            ]
-        return carry
-
-    lax.fori_loop(0, owners // group, owner_group, 0)
-
-
-def handover(grain_ids, euler_angles, owner, element, owners):
+            for member in range(group):
+                first = member * split_rows
+                total = product[first : first + ROWS] + product[first + ROWS : first + 2 * ROWS]
+                counts = product[first + 2 * ROWS : first + 2 * ROWS + 8]
+                out_ref[step * group + member, pl.ds(0, 8), :] = jnp.where(
+                    in_counts, counts, total[:8]
+                )
+                out_ref[step * group + member, pl.ds(8, ROWS - 8), :] = total[8:]
+            return carry
+
+        lax.fori_loop(0, half_places // group, place_group, 0)
+
+
+def handover(grain_ids, euler_angles, place, element, places):
     bricks = grain_ids.shape[1]
     table_rows = euler_angles.shape[1] // LANES
     group = 8
+    half = jax.ShapeDtypeStruct((places // 2, ROWS, COLUMNS), jnp.float32)
     return pl.pallas_call(
         handover_kernel,
-        out_shape=jax.ShapeDtypeStruct((owners, ROWS, COLUMNS), jnp.float32),
+        out_shape=(half, half),
         scratch_shapes=[
             pltpu.VMEM((2 * table_rows, LANES), jnp.int32),
             pltpu.VMEM((grain_ids.shape[0], LANES), jnp.int32),
-            pltpu.VMEM((144, bricks), jnp.bfloat16),
-            pltpu.VMEM((group * 160, bricks), jnp.bfloat16),
+            pltpu.VMEM((2 * ROWS + 16, bricks), jnp.bfloat16),
+            pltpu.VMEM((group * (2 * ROWS + 16), bricks), jnp.bfloat16),
         ],
         compiler_params=pltpu.CompilerParams(vmem_limit_bytes=48 * 1024 * 1024),
+        cost_estimate=pl.CostEstimate(
+            flops=2 * 160 * places * bricks * COLUMNS,
+            bytes_accessed=100 * 1024 * 1024,
+            transcendentals=0,
+        ),
         name="handover",
-    )(grain_ids, euler_angles.reshape(3, table_rows, LANES), owner, element)
+    )(grain_ids, euler_angles.reshape(3, table_rows, LANES), place, element)
 
 
 def three_parts(value):
@@ -237,9 +279,21 @@
     nodal_ref,
 ):
     elements = stress_ref.shape[2]
-    counts = gathered_ref[72:73, 0:elements]
+    gathered = gathered_ref[0]
+    for source in range(1, gathered_ref.shape[0]):
+        gathered = gathered + gathered_ref[source]
+    element_row = lax.broadcasted_iota(jnp.int32, (8, elements), 1)
+    count_at = lax.broadcasted_iota(jnp.int32, (COLUMNS, elements), 1)
+    count_at = count_at - count_row(count_at) * COUNT_SPAN + (COLUMNS - COUNT_SPAN)
+    spread = dot_selected(
+        gathered[:8],
+        (lax.broadcasted_iota(jnp.int32, (COLUMNS, elements), 0) == count_at).astype(jnp.bfloat16),
+        0,
+    )
+    in_row = count_row(element_row) == lax.broadcasted_iota(jnp.int32, (8, elements), 0)
+    counts = jnp.sum(jnp.where(in_row, spread, 0.0), axis=0, keepdims=True)
     per_brick = 1.0 / (8.0 * jnp.maximum(counts, 1.0))
-    frames = [gathered_ref[8 * k : 8 * k + 8, 0:elements] * per_brick for k in range(9)]
+    frames = [gathered[8 * k : 8 * k + 8, 0:elements] * per_brick for k in range(9)]
 
     node = lax.broadcasted_iota(jnp.int32, (COLUMNS, elements), 0)
     element = lax.broadcasted_iota(jnp.int32, (COLUMNS, elements), 1)
@@ -379,12 +433,25 @@
     resistance,
     quad_weights,
 ):
-    devices = lax.axis_size("ca") * lax.axis_size("fe")
+    groups, members = lax.axis_size("ca"), lax.axis_size("fe")
     bricks = grain_ids.shape[1]
     upper_layer = passed_along(displacement, "fe", -1)
-    owner = jnp.where(brick_active > 0, brick_owner[:, 0], -1).reshape(1, bricks)
-    partial = handover(grain_ids, euler_angles, owner, brick_element.reshape(1, bricks), devices)
-    gathered = lax.psum_scatter(partial, ("ca", "fe"), scatter_dimension=0)
+    owner = brick_owner[:, 0]
+    owner_ca, owner_fe = owner // members, owner % members
+    other_core = (owner_ca + lax.axis_index("ca")) & 1
+    place = ((other_core * (groups // 2) + owner_ca // 2) * members) + owner_fe
+    place = jnp.where(brick_active > 0, place, -1).reshape(1, bricks)
+    keep, send = handover(
+        grain_ids, euler_angles, place, brick_element.reshape(1, bricks), groups * members
+    )
+    keep = keep + lax.ppermute(send, "ca", [(i, i ^ 1) for i in range(groups)])
+    same_core = [
+        [(2 * pair + core) * members + member for pair in range(groups // 2) for member in range(members)]
+        for core in range(2)
+    ]
+    gathered = lax.all_to_all(
+        keep, ("ca", "fe"), split_axis=0, concat_axis=0, axis_index_groups=same_core, tiled=True
+    )
     stress_new, nodal = element_update(
         gathered, displacement, upper_layer, stress_old, resistance, quad_weights
     )

time: 208 us -> 94.5 us (0.45)
  waiting for transfers between devices: 142 us -> 31.8 us
  between operations: 14.1 us -> 0.73 us
  starting transfers between devices: 2.62 us -> 12.5 us
    reduce_scatter x1 -> x0, waiting for transfers between devices: 136 us -> none  [body(): gathered = lax.psum_scatter(partial, ('ca', 'fe'), scatter_dimension=0)]
    all_to_all x0 -> x1, waiting for transfers between devices: none -> 23.6 us  [body(): lax.all_to_all(keep, ('ca', 'fe'), split_axis=0, concat_axis=0, axis_inde...]
    all_to_all x0 -> x1, starting transfers between devices: none -> 8.38 us  [body(): lax.all_to_all(keep, ('ca', 'fe'), split_axis=0, concat_axis=0, axis_inde...]
    ppermute x0 -> x1, waiting for transfers between devices: none -> 2.47 us  [body(): keep = keep + lax.ppermute(send, 'ca', [(i, i ^ 1) for i in range(groups)])]
  transfers between devices with their start and end apart: 3 -> 4, of which waited for: 3 -> 4; matrix products, arithmetic and copies ran while one was open for 0% -> 0% of each run, Pallas kernels for 0% -> 0%
where the time goes in v2:
time: 94.5 us; the launch traced here: 93 us
  Pallas kernels  42.5 us (45%)
  waiting for transfers between devices  31.8 us (34%)
  starting transfers between devices  12.5 us (13%)
  local copies, waits for them, and re-layouts  3.04 us (3%)
  other arithmetic  2.5 us (3%)
    pallas_call x1, Pallas kernels, handover(): pl.pallas_call(handover_kernel, out_shape=(half, half), scratch_shapes=[p...  40.8 us
    all_to_all x1, waiting for transfers between devices, body(): lax.all_to_all(keep, ('ca', 'fe'), split_axis=0, concat_axis=0, axis_inde...  23.6 us
    all_to_all x1, starting transfers between devices, body(): lax.all_to_all(keep, ('ca', 'fe'), split_axis=0, concat_axis=0, axis_inde...  8.38 us
    ppermute x2, waiting for transfers between devices, passed_along(): return lax.ppermute(block, axis, route)  5.77 us
    ppermute x2, starting transfers between devices, passed_along(): return lax.ppermute(block, axis, route)  3.57 us
    unnamed x15, local copies, waits for them, and re-layouts  3.03 us
    ppermute x1, waiting for transfers between devices, body(): keep = keep + lax.ppermute(send, 'ca', [(i, i ^ 1) for i in range(groups)])  2.47 us
  transfers between devices with their start and end apart: 4, of which 4 were waited for; matrix products, arithmetic and copies ran while one was open for 0% of the time, Pallas kernels for 0%

profile of v2, /device:TPU:0, one launch (start us, length us, event | category | flops | bytes accessed | tf_op | source)
XLA Modules:
  0.0 93.0 jit_solution(1147592591153295709)
XLA Ops:
  0.6 0.8 copy.14
  1.5 0.7 fusion.4
  2.2 0.0 copy-start.5
  2.2 1.5 %copy-done.5 = s32[216,2048]{1,0:T(8,128)S(1)} copy-done((s32[216,2048]{1,0:T(8,128)S(1)}, s32[216,2048]{1,0:T(8,128)}, u32[]{:S(2)}) %copy-start.5) | copy-done | bytes 1769496
  3.7 0.0 copy-start.6
  3.7 0.7 copy-done.6
  4.4 40.8 %handover.1 = (f32[16,72,256]{2,1,0:T(8,128)S(1)}, f32[16,72,256]{2,1,0:T(8,128)S(1)}) custom-call(s32[216,2048]{1,0:T(8,128)S(1)} %copy-done.5, f32[3,32,128]{2,1,0:T(8,128)S(1)} %bitcast.11, s32[1,2048]{1,0:T(1,128)S(1)} %bitcast.12, s32[1,2048]{1,0:T(1,128)S(1)} %bitcast.13), custom_call_target="tpu_custom_call" | custom-call | flops 5368709120 | bytes 104857600 | tf_op jit(solution)/shard_map/handover/pallas_call | solution.py:233
  45.2 0.5 collective-permute-start
  45.7 2.5 %collective-permute-done = f32[16,72,256]{2,1,0:T(8,128)S(1)} collective-permute-done((f32[16,72,256]{2,1,0:T(8,128)S(1)}, f32[16,72,256]{2,1,0:T(8,128)S(1)}, u32[]{:S(2)}, u32[]{:S(2)}) %collective-permute-start) | collective-permute-done | bytes 1179680 | tf_op jit(solution)/shard_map/ppermute | solution.py:447
  48.2 1.2 %add.31 = f32[16,72,256]{2,1,0:T(8,128)} add(f32[16,72,256]{2,1,0:T(8,128)S(1)} %get-tuple-element.6, f32[16,72,256]{2,1,0:T(8,128)S(1)} %collective-permute-done) | non-fusion elementwise | flops 294912 | bytes 3538944 | tf_op jit(solution)/shard_map/add | solution.py:447
  49.4 0.0 copy-start.4
  49.4 0.0 copy-start
  49.4 0.0 copy-start.1
  49.4 0.0 copy-start.2
  49.4 0.0 copy-start.3
  49.4 8.4 %all-to-all-start = ((f32[16,72,256]{2,1,0:T(8,128)}), f32[16,72,256]{2,1,0:T(8,128)S(1)}, u32[]{:S(2)}, u32[]{:S(2)}) async-start(f32[16,72,256]{2,1,0:T(8,128)} %add.31), calls=%async_computation | async-start | bytes 2359296 | tf_op jit(solution)/shard_map/all_to_all | solution.py:452
  57.8 0.0 copy-done.4
  57.8 1.3 %collective-permute-start.1 = (f32[3,1,256]{2,1,0:T(1,128)S(1)}, f32[3,1,256]{2,1,0:T(1,128)S(1)}, u32[]{:S(2)}, u32[]{:S(2)}) collective-permute-start(f32[3,1,256]{2,1,0:T(1,128)S(1)} %copy-done.4), channel_id=1, source_target_pairs={{1,0},{2,1},{3,2},{4,3},{5,4},{6,5},{7,6},{9,8},{10,9},{11,10},{12... | collective-permute-start | bytes 9224 | tf_op jit(solution)/shard_map/ppermute | solution.py:49
  59.1 4.5 %collective-permute-done.1.upper_ref = f32[3,1,256]{2,1,0:T(1,128)S(1)} collective-permute-done((f32[3,1,256]{2,1,0:T(1,128)S(1)}, f32[3,1,256]{2,1,0:T(1,128)S(1)}, u32[]{:S(2)}, u32[]{:S(2)}) %collective-permute-start.1) | collective-permute-done | bytes 3104 | tf_op jit(solution)/shard_map/ppermute | solution.py:49
  63.6 23.6 %all-to-all-done.gathered_ref = f32[16,72,256]{2,1,0:T(8,128)S(1)} async-done(((f32[16,72,256]{2,1,0:T(8,128)}), f32[16,72,256]{2,1,0:T(8,128)S(1)}, u32[]{:S(2)}, u32[]{:S(2)}) %all-to-all-start) | async-done | bytes 1179680 | tf_op jit(solution)/shard_map/all_to_all | solution.py:452
  87.1 0.0 copy-done
  87.1 0.0 copy-done.1
  87.1 0.0 copy-done.2
  87.2 0.0 copy-done.3
  87.2 1.7 %stress_update.1 = (f32[6,8,225]{2,1,0:T(8,128)}, f32[2,3,1,256]{3,2,1,0:T(1,128)S(1)}) custom-call(f32[16,72,256]{2,1,0:T(8,128)S(1)} %all-to-all-done.gathered_ref, f32[3,1,256]{2,1,0:T(1,128)S(1)} %copy-done.4, f32[3,1,256]{2,1,0:T(1,128)S(1)} %collective-permute-done.1.upper_ref, f32[6,8,225]{2,1,0:T(8,128)S(1)} %copy-done.1, f32[12,8,225]{2,1,0:T(8,128)S(1)} %copy-done, ...), custom_call_target="tpu_custom_call" | custom-call | tf_op jit(solution)/shard_map/stress_update/pallas_call | solution.py:414
  88.8 2.3 %collective-permute-start.2 = (f32[3,1,256]{2,1,0:T(1,128)S(1)}, f32[3,1,256]{2,1,0:T(1,128)S(1)}, u32[]{:S(2)}, u32[]{:S(2)}) collective-permute-start(f32[3,1,256]{2,1,0:T(1,128)S(1)} %slice_bitcast_fusion), channel_id=1, source_target_pairs={{0,1},{1,2},{2,3},{3,4},{4,5},{5,6},{6,7},{8,9},{9,10},{10,11},{11... | collective-permute-start | bytes 9224 | tf_op jit(solution)/shard_map/ppermute | solution.py:49
  91.1 1.3 %collective-permute-done.2 = f32[3,1,256]{2,1,0:T(1,128)S(1)} collective-permute-done((f32[3,1,256]{2,1,0:T(1,128)S(1)}, f32[3,1,256]{2,1,0:T(1,128)S(1)}, u32[]{:S(2)}, u32[]{:S(2)}) %collective-permute-start.2) | collective-permute-done | bytes 3104 | tf_op jit(solution)/shard_map/ppermute | solution.py:49
  92.4 0.6 bitcast_add_fusion
  (1 shorter events, 0.0 us)
Async XLA Ops:
  2.2 1.5 %copy-start.5 = (s32[216,2048]{1,0:T(8,128)S(1)}, s32[216,2048]{1,0:T(8,128)}, u32[]{:S(2)}) copy-start(s32[216,2048]{1,0:T(8,128)} %ids_ref.1) | copy-start | bytes 5308420
  3.7 0.7 copy-start.6
  45.2 3.0 %collective-permute-start = (f32[16,72,256]{2,1,0:T(8,128)S(1)}, f32[16,72,256]{2,1,0:T(8,128)S(1)}, u32[]{:S(2)}, u32[]{:S(2)}) collective-permute-start(f32[16,72,256]{2,1,0:T(8,128)S(1)} %get-tuple-element.7), channel_id=1, source_target_pairs={{0,8},{8,0},{16,24},{24,16},{1,9},{9,1},{17,25},{25,17},{2,10},{10... | collective-permute-start | bytes 3538952 | tf_op jit(solution)/shard_map/ppermute | solution.py:447
  49.4 8.4 %copy-start.4 = (f32[3,1,256]{2,1,0:T(1,128)S(1)}, f32[3,1,256]{2,1,0:T(1,128)}, u32[]{:S(2)}) copy-start(f32[3,1,256]{2,1,0:T(1,128)} %own_ref.1) | copy-start | bytes 9220
  49.4 37.8 %copy-start = (f32[12,8,225]{2,1,0:T(8,128)S(1)}, f32[12,8,225]{2,1,0:T(8,128)}, u32[]{:S(2)}) copy-start(f32[12,8,225]{2,1,0:T(8,128)} %resistance_ref.1) | copy-start | bytes 259204
  49.4 37.8 %copy-start.1 = (f32[6,8,225]{2,1,0:T(8,128)S(1)}, f32[6,8,225]{2,1,0:T(8,128)}, u32[]{:S(2)}) copy-start(f32[6,8,225]{2,1,0:T(8,128)} %stress_ref.1) | copy-start | bytes 129604
  49.4 37.8 %copy-start.2 = (f32[24,8]{1,0:T(8,128)S(1)}, f32[24,8]{1,0:T(8,128)}, u32[]{:S(2)}) copy-start(f32[24,8]{1,0:T(8,128)} %constant.50.clone.table_ref) | copy-start | bytes 2308
  49.4 37.8 %copy-start.3 = (s32[8,225]{1,0:T(8,128)S(1)}, s32[8,225]{1,0:T(8,128)}, u32[]{:S(2)}) copy-start(s32[8,225]{1,0:T(8,128)} %weights_ref.1) | copy-start | bytes 21604
  49.4 37.7 %all-to-all-start = ((f32[16,72,256]{2,1,0:T(8,128)}), f32[16,72,256]{2,1,0:T(8,128)S(1)}, u32[]{:S(2)}, u32[]{:S(2)}) async-start(f32[16,72,256]{2,1,0:T(8,128)} %add.31), calls=%async_computation | async-start | bytes 2359296 | tf_op jit(solution)/shard_map/all_to_all | solution.py:452
  57.8 5.8 %collective-permute-start.1 = (f32[3,1,256]{2,1,0:T(1,128)S(1)}, f32[3,1,256]{2,1,0:T(1,128)S(1)}, u32[]{:S(2)}, u32[]{:S(2)}) collective-permute-start(f32[3,1,256]{2,1,0:T(1,128)S(1)} %copy-done.4), channel_id=1, source_target_pairs={{1,0},{2,1},{3,2},{4,3},{5,4},{6,5},{7,6},{9,8},{10,9},{11,10},{12... | collective-permute-start | bytes 9224 | tf_op jit(solution)/shard_map/ppermute | solution.py:49
  88.8 3.6 %collective-permute-start.2 = (f32[3,1,256]{2,1,0:T(1,128)S(1)}, f32[3,1,256]{2,1,0:T(1,128)S(1)}, u32[]{:S(2)}, u32[]{:S(2)}) collective-permute-start(f32[3,1,256]{2,1,0:T(1,128)S(1)} %slice_bitcast_fusion), channel_id=1, source_target_pairs={{0,1},{1,2},{2,3},{3,4},{4,5},{5,6},{6,7},{8,9},{9,10},{10,11},{11... | collective-permute-start | bytes 9224 | tf_op jit(solution)/shard_map/ppermute | solution.py:49

commit v3 on v2

--- a/solution.py
+++ b/solution.py
@@ -1,3 +1,4 @@
+import functools
 import functools
 import math
 
@@ -11,8 +12,7 @@
 GX = 15
 LANES = 128
 COLUMNS = 256
-ROWS = 72
-COUNT_SPAN = 31
+CHUNKS = ((0, 4), (4, 2), (6, 2))
 SPARE = 11
 QUANTUM = float((1 << 20) - 1)
 
@@ -81,10 +81,10 @@
     return cosine, sine * angle
 
 
-def rotation_words(euler_ref):
-    cos_one, sin_one = cos_sin(0.5 * euler_ref[0])
-    cos_mid, sin_mid = cos_sin(0.5 * euler_ref[1])
-    cos_two, sin_two = cos_sin(0.5 * euler_ref[2])
+def rotation_words(euler):
+    cos_one, sin_one = cos_sin(0.5 * euler[0 : 0 + 1])
+    cos_mid, sin_mid = cos_sin(0.5 * euler[1 : 1 + 1])
+    cos_two, sin_two = cos_sin(0.5 * euler[2 : 2 + 1])
     w = cos_mid * (cos_one * cos_two - sin_one * sin_two)
     factor = jnp.where(w < 0.0, -QUANTUM, QUANTUM) / (1.0 + jnp.abs(w))
     x = sin_mid * (cos_one * cos_two + sin_one * sin_two) * factor
@@ -125,45 +125,47 @@
     return jnp.where(bits[level], high, low)
 
 
-def count_row(element):
-    return lax.shift_right_logical(element * (65536 // COUNT_SPAN + 1), 16)
-
-
-def handover_kernel(
-    ids_ref,
-    euler_ref,
-    place_ref,
-    element_ref,
-    keep_ref,
-    send_ref,
-    table_ref,
-    tile_ref,
-    split_ref,
-    masked_ref,
-):
+def cell_sum_kernel(first, count, *refs):
+    if first == 0:
+        ids_ref, label_ref, euler_ref, split_ref, label_out_ref, table_ref, tile_ref = refs
+    else:
+        ids_ref, label_ref, table_ref, split_ref, label_out_ref, tile_ref = refs
     per_octant = ids_ref.shape[0] // 8
-    bricks = ids_ref.shape[1]
-    table_rows = euler_ref.shape[1]
-    half_places = keep_ref.shape[0]
-    words = rotation_words(euler_ref)
-    table_ref[pl.ds(0, table_rows), :] = words[0]
-    table_ref[pl.ds(table_rows, table_rows), :] = words[1]
+    table_rows = table_ref.shape[0] // 2
+    label_out_ref[...] = label_ref[...]
+    if first == 0:
+        words = rotation_words(euler_ref[...])
+        for word in range(2):
+            for row in range(table_rows):
+                table_ref[pl.ds(word * table_rows + row, 1), :] = words[word][
+                    :, row * LANES : (row + 1) * LANES
+                ]
+    groups = tile_ref.shape[0] // 8
+    rows_left = count * per_octant - 8 * (groups - 1)
 
     def tile_sums(tile, carry):
         lanes = pl.ds(pl.multiple_of(tile * LANES, LANES), LANES)
-        tile_ref[...] = ids_ref[:, lanes]
+        for octant in range(count):
+            tile_ref[pl.ds(octant, per_octant, stride=count), :] = ids_ref[
+                pl.ds((first + octant) * per_octant, per_octant), lanes
+            ]
         sums = [jnp.zeros((8, LANES), jnp.float32) for pair in range(9)]
-        for cell in range(per_octant):
-            ids = tile_ref[pl.ds(cell, 8, stride=per_octant), :]
+        for group in range(groups):
+            ids = tile_ref[pl.ds(8 * group, 8), :]
             lane = ids & (LANES - 1)
             row = lax.shift_right_logical(ids, 7)
             bits = [(row & (1 << level)) != 0 for level in range(table_rows.bit_length() - 1)]
-            first = looked_up(table_ref, 0, table_rows, lane, bits)
-            second = looked_up(table_ref, table_rows, table_rows, lane, bits)
-            sums = [
-                total + product
-                for total, product in zip(sums, rotation_products(first, second))
-            ]
+            leading = looked_up(table_ref, 0, table_rows, lane, bits)
+            trailing = looked_up(table_ref, table_rows, table_rows, lane, bits)
+            products = rotation_products(leading, trailing)
+            if group == groups - 1 and rows_left < 8:
+                there = lax.broadcasted_iota(jnp.int32, (8, LANES), 0) < rows_left
+                products = [jnp.where(there, product, 0.0) for product in products]
+            sums = [total + product for total, product in zip(sums, products)]
+        sums = [
+            sum(total[count * part : count * (part + 1)] for part in range(8 // count))
+            for total in sums
+        ]
         vector = 2.0 / (QUANTUM * QUANTUM)
         xx, yy, zz, xy, xz, yz = [value * vector for value in sums[:6]]
         wx, wy, wz = [value * (2.0 / QUANTUM) for value in sums[6:]]
@@ -177,34 +179,37 @@
             xz - wy,
             yz + wx,
             per_octant - (xx + yy),
+            jnp.ones((split_ref.shape[0] // 2 - 9 * count, LANES), jnp.float32),
         ]
         stacked = jnp.concatenate(entries, axis=0)
-        leading = stacked.astype(jnp.bfloat16)
-        trailing = (stacked - leading.astype(jnp.float32)).astype(jnp.bfloat16)
-        split_ref[pl.ds(0, 2 * ROWS), lanes] = jnp.concatenate([leading, trailing], axis=0)
+        leading = stacked.astype(jnp.bfloat16).astype(jnp.float32)
+        split_ref[:, lanes] = jnp.concatenate([leading, stacked - leading], axis=0).astype(
+            jnp.bfloat16
+        )
         return carry
 
-    lax.fori_loop(0, bricks // LANES, tile_sums, 0)
-
-    element = element_ref[...]
+    lax.fori_loop(0, ids_ref.shape[1] // LANES, tile_sums, 0)
+
+
+def brick_sum_kernel(split_ref, label_ref, keep_ref, send_ref, label_out_ref, place_ref, masked_ref):
+    bricks = split_ref.shape[1]
+    half_places = keep_ref.shape[0]
+    labels = label_ref[...]
+    label_out_ref[...] = labels
+    place_ref[...] = jnp.where(
+        labels < 0, -1, place_of(lax.shift_right_arithmetic(labels, COLUMNS.bit_length() - 1))
+    )
     column = lax.broadcasted_iota(jnp.int32, (COLUMNS, bricks), 0)
-    row_of = count_row(element)
-    chosen = (
-        (column == element) | (column == element - row_of * COUNT_SPAN + (COLUMNS - COUNT_SPAN))
-    ).astype(jnp.bfloat16)
-    split_ref[pl.ds(2 * ROWS, 16), :] = (
-        lax.broadcasted_iota(jnp.int32, (16, bricks), 0) == row_of
-    ).astype(jnp.bfloat16)
+    chosen = (column == labels & (COLUMNS - 1)).astype(jnp.bfloat16)
     split_rows = split_ref.shape[0]
-    group = masked_ref.shape[0] // split_rows
-    in_counts = lax.broadcasted_iota(jnp.int32, (8, COLUMNS), 1) >= COLUMNS - COUNT_SPAN
-
-    for base, out_ref in ((0, keep_ref), (half_places, send_ref)):
+    half_rows = split_rows // 2
+    members = masked_ref.shape[0] // split_rows
+    for base, out_ref in ((half_places, send_ref), (0, keep_ref)):
 
         def place_group(step, carry):
             place = place_ref[...] - base
-            for member in range(group):
-                mask = (place == step * group + member).astype(jnp.bfloat16)
+            for member in range(members):
+                mask = (place == step * members + member).astype(jnp.bfloat16)
                 masked_ref[pl.ds(member * split_rows, split_rows), :] = split_ref[...] * mask
             product = lax.dot_general(
                 masked_ref[...],
@@ -212,41 +217,121 @@
                 (((1,), (1,)), ((), ())),
                 preferred_element_type=jnp.float32,
             )
-            for member in range(group):
-                first = member * split_rows
-                total = product[first : first + ROWS] + product[first + ROWS : first + 2 * ROWS]
-                counts = product[first + 2 * ROWS : first + 2 * ROWS + 8]
-                out_ref[step * group + member, pl.ds(0, 8), :] = jnp.where(
-                    in_counts, counts, total[:8]
+            for member in range(members):
+                at = member * split_rows
+                out_ref[step * members + member] = (
+                    product[at : at + half_rows] + product[at + half_rows : at + split_rows]
                 )
-                out_ref[step * group + member, pl.ds(8, ROWS - 8), :] = total[8:]
             return carry
 
-        lax.fori_loop(0, half_places // group, place_group, 0)
-
-
-def handover(grain_ids, euler_angles, place, element, places):
+        lax.fori_loop(0, half_places // members, place_group, 0)
+
+
+def place_of(owner):
+    groups, members = lax.axis_size("ca"), lax.axis_size("fe")
+    owner_ca = lax.shift_right_logical(owner, members.bit_length() - 1) ^ lax.axis_index("ca")
+    owner_fe = (owner & (members - 1)) ^ lax.axis_index("fe")
+    place = (owner_ca & 1) * (groups // 2) + lax.shift_right_logical(owner_ca, 1)
+    place = place * 2 + (owner_fe & 1)
+    return place * (members // 2) + lax.shift_right_logical(owner_fe, 1)
+
+
+def cell_sums(first, count, grain_ids, labels, table):
     bricks = grain_ids.shape[1]
-    table_rows = euler_angles.shape[1] // LANES
-    group = 8
-    half = jax.ShapeDtypeStruct((places // 2, ROWS, COLUMNS), jnp.float32)
+    per_octant = grain_ids.shape[0] // 8
+    out_shape = [
+        jax.ShapeDtypeStruct((2 * padded_rows(count), bricks), jnp.bfloat16),
+        jax.ShapeDtypeStruct(labels.shape, jnp.int32),
+    ]
+    if first == 0:
+        grains = table.shape[1]
+        out_shape.append(jax.ShapeDtypeStruct((2 * grains // LANES, LANES), jnp.int32))
     return pl.pallas_call(
-        handover_kernel,
-        out_shape=(half, half),
+        functools.partial(cell_sum_kernel, first, count),
+        out_shape=out_shape,
+        scratch_shapes=[pltpu.VMEM((-(-count * per_octant // 8) * 8, LANES), jnp.int32)],
+        compiler_params=pltpu.CompilerParams(vmem_limit_bytes=24 * 1024 * 1024),
+        cost_estimate=pl.CostEstimate(
+            flops=count * 4 * 10**9, bytes_accessed=count * 10**7, transcendentals=0
+        ),
+        name="cell_sums",
+    )(grain_ids, labels, table)
+
+
+def padded_rows(count):
+    return -(-9 * count // 8) * 8
+
+
+def brick_sums(split, labels, places):
+    rows, bricks = split.shape
+    members = min(16, places // 2)
+    half = jax.ShapeDtypeStruct((places // 2, rows // 2, COLUMNS), jnp.float32)
+    return pl.pallas_call(
+        brick_sum_kernel,
+        out_shape=[half, half, jax.ShapeDtypeStruct(labels.shape, jnp.int32)],
         scratch_shapes=[
-            pltpu.VMEM((2 * table_rows, LANES), jnp.int32),
-            pltpu.VMEM((grain_ids.shape[0], LANES), jnp.int32),
-            pltpu.VMEM((2 * ROWS + 16, bricks), jnp.bfloat16),
-            pltpu.VMEM((group * (2 * ROWS + 16), bricks), jnp.bfloat16),
+            pltpu.VMEM((1, bricks), jnp.int32),
+            pltpu.VMEM((members * rows, bricks), jnp.bfloat16),
         ],
-        compiler_params=pltpu.CompilerParams(vmem_limit_bytes=48 * 1024 * 1024),
+        compiler_params=pltpu.CompilerParams(vmem_limit_bytes=32 * 1024 * 1024),
         cost_estimate=pl.CostEstimate(
-            flops=2 * 160 * places * bricks * COLUMNS,
-            bytes_accessed=100 * 1024 * 1024,
-            transcendentals=0,
+            flops=rows * 3 * 10**7, bytes_accessed=rows * 10**5, transcendentals=0
         ),
-        name="handover",
-    )(grain_ids, euler_angles.reshape(3, table_rows, LANES), place, element)
+        name="brick_sums",
+    )(split, labels)
+
+
+def part_sum_kernel(terms, passed, *refs):
+    flat = sum(terms)
+    outs = refs[flat + passed :]
+    for index in range(len(outs) - passed):
+        at = row = 0
+        for group in terms:
+            total = refs[at][index]
+            for term in refs[at + 1 : at + group]:
+                total = total + term[index]
+            at += group
+            axis = total.ndim - 2
+            where = (slice(None),) * axis + (pl.ds(row, total.shape[axis]),)
+            outs[index][where] = total
+            row += total.shape[axis]
+    for i in range(passed):
+        outs[len(outs) - passed + i][...] = refs[flat + i][...]
+
+
+def part_sum(groups, passed, name):
+    shape = groups[0][0].shape
+    rows = sum(terms[0].shape[-2] for terms in groups)
+    part = jax.ShapeDtypeStruct(shape[1:-2] + (rows, shape[-1]), jnp.float32)
+    out = pl.pallas_call(
+        functools.partial(part_sum_kernel, [len(terms) for terms in groups], len(passed)),
+        out_shape=[part] * shape[0]
+        + [jax.ShapeDtypeStruct(array.shape, array.dtype) for array in passed],
+        name=name,
+    )(*[term for terms in groups for term in terms], *passed)
+    return out[: shape[0]], *out[shape[0] :]
+
+
+def to_relative(block, core, pair, last, rest):
+    groups, members = lax.axis_size("ca"), lax.axis_size("fe")
+    flip = (2 * pair + core) * members + 2 * rest + last
+    return lax.ppermute(block, ("ca", "fe"), [(i, i ^ flip) for i in range(groups * members)])
+
+
+def across_cores(keep, send):
+    pairs, rests = lax.axis_size("ca") // 2, lax.axis_size("fe") // 2
+    split = (2 * pairs, rests) + keep.shape[1:]
+    return [keep.reshape(split), to_relative(send, 1, 0, 0, 0).reshape(split)]
+
+
+def across_plane(parts):
+    return [parts[0]] + [
+        to_relative(parts[index], 0, index // 2, index % 2, 0) for index in range(1, len(parts))
+    ]
+
+
+def across_height(parts):
+    return [parts[0]] + [to_relative(parts[rest], 0, 0, 0, rest) for rest in range(1, len(parts))]
 
 
 def three_parts(value):
@@ -267,33 +352,31 @@
     return total
 
 
-def update_kernel(
-    gathered_ref,
-    own_ref,
-    upper_ref,
-    stress_ref,
-    resistance_ref,
-    weights_ref,
-    table_ref,
-    stress_out_ref,
-    nodal_ref,
-):
+def update_kernel(sources, *refs):
+    own_ref, upper_ref, stress_ref, resistance_ref, weights_ref, table_ref = refs[2 * sources : -2]
+    stress_out_ref, nodal_ref = refs[-2:]
     elements = stress_ref.shape[2]
-    gathered = gathered_ref[0]
-    for source in range(1, gathered_ref.shape[0]):
-        gathered = gathered + gathered_ref[source]
-    element_row = lax.broadcasted_iota(jnp.int32, (8, elements), 1)
-    count_at = lax.broadcasted_iota(jnp.int32, (COLUMNS, elements), 1)
-    count_at = count_at - count_row(count_at) * COUNT_SPAN + (COLUMNS - COUNT_SPAN)
-    spread = dot_selected(
-        gathered[:8],
-        (lax.broadcasted_iota(jnp.int32, (COLUMNS, elements), 0) == count_at).astype(jnp.bfloat16),
-        0,
-    )
-    in_row = count_row(element_row) == lax.broadcasted_iota(jnp.int32, (8, elements), 0)
-    counts = jnp.sum(jnp.where(in_row, spread, 0.0), axis=0, keepdims=True)
+    gathered = [
+        sum(ref[:, 0:elements] for ref in refs[at : at + sources]) for at in (0, sources)
+    ]
+    chunk_sums = [
+        gathered[0],
+        gathered[1][: padded_rows(CHUNKS[1][1])],
+        gathered[1][padded_rows(CHUNKS[1][1]) :],
+    ]
+    counts = gathered[0][9 * CHUNKS[0][1] : 9 * CHUNKS[0][1] + 1]
     per_brick = 1.0 / (8.0 * jnp.maximum(counts, 1.0))
-    frames = [gathered[8 * k : 8 * k + 8, 0:elements] * per_brick for k in range(9)]
+    frames = [
+        jnp.concatenate(
+            [
+                sums[count * k : count * (k + 1)]
+                for sums, (first, count) in zip(chunk_sums, CHUNKS)
+            ],
+            axis=0,
+        )
+        * per_brick
+        for k in range(9)
+    ]
 
     node = lax.broadcasted_iota(jnp.int32, (COLUMNS, elements), 0)
     element = lax.broadcasted_iota(jnp.int32, (COLUMNS, elements), 1)
@@ -412,14 +495,14 @@
         dtype=jnp.float32,
     )
     return pl.pallas_call(
-        update_kernel,
+        functools.partial(update_kernel, len(gathered) // 2),
         out_shape=(
             jax.ShapeDtypeStruct(stress_old.shape, jnp.float32),
             jax.ShapeDtypeStruct((2,) + own.shape, jnp.float32),
         ),
         compiler_params=pltpu.CompilerParams(vmem_limit_bytes=32 * 1024 * 1024),
         name="stress_update",
-    )(gathered, own, upper, stress_old, resistance, quad_weights, table)
+    )(*gathered, own, upper, stress_old, resistance, quad_weights, table)
 
 
 def body(
@@ -433,25 +516,29 @@
     resistance,
     quad_weights,
 ):
-    groups, members = lax.axis_size("ca"), lax.axis_size("fe")
+    places = lax.axis_size("ca") * lax.axis_size("fe")
     bricks = grain_ids.shape[1]
     upper_layer = passed_along(displacement, "fe", -1)
-    owner = brick_owner[:, 0]
-    owner_ca, owner_fe = owner // members, owner % members
-    other_core = (owner_ca + lax.axis_index("ca")) & 1
-    place = ((other_core * (groups // 2) + owner_ca // 2) * members) + owner_fe
-    place = jnp.where(brick_active > 0, place, -1).reshape(1, bricks)
-    keep, send = handover(
-        grain_ids, euler_angles, place, brick_element.reshape(1, bricks), groups * members
-    )
-    keep = keep + lax.ppermute(send, "ca", [(i, i ^ 1) for i in range(groups)])
-    same_core = [
-        [(2 * pair + core) * members + member for pair in range(groups // 2) for member in range(members)]
-        for core in range(2)
-    ]
-    gathered = lax.all_to_all(
-        keep, ("ca", "fe"), split_axis=0, concat_axis=0, axis_index_groups=same_core, tiled=True
-    )
+    labels = jnp.where(
+        brick_active > 0, brick_owner[:, 0] * COLUMNS + brick_element, -1
+    ).reshape(1, bricks)
+    (first_a, count_a), (first_b, count_b), (first_c, count_c) = CHUNKS
+    split_a, labels, table = cell_sums(first_a, count_a, grain_ids, labels, euler_angles)
+    keep_a, send_a, labels = brick_sums(split_a, labels, places)
+    split_b, labels = cell_sums(first_b, count_b, grain_ids, labels, table)
+    core_a, labels, upper_layer = part_sum(
+        [across_cores(keep_a, send_a)], [labels, upper_layer], "core_sum_a"
+    )
+    keep_b, send_b, labels = brick_sums(split_b, labels, places)
+    split_c, labels = cell_sums(first_c, count_c, grain_ids, labels, table)
+    plane_a, labels = part_sum([across_plane(core_a)], [labels], "plane_sum_a")
+    core_b, labels = part_sum([across_cores(keep_b, send_b)], [labels], "core_sum_b")
+    keep_c, send_c, labels = brick_sums(split_c, labels, places)
+    core_c, labels = part_sum([across_cores(keep_c, send_c)], [labels], "core_sum_c")
+    plane_bc, labels = part_sum(
+        [across_plane(core_b), across_plane(core_c)], [labels], "plane_sum_b_c"
+    )
+    gathered = across_height(plane_a) + across_height(plane_bc)
     stress_new, nodal = element_update(
         gathered, displacement, upper_layer, stress_old, resistance, quad_weights
     )

time: 94.5 us -> 107 us (1.13)
  waiting for transfers between devices: 31.8 us -> 7.92 us
  starting transfers between devices: 12.5 us -> 28.8 us
  Pallas kernels: 42.5 us -> 56 us
  local copies, waits for them, and re-layouts: 3.04 us -> 10.2 us
    ppermute x1 -> x18, starting transfers between devices: 0.51 us -> 24.2 us  [to_relative(): lax.ppermute(block, ('ca', 'fe'), [(i, i ^ flip) for i in range(groups *...]
    all_to_all x1 -> x0, waiting for transfers between devices: 23.6 us -> none  [body(): lax.all_to_all(keep, ('ca', 'fe'), split_axis=0, concat_axis=0, axis_inde...]
    pallas_call x2 -> x12, Pallas kernels: 42.5 us -> 56 us  [the longest x3 38.1 us: cell_sums(): pl.pallas_call(functools.partial(cell_sum_kernel, first, count), out_shap...]
    all_to_all x1 -> x0, starting transfers between devices: 8.38 us -> none  [body(): lax.all_to_all(keep, ('ca', 'fe'), split_axis=0, concat_axis=0, axis_inde...]
    unnamed x15 -> x76, local copies, waits for them, and re-layouts: 3.03 us -> 10.2 us
    ppermute x2, waiting for transfers between devices: 5.77 us -> 1.3 us  [passed_along(): return lax.ppermute(block, axis, route)]
    ppermute x1 -> x18, waiting for transfers between devices: 2.47 us -> 6.62 us  [to_relative(): lax.ppermute(block, ('ca', 'fe'), [(i, i ^ flip) for i in range(groups *...]
    add x1 -> x0, other arithmetic: 1.18 us -> none  [body(): keep = keep + lax.ppermute(send, 'ca', [(i, i ^ 1) for i in range(groups)])]
  transfers between devices with their start and end apart: 4 -> 20, of which waited for: 4 -> 5; matrix products, arithmetic and copies ran while one was open for 0% -> 1% of each run, Pallas kernels for 0% -> 46%
where the time goes in v3:
time: 107 us; the launch traced here: 106 us
  Pallas kernels  56 us (52%)
  starting transfers between devices  28.8 us (27%)
  local copies, waits for them, and re-layouts  10.2 us (10%)
  waiting for transfers between devices  7.92 us (7%)
  other arithmetic  2 us (2%)
  between operations  1.07 us (1%)
    pallas_call x3, Pallas kernels, cell_sums(): pl.pallas_call(functools.partial(cell_sum_kernel, first, count), out_shap...  38.1 us
    ppermute x18, starting transfers between devices, to_relative(): lax.ppermute(block, ('ca', 'fe'), [(i, i ^ flip) for i in range(groups *...  24.2 us
    unnamed x76, local copies, waits for them, and re-layouts  10.2 us
    pallas_call x5, Pallas kernels, part_sum(): pl.pallas_call(functools.partial(part_sum_kernel, [len(terms) for terms i...  9.66 us
    ppermute x18, waiting for transfers between devices, to_relative(): lax.ppermute(block, ('ca', 'fe'), [(i, i ^ flip) for i in range(groups *...  6.62 us
    pallas_call x3, Pallas kernels, brick_sums(): pl.pallas_call(brick_sum_kernel, out_shape=[half, half, jax.ShapeDtypeStr...  6.55 us
    ppermute x2, starting transfers between devices, passed_along(): return lax.ppermute(block, axis, route)  4.58 us
  transfers between devices with their start and end apart: 20, of which 5 were waited for; matrix products, arithmetic and copies ran while one was open for 1% of the time, Pallas kernels for 46%

profile of v3, /device:TPU:0, one launch (start us, length us, event | category | flops | bytes accessed | tf_op | source)
XLA Modules:
  0.0 106.0 jit_solution(14408661938259556348)
XLA Ops:
  0.6 1.3 %collective-permute-start.1 = (f32[3,1,256]{2,1,0:T(1,128)}, f32[3,1,256]{2,1,0:T(1,128)S(1)}, u32[]{:S(2)}, u32[]{:S(2)}) collective-permute-start(f32[3,1,256]{2,1,0:T(1,128)} %refs_8_.1), channel_id=1, source_target_pairs={{1,0},{2,1},{3,2},{4,3},{5,4},{6,5},{7,6},{9,8},{10,9},{11,10},{12... | collective-permute-start | bytes 9224 | tf_op jit(solution)/shard_map/ppermute | solution.py:49
  3.4 1.5 %copy-done.14 = s32[216,2048]{1,0:T(8,128)S(1)} copy-done((s32[216,2048]{1,0:T(8,128)S(1)}, s32[216,2048]{1,0:T(8,128)}, u32[]{:S(2)}) %copy-start.14) | copy-done | bytes 1769496
  4.8 0.8 copy-done.16
  5.7 18.3 %cell_sums.3 = (bf16[80,2048]{1,0:T(8,128)(2,1)S(1)}, s32[1,2048]{1,0:T(1,128)S(1)}, s32[64,128]{1,0:T(8,128)S(1)}) custom-call(s32[216,2048]{1,0:T(8,128)S(1)} %copy-done.14, s32[1,2048]{1,0:T(1,128)S(1)} %bitcast.15, f32[3,4096]{1,0:T(4,128)S(1)} %copy-done.16), custom_call_target="tpu_custom_call" | custom-call | flops 16000000000 | bytes 40000000 | tf_op jit(solution)/shard_map/cell_sums/pallas_call | solution.py:249
  24.0 2.9 %brick_sums.3 = (f32[16,40,256]{2,1,0:T(8,128)S(1)}, f32[16,40,256]{2,1,0:T(8,128)S(1)}, s32[1,2048]{1,0:T(1,128)S(1)}) custom-call(bf16[80,2048]{1,0:T(8,128)(2,1)S(1)} %get-tuple-element.45.split_ref, s32[1,2048]{1,0:T(1,128)S(1)} %get-tuple-element.46.label_ref), custom_call_target="tpu_custom_call" | custom-call | flops 2400000000 | bytes 8000000 | tf_op jit(solution)/shard_map/brick_sums/pallas_call | solution.py:269
  27.4 9.9 %cell_sums.4 = (bf16[48,2048]{1,0:T(8,128)(2,1)S(1)}, s32[1,2048]{1,0:T(1,128)S(1)}) custom-call(s32[216,2048]{1,0:T(8,128)S(1)} %copy-done.15, s32[1,2048]{1,0:T(1,128)S(1)} %get-tuple-element.49.refs_1_, s32[64,128]{1,0:T(8,128)S(1)} %get-tuple-element.50.refs_2_), custom_call_target="tpu_custom_call" | custom-call | flops 8000000000 | bytes 20000000 | tf_op jit(solution)/shard_map/cell_sums/pallas_call | solution.py:249
  38.8 2.2 %core_sum_a.1 = (f32[4,40,256]{2,1,0:T(8,128)}, f32[4,40,256]{2,1,0:T(8,128)}, f32[4,40,256]{2,1,0:T(8,128)}, f32[4,40,256]{2,1,0:T(8,128)}, s32[1,2048]{1,0:T(1,128)}, /*index=5*/f32[3,1,256]{2,1,0:T(1,128)}) custom-call(f32[4,4,40,256]{3,2,1,0:T(8,128)} %bitcast.12, f32[4,4,40,256]{3,2,1,0:T(8,128)} %bitcast.16, s32[1,2048]{1,0:T(1,128)} %copy-done.10, ...), custom_call_target="tpu_custom_call" | custom-call | tf_op jit(solution)/shard_map/core_sum_a/pallas_call | solution.py:306
  41.0 3.1 %collective-permute-start.2 = (f32[4,40,256]{2,1,0:T(8,128)}, f32[4,40,256]{2,1,0:T(8,128)S(1)}, u32[]{:S(2)}, u32[]{:S(2)}) collective-permute-start(f32[4,40,256]{2,1,0:T(8,128)} %get-tuple-element.53), channel_id=1, source_target_pairs={{0,1},{1,0},{2,3},{3,2},{4,5},{5,4},{6,7},{7,6},{8,9},{9,8},{10,11... | collective-permute-start | bytes 491528 | tf_op jit(solution)/shard_map/ppermute | solution.py:318
  44.1 2.0 %collective-permute-start.3 = (f32[4,40,256]{2,1,0:T(8,128)}, f32[4,40,256]{2,1,0:T(8,128)S(1)}, u32[]{:S(2)}, u32[]{:S(2)}) collective-permute-start(f32[4,40,256]{2,1,0:T(8,128)} %get-tuple-element.54), channel_id=1, source_target_pairs={{0,16},{1,17},{2,18},{3,19},{4,20},{5,21},{6,22},{7,23},{8,24},{9,... | collective-permute-start | bytes 491528 | tf_op jit(solution)/shard_map/ppermute | solution.py:318
  46.9 1.8 %brick_sums.4 = (f32[16,24,256]{2,1,0:T(8,128)S(1)}, f32[16,24,256]{2,1,0:T(8,128)S(1)}, s32[1,2048]{1,0:T(1,128)S(1)}) custom-call(bf16[48,2048]{1,0:T(8,128)(2,1)S(1)} %get-tuple-element.56.split_ref, s32[1,2048]{1,0:T(1,128)S(1)} %copy-done.17), custom_call_target="tpu_custom_call" | custom-call | flops 1440000000 | bytes 4800000 | tf_op jit(solution)/shard_map/brick_sums/pallas_call | solution.py:269
  48.8 9.9 %cell_sums.5 = (bf16[48,2048]{1,0:T(8,128)(2,1)S(1)}, s32[1,2048]{1,0:T(1,128)S(1)}) custom-call(s32[216,2048]{1,0:T(8,128)S(1)} %copy-done.15, s32[1,2048]{1,0:T(1,128)S(1)} %get-tuple-element.58.refs_1_, s32[64,128]{1,0:T(8,128)S(1)} %get-tuple-element.50.refs_2_), custom_call_target="tpu_custom_call" | custom-call | flops 8000000000 | bytes 20000000 | tf_op jit(solution)/shard_map/cell_sums/pallas_call | solution.py:249
  60.1 1.8 %plane_sum_a.1 = (f32[40,256]{1,0:T(8,128)}, f32[40,256]{1,0:T(8,128)}, f32[40,256]{1,0:T(8,128)}, f32[40,256]{1,0:T(8,128)}, s32[1,2048]{1,0:T(1,128)}) custom-call(f32[4,40,256]{2,1,0:T(8,128)} %get-tuple-element.52.refs_0_, f32[4,40,256]{2,1,0:T(8,128)} %copy-done.22, f32[4,40,256]{2,1,0:T(8,128)} %copy-done.23, f32[4,40,256]{2,1,0:T(8,128)} %copy-done.24, ...), custom_call_target="tpu_custom_call" | custom-call | tf_op jit(solution)/shard_map/plane_sum_a/pallas_call | solution.py:306
  62.7 1.9 %core_sum_b.1 = (f32[4,24,256]{2,1,0:T(8,128)}, f32[4,24,256]{2,1,0:T(8,128)}, f32[4,24,256]{2,1,0:T(8,128)}, f32[4,24,256]{2,1,0:T(8,128)}, s32[1,2048]{1,0:T(1,128)}) custom-call(f32[4,4,24,256]{3,2,1,0:T(8,128)} %bitcast.13, f32[4,4,24,256]{3,2,1,0:T(8,128)} %bitcast.17, s32[1,2048]{1,0:T(1,128)} %get-tuple-element.66.refs_2_), custom_call_target="tpu_custom_call" | custom-call | tf_op jit(solution)/shard_map/core_sum_b/pallas_call | solution.py:306
  65.3 1.8 %brick_sums.5 = (f32[16,24,256]{2,1,0:T(8,128)S(1)}, f32[16,24,256]{2,1,0:T(8,128)S(1)}, s32[1,2048]{1,0:T(1,128)S(1)}) custom-call(bf16[48,2048]{1,0:T(8,128)(2,1)S(1)} %get-tuple-element.71.split_ref, s32[1,2048]{1,0:T(1,128)S(1)} %copy-done.18), custom_call_target="tpu_custom_call" | custom-call | flops 1440000000 | bytes 4800000 | tf_op jit(solution)/shard_map/brick_sums/pallas_call | solution.py:269
  68.4 1.5 %collective-permute-start.9 = (f32[4,24,256]{2,1,0:T(8,128)S(1)}, f32[4,24,256]{2,1,0:T(8,128)S(1)}, u32[]{:S(2)}, u32[]{:S(2)}) collective-permute-start(f32[4,24,256]{2,1,0:T(8,128)S(1)} %copy-done.34), channel_id=1, source_target_pairs={{0,1},{1,0},{2,3},{3,2},{4,5},{5,4},{6,7},{7,6},{8,9},{9,8},{10,11... | collective-permute-start | bytes 294920 | tf_op jit(solution)/shard_map/ppermute | solution.py:318
  69.9 2.0 %collective-permute-start.10 = (f32[4,24,256]{2,1,0:T(8,128)S(1)}, f32[4,24,256]{2,1,0:T(8,128)S(1)}, u32[]{:S(2)}, u32[]{:S(2)}) collective-permute-start(f32[4,24,256]{2,1,0:T(8,128)S(1)} %copy-done.33), channel_id=1, source_target_pairs={{0,16},{1,17},{2,18},{3,19},{4,20},{5,21},{6,22},{7,23},{8,24},{9,... | collective-permute-start | bytes 294920 | tf_op jit(solution)/shard_map/ppermute | solution.py:318
  72.7 1.9 %core_sum_c.1 = (f32[4,24,256]{2,1,0:T(8,128)}, f32[4,24,256]{2,1,0:T(8,128)}, f32[4,24,256]{2,1,0:T(8,128)}, f32[4,24,256]{2,1,0:T(8,128)}, s32[1,2048]{1,0:T(1,128)}) custom-call(f32[4,4,24,256]{3,2,1,0:T(8,128)} %bitcast.14, f32[4,4,24,256]{3,2,1,0:T(8,128)} %bitcast.18, s32[1,2048]{1,0:T(1,128)} %copy-done.9), custom_call_target="tpu_custom_call" | custom-call | tf_op jit(solution)/shard_map/core_sum_c/pallas_call | solution.py:306
  74.6 1.5 %collective-permute-start.13 = (f32[4,24,256]{2,1,0:T(8,128)}, f32[4,24,256]{2,1,0:T(8,128)S(1)}, u32[]{:S(2)}, u32[]{:S(2)}) collective-permute-start(f32[4,24,256]{2,1,0:T(8,128)} %get-tuple-element.77), channel_id=1, source_target_pairs={{0,1},{1,0},{2,3},{3,2},{4,5},{5,4},{6,7},{7,6},{8,9},{9,8},{10,11... | collective-permute-start | bytes 294920 | tf_op jit(solution)/shard_map/ppermute | solution.py:318
  76.1 2.0 %collective-permute-start.14 = (f32[4,24,256]{2,1,0:T(8,128)}, f32[4,24,256]{2,1,0:T(8,128)S(1)}, u32[]{:S(2)}, u32[]{:S(2)}) collective-permute-start(f32[4,24,256]{2,1,0:T(8,128)} %get-tuple-element.78), channel_id=1, source_target_pairs={{0,16},{1,17},{2,18},{3,19},{4,20},{5,21},{6,22},{7,23},{8,24},{9,... | collective-permute-start | bytes 294920 | tf_op jit(solution)/shard_map/ppermute | solution.py:318
  78.1 2.9 %collective-permute-start.5 = (f32[40,256]{1,0:T(8,128)S(1)}, f32[40,256]{1,0:T(8,128)S(1)}, u32[]{:S(2)}, u32[]{:S(2)}) collective-permute-start(f32[40,256]{1,0:T(8,128)S(1)} %copy-done.37), channel_id=1, source_target_pairs={{0,2},{1,3},{2,0},{3,1},{4,6},{5,7},{6,4},{7,5},{8,10},{9,11},{10,... | collective-permute-start | bytes 122888 | tf_op jit(solution)/shard_map/ppermute | solution.py:318
  81.1 0.9 collective-permute-done.14.refs_6_
  82.0 1.8 %collective-permute-done.15.refs_7_ = f32[4,24,256]{2,1,0:T(8,128)S(1)} collective-permute-done((f32[4,24,256]{2,1,0:T(8,128)}, f32[4,24,256]{2,1,0:T(8,128)S(1)}, u32[]{:S(2)}, u32[]{:S(2)}) %collective-permute-start.15) | collective-permute-done | bytes 98336 | tf_op jit(solution)/shard_map/ppermute | solution.py:318
  84.4 1.9 %plane_sum_b_c.1 = (f32[48,256]{1,0:T(8,128)}, f32[48,256]{1,0:T(8,128)}, f32[48,256]{1,0:T(8,128)}, f32[48,256]{1,0:T(8,128)}, s32[1,2048]{1,0:T(1,128)}) custom-call(f32[4,24,256]{2,1,0:T(8,128)} %get-tuple-element.67.refs_0_, f32[4,24,256]{2,1,0:T(8,128)} %copy-done.25, f32[4,24,256]{2,1,0:T(8,128)} %copy-done.26, f32[4,24,256]{2,1,0:T(8,128)} %copy-done.27, ...), custom_call_target="tpu_custom_call" | custom-call | tf_op jit(solution)/shard_map/plane_sum_b_c/pallas_call | solution.py:306
  86.3 1.6 %collective-permute-start.16 = (f32[48,256]{1,0:T(8,128)}, f32[48,256]{1,0:T(8,128)S(1)}, u32[]{:S(2)}, u32[]{:S(2)}) collective-permute-start(f32[48,256]{1,0:T(8,128)} %get-tuple-element.82), channel_id=1, source_target_pairs={{0,2},{1,3},{2,0},{3,1},{4,6},{5,7},{6,4},{7,5},{8,10},{9,11},{10,... | collective-permute-start | bytes 147464 | tf_op jit(solution)/shard_map/ppermute | solution.py:318
  87.9 2.6 %collective-permute-start.17 = (f32[48,256]{1,0:T(8,128)}, f32[48,256]{1,0:T(8,128)S(1)}, u32[]{:S(2)}, u32[]{:S(2)}) collective-permute-start(f32[48,256]{1,0:T(8,128)} %get-tuple-element.83), channel_id=1, source_target_pairs={{0,4},{1,5},{2,6},{3,7},{4,0},{5,1},{6,2},{7,3},{8,12},{9,13},{10,... | collective-permute-start | bytes 147464 | tf_op jit(solution)/shard_map/ppermute | solution.py:318
  90.7 1.7 %collective-permute-start.6 = (f32[40,256]{1,0:T(8,128)S(1)}, f32[40,256]{1,0:T(8,128)S(1)}, u32[]{:S(2)}, u32[]{:S(2)}) collective-permute-start(f32[40,256]{1,0:T(8,128)S(1)} %copy-done.36), channel_id=1, source_target_pairs={{0,4},{1,5},{2,6},{3,7},{4,0},{5,1},{6,2},{7,3},{8,12},{9,13},{10,... | collective-permute-start | bytes 122888 | tf_op jit(solution)/shard_map/ppermute | solution.py:318
  92.4 2.0 %collective-permute-start.7 = (f32[40,256]{1,0:T(8,128)S(1)}, f32[40,256]{1,0:T(8,128)S(1)}, u32[]{:S(2)}, u32[]{:S(2)}) collective-permute-start(f32[40,256]{1,0:T(8,128)S(1)} %copy-done.35), channel_id=1, source_target_pairs={{0,6},{1,7},{2,4},{3,5},{4,2},{5,3},{6,0},{7,1},{8,14},{9,15},{10,... | collective-permute-start | bytes 122888 | tf_op jit(solution)/shard_map/ppermute | solution.py:318
  94.4 3.0 %collective-permute-done.6.refs_2_ = f32[40,256]{1,0:T(8,128)S(1)} collective-permute-done((f32[40,256]{1,0:T(8,128)S(1)}, f32[40,256]{1,0:T(8,128)S(1)}, u32[]{:S(2)}, u32[]{:S(2)}) %collective-permute-start.6) | collective-permute-done | bytes 40992 | tf_op jit(solution)/shard_map/ppermute | solution.py:318
  97.4 0.8 collective-permute-done.7.refs_3_
  99.1 1.7 %stress_update.1 = (f32[6,8,225]{2,1,0:T(8,128)}, f32[2,3,1,256]{3,2,1,0:T(1,128)S(1)}) custom-call(f32[40,256]{1,0:T(8,128)S(1)} %copy-done.6, f32[40,256]{1,0:T(8,128)S(1)} %collective-permute-done.5.refs_1_, f32[40,256]{1,0:T(8,128)S(1)} %collective-permute-done.6.refs_2_, f32[40,256]{1,0:T(8,128)S(1)} %collective-permute-done.7.refs_3_, ...), custom_call_target="tpu_custom_call" | custom-call | tf_op jit(solution)/shard_map/stress_update/pallas_call | solution.py:497
  100.9 3.3 %collective-permute-start.19 = (f32[3,1,256]{2,1,0:T(1,128)S(1)}, f32[3,1,256]{2,1,0:T(1,128)S(1)}, u32[]{:S(2)}, u32[]{:S(2)}) collective-permute-start(f32[3,1,256]{2,1,0:T(1,128)S(1)} %slice_bitcast_fusion), channel_id=1, source_target_pairs={{0,1},{1,2},{2,3},{3,4},{4,5},{5,6},{6,7},{8,9},{9,10},{10,11},{11... | collective-permute-start | bytes 9224 | tf_op jit(solution)/shard_map/ppermute | solution.py:49
  104.1 1.3 %collective-permute-done.19 = f32[3,1,256]{2,1,0:T(1,128)S(1)} collective-permute-done((f32[3,1,256]{2,1,0:T(1,128)S(1)}, f32[3,1,256]{2,1,0:T(1,128)S(1)}, u32[]{:S(2)}, u32[]{:S(2)}) %collective-permute-start.19) | collective-permute-done | bytes 3104 | tf_op jit(solution)/shard_map/ppermute | solution.py:49
  (100 shorter events, 11.3 us)
Async XLA Ops:
  0.6 37.3 %collective-permute-start.1 = (f32[3,1,256]{2,1,0:T(1,128)}, f32[3,1,256]{2,1,0:T(1,128)S(1)}, u32[]{:S(2)}, u32[]{:S(2)}) collective-permute-start(f32[3,1,256]{2,1,0:T(1,128)} %refs_8_.1), channel_id=1, source_target_pairs={{1,0},{2,1},{3,2},{4,3},{5,4},{6,5},{7,6},{9,8},{10,9},{11,10},{12... | collective-permute-start | bytes 9224 | tf_op jit(solution)/shard_map/ppermute | solution.py:49
  26.9 10.5 %copy-start = (f32[16,40,256]{2,1,0:T(8,128)}, f32[16,40,256]{2,1,0:T(8,128)S(1)}, u32[]{:S(2)}) copy-start(f32[16,40,256]{2,1,0:T(8,128)S(1)} %get-tuple-element.47) | copy-start | bytes 1966084
  26.9 11.1 %collective-permute-start = (f32[16,40,256]{2,1,0:T(8,128)S(1)}, f32[16,40,256]{2,1,0:T(8,128)S(1)}, u32[]{:S(2)}, u32[]{:S(2)}) collective-permute-start(f32[16,40,256]{2,1,0:T(8,128)S(1)} %get-tuple-element.48), channel_id=1, source_target_pairs={{0,8},{1,9},{2,10},{3,11},{4,12},{5,13},{6,14},{7,15},{8,0},{9,1},... | collective-permute-start | bytes 1966088 | tf_op jit(solution)/shard_map/ppermute | solution.py:318
  41.0 18.3 %collective-permute-start.2 = (f32[4,40,256]{2,1,0:T(8,128)}, f32[4,40,256]{2,1,0:T(8,128)S(1)}, u32[]{:S(2)}, u32[]{:S(2)}) collective-permute-start(f32[4,40,256]{2,1,0:T(8,128)} %get-tuple-element.53), channel_id=1, source_target_pairs={{0,1},{1,0},{2,3},{3,2},{4,5},{5,4},{6,7},{7,6},{8,9},{9,8},{10,11... | collective-permute-start | bytes 491528 | tf_op jit(solution)/shard_map/ppermute | solution.py:318
  44.1 15.2 %collective-permute-start.3 = (f32[4,40,256]{2,1,0:T(8,128)}, f32[4,40,256]{2,1,0:T(8,128)S(1)}, u32[]{:S(2)}, u32[]{:S(2)}) collective-permute-start(f32[4,40,256]{2,1,0:T(8,128)} %get-tuple-element.54), channel_id=1, source_target_pairs={{0,16},{1,17},{2,18},{3,19},{4,20},{5,21},{6,22},{7,23},{8,24},{9,... | collective-permute-start | bytes 491528 | tf_op jit(solution)/shard_map/ppermute | solution.py:318
  46.2 13.2 %collective-permute-start.4 = (f32[4,40,256]{2,1,0:T(8,128)}, f32[4,40,256]{2,1,0:T(8,128)S(1)}, u32[]{:S(2)}, u32[]{:S(2)}) collective-permute-start(f32[4,40,256]{2,1,0:T(8,128)} %get-tuple-element.55), channel_id=1, source_target_pairs={{0,17},{1,16},{2,19},{3,18},{4,21},{5,20},{6,23},{7,22},{8,25},{9,... | collective-permute-start | bytes 491528 | tf_op jit(solution)/shard_map/ppermute | solution.py:318
  48.7 10.0 %copy-start.1 = (f32[16,24,256]{2,1,0:T(8,128)}, f32[16,24,256]{2,1,0:T(8,128)S(1)}, u32[]{:S(2)}) copy-start(f32[16,24,256]{2,1,0:T(8,128)S(1)} %get-tuple-element.64) | copy-start | bytes 1179652
  48.7 13.2 %collective-permute-start.8 = (f32[16,24,256]{2,1,0:T(8,128)S(1)}, f32[16,24,256]{2,1,0:T(8,128)S(1)}, u32[]{:S(2)}, u32[]{:S(2)}) collective-permute-start(f32[16,24,256]{2,1,0:T(8,128)S(1)} %get-tuple-element.65), channel_id=1, source_target_pairs={{0,8},{1,9},{2,10},{3,11},{4,12},{5,13},{6,14},{7,15},{8,0},{9,1},... | collective-permute-start | bytes 1179656 | tf_op jit(solution)/shard_map/ppermute | solution.py:318
  65.2 12.9 %copy-start.37 = (f32[40,256]{1,0:T(8,128)S(1)}, f32[40,256]{1,0:T(8,128)}, u32[]{:S(2)}) copy-start(f32[40,256]{1,0:T(8,128)} %get-tuple-element.61) | copy-start | bytes 122884
  65.2 25.5 %copy-start.36 = (f32[40,256]{1,0:T(8,128)S(1)}, f32[40,256]{1,0:T(8,128)}, u32[]{:S(2)}) copy-start(f32[40,256]{1,0:T(8,128)} %get-tuple-element.62) | copy-start | bytes 122884
  65.3 27.2 %copy-start.35 = (f32[40,256]{1,0:T(8,128)S(1)}, f32[40,256]{1,0:T(8,128)}, u32[]{:S(2)}) copy-start(f32[40,256]{1,0:T(8,128)} %get-tuple-element.63) | copy-start | bytes 122884
  65.3 33.0 %copy-start.3 = (f32[12,8,225]{2,1,0:T(8,128)S(1)}, f32[12,8,225]{2,1,0:T(8,128)}, u32[]{:S(2)}) copy-start(f32[12,8,225]{2,1,0:T(8,128)} %refs_11_.1) | copy-start | bytes 259204
  65.3 33.0 %copy-start.4 = (f32[6,8,225]{2,1,0:T(8,128)S(1)}, f32[6,8,225]{2,1,0:T(8,128)}, u32[]{:S(2)}) copy-start(f32[6,8,225]{2,1,0:T(8,128)} %refs_10_.1) | copy-start | bytes 129604
  65.3 33.0 %copy-start.6 = (f32[40,256]{1,0:T(8,128)S(1)}, f32[40,256]{1,0:T(8,128)}, u32[]{:S(2)}) copy-start(f32[40,256]{1,0:T(8,128)} %get-tuple-element.60.refs_0_) | copy-start | bytes 122884
  65.3 33.0 %copy-start.7 = (f32[24,8]{1,0:T(8,128)S(1)}, f32[24,8]{1,0:T(8,128)}, u32[]{:S(2)}) copy-start(f32[24,8]{1,0:T(8,128)} %constant.8.clone.refs_13_) | copy-start | bytes 2308
  65.3 33.0 %copy-start.8 = (s32[8,225]{1,0:T(8,128)S(1)}, s32[8,225]{1,0:T(8,128)}, u32[]{:S(2)}) copy-start(s32[8,225]{1,0:T(8,128)} %refs_12_.1) | copy-start | bytes 21604
  65.3 33.0 %copy-start.12 = (f32[3,1,256]{2,1,0:T(1,128)S(1)}, f32[3,1,256]{2,1,0:T(1,128)}, u32[]{:S(2)}) copy-start(f32[3,1,256]{2,1,0:T(1,128)} %refs_8_.1) | copy-start | bytes 9220
  65.3 33.0 %copy-start.13 = (f32[3,1,256]{2,1,0:T(1,128)S(1)}, f32[3,1,256]{2,1,0:T(1,128)}, u32[]{:S(2)}) copy-start(f32[3,1,256]{2,1,0:T(1,128)} %get-tuple-element.85.refs_9_) | copy-start | bytes 9220
  67.9 4.0 %collective-permute-start.12 = (f32[16,24,256]{2,1,0:T(8,128)S(1)}, f32[16,24,256]{2,1,0:T(8,128)S(1)}, u32[]{:S(2)}, u32[]{:S(2)}) collective-permute-start(f32[16,24,256]{2,1,0:T(8,128)S(1)} %get-tuple-element.74), channel_id=1, source_target_pairs={{0,8},{1,9},{2,10},{3,11},{4,12},{5,13},{6,14},{7,15},{8,0},{9,1},... | collective-permute-start | bytes 1179656 | tf_op jit(solution)/shard_map/ppermute | solution.py:318
  68.4 9.6 %collective-permute-start.9 = (f32[4,24,256]{2,1,0:T(8,128)S(1)}, f32[4,24,256]{2,1,0:T(8,128)S(1)}, u32[]{:S(2)}, u32[]{:S(2)}) collective-permute-start(f32[4,24,256]{2,1,0:T(8,128)S(1)} %copy-done.34), channel_id=1, source_target_pairs={{0,1},{1,0},{2,3},{3,2},{4,5},{5,4},{6,7},{7,6},{8,9},{9,8},{10,11... | collective-permute-start | bytes 294920 | tf_op jit(solution)/shard_map/ppermute | solution.py:318
  69.9 8.2 %collective-permute-start.10 = (f32[4,24,256]{2,1,0:T(8,128)S(1)}, f32[4,24,256]{2,1,0:T(8,128)S(1)}, u32[]{:S(2)}, u32[]{:S(2)}) collective-permute-start(f32[4,24,256]{2,1,0:T(8,128)S(1)} %copy-done.33), channel_id=1, source_target_pairs={{0,16},{1,17},{2,18},{3,19},{4,20},{5,21},{6,22},{7,23},{8,24},{9,... | collective-permute-start | bytes 294920 | tf_op jit(solution)/shard_map/ppermute | solution.py:318
  71.9 9.1 %collective-permute-start.11 = (f32[4,24,256]{2,1,0:T(8,128)S(1)}, f32[4,24,256]{2,1,0:T(8,128)S(1)}, u32[]{:S(2)}, u32[]{:S(2)}) collective-permute-start(f32[4,24,256]{2,1,0:T(8,128)S(1)} %copy-done.32), channel_id=1, source_target_pairs={{0,17},{1,16},{2,19},{3,18},{4,21},{5,20},{6,23},{7,22},{8,25},{9,... | collective-permute-start | bytes 294920 | tf_op jit(solution)/shard_map/ppermute | solution.py:318
  74.6 6.5 %collective-permute-start.13 = (f32[4,24,256]{2,1,0:T(8,128)}, f32[4,24,256]{2,1,0:T(8,128)S(1)}, u32[]{:S(2)}, u32[]{:S(2)}) collective-permute-start(f32[4,24,256]{2,1,0:T(8,128)} %get-tuple-element.77), channel_id=1, source_target_pairs={{0,1},{1,0},{2,3},{3,2},{4,5},{5,4},{6,7},{7,6},{8,9},{9,8},{10,11... | collective-permute-start | bytes 294920 | tf_op jit(solution)/shard_map/ppermute | solution.py:318
  76.1 5.9 %collective-permute-start.14 = (f32[4,24,256]{2,1,0:T(8,128)}, f32[4,24,256]{2,1,0:T(8,128)S(1)}, u32[]{:S(2)}, u32[]{:S(2)}) collective-permute-start(f32[4,24,256]{2,1,0:T(8,128)} %get-tuple-element.78), channel_id=1, source_target_pairs={{0,16},{1,17},{2,18},{3,19},{4,20},{5,21},{6,22},{7,23},{8,24},{9,... | collective-permute-start | bytes 294920 | tf_op jit(solution)/shard_map/ppermute | solution.py:318
  78.1 5.7 %collective-permute-start.15 = (f32[4,24,256]{2,1,0:T(8,128)}, f32[4,24,256]{2,1,0:T(8,128)S(1)}, u32[]{:S(2)}, u32[]{:S(2)}) collective-permute-start(f32[4,24,256]{2,1,0:T(8,128)} %get-tuple-element.79), channel_id=1, source_target_pairs={{0,17},{1,16},{2,19},{3,18},{4,21},{5,20},{6,23},{7,22},{8,25},{9,... | collective-permute-start | bytes 294920 | tf_op jit(solution)/shard_map/ppermute | solution.py:318
  78.1 14.3 %collective-permute-start.5 = (f32[40,256]{1,0:T(8,128)S(1)}, f32[40,256]{1,0:T(8,128)S(1)}, u32[]{:S(2)}, u32[]{:S(2)}) collective-permute-start(f32[40,256]{1,0:T(8,128)S(1)} %copy-done.37), channel_id=1, source_target_pairs={{0,2},{1,3},{2,0},{3,1},{4,6},{5,7},{6,4},{7,5},{8,10},{9,11},{10,... | collective-permute-start | bytes 122888 | tf_op jit(solution)/shard_map/ppermute | solution.py:318
  86.3 11.9 %collective-permute-start.16 = (f32[48,256]{1,0:T(8,128)}, f32[48,256]{1,0:T(8,128)S(1)}, u32[]{:S(2)}, u32[]{:S(2)}) collective-permute-start(f32[48,256]{1,0:T(8,128)} %get-tuple-element.82), channel_id=1, source_target_pairs={{0,2},{1,3},{2,0},{3,1},{4,6},{5,7},{6,4},{7,5},{8,10},{9,11},{10,... | collective-permute-start | bytes 147464 | tf_op jit(solution)/shard_map/ppermute | solution.py:318
  87.9 10.4 %collective-permute-start.17 = (f32[48,256]{1,0:T(8,128)}, f32[48,256]{1,0:T(8,128)S(1)}, u32[]{:S(2)}, u32[]{:S(2)}) collective-permute-start(f32[48,256]{1,0:T(8,128)} %get-tuple-element.83), channel_id=1, source_target_pairs={{0,4},{1,5},{2,6},{3,7},{4,0},{5,1},{6,2},{7,3},{8,12},{9,13},{10,... | collective-permute-start | bytes 147464 | tf_op jit(solution)/shard_map/ppermute | solution.py:318
  90.5 7.8 %collective-permute-start.18 = (f32[48,256]{1,0:T(8,128)}, f32[48,256]{1,0:T(8,128)S(1)}, u32[]{:S(2)}, u32[]{:S(2)}) collective-permute-start(f32[48,256]{1,0:T(8,128)} %get-tuple-element.84), channel_id=1, source_target_pairs={{0,6},{1,7},{2,4},{3,5},{4,2},{5,3},{6,0},{7,1},{8,14},{9,15},{10,... | collective-permute-start | bytes 147464 | tf_op jit(solution)/shard_map/ppermute | solution.py:318
  90.7 6.7 %collective-permute-start.6 = (f32[40,256]{1,0:T(8,128)S(1)}, f32[40,256]{1,0:T(8,128)S(1)}, u32[]{:S(2)}, u32[]{:S(2)}) collective-permute-start(f32[40,256]{1,0:T(8,128)S(1)} %copy-done.36), channel_id=1, source_target_pairs={{0,4},{1,5},{2,6},{3,7},{4,0},{5,1},{6,2},{7,3},{8,12},{9,13},{10,... | collective-permute-start | bytes 122888 | tf_op jit(solution)/shard_map/ppermute | solution.py:318
  92.4 5.8 %collective-permute-start.7 = (f32[40,256]{1,0:T(8,128)S(1)}, f32[40,256]{1,0:T(8,128)S(1)}, u32[]{:S(2)}, u32[]{:S(2)}) collective-permute-start(f32[40,256]{1,0:T(8,128)S(1)} %copy-done.35), channel_id=1, source_target_pairs={{0,6},{1,7},{2,4},{3,5},{4,2},{5,3},{6,0},{7,1},{8,14},{9,15},{10,... | collective-permute-start | bytes 122888 | tf_op jit(solution)/shard_map/ppermute | solution.py:318
  100.9 4.6 %collective-permute-start.19 = (f32[3,1,256]{2,1,0:T(1,128)S(1)}, f32[3,1,256]{2,1,0:T(1,128)S(1)}, u32[]{:S(2)}, u32[]{:S(2)}) collective-permute-start(f32[3,1,256]{2,1,0:T(1,128)S(1)} %slice_bitcast_fusion), channel_id=1, source_target_pairs={{0,1},{1,2},{2,3},{3,4},{4,5},{5,6},{6,7},{8,9},{9,10},{10,11},{11... | collective-permute-start | bytes 9224 | tf_op jit(solution)/shard_map/ppermute | solution.py:49
  (26 other events, 53.0 us)

commit v4 on v3

--- a/solution.py
+++ b/solution.py
@@ -12,7 +12,7 @@
 GX = 15
 LANES = 128
 COLUMNS = 256
-CHUNKS = ((0, 4), (4, 2), (6, 2))
+CHUNKS = ((0, 4), (4, 4))
 SPARE = 11
 QUANTUM = float((1 << 20) - 1)
 
@@ -116,8 +116,20 @@
 
 def looked_up(table_ref, first_row, rows, lane, bits):
     if rows == 1:
-        row = jnp.broadcast_to(table_ref[pl.ds(first_row, 1), :], lane.shape)
-        return jnp.take_along_axis(row, lane, axis=1, mode="promise_in_bounds")
+        row = jnp.broadcast_to(table_ref[pl.ds(first_row, 1), :], lane.shape[:2])
+        return lax.gather(
+            row,
+            lane,
+            lax.GatherDimensionNumbers(
+                offset_dims=(),
+                collapsed_slice_dims=(1,),
+                start_index_map=(1,),
+                operand_batching_dims=(0,),
+                start_indices_batching_dims=(0,),
+            ),
+            slice_sizes=(1, 1),
+            mode=lax.GatherScatterMode.PROMISE_IN_BOUNDS,
+        )
     half = rows // 2
     level = half.bit_length() - 1
     low = looked_up(table_ref, first_row, half, lane, bits)
@@ -152,7 +164,7 @@
         sums = [jnp.zeros((8, LANES), jnp.float32) for pair in range(9)]
         for group in range(groups):
             ids = tile_ref[pl.ds(8 * group, 8), :]
-            lane = ids & (LANES - 1)
+            lane = (ids & (LANES - 1))[:, :, None]
             row = lax.shift_right_logical(ids, 7)
             bits = [(row & (1 << level)) != 0 for level in range(table_rows.bit_length() - 1)]
             leading = looked_up(table_ref, 0, table_rows, lane, bits)
@@ -250,7 +262,7 @@
         functools.partial(cell_sum_kernel, first, count),
         out_shape=out_shape,
         scratch_shapes=[pltpu.VMEM((-(-count * per_octant // 8) * 8, LANES), jnp.int32)],
-        compiler_params=pltpu.CompilerParams(vmem_limit_bytes=24 * 1024 * 1024),
+        compiler_params=pltpu.CompilerParams(vmem_limit_bytes=8 * 1024 * 1024),
         cost_estimate=pl.CostEstimate(
             flops=count * 4 * 10**9, bytes_accessed=count * 10**7, transcendentals=0
         ),
@@ -273,7 +285,7 @@
             pltpu.VMEM((1, bricks), jnp.int32),
             pltpu.VMEM((members * rows, bricks), jnp.bfloat16),
         ],
-        compiler_params=pltpu.CompilerParams(vmem_limit_bytes=32 * 1024 * 1024),
+        compiler_params=pltpu.CompilerParams(vmem_limit_bytes=24 * 1024 * 1024),
         cost_estimate=pl.CostEstimate(
             flops=rows * 3 * 10**7, bytes_accessed=rows * 10**5, transcendentals=0
         ),
@@ -307,6 +319,7 @@
         functools.partial(part_sum_kernel, [len(terms) for terms in groups], len(passed)),
         out_shape=[part] * shape[0]
         + [jax.ShapeDtypeStruct(array.shape, array.dtype) for array in passed],
+        compiler_params=pltpu.CompilerParams(vmem_limit_bytes=16 * 1024 * 1024),
         name=name,
     )(*[term for terms in groups for term in terms], *passed)
     return out[: shape[0]], *out[shape[0] :]
@@ -359,18 +372,13 @@
     gathered = [
         sum(ref[:, 0:elements] for ref in refs[at : at + sources]) for at in (0, sources)
     ]
-    chunk_sums = [
-        gathered[0],
-        gathered[1][: padded_rows(CHUNKS[1][1])],
-        gathered[1][padded_rows(CHUNKS[1][1]) :],
-    ]
     counts = gathered[0][9 * CHUNKS[0][1] : 9 * CHUNKS[0][1] + 1]
     per_brick = 1.0 / (8.0 * jnp.maximum(counts, 1.0))
     frames = [
         jnp.concatenate(
             [
                 sums[count * k : count * (k + 1)]
-                for sums, (first, count) in zip(chunk_sums, CHUNKS)
+                for sums, (first, count) in zip(gathered, CHUNKS)
             ],
             axis=0,
         )
@@ -500,7 +508,7 @@
             jax.ShapeDtypeStruct(stress_old.shape, jnp.float32),
             jax.ShapeDtypeStruct((2,) + own.shape, jnp.float32),
         ),
-        compiler_params=pltpu.CompilerParams(vmem_limit_bytes=32 * 1024 * 1024),
+        compiler_params=pltpu.CompilerParams(vmem_limit_bytes=8 * 1024 * 1024),
         name="stress_update",
     )(*gathered, own, upper, stress_old, resistance, quad_weights, table)
 
@@ -519,26 +527,18 @@
     places = lax.axis_size("ca") * lax.axis_size("fe")
     bricks = grain_ids.shape[1]
     upper_layer = passed_along(displacement, "fe", -1)
-    labels = jnp.where(
-        brick_active > 0, brick_owner[:, 0] * COLUMNS + brick_element, -1
-    ).reshape(1, bricks)
-    (first_a, count_a), (first_b, count_b), (first_c, count_c) = CHUNKS
+    owner = lax.optimization_barrier(brick_owner.reshape(bricks))
+    labels = jnp.where(brick_active > 0, owner * COLUMNS + brick_element, -1).reshape(1, bricks)
+    (first_a, count_a), (first_b, count_b) = CHUNKS
     split_a, labels, table = cell_sums(first_a, count_a, grain_ids, labels, euler_angles)
     keep_a, send_a, labels = brick_sums(split_a, labels, places)
     split_b, labels = cell_sums(first_b, count_b, grain_ids, labels, table)
-    core_a, labels, upper_layer = part_sum(
-        [across_cores(keep_a, send_a)], [labels, upper_layer], "core_sum_a"
-    )
+    core_a, labels = part_sum([across_cores(keep_a, send_a)], [labels], "core_sum_a")
     keep_b, send_b, labels = brick_sums(split_b, labels, places)
-    split_c, labels = cell_sums(first_c, count_c, grain_ids, labels, table)
+    core_b, labels = part_sum([across_cores(keep_b, send_b)], [labels], "core_sum_b")
     plane_a, labels = part_sum([across_plane(core_a)], [labels], "plane_sum_a")
-    core_b, labels = part_sum([across_cores(keep_b, send_b)], [labels], "core_sum_b")
-    keep_c, send_c, labels = brick_sums(split_c, labels, places)
-    core_c, labels = part_sum([across_cores(keep_c, send_c)], [labels], "core_sum_c")
-    plane_bc, labels = part_sum(
-        [across_plane(core_b), across_plane(core_c)], [labels], "plane_sum_b_c"
-    )
-    gathered = across_height(plane_a) + across_height(plane_bc)
+    plane_b, labels = part_sum([across_plane(core_b)], [labels], "plane_sum_b")
+    gathered = across_height(plane_a) + across_height(plane_b)
     stress_new, nodal = element_update(
         gathered, displacement, upper_layer, stress_old, resistance, quad_weights
     )

time: 107 us -> 85.6 us (0.80)
  Pallas kernels: 56 us -> 45.4 us
  local copies, waits for them, and re-layouts: 10.2 us -> 2.36 us
  waiting for transfers between devices: 7.92 us -> 6.09 us
    pallas_call x5 -> x4, Pallas kernels: 9.66 us -> 0.86 us  [part_sum(): pl.pallas_call(functools.partial(part_sum_kernel, [len(terms) for terms i...]
    unnamed x76 -> x16, local copies, waits for them, and re-layouts: 10.2 us -> 2.35 us
    ppermute x18 -> x14, waiting for transfers between devices: 6.62 us -> 4.79 us  [to_relative(): lax.ppermute(block, ('ca', 'fe'), [(i, i ^ flip) for i in range(groups *...]
    pallas_call x3 -> x2, Pallas kernels: 38.1 us -> 37.1 us  [cell_sums(): pl.pallas_call(functools.partial(cell_sum_kernel, first, count), out_shap...]
    pallas_call x3 -> x2, Pallas kernels: 6.55 us -> 5.83 us  [brick_sums(): pl.pallas_call(brick_sum_kernel, out_shape=[half, half, jax.ShapeDtypeStr...]
    ppermute x18 -> x14, starting transfers between devices: 24.2 us -> 24.3 us  [to_relative(): lax.ppermute(block, ('ca', 'fe'), [(i, i ^ flip) for i in range(groups *...]
  transfers between devices with their start and end apart: 20 -> 16, of which waited for: 5 -> 4; matrix products, arithmetic and copies ran while one was open for 1% -> 0% of each run, Pallas kernels for 46% -> 23%
where the time goes in v4:
time: 85.6 us; the launch traced here: 85.3 us
  Pallas kernels  45.4 us (53%)
  starting transfers between devices  29.3 us (34%)
  waiting for transfers between devices  6.09 us (7%)
  local copies, waits for them, and re-layouts  2.36 us (3%)
  other arithmetic  1.32 us (2%)
    pallas_call x2, Pallas kernels, cell_sums(): pl.pallas_call(functools.partial(cell_sum_kernel, first, count), out_shap...  37.1 us
    ppermute x14, starting transfers between devices, to_relative(): lax.ppermute(block, ('ca', 'fe'), [(i, i ^ flip) for i in range(groups *...  24.3 us
    pallas_call x2, Pallas kernels, brick_sums(): pl.pallas_call(brick_sum_kernel, out_shape=[half, half, jax.ShapeDtypeStr...  5.83 us
    ppermute x2, starting transfers between devices, passed_along(): return lax.ppermute(block, axis, route)  4.99 us
    ppermute x14, waiting for transfers between devices, to_relative(): lax.ppermute(block, ('ca', 'fe'), [(i, i ^ flip) for i in range(groups *...  4.79 us
    unnamed x16, local copies, waits for them, and re-layouts  2.35 us
  transfers between devices with their start and end apart: 16, of which 4 were waited for; matrix products, arithmetic and copies ran while one was open for 0% of the time, Pallas kernels for 23%

profile of v4, /device:TPU:0, one launch (start us, length us, event | category | flops | bytes accessed | tf_op | source)
XLA Modules:
  0.0 85.3 jit_solution(12244866796728051808)
XLA Ops:
  0.6 0.7 add_select_fusion
  1.4 1.5 %copy-done.5 = s32[216,2048]{1,0:T(8,128)S(1)} copy-done((s32[216,2048]{1,0:T(8,128)S(1)}, s32[216,2048]{1,0:T(8,128)}, u32[]{:S(2)}) %copy-start.5) | copy-done | bytes 1769496
  2.8 0.8 copy-done.7
  3.7 18.6 %cell_sums.2 = (bf16[80,2048]{1,0:T(8,128)(2,1)S(1)}, s32[1,2048]{1,0:T(1,128)S(1)}, s32[64,128]{1,0:T(8,128)S(1)}) custom-call(s32[216,2048]{1,0:T(8,128)S(1)} %copy-done.5, s32[1,2048]{1,0:T(1,128)S(1)} %bitcast.14, f32[3,4096]{1,0:T(4,128)S(1)} %copy-done.7), custom_call_target="tpu_custom_call" | custom-call | flops 16000000000 | bytes 40000000 | tf_op jit(solution)/shard_map/cell_sums/pallas_call | solution.py:261
  22.3 2.9 %brick_sums.2 = (f32[16,40,256]{2,1,0:T(8,128)S(1)}, f32[16,40,256]{2,1,0:T(8,128)S(1)}, s32[1,2048]{1,0:T(1,128)S(1)}) custom-call(bf16[80,2048]{1,0:T(8,128)(2,1)S(1)} %get-tuple-element.34.split_ref, s32[1,2048]{1,0:T(1,128)S(1)} %get-tuple-element.35.label_ref), custom_call_target="tpu_custom_call" | custom-call | flops 2400000000 | bytes 8000000 | tf_op jit(solution)/shard_map/brick_sums/pallas_call | solution.py:281
  25.2 0.5 collective-permute-start
  25.7 18.5 %cell_sums.3 = (bf16[80,2048]{1,0:T(8,128)(2,1)S(1)}, s32[1,2048]{1,0:T(1,128)S(1)}) custom-call(s32[216,2048]{1,0:T(8,128)S(1)} %copy-done.6, s32[1,2048]{1,0:T(1,128)S(1)} %get-tuple-element.38.refs_1_, s32[64,128]{1,0:T(8,128)S(1)} %get-tuple-element.39.refs_2_), custom_call_target="tpu_custom_call" | custom-call | flops 16000000000 | bytes 40000000 | tf_op jit(solution)/shard_map/cell_sums/pallas_call | solution.py:261
  44.2 0.1 core_sum_a.1
  44.3 2.9 %brick_sums.3 = (f32[16,40,256]{2,1,0:T(8,128)S(1)}, f32[16,40,256]{2,1,0:T(8,128)S(1)}, s32[1,2048]{1,0:T(1,128)S(1)}) custom-call(bf16[80,2048]{1,0:T(8,128)(2,1)S(1)} %get-tuple-element.45.split_ref, s32[1,2048]{1,0:T(1,128)S(1)} %get-tuple-element.46.label_ref), custom_call_target="tpu_custom_call" | custom-call | flops 2400000000 | bytes 8000000 | tf_op jit(solution)/shard_map/brick_sums/pallas_call | solution.py:281
  47.3 0.0 copy-start.2
  47.3 0.1 collective-permute-start.4
  47.4 2.9 %collective-permute-start.1 = (f32[4,40,256]{2,1,0:T(8,128)S(1)}, f32[4,40,256]{2,1,0:T(8,128)S(1)}, u32[]{:S(2)}, u32[]{:S(2)}) collective-permute-start(f32[4,40,256]{2,1,0:T(8,128)S(1)} %get-tuple-element.42), channel_id=1, source_target_pairs={{0,1},{1,0},{2,3},{3,2},{4,5},{5,4},{6,7},{7,6},{8,9},{9,8},{10,11... | collective-permute-start | bytes 491528 | tf_op jit(solution)/shard_map/ppermute | solution.py:331
  50.4 1.5 %collective-permute-start.2 = (f32[4,40,256]{2,1,0:T(8,128)S(1)}, f32[4,40,256]{2,1,0:T(8,128)S(1)}, u32[]{:S(2)}, u32[]{:S(2)}) collective-permute-start(f32[4,40,256]{2,1,0:T(8,128)S(1)} %get-tuple-element.43), channel_id=1, source_target_pairs={{0,16},{1,17},{2,18},{3,19},{4,20},{5,21},{6,22},{7,23},{8,24},{9,... | collective-permute-start | bytes 491528 | tf_op jit(solution)/shard_map/ppermute | solution.py:331
  51.9 0.1 core_sum_b.1
  52.0 2.0 %collective-permute-start.8 = (f32[4,40,256]{2,1,0:T(8,128)S(1)}, f32[4,40,256]{2,1,0:T(8,128)S(1)}, u32[]{:S(2)}, u32[]{:S(2)}) collective-permute-start(f32[4,40,256]{2,1,0:T(8,128)S(1)} %get-tuple-element.56), channel_id=1, source_target_pairs={{0,1},{1,0},{2,3},{3,2},{4,5},{5,4},{6,7},{7,6},{8,9},{9,8},{10,11... | collective-permute-start | bytes 491528 | tf_op jit(solution)/shard_map/ppermute | solution.py:331
  54.0 1.5 %collective-permute-start.9 = (f32[4,40,256]{2,1,0:T(8,128)S(1)}, f32[4,40,256]{2,1,0:T(8,128)S(1)}, u32[]{:S(2)}, u32[]{:S(2)}) collective-permute-start(f32[4,40,256]{2,1,0:T(8,128)S(1)} %get-tuple-element.57), channel_id=1, source_target_pairs={{0,16},{1,17},{2,18},{3,19},{4,20},{5,21},{6,22},{7,23},{8,24},{9,... | collective-permute-start | bytes 491528 | tf_op jit(solution)/shard_map/ppermute | solution.py:331
  55.5 2.8 %collective-permute-start.10 = (f32[4,40,256]{2,1,0:T(8,128)S(1)}, f32[4,40,256]{2,1,0:T(8,128)S(1)}, u32[]{:S(2)}, u32[]{:S(2)}) collective-permute-start(f32[4,40,256]{2,1,0:T(8,128)S(1)} %get-tuple-element.58), channel_id=1, source_target_pairs={{0,17},{1,16},{2,19},{3,18},{4,21},{5,20},{6,23},{7,22},{8,25},{9,... | collective-permute-start | bytes 491528 | tf_op jit(solution)/shard_map/ppermute | solution.py:331
  58.4 2.3 %collective-permute-done.2.refs_2_ = f32[4,40,256]{2,1,0:T(8,128)S(1)} collective-permute-done((f32[4,40,256]{2,1,0:T(8,128)S(1)}, f32[4,40,256]{2,1,0:T(8,128)S(1)}, u32[]{:S(2)}, u32[]{:S(2)}) %collective-permute-start.2) | collective-permute-done | bytes 163872 | tf_op jit(solution)/shard_map/ppermute | solution.py:331
  60.6 0.1 plane_sum_a.1
  60.7 1.6 %collective-permute-start.5 = (f32[40,256]{1,0:T(8,128)S(1)}, f32[40,256]{1,0:T(8,128)S(1)}, u32[]{:S(2)}, u32[]{:S(2)}) collective-permute-start(f32[40,256]{1,0:T(8,128)S(1)} %get-tuple-element.52), channel_id=1, source_target_pairs={{0,2},{1,3},{2,0},{3,1},{4,6},{5,7},{6,4},{7,5},{8,10},{9,11},{10,... | collective-permute-start | bytes 122888 | tf_op jit(solution)/shard_map/ppermute | solution.py:331
  62.3 1.3 %collective-permute-start.14 = (f32[3,1,256]{2,1,0:T(1,128)S(1)}, f32[3,1,256]{2,1,0:T(1,128)S(1)}, u32[]{:S(2)}, u32[]{:S(2)}) collective-permute-start(f32[3,1,256]{2,1,0:T(1,128)S(1)} %copy-done.4), channel_id=1, source_target_pairs={{1,0},{2,1},{3,2},{4,3},{5,4},{6,5},{7,6},{9,8},{10,9},{11,10},{12... | collective-permute-start | bytes 9224 | tf_op jit(solution)/shard_map/ppermute | solution.py:49
  63.6 3.3 %collective-permute-start.6 = (f32[40,256]{1,0:T(8,128)S(1)}, f32[40,256]{1,0:T(8,128)S(1)}, u32[]{:S(2)}, u32[]{:S(2)}) collective-permute-start(f32[40,256]{1,0:T(8,128)S(1)} %get-tuple-element.53), channel_id=1, source_target_pairs={{0,4},{1,5},{2,6},{3,7},{4,0},{5,1},{6,2},{7,3},{8,12},{9,13},{10,... | collective-permute-start | bytes 122888 | tf_op jit(solution)/shard_map/ppermute | solution.py:331
  67.0 3.4 %collective-permute-start.7 = (f32[40,256]{1,0:T(8,128)S(1)}, f32[40,256]{1,0:T(8,128)S(1)}, u32[]{:S(2)}, u32[]{:S(2)}) collective-permute-start(f32[40,256]{1,0:T(8,128)S(1)} %get-tuple-element.54), channel_id=1, source_target_pairs={{0,6},{1,7},{2,4},{3,5},{4,2},{5,3},{6,0},{7,1},{8,14},{9,15},{10,... | collective-permute-start | bytes 122888 | tf_op jit(solution)/shard_map/ppermute | solution.py:331
  70.4 0.6 plane_sum_b.1
  71.1 0.9 %collective-permute-start.12 = (f32[40,256]{1,0:T(8,128)S(1)}, f32[40,256]{1,0:T(8,128)S(1)}, u32[]{:S(2)}, u32[]{:S(2)}) collective-permute-start(f32[40,256]{1,0:T(8,128)S(1)} %get-tuple-element.62), channel_id=1, source_target_pairs={{0,4},{1,5},{2,6},{3,7},{4,0},{5,1},{6,2},{7,3},{8,12},{9,13},{10,... | collective-permute-start | bytes 122888 | tf_op jit(solution)/shard_map/ppermute | solution.py:331
  72.0 3.4 %collective-permute-start.13 = (f32[40,256]{1,0:T(8,128)S(1)}, f32[40,256]{1,0:T(8,128)S(1)}, u32[]{:S(2)}, u32[]{:S(2)}) collective-permute-start(f32[40,256]{1,0:T(8,128)S(1)} %get-tuple-element.63), channel_id=1, source_target_pairs={{0,6},{1,7},{2,4},{3,5},{4,2},{5,3},{6,0},{7,1},{8,14},{9,15},{10,... | collective-permute-start | bytes 122888 | tf_op jit(solution)/shard_map/ppermute | solution.py:331
  75.5 0.5 collective-permute-done.12.refs_6_
  76.0 2.0 %collective-permute-done.13.refs_7_ = f32[40,256]{1,0:T(8,128)S(1)} collective-permute-done((f32[40,256]{1,0:T(8,128)S(1)}, f32[40,256]{1,0:T(8,128)S(1)}, u32[]{:S(2)}, u32[]{:S(2)}) %collective-permute-start.13) | collective-permute-done | bytes 40992 | tf_op jit(solution)/shard_map/ppermute | solution.py:331
  78.0 1.7 %stress_update.1 = (f32[6,8,225]{2,1,0:T(8,128)}, f32[2,3,1,256]{3,2,1,0:T(1,128)S(1)}) custom-call(f32[40,256]{1,0:T(8,128)S(1)} %get-tuple-element.51.refs_0_, f32[40,256]{1,0:T(8,128)S(1)} %collective-permute-done.5.refs_1_, f32[40,256]{1,0:T(8,128)S(1)} %collective-permute-done.6.refs_2_, f32[40,256]{1,0:T(8,128)S(1)} %collective-permute-done.7.refs_3_, ...), custom_call_target="tpu_custom_call" | custom-call | tf_op jit(solution)/shard_map/stress_update/pallas_call | solution.py:505
  79.7 3.7 %collective-permute-start.15 = (f32[3,1,256]{2,1,0:T(1,128)S(1)}, f32[3,1,256]{2,1,0:T(1,128)S(1)}, u32[]{:S(2)}, u32[]{:S(2)}) collective-permute-start(f32[3,1,256]{2,1,0:T(1,128)S(1)} %slice_bitcast_fusion), channel_id=1, source_target_pairs={{0,1},{1,2},{2,3},{3,4},{4,5},{5,6},{6,7},{8,9},{9,10},{10,11},{11... | collective-permute-start | bytes 9224 | tf_op jit(solution)/shard_map/ppermute | solution.py:49
  83.4 1.3 %collective-permute-done.15 = f32[3,1,256]{2,1,0:T(1,128)S(1)} collective-permute-done((f32[3,1,256]{2,1,0:T(1,128)S(1)}, f32[3,1,256]{2,1,0:T(1,128)S(1)}, u32[]{:S(2)}, u32[]{:S(2)}) %collective-permute-start.15) | collective-permute-done | bytes 3104 | tf_op jit(solution)/shard_map/ppermute | solution.py:49
  84.7 0.6 bitcast_add_fusion
  (28 shorter events, 0.1 us)
Async XLA Ops:
  1.4 1.5 %copy-start.5 = (s32[216,2048]{1,0:T(8,128)S(1)}, s32[216,2048]{1,0:T(8,128)}, u32[]{:S(2)}) copy-start(s32[216,2048]{1,0:T(8,128)} %refs_0_.3) | copy-start | bytes 5308420
  2.8 0.8 copy-start.7
  22.3 3.5 %copy-start.6 = (s32[216,2048]{1,0:T(8,128)S(1)}, s32[216,2048]{1,0:T(8,128)}, u32[]{:S(2)}) copy-start(s32[216,2048]{1,0:T(8,128)} %refs_0_.3) | copy-start | bytes 5308420
  25.2 19.0 %collective-permute-start = (f32[16,40,256]{2,1,0:T(8,128)S(1)}, f32[16,40,256]{2,1,0:T(8,128)S(1)}, u32[]{:S(2)}, u32[]{:S(2)}) collective-permute-start(f32[16,40,256]{2,1,0:T(8,128)S(1)} %get-tuple-element.37), channel_id=1, source_target_pairs={{0,8},{1,9},{2,10},{3,11},{4,12},{5,13},{6,14},{7,15},{8,0},{9,1},... | collective-permute-start | bytes 1966088 | tf_op jit(solution)/shard_map/ppermute | solution.py:331
  47.3 15.1 %copy-start.4 = (f32[3,1,256]{2,1,0:T(1,128)S(1)}, f32[3,1,256]{2,1,0:T(1,128)}, u32[]{:S(2)}) copy-start(f32[3,1,256]{2,1,0:T(1,128)} %refs_8_.1) | copy-start | bytes 9220
  47.3 30.7 %copy-start = (f32[12,8,225]{2,1,0:T(8,128)S(1)}, f32[12,8,225]{2,1,0:T(8,128)}, u32[]{:S(2)}) copy-start(f32[12,8,225]{2,1,0:T(8,128)} %refs_11_.1) | copy-start | bytes 259204
  47.3 30.7 %copy-start.1 = (f32[6,8,225]{2,1,0:T(8,128)S(1)}, f32[6,8,225]{2,1,0:T(8,128)}, u32[]{:S(2)}) copy-start(f32[6,8,225]{2,1,0:T(8,128)} %refs_10_.1) | copy-start | bytes 129604
  47.3 30.7 %copy-start.2 = (f32[24,8]{1,0:T(8,128)S(1)}, f32[24,8]{1,0:T(8,128)}, u32[]{:S(2)}) copy-start(f32[24,8]{1,0:T(8,128)} %constant.8.clone.refs_13_) | copy-start | bytes 2308
  47.3 30.7 %copy-start.3 = (s32[8,225]{1,0:T(8,128)S(1)}, s32[8,225]{1,0:T(8,128)}, u32[]{:S(2)}) copy-start(s32[8,225]{1,0:T(8,128)} %refs_12_.1) | copy-start | bytes 21604
  47.3 4.6 %collective-permute-start.4 = (f32[16,40,256]{2,1,0:T(8,128)S(1)}, f32[16,40,256]{2,1,0:T(8,128)S(1)}, u32[]{:S(2)}, u32[]{:S(2)}) collective-permute-start(f32[16,40,256]{2,1,0:T(8,128)S(1)} %get-tuple-element.48), channel_id=1, source_target_pairs={{0,8},{1,9},{2,10},{3,11},{4,12},{5,13},{6,14},{7,15},{8,0},{9,1},... | collective-permute-start | bytes 1966088 | tf_op jit(solution)/shard_map/ppermute | solution.py:331
  47.4 8.1 %collective-permute-start.1 = (f32[4,40,256]{2,1,0:T(8,128)S(1)}, f32[4,40,256]{2,1,0:T(8,128)S(1)}, u32[]{:S(2)}, u32[]{:S(2)}) collective-permute-start(f32[4,40,256]{2,1,0:T(8,128)S(1)} %get-tuple-element.42), channel_id=1, source_target_pairs={{0,1},{1,0},{2,3},{3,2},{4,5},{5,4},{6,7},{7,6},{8,9},{9,8},{10,11... | collective-permute-start | bytes 491528 | tf_op jit(solution)/shard_map/ppermute | solution.py:331
  50.4 10.3 %collective-permute-start.2 = (f32[4,40,256]{2,1,0:T(8,128)S(1)}, f32[4,40,256]{2,1,0:T(8,128)S(1)}, u32[]{:S(2)}, u32[]{:S(2)}) collective-permute-start(f32[4,40,256]{2,1,0:T(8,128)S(1)} %get-tuple-element.43), channel_id=1, source_target_pairs={{0,16},{1,17},{2,18},{3,19},{4,20},{5,21},{6,22},{7,23},{8,24},{9,... | collective-permute-start | bytes 491528 | tf_op jit(solution)/shard_map/ppermute | solution.py:331
  51.9 8.7 %collective-permute-start.3 = (f32[4,40,256]{2,1,0:T(8,128)S(1)}, f32[4,40,256]{2,1,0:T(8,128)S(1)}, u32[]{:S(2)}, u32[]{:S(2)}) collective-permute-start(f32[4,40,256]{2,1,0:T(8,128)S(1)} %get-tuple-element.44), channel_id=1, source_target_pairs={{0,17},{1,16},{2,19},{3,18},{4,21},{5,20},{6,23},{7,22},{8,25},{9,... | collective-permute-start | bytes 491528 | tf_op jit(solution)/shard_map/ppermute | solution.py:331
  52.0 11.6 %collective-permute-start.8 = (f32[4,40,256]{2,1,0:T(8,128)S(1)}, f32[4,40,256]{2,1,0:T(8,128)S(1)}, u32[]{:S(2)}, u32[]{:S(2)}) collective-permute-start(f32[4,40,256]{2,1,0:T(8,128)S(1)} %get-tuple-element.56), channel_id=1, source_target_pairs={{0,1},{1,0},{2,3},{3,2},{4,5},{5,4},{6,7},{7,6},{8,9},{9,8},{10,11... | collective-permute-start | bytes 491528 | tf_op jit(solution)/shard_map/ppermute | solution.py:331
  54.0 13.0 %collective-permute-start.9 = (f32[4,40,256]{2,1,0:T(8,128)S(1)}, f32[4,40,256]{2,1,0:T(8,128)S(1)}, u32[]{:S(2)}, u32[]{:S(2)}) collective-permute-start(f32[4,40,256]{2,1,0:T(8,128)S(1)} %get-tuple-element.57), channel_id=1, source_target_pairs={{0,16},{1,17},{2,18},{3,19},{4,20},{5,21},{6,22},{7,23},{8,24},{9,... | collective-permute-start | bytes 491528 | tf_op jit(solution)/shard_map/ppermute | solution.py:331
  55.5 14.9 %collective-permute-start.10 = (f32[4,40,256]{2,1,0:T(8,128)S(1)}, f32[4,40,256]{2,1,0:T(8,128)S(1)}, u32[]{:S(2)}, u32[]{:S(2)}) collective-permute-start(f32[4,40,256]{2,1,0:T(8,128)S(1)} %get-tuple-element.58), channel_id=1, source_target_pairs={{0,17},{1,16},{2,19},{3,18},{4,21},{5,20},{6,23},{7,22},{8,25},{9,... | collective-permute-start | bytes 491528 | tf_op jit(solution)/shard_map/ppermute | solution.py:331
  60.7 11.3 %collective-permute-start.5 = (f32[40,256]{1,0:T(8,128)S(1)}, f32[40,256]{1,0:T(8,128)S(1)}, u32[]{:S(2)}, u32[]{:S(2)}) collective-permute-start(f32[40,256]{1,0:T(8,128)S(1)} %get-tuple-element.52), channel_id=1, source_target_pairs={{0,2},{1,3},{2,0},{3,1},{4,6},{5,7},{6,4},{7,5},{8,10},{9,11},{10,... | collective-permute-start | bytes 122888 | tf_op jit(solution)/shard_map/ppermute | solution.py:331
  62.3 8.7 %collective-permute-start.14 = (f32[3,1,256]{2,1,0:T(1,128)S(1)}, f32[3,1,256]{2,1,0:T(1,128)S(1)}, u32[]{:S(2)}, u32[]{:S(2)}) collective-permute-start(f32[3,1,256]{2,1,0:T(1,128)S(1)} %copy-done.4), channel_id=1, source_target_pairs={{1,0},{2,1},{3,2},{4,3},{5,4},{6,5},{7,6},{9,8},{10,9},{11,10},{12... | collective-permute-start | bytes 9224 | tf_op jit(solution)/shard_map/ppermute | solution.py:49
  63.6 11.8 %collective-permute-start.6 = (f32[40,256]{1,0:T(8,128)S(1)}, f32[40,256]{1,0:T(8,128)S(1)}, u32[]{:S(2)}, u32[]{:S(2)}) collective-permute-start(f32[40,256]{1,0:T(8,128)S(1)} %get-tuple-element.53), channel_id=1, source_target_pairs={{0,4},{1,5},{2,6},{3,7},{4,0},{5,1},{6,2},{7,3},{8,12},{9,13},{10,... | collective-permute-start | bytes 122888 | tf_op jit(solution)/shard_map/ppermute | solution.py:331
  67.0 8.5 %collective-permute-start.7 = (f32[40,256]{1,0:T(8,128)S(1)}, f32[40,256]{1,0:T(8,128)S(1)}, u32[]{:S(2)}, u32[]{:S(2)}) collective-permute-start(f32[40,256]{1,0:T(8,128)S(1)} %get-tuple-element.54), channel_id=1, source_target_pairs={{0,6},{1,7},{2,4},{3,5},{4,2},{5,3},{6,0},{7,1},{8,14},{9,15},{10,... | collective-permute-start | bytes 122888 | tf_op jit(solution)/shard_map/ppermute | solution.py:331
  71.0 4.4 %collective-permute-start.11 = (f32[40,256]{1,0:T(8,128)S(1)}, f32[40,256]{1,0:T(8,128)S(1)}, u32[]{:S(2)}, u32[]{:S(2)}) collective-permute-start(f32[40,256]{1,0:T(8,128)S(1)} %get-tuple-element.61), channel_id=1, source_target_pairs={{0,2},{1,3},{2,0},{3,1},{4,6},{5,7},{6,4},{7,5},{8,10},{9,11},{10,... | collective-permute-start | bytes 122888 | tf_op jit(solution)/shard_map/ppermute | solution.py:331
  71.1 4.9 %collective-permute-start.12 = (f32[40,256]{1,0:T(8,128)S(1)}, f32[40,256]{1,0:T(8,128)S(1)}, u32[]{:S(2)}, u32[]{:S(2)}) collective-permute-start(f32[40,256]{1,0:T(8,128)S(1)} %get-tuple-element.62), channel_id=1, source_target_pairs={{0,4},{1,5},{2,6},{3,7},{4,0},{5,1},{6,2},{7,3},{8,12},{9,13},{10,... | collective-permute-start | bytes 122888 | tf_op jit(solution)/shard_map/ppermute | solution.py:331
  72.0 6.0 %collective-permute-start.13 = (f32[40,256]{1,0:T(8,128)S(1)}, f32[40,256]{1,0:T(8,128)S(1)}, u32[]{:S(2)}, u32[]{:S(2)}) collective-permute-start(f32[40,256]{1,0:T(8,128)S(1)} %get-tuple-element.63), channel_id=1, source_target_pairs={{0,6},{1,7},{2,4},{3,5},{4,2},{5,3},{6,0},{7,1},{8,14},{9,15},{10,... | collective-permute-start | bytes 122888 | tf_op jit(solution)/shard_map/ppermute | solution.py:331
  79.7 5.0 %collective-permute-start.15 = (f32[3,1,256]{2,1,0:T(1,128)S(1)}, f32[3,1,256]{2,1,0:T(1,128)S(1)}, u32[]{:S(2)}, u32[]{:S(2)}) collective-permute-start(f32[3,1,256]{2,1,0:T(1,128)S(1)} %slice_bitcast_fusion), channel_id=1, source_target_pairs={{0,1},{1,2},{2,3},{3,4},{4,5},{5,6},{6,7},{8,9},{9,10},{10,11},{11... | collective-permute-start | bytes 9224 | tf_op jit(solution)/shard_map/ppermute | solution.py:49

commit v5 on v4

--- a/solution.py
+++ b/solution.py
@@ -116,9 +116,8 @@
 
 def looked_up(table_ref, first_row, rows, lane, bits):
     if rows == 1:
-        row = jnp.broadcast_to(table_ref[pl.ds(first_row, 1), :], lane.shape[:2])
         return lax.gather(
-            row,
+            table_ref[first_row],
             lane,
             lax.GatherDimensionNumbers(
                 offset_dims=(),
@@ -149,9 +148,9 @@
         words = rotation_words(euler_ref[...])
         for word in range(2):
             for row in range(table_rows):
-                table_ref[pl.ds(word * table_rows + row, 1), :] = words[word][
-                    :, row * LANES : (row + 1) * LANES
-                ]
+                table_ref[word * table_rows + row] = jnp.broadcast_to(
+                    words[word][:, row * LANES : (row + 1) * LANES], (8, LANES)
+                )
     groups = tile_ref.shape[0] // 8
     rows_left = count * per_octant - 8 * (groups - 1)
 
@@ -203,40 +202,36 @@
     lax.fori_loop(0, ids_ref.shape[1] // LANES, tile_sums, 0)
 
 
-def brick_sum_kernel(split_ref, label_ref, keep_ref, send_ref, label_out_ref, place_ref, masked_ref):
+def brick_sum_kernel(base, split_ref, label_ref, out_ref, label_out_ref, place_ref, masked_ref):
     bricks = split_ref.shape[1]
-    half_places = keep_ref.shape[0]
     labels = label_ref[...]
     label_out_ref[...] = labels
-    place_ref[...] = jnp.where(
-        labels < 0, -1, place_of(lax.shift_right_arithmetic(labels, COLUMNS.bit_length() - 1))
-    )
+    place = place_of(lax.shift_right_arithmetic(labels, COLUMNS.bit_length() - 1))
+    place_ref[...] = jnp.where(labels < 0, -1, place - base)
     column = lax.broadcasted_iota(jnp.int32, (COLUMNS, bricks), 0)
     chosen = (column == labels & (COLUMNS - 1)).astype(jnp.bfloat16)
     split_rows = split_ref.shape[0]
     half_rows = split_rows // 2
     members = masked_ref.shape[0] // split_rows
-    for base, out_ref in ((half_places, send_ref), (0, keep_ref)):
-
-        def place_group(step, carry):
-            place = place_ref[...] - base
-            for member in range(members):
-                mask = (place == step * members + member).astype(jnp.bfloat16)
-                masked_ref[pl.ds(member * split_rows, split_rows), :] = split_ref[...] * mask
-            product = lax.dot_general(
-                masked_ref[...],
-                chosen,
-                (((1,), (1,)), ((), ())),
-                preferred_element_type=jnp.float32,
+
+    def place_group(step, carry):
+        for member in range(members):
+            mask = (place_ref[...] == step * members + member).astype(jnp.bfloat16)
+            masked_ref[pl.ds(member * split_rows, split_rows), :] = split_ref[...] * mask
+        product = lax.dot_general(
+            masked_ref[...],
+            chosen,
+            (((1,), (1,)), ((), ())),
+            preferred_element_type=jnp.float32,
+        )
+        for member in range(members):
+            at = member * split_rows
+            out_ref[step * members + member] = (
+                product[at : at + half_rows] + product[at + half_rows : at + split_rows]
             )
-            for member in range(members):
-                at = member * split_rows
-                out_ref[step * members + member] = (
-                    product[at : at + half_rows] + product[at + half_rows : at + split_rows]
-                )
-            return carry
-
-        lax.fori_loop(0, half_places // members, place_group, 0)
+        return carry
+
+    lax.fori_loop(0, out_ref.shape[0] // members, place_group, 0)
 
 
 def place_of(owner):
@@ -257,7 +252,7 @@
     ]
     if first == 0:
         grains = table.shape[1]
-        out_shape.append(jax.ShapeDtypeStruct((2 * grains // LANES, LANES), jnp.int32))
+        out_shape.append(jax.ShapeDtypeStruct((2 * grains // LANES, 8, LANES), jnp.int32))
     return pl.pallas_call(
         functools.partial(cell_sum_kernel, first, count),
         out_shape=out_shape,
@@ -274,20 +269,22 @@
     return -(-9 * count // 8) * 8
 
 
-def brick_sums(split, labels, places):
+def brick_sums(split, labels, places, base):
     rows, bricks = split.shape
-    members = min(16, places // 2)
-    half = jax.ShapeDtypeStruct((places // 2, rows // 2, COLUMNS), jnp.float32)
+    members = min(16, places)
     return pl.pallas_call(
-        brick_sum_kernel,
-        out_shape=[half, half, jax.ShapeDtypeStruct(labels.shape, jnp.int32)],
+        functools.partial(brick_sum_kernel, base),
+        out_shape=[
+            jax.ShapeDtypeStruct((places, rows // 2, COLUMNS), jnp.float32),
+            jax.ShapeDtypeStruct(labels.shape, jnp.int32),
+        ],
         scratch_shapes=[
             pltpu.VMEM((1, bricks), jnp.int32),
             pltpu.VMEM((members * rows, bricks), jnp.bfloat16),
         ],
         compiler_params=pltpu.CompilerParams(vmem_limit_bytes=24 * 1024 * 1024),
         cost_estimate=pl.CostEstimate(
-            flops=rows * 3 * 10**7, bytes_accessed=rows * 10**5, transcendentals=0
+            flops=rows * 15 * 10**6, bytes_accessed=rows * 5 * 10**4, transcendentals=0
         ),
         name="brick_sums",
     )(split, labels)
@@ -366,7 +363,7 @@
 
 
 def update_kernel(sources, *refs):
-    own_ref, upper_ref, stress_ref, resistance_ref, weights_ref, table_ref = refs[2 * sources : -2]
+    own_ref, layers_ref, stress_ref, resistance_ref, weights_ref, table_ref = refs[2 * sources : -2]
     stress_out_ref, nodal_ref = refs[-2:]
     elements = stress_ref.shape[2]
     gathered = [
@@ -396,9 +393,15 @@
     ]
     corner = lax.broadcasted_iota(jnp.int32, (24, 1), 0) & 7
     upper_corner = (corner & 1) == 1
+    above = lax.axis_index("fe") + 1
+    clamped = above == layers_ref.shape[0]
+    above = jnp.minimum(above, layers_ref.shape[0] - 1)
+    free = jnp.where(clamped, 0.0, 1.0)
     values = jnp.where(
         upper_corner,
-        jnp.concatenate([jnp.broadcast_to(upper_ref[c], (8, COLUMNS)) for c in range(3)], axis=0),
+        jnp.concatenate(
+            [jnp.broadcast_to(layers_ref[above, c] * free, (8, COLUMNS)) for c in range(3)], axis=0
+        ),
         jnp.concatenate([jnp.broadcast_to(own_ref[c], (8, COLUMNS)) for c in range(3)], axis=0),
     )
     corners = jnp.zeros((24, elements), jnp.float32)
@@ -492,7 +495,7 @@
         nodal_ref[1, c] = jnp.sum(above[8 * c : 8 * c + 8], axis=0, keepdims=True)
 
 
-def element_update(gathered, own, upper, stress_old, resistance, quad_weights):
+def element_update(gathered, own, layers, stress_old, resistance, quad_weights):
     grad_table = shape_gradients()
     table = jnp.asarray(
         [
@@ -510,7 +513,7 @@
         ),
         compiler_params=pltpu.CompilerParams(vmem_limit_bytes=8 * 1024 * 1024),
         name="stress_update",
-    )(*gathered, own, upper, stress_old, resistance, quad_weights, table)
+    )(*gathered, own, layers, stress_old, resistance, quad_weights, table)
 
 
 def body(
@@ -524,23 +527,25 @@
     resistance,
     quad_weights,
 ):
-    places = lax.axis_size("ca") * lax.axis_size("fe")
+    half = lax.axis_size("ca") * lax.axis_size("fe") // 2
     bricks = grain_ids.shape[1]
-    upper_layer = passed_along(displacement, "fe", -1)
+    layers = lax.all_gather(displacement, "fe")
     owner = lax.optimization_barrier(brick_owner.reshape(bricks))
     labels = jnp.where(brick_active > 0, owner * COLUMNS + brick_element, -1).reshape(1, bricks)
     (first_a, count_a), (first_b, count_b) = CHUNKS
-    split_a, labels, table = cell_sums(first_a, count_a, grain_ids, labels, euler_angles)
-    keep_a, send_a, labels = brick_sums(split_a, labels, places)
-    split_b, labels = cell_sums(first_b, count_b, grain_ids, labels, table)
-    core_a, labels = part_sum([across_cores(keep_a, send_a)], [labels], "core_sum_a")
-    keep_b, send_b, labels = brick_sums(split_b, labels, places)
-    core_b, labels = part_sum([across_cores(keep_b, send_b)], [labels], "core_sum_b")
-    plane_a, labels = part_sum([across_plane(core_a)], [labels], "plane_sum_a")
+    split, labels, table = cell_sums(first_a, count_a, grain_ids, labels, euler_angles)
+    send, labels = brick_sums(split, labels, half, half)
+    keep, labels = brick_sums(split, labels, half, 0)
+    core_a, labels = part_sum([across_cores(keep, send)], [labels], "core_sum_a")
+    split, labels = cell_sums(first_b, count_b, grain_ids, labels, table)
+    plane_a, labels, layers = part_sum([across_plane(core_a)], [labels, layers], "plane_sum_a")
+    send, labels = brick_sums(split, labels, half, half)
+    keep, labels = brick_sums(split, labels, half, 0)
+    core_b, labels = part_sum([across_cores(keep, send)], [labels], "core_sum_b")
     plane_b, labels = part_sum([across_plane(core_b)], [labels], "plane_sum_b")
     gathered = across_height(plane_a) + across_height(plane_b)
     stress_new, nodal = element_update(
-        gathered, displacement, upper_layer, stress_old, resistance, quad_weights
+        gathered, displacement, layers, stress_old, resistance, quad_weights
     )
     forces = nodal[0] + passed_along(nodal[1], "fe", 1)
     return (stress_new, forces)

time: 85.6 us -> 111 us (1.30)
  blocking collectives: 0 us -> 31.8 us
  starting transfers between devices: 29.3 us -> 21.6 us
  waiting for transfers between devices: 6.09 us -> 7.96 us
    all_gather x0 -> x1, blocking collectives: none -> 31.8 us  [body(): layers = lax.all_gather(displacement, 'fe')]
    ppermute x14, starting transfers between devices: 24.3 us -> 17.9 us  [to_relative(): lax.ppermute(block, ('ca', 'fe'), [(i, i ^ flip) for i in range(groups *...]
    ppermute x14, waiting for transfers between devices: 4.79 us -> 6.66 us  [to_relative(): lax.ppermute(block, ('ca', 'fe'), [(i, i ^ flip) for i in range(groups *...]
    ppermute x2 -> x1, starting transfers between devices: 4.99 us -> 3.69 us  [passed_along(): return lax.ppermute(block, axis, route)]
    pallas_call x2 -> x4, Pallas kernels: 5.83 us -> 6.27 us  [brick_sums(): pl.pallas_call(functools.partial(brick_sum_kernel, base), out_shape=[jax....]
  transfers between devices with their start and end apart: 16 -> 15, of which waited for: 4 -> 6; matrix products, arithmetic and copies ran while one was open for 0% -> 0% of each run, Pallas kernels for 23% -> 20%
where the time goes in v5:
time: 111 us
  Pallas kernels  45.3 us (41%)
  blocking collectives  31.8 us (29%)
  starting transfers between devices  21.6 us (19%)
  waiting for transfers between devices  7.96 us (7%)
  local copies, waits for them, and re-layouts  2.35 us (2%)
  other arithmetic  1.32 us (1%)
    pallas_call x2, Pallas kernels, cell_sums(): pl.pallas_call(functools.partial(cell_sum_kernel, first, count), out_shap...  36.4 us
    all_gather x1, blocking collectives, body(): layers = lax.all_gather(displacement, 'fe')  31.8 us
    ppermute x14, starting transfers between devices, to_relative(): lax.ppermute(block, ('ca', 'fe'), [(i, i ^ flip) for i in range(groups *...  17.9 us
    ppermute x14, waiting for transfers between devices, to_relative(): lax.ppermute(block, ('ca', 'fe'), [(i, i ^ flip) for i in range(groups *...  6.66 us
    pallas_call x4, Pallas kernels, brick_sums(): pl.pallas_call(functools.partial(brick_sum_kernel, base), out_shape=[jax....  6.27 us
    ppermute x1, starting transfers between devices, passed_along(): return lax.ppermute(block, axis, route)  3.69 us
    unnamed x16, local copies, waits for them, and re-layouts  2.35 us
  transfers between devices with their start and end apart: 15, of which 6 were waited for; matrix products, arithmetic and copies ran while one was open for 0% of the time, Pallas kernels for 20%

profile of v5, /device:TPU:0, one launch (start us, length us, event | category | flops | bytes accessed | tf_op | source)
XLA Modules:
  0.0 111.1 jit_solution(3931633490240114329)
XLA Ops:
  0.6 0.7 add_select_fusion
  1.4 1.5 %copy-done.5 = s32[216,2048]{1,0:T(8,128)S(1)} copy-done((s32[216,2048]{1,0:T(8,128)S(1)}, s32[216,2048]{1,0:T(8,128)}, u32[]{:S(2)}) %copy-start.5) | copy-done | bytes 1769496
  2.8 0.8 copy-done.7
  3.7 18.3 %cell_sums.2 = (bf16[80,2048]{1,0:T(8,128)(2,1)S(1)}, s32[1,2048]{1,0:T(1,128)S(1)}, s32[64,8,128]{2,1,0:T(8,128)S(1)}) custom-call(s32[216,2048]{1,0:T(8,128)S(1)} %copy-done.5, s32[1,2048]{1,0:T(1,128)S(1)} %bitcast.16, f32[3,4096]{1,0:T(4,128)S(1)} %copy-done.7), custom_call_target="tpu_custom_call" | custom-call | flops 16000000000 | bytes 40000000 | tf_op jit(solution)/shard_map/cell_sums/pallas_call | solution.py:256
  22.0 1.6 %brick_sums.4 = (f32[16,40,256]{2,1,0:T(8,128)S(1)}, s32[1,2048]{1,0:T(1,128)S(1)}) custom-call(bf16[80,2048]{1,0:T(8,128)(2,1)S(1)} %get-tuple-element.37.split_ref, s32[1,2048]{1,0:T(1,128)S(1)} %get-tuple-element.38.label_ref), custom_call_target="tpu_custom_call" | custom-call | flops 1200000000 | bytes 4000000 | tf_op jit(solution)/shard_map/brick_sums/pallas_call | solution.py:275
  23.6 0.5 collective-permute-start
  24.1 31.8 %all-gather = f32[24,1,256]{2,1,0:T(1,128)S(1)} all-gather(f32[3,1,256]{2,1,0:T(1,128)S(1)} %copy-done.2), channel_id=2, replica_groups=mesh['ca'=4,'fe'=8] {'fe'}, dimensions={0}, use_global_device_ids=true | all-gather | bytes 27648 | tf_op jit(solution)/shard_map/all_gather | solution.py:532
  55.9 1.6 %brick_sums.5 = (f32[16,40,256]{2,1,0:T(8,128)S(1)}, s32[1,2048]{1,0:T(1,128)S(1)}) custom-call(bf16[80,2048]{1,0:T(8,128)(2,1)S(1)} %get-tuple-element.37.split_ref, s32[1,2048]{1,0:T(1,128)S(1)} %get-tuple-element.39.label_ref), custom_call_target="tpu_custom_call" | custom-call | flops 1200000000 | bytes 4000000 | tf_op jit(solution)/shard_map/brick_sums/pallas_call | solution.py:275
  57.5 0.1 core_sum_a.1
  57.6 1.6 %collective-permute-start.1 = (f32[4,40,256]{2,1,0:T(8,128)S(1)}, f32[4,40,256]{2,1,0:T(8,128)S(1)}, u32[]{:S(2)}, u32[]{:S(2)}) collective-permute-start(f32[4,40,256]{2,1,0:T(8,128)S(1)} %get-tuple-element.44), channel_id=1, source_target_pairs={{0,1},{1,0},{2,3},{3,2},{4,5},{5,4},{6,7},{7,6},{8,9},{9,8},{10,11... | collective-permute-start | bytes 491528 | tf_op jit(solution)/shard_map/ppermute | solution.py:328
  59.2 1.5 %collective-permute-start.2 = (f32[4,40,256]{2,1,0:T(8,128)S(1)}, f32[4,40,256]{2,1,0:T(8,128)S(1)}, u32[]{:S(2)}, u32[]{:S(2)}) collective-permute-start(f32[4,40,256]{2,1,0:T(8,128)S(1)} %get-tuple-element.45), channel_id=1, source_target_pairs={{0,16},{1,17},{2,18},{3,19},{4,20},{5,21},{6,22},{7,23},{8,24},{9,... | collective-permute-start | bytes 491528 | tf_op jit(solution)/shard_map/ppermute | solution.py:328
  60.7 0.4 collective-permute-start.3
  61.1 18.1 %cell_sums.3 = (bf16[80,2048]{1,0:T(8,128)(2,1)S(1)}, s32[1,2048]{1,0:T(1,128)S(1)}) custom-call(s32[216,2048]{1,0:T(8,128)S(1)} %copy-done.6, s32[1,2048]{1,0:T(1,128)S(1)} %get-tuple-element.47.refs_1_, s32[64,8,128]{2,1,0:T(8,128)S(1)} %get-tuple-element.48.refs_2_), custom_call_target="tpu_custom_call" | custom-call | flops 16000000000 | bytes 40000000 | tf_op jit(solution)/shard_map/cell_sums/pallas_call | solution.py:256
  79.3 1.6 %brick_sums.6 = (f32[16,40,256]{2,1,0:T(8,128)S(1)}, s32[1,2048]{1,0:T(1,128)S(1)}) custom-call(bf16[80,2048]{1,0:T(8,128)(2,1)S(1)} %get-tuple-element.54.split_ref, s32[1,2048]{1,0:T(1,128)S(1)} %get-tuple-element.55.label_ref), custom_call_target="tpu_custom_call" | custom-call | flops 1200000000 | bytes 4000000 | tf_op jit(solution)/shard_map/brick_sums/pallas_call | solution.py:275
  81.0 1.6 %brick_sums.7 = (f32[16,40,256]{2,1,0:T(8,128)S(1)}, s32[1,2048]{1,0:T(1,128)S(1)}) custom-call(bf16[80,2048]{1,0:T(8,128)(2,1)S(1)} %get-tuple-element.54.split_ref, s32[1,2048]{1,0:T(1,128)S(1)} %get-tuple-element.56.label_ref), custom_call_target="tpu_custom_call" | custom-call | flops 1200000000 | bytes 4000000 | tf_op jit(solution)/shard_map/brick_sums/pallas_call | solution.py:275
  82.6 0.5 collective-permute-done.7
  83.2 2.6 %collective-permute-start.10 = (f32[4,40,256]{2,1,0:T(8,128)S(1)}, f32[4,40,256]{2,1,0:T(8,128)S(1)}, u32[]{:S(2)}, u32[]{:S(2)}) collective-permute-start(f32[4,40,256]{2,1,0:T(8,128)S(1)} %get-tuple-element.63), channel_id=1, source_target_pairs={{0,17},{1,16},{2,19},{3,18},{4,21},{5,20},{6,23},{7,22},{8,25},{9,... | collective-permute-start | bytes 491528 | tf_op jit(solution)/shard_map/ppermute | solution.py:328
  85.7 0.5 collective-permute-start.8
  86.2 0.5 collective-permute-start.9
  86.7 3.2 %collective-permute-start.5 = (f32[40,256]{1,0:T(8,128)S(1)}, f32[40,256]{1,0:T(8,128)S(1)}, u32[]{:S(2)}, u32[]{:S(2)}) collective-permute-start(f32[40,256]{1,0:T(8,128)S(1)} %get-tuple-element.52), channel_id=1, source_target_pairs={{0,4},{1,5},{2,6},{3,7},{4,0},{5,1},{6,2},{7,3},{8,12},{9,13},{10,... | collective-permute-start | bytes 122888 | tf_op jit(solution)/shard_map/ppermute | solution.py:328
  90.0 1.2 %collective-permute-done.10.refs_3_ = f32[4,40,256]{2,1,0:T(8,128)S(1)} collective-permute-done((f32[4,40,256]{2,1,0:T(8,128)S(1)}, f32[4,40,256]{2,1,0:T(8,128)S(1)}, u32[]{:S(2)}, u32[]{:S(2)}) %collective-permute-start.10) | collective-permute-done | bytes 163872 | tf_op jit(solution)/shard_map/ppermute | solution.py:328
  91.2 2.6 %collective-permute-start.6 = (f32[40,256]{1,0:T(8,128)S(1)}, f32[40,256]{1,0:T(8,128)S(1)}, u32[]{:S(2)}, u32[]{:S(2)}) collective-permute-start(f32[40,256]{1,0:T(8,128)S(1)} %get-tuple-element.53), channel_id=1, source_target_pairs={{0,6},{1,7},{2,4},{3,5},{4,2},{5,3},{6,0},{7,1},{8,14},{9,15},{10,... | collective-permute-start | bytes 122888 | tf_op jit(solution)/shard_map/ppermute | solution.py:328
  93.8 0.2 collective-permute-done.8.refs_1_
  94.0 0.6 plane_sum_b.1
  94.6 3.3 %collective-permute-start.12 = (f32[40,256]{1,0:T(8,128)S(1)}, f32[40,256]{1,0:T(8,128)S(1)}, u32[]{:S(2)}, u32[]{:S(2)}) collective-permute-start(f32[40,256]{1,0:T(8,128)S(1)} %get-tuple-element.67), channel_id=1, source_target_pairs={{0,4},{1,5},{2,6},{3,7},{4,0},{5,1},{6,2},{7,3},{8,12},{9,13},{10,... | collective-permute-start | bytes 122888 | tf_op jit(solution)/shard_map/ppermute | solution.py:328
  98.0 1.1 collective-permute-start.13
  99.0 1.5 %collective-permute-done.12.refs_6_ = f32[40,256]{1,0:T(8,128)S(1)} collective-permute-done((f32[40,256]{1,0:T(8,128)S(1)}, f32[40,256]{1,0:T(8,128)S(1)}, u32[]{:S(2)}, u32[]{:S(2)}) %collective-permute-start.12) | collective-permute-done | bytes 40992 | tf_op jit(solution)/shard_map/ppermute | solution.py:328
  100.5 3.2 %collective-permute-done.13.refs_7_ = f32[40,256]{1,0:T(8,128)S(1)} collective-permute-done((f32[40,256]{1,0:T(8,128)S(1)}, f32[40,256]{1,0:T(8,128)S(1)}, u32[]{:S(2)}, u32[]{:S(2)}) %collective-permute-start.13) | collective-permute-done | bytes 40992 | tf_op jit(solution)/shard_map/ppermute | solution.py:328
  103.8 1.7 %stress_update.1 = (f32[6,8,225]{2,1,0:T(8,128)}, f32[2,3,1,256]{3,2,1,0:T(1,128)S(1)}) custom-call(f32[40,256]{1,0:T(8,128)S(1)} %get-tuple-element.50.refs_0_, f32[40,256]{1,0:T(8,128)S(1)} %collective-permute-done.4.refs_1_, f32[40,256]{1,0:T(8,128)S(1)} %collective-permute-done.5.refs_2_, f32[40,256]{1,0:T(8,128)S(1)} %collective-permute-done.6.refs_3_, ...), custom_call_target="tpu_custom_call" | custom-call | tf_op jit(solution)/shard_map/stress_update/pallas_call | solution.py:508
  105.5 3.7 %collective-permute-start.14 = (f32[3,1,256]{2,1,0:T(1,128)S(1)}, f32[3,1,256]{2,1,0:T(1,128)S(1)}, u32[]{:S(2)}, u32[]{:S(2)}) collective-permute-start(f32[3,1,256]{2,1,0:T(1,128)S(1)} %slice_bitcast_fusion), channel_id=1, source_target_pairs={{0,1},{1,2},{2,3},{3,4},{4,5},{5,6},{6,7},{8,9},{9,10},{10,11},{11... | collective-permute-start | bytes 9224 | tf_op jit(solution)/shard_map/ppermute | solution.py:49
  109.2 1.3 %collective-permute-done.14 = f32[3,1,256]{2,1,0:T(1,128)S(1)} collective-permute-done((f32[3,1,256]{2,1,0:T(1,128)S(1)}, f32[3,1,256]{2,1,0:T(1,128)S(1)}, u32[]{:S(2)}, u32[]{:S(2)}) %collective-permute-start.14) | collective-permute-done | bytes 3104 | tf_op jit(solution)/shard_map/ppermute | solution.py:49
  110.5 0.6 bitcast_add_fusion
  (29 shorter events, 0.3 us)
Async XLA Ops:
  1.4 1.5 %copy-start.5 = (s32[216,2048]{1,0:T(8,128)S(1)}, s32[216,2048]{1,0:T(8,128)}, u32[]{:S(2)}) copy-start(s32[216,2048]{1,0:T(8,128)} %refs_0_.3) | copy-start | bytes 5308420
  2.8 0.8 copy-start.7
  22.0 2.1 %copy-start.2 = (f32[3,1,256]{2,1,0:T(1,128)S(1)}, f32[3,1,256]{2,1,0:T(1,128)}, u32[]{:S(2)}) copy-start(f32[3,1,256]{2,1,0:T(1,128)} %refs_8_.1) | copy-start | bytes 9220
  23.6 33.9 %collective-permute-start = (f32[16,40,256]{2,1,0:T(8,128)S(1)}, f32[16,40,256]{2,1,0:T(8,128)S(1)}, u32[]{:S(2)}, u32[]{:S(2)}) collective-permute-start(f32[16,40,256]{2,1,0:T(8,128)S(1)} %get-tuple-element.41), channel_id=1, source_target_pairs={{0,8},{1,9},{2,10},{3,11},{4,12},{5,13},{6,14},{7,15},{8,0},{9,1},... | collective-permute-start | bytes 1966088 | tf_op jit(solution)/shard_map/ppermute | solution.py:328
  55.9 5.2 %copy-start.6 = (s32[216,2048]{1,0:T(8,128)S(1)}, s32[216,2048]{1,0:T(8,128)}, u32[]{:S(2)}) copy-start(s32[216,2048]{1,0:T(8,128)} %refs_0_.3) | copy-start | bytes 5308420
  57.6 21.7 %collective-permute-start.1 = (f32[4,40,256]{2,1,0:T(8,128)S(1)}, f32[4,40,256]{2,1,0:T(8,128)S(1)}, u32[]{:S(2)}, u32[]{:S(2)}) collective-permute-start(f32[4,40,256]{2,1,0:T(8,128)S(1)} %get-tuple-element.44), channel_id=1, source_target_pairs={{0,1},{1,0},{2,3},{3,2},{4,5},{5,4},{6,7},{7,6},{8,9},{9,8},{10,11... | collective-permute-start | bytes 491528 | tf_op jit(solution)/shard_map/ppermute | solution.py:328
  59.2 20.1 %collective-permute-start.2 = (f32[4,40,256]{2,1,0:T(8,128)S(1)}, f32[4,40,256]{2,1,0:T(8,128)S(1)}, u32[]{:S(2)}, u32[]{:S(2)}) collective-permute-start(f32[4,40,256]{2,1,0:T(8,128)S(1)} %get-tuple-element.45), channel_id=1, source_target_pairs={{0,16},{1,17},{2,18},{3,19},{4,20},{5,21},{6,22},{7,23},{8,24},{9,... | collective-permute-start | bytes 491528 | tf_op jit(solution)/shard_map/ppermute | solution.py:328
  60.7 18.6 %collective-permute-start.3 = (f32[4,40,256]{2,1,0:T(8,128)S(1)}, f32[4,40,256]{2,1,0:T(8,128)S(1)}, u32[]{:S(2)}, u32[]{:S(2)}) collective-permute-start(f32[4,40,256]{2,1,0:T(8,128)S(1)} %get-tuple-element.46), channel_id=1, source_target_pairs={{0,17},{1,16},{2,19},{3,18},{4,21},{5,20},{6,23},{7,22},{8,25},{9,... | collective-permute-start | bytes 491528 | tf_op jit(solution)/shard_map/ppermute | solution.py:328
  80.9 2.2 %collective-permute-start.7 = (f32[16,40,256]{2,1,0:T(8,128)S(1)}, f32[16,40,256]{2,1,0:T(8,128)S(1)}, u32[]{:S(2)}, u32[]{:S(2)}) collective-permute-start(f32[16,40,256]{2,1,0:T(8,128)S(1)} %get-tuple-element.58), channel_id=1, source_target_pairs={{0,8},{1,9},{2,10},{3,11},{4,12},{5,13},{6,14},{7,15},{8,0},{9,1},... | collective-permute-start | bytes 1966088 | tf_op jit(solution)/shard_map/ppermute | solution.py:328
  82.6 21.2 %copy-start = (f32[12,8,225]{2,1,0:T(8,128)S(1)}, f32[12,8,225]{2,1,0:T(8,128)}, u32[]{:S(2)}) copy-start(f32[12,8,225]{2,1,0:T(8,128)} %refs_11_.1) | copy-start | bytes 259204
  82.6 21.2 %copy-start.1 = (f32[6,8,225]{2,1,0:T(8,128)S(1)}, f32[6,8,225]{2,1,0:T(8,128)}, u32[]{:S(2)}) copy-start(f32[6,8,225]{2,1,0:T(8,128)} %refs_10_.1) | copy-start | bytes 129604
  82.6 21.2 %copy-start.3 = (f32[24,8]{1,0:T(8,128)S(1)}, f32[24,8]{1,0:T(8,128)}, u32[]{:S(2)}) copy-start(f32[24,8]{1,0:T(8,128)} %constant.8.clone.refs_13_) | copy-start | bytes 2308
  82.6 21.2 %copy-start.4 = (s32[8,225]{1,0:T(8,128)S(1)}, s32[8,225]{1,0:T(8,128)}, u32[]{:S(2)}) copy-start(s32[8,225]{1,0:T(8,128)} %refs_12_.1) | copy-start | bytes 21604
  83.2 8.0 %collective-permute-start.10 = (f32[4,40,256]{2,1,0:T(8,128)S(1)}, f32[4,40,256]{2,1,0:T(8,128)S(1)}, u32[]{:S(2)}, u32[]{:S(2)}) collective-permute-start(f32[4,40,256]{2,1,0:T(8,128)S(1)} %get-tuple-element.63), channel_id=1, source_target_pairs={{0,17},{1,16},{2,19},{3,18},{4,21},{5,20},{6,23},{7,22},{8,25},{9,... | collective-permute-start | bytes 491528 | tf_op jit(solution)/shard_map/ppermute | solution.py:328
  85.7 8.3 %collective-permute-start.8 = (f32[4,40,256]{2,1,0:T(8,128)S(1)}, f32[4,40,256]{2,1,0:T(8,128)S(1)}, u32[]{:S(2)}, u32[]{:S(2)}) collective-permute-start(f32[4,40,256]{2,1,0:T(8,128)S(1)} %get-tuple-element.61), channel_id=1, source_target_pairs={{0,1},{1,0},{2,3},{3,2},{4,5},{5,4},{6,7},{7,6},{8,9},{9,8},{10,11... | collective-permute-start | bytes 491528 | tf_op jit(solution)/shard_map/ppermute | solution.py:328
  86.2 7.8 %collective-permute-start.9 = (f32[4,40,256]{2,1,0:T(8,128)S(1)}, f32[4,40,256]{2,1,0:T(8,128)S(1)}, u32[]{:S(2)}, u32[]{:S(2)}) collective-permute-start(f32[4,40,256]{2,1,0:T(8,128)S(1)} %get-tuple-element.62), channel_id=1, source_target_pairs={{0,16},{1,17},{2,18},{3,19},{4,20},{5,21},{6,22},{7,23},{8,24},{9,... | collective-permute-start | bytes 491528 | tf_op jit(solution)/shard_map/ppermute | solution.py:328
  86.7 11.3 %collective-permute-start.4 = (f32[40,256]{1,0:T(8,128)S(1)}, f32[40,256]{1,0:T(8,128)S(1)}, u32[]{:S(2)}, u32[]{:S(2)}) collective-permute-start(f32[40,256]{1,0:T(8,128)S(1)} %get-tuple-element.51), channel_id=1, source_target_pairs={{0,2},{1,3},{2,0},{3,1},{4,6},{5,7},{6,4},{7,5},{8,10},{9,11},{10,... | collective-permute-start | bytes 122888 | tf_op jit(solution)/shard_map/ppermute | solution.py:328
  86.7 12.3 %collective-permute-start.5 = (f32[40,256]{1,0:T(8,128)S(1)}, f32[40,256]{1,0:T(8,128)S(1)}, u32[]{:S(2)}, u32[]{:S(2)}) collective-permute-start(f32[40,256]{1,0:T(8,128)S(1)} %get-tuple-element.52), channel_id=1, source_target_pairs={{0,4},{1,5},{2,6},{3,7},{4,0},{5,1},{6,2},{7,3},{8,12},{9,13},{10,... | collective-permute-start | bytes 122888 | tf_op jit(solution)/shard_map/ppermute | solution.py:328
  91.2 7.9 %collective-permute-start.6 = (f32[40,256]{1,0:T(8,128)S(1)}, f32[40,256]{1,0:T(8,128)S(1)}, u32[]{:S(2)}, u32[]{:S(2)}) collective-permute-start(f32[40,256]{1,0:T(8,128)S(1)} %get-tuple-element.53), channel_id=1, source_target_pairs={{0,6},{1,7},{2,4},{3,5},{4,2},{5,3},{6,0},{7,1},{8,14},{9,15},{10,... | collective-permute-start | bytes 122888 | tf_op jit(solution)/shard_map/ppermute | solution.py:328
  94.6 4.4 %collective-permute-start.11 = (f32[40,256]{1,0:T(8,128)S(1)}, f32[40,256]{1,0:T(8,128)S(1)}, u32[]{:S(2)}, u32[]{:S(2)}) collective-permute-start(f32[40,256]{1,0:T(8,128)S(1)} %get-tuple-element.66), channel_id=1, source_target_pairs={{0,2},{1,3},{2,0},{3,1},{4,6},{5,7},{6,4},{7,5},{8,10},{9,11},{10,... | collective-permute-start | bytes 122888 | tf_op jit(solution)/shard_map/ppermute | solution.py:328
  94.6 5.9 %collective-permute-start.12 = (f32[40,256]{1,0:T(8,128)S(1)}, f32[40,256]{1,0:T(8,128)S(1)}, u32[]{:S(2)}, u32[]{:S(2)}) collective-permute-start(f32[40,256]{1,0:T(8,128)S(1)} %get-tuple-element.67), channel_id=1, source_target_pairs={{0,4},{1,5},{2,6},{3,7},{4,0},{5,1},{6,2},{7,3},{8,12},{9,13},{10,... | collective-permute-start | bytes 122888 | tf_op jit(solution)/shard_map/ppermute | solution.py:328
  98.0 5.8 %collective-permute-start.13 = (f32[40,256]{1,0:T(8,128)S(1)}, f32[40,256]{1,0:T(8,128)S(1)}, u32[]{:S(2)}, u32[]{:S(2)}) collective-permute-start(f32[40,256]{1,0:T(8,128)S(1)} %get-tuple-element.68), channel_id=1, source_target_pairs={{0,6},{1,7},{2,4},{3,5},{4,2},{5,3},{6,0},{7,1},{8,14},{9,15},{10,... | collective-permute-start | bytes 122888 | tf_op jit(solution)/shard_map/ppermute | solution.py:328
  105.5 5.0 %collective-permute-start.14 = (f32[3,1,256]{2,1,0:T(1,128)S(1)}, f32[3,1,256]{2,1,0:T(1,128)S(1)}, u32[]{:S(2)}, u32[]{:S(2)}) collective-permute-start(f32[3,1,256]{2,1,0:T(1,128)S(1)} %slice_bitcast_fusion), channel_id=1, source_target_pairs={{0,1},{1,2},{2,3},{3,4},{4,5},{5,6},{6,7},{8,9},{9,10},{10,11},{11... | collective-permute-start | bytes 9224 | tf_op jit(solution)/shard_map/ppermute | solution.py:49

commit v6 on v5

--- a/solution.py
+++ b/solution.py
@@ -13,8 +13,7 @@
 LANES = 128
 COLUMNS = 256
 CHUNKS = ((0, 4), (4, 4))
-SPARE = 11
-QUANTUM = float((1 << 20) - 1)
+QUANTUM = float((1 << 17) - 1)
 
 SLIP_PLANES = [
     [value / math.sqrt(3.0) for value in row]
@@ -93,25 +92,26 @@
     x, y, z = [
         jnp.clip(jnp.round(value), -QUANTUM, QUANTUM).astype(jnp.int32) for value in (x, y, z)
     ]
-    low = (1 << SPARE) - 1
     return [
-        lax.shift_left(x, SPARE) | (lax.shift_right_arithmetic(z, SPARE) & low),
-        lax.shift_left(y, SPARE) | (z & low),
-    ]
-
-
-def rotation_products(first, second):
-    x = lax.shift_right_arithmetic(first, SPARE).astype(jnp.float32)
-    y = lax.shift_right_arithmetic(second, SPARE).astype(jnp.float32)
-    z = (
-        lax.shift_right_arithmetic(lax.shift_left(first, 32 - SPARE), 32 - 2 * SPARE)
-        | (second & ((1 << SPARE) - 1))
-    ).astype(jnp.float32)
-    square = x * x + y * y + z * z
-    scale = 2.0 / (1.0 + square * (1.0 / (QUANTUM * QUANTUM)))
-    w = scale - 1.0
-    x, y, z = x * scale, y * scale, z * scale
-    return [x * x, y * y, z * z, x * y, x * z, y * z, w * x, w * y, w * z]
+        (lax.shift_left(x, 14) | (lax.shift_right_arithmetic(y, 4) & 0x3FFF), 32),
+        (lax.shift_left(y & 0xF, 12) | (lax.shift_right_arithmetic(z, 6) & 0xFFF), 16),
+        (lax.shift_right_arithmetic(z, 2) & 0xF, 4),
+        (z & 0x3, 2),
+    ]
+
+
+def fill_table(table_ref, euler):
+    at = 0
+    for field, width in rotation_words(euler):
+        rows = field.shape[1] // LANES
+        shared = 32 // width
+        for first in range(0, rows, shared):
+            word = field[:, first * LANES : (first + 1) * LANES]
+            for other in range(1, shared):
+                row = field[:, (first + other) * LANES : (first + other + 1) * LANES]
+                word = word | lax.shift_left(row, other * width)
+            table_ref[at] = jnp.broadcast_to(word, (8, LANES))
+            at += 1
 
 
 def looked_up(table_ref, first_row, rows, lane, bits):
@@ -136,21 +136,47 @@
     return jnp.where(bits[level], high, low)
 
 
+def rotation_products(table_ref, table_rows, ids):
+    lane = (ids & (LANES - 1))[:, :, None]
+    row = lax.shift_right_logical(ids, 7)
+    bits = [(row & (1 << level)) != 0 for level in range(table_rows.bit_length() - 1)]
+    fields = []
+    at = 0
+    for width in (32, 16, 4, 2):
+        shared = 32 // width
+        skipped = shared.bit_length() - 1
+        rows = table_rows // shared
+        field = looked_up(table_ref, at, rows, lane, bits[skipped:])
+        if shared > 1:
+            field = lax.shift_right_logical(field, (row & (shared - 1)) * width)
+        fields.append(field)
+        at += rows
+    first, second, third, fourth = fields
+    x = lax.shift_right_arithmetic(first, 14).astype(jnp.float32)
+    y = lax.shift_right_arithmetic(lax.shift_left(first, 18), 14) | (
+        lax.shift_right_logical(second, 12) & 0xF
+    )
+    z = lax.shift_right_arithmetic(lax.shift_left(second, 20), 14) | (
+        lax.shift_left(third & 0xF, 2) | (fourth & 0x3)
+    )
+    y, z = y.astype(jnp.float32), z.astype(jnp.float32)
+    square = x * x + y * y + z * z
+    scale = 2.0 / (1.0 + square * (1.0 / (QUANTUM * QUANTUM)))
+    w = scale - 1.0
+    x, y, z = x * scale, y * scale, z * scale
+    return [x * x, y * y, z * z, x * y, x * z, y * z, w * x, w * y, w * z]
+
+
 def cell_sum_kernel(first, count, *refs):
     if first == 0:
         ids_ref, label_ref, euler_ref, split_ref, label_out_ref, table_ref, tile_ref = refs
     else:
         ids_ref, label_ref, table_ref, split_ref, label_out_ref, tile_ref = refs
     per_octant = ids_ref.shape[0] // 8
-    table_rows = table_ref.shape[0] // 2
+    table_rows = table_ref.shape[0] * 16 // 27
     label_out_ref[...] = label_ref[...]
     if first == 0:
-        words = rotation_words(euler_ref[...])
-        for word in range(2):
-            for row in range(table_rows):
-                table_ref[word * table_rows + row] = jnp.broadcast_to(
-                    words[word][:, row * LANES : (row + 1) * LANES], (8, LANES)
-                )
+        fill_table(table_ref, euler_ref[...])
     groups = tile_ref.shape[0] // 8
     rows_left = count * per_octant - 8 * (groups - 1)
 
@@ -163,12 +189,7 @@
         sums = [jnp.zeros((8, LANES), jnp.float32) for pair in range(9)]
         for group in range(groups):
             ids = tile_ref[pl.ds(8 * group, 8), :]
-            lane = (ids & (LANES - 1))[:, :, None]
-            row = lax.shift_right_logical(ids, 7)
-            bits = [(row & (1 << level)) != 0 for level in range(table_rows.bit_length() - 1)]
-            leading = looked_up(table_ref, 0, table_rows, lane, bits)
-            trailing = looked_up(table_ref, table_rows, table_rows, lane, bits)
-            products = rotation_products(leading, trailing)
+            products = rotation_products(table_ref, table_rows, ids)
             if group == groups - 1 and rows_left < 8:
                 there = lax.broadcasted_iota(jnp.int32, (8, LANES), 0) < rows_left
                 products = [jnp.where(there, product, 0.0) for product in products]
@@ -236,9 +257,10 @@
 
 def place_of(owner):
     groups, members = lax.axis_size("ca"), lax.axis_size("fe")
-    owner_ca = lax.shift_right_logical(owner, members.bit_length() - 1) ^ lax.axis_index("ca")
-    owner_fe = (owner & (members - 1)) ^ lax.axis_index("fe")
-    place = (owner_ca & 1) * (groups // 2) + lax.shift_right_logical(owner_ca, 1)
+    owner_ca = lax.shift_right_logical(owner, members.bit_length() - 1)
+    owner_fe = owner & (members - 1)
+    place = ((owner_ca ^ lax.axis_index("ca")) & 1) * (groups // 2)
+    place = place + lax.shift_right_logical(owner_ca, 1)
     place = place * 2 + (owner_fe & 1)
     return place * (members // 2) + lax.shift_right_logical(owner_fe, 1)
 
@@ -252,7 +274,7 @@
     ]
     if first == 0:
         grains = table.shape[1]
-        out_shape.append(jax.ShapeDtypeStruct((2 * grains // LANES, 8, LANES), jnp.int32))
+        out_shape.append(jax.ShapeDtypeStruct((27 * grains // LANES // 16, 8, LANES), jnp.int32))
     return pl.pallas_call(
         functools.partial(cell_sum_kernel, first, count),
         out_shape=out_shape,
@@ -290,58 +312,79 @@
     )(split, labels)
 
 
-def part_sum_kernel(terms, passed, *refs):
-    flat = sum(terms)
-    outs = refs[flat + passed :]
-    for index in range(len(outs) - passed):
-        at = row = 0
-        for group in terms:
-            total = refs[at][index]
-            for term in refs[at + 1 : at + group]:
-                total = total + term[index]
-            at += group
-            axis = total.ndim - 2
-            where = (slice(None),) * axis + (pl.ds(row, total.shape[axis]),)
-            outs[index][where] = total
-            row += total.shape[axis]
-    for i in range(passed):
-        outs[len(outs) - passed + i][...] = refs[flat + i][...]
-
-
-def part_sum(groups, passed, name):
-    shape = groups[0][0].shape
-    rows = sum(terms[0].shape[-2] for terms in groups)
-    part = jax.ShapeDtypeStruct(shape[1:-2] + (rows, shape[-1]), jnp.float32)
-    out = pl.pallas_call(
-        functools.partial(part_sum_kernel, [len(terms) for terms in groups], len(passed)),
-        out_shape=[part] * shape[0]
-        + [jax.ShapeDtypeStruct(array.shape, array.dtype) for array in passed],
+def core_sum_kernel(kept_ref, received_ref, own_ref, label_ref, out_ref, label_out_ref):
+    out_ref[...] = kept_ref[...] + received_ref[...]
+    for c in range(3):
+        row = out_ref.shape[2] - 3 + c
+        out_ref[:, :, row : row + 1, :] = jnp.broadcast_to(
+            own_ref[c][None, None], out_ref.shape[:2] + (1, COLUMNS)
+        )
+    label_out_ref[...] = label_ref[...]
+
+
+def core_sum(kept, received, own, labels, name):
+    pairs, rests = lax.axis_size("ca") // 2, lax.axis_size("fe") // 2
+    shape = (2 * pairs, rests) + kept.shape[1:]
+    return pl.pallas_call(
+        core_sum_kernel,
+        out_shape=[
+            jax.ShapeDtypeStruct(shape, jnp.float32),
+            jax.ShapeDtypeStruct(labels.shape, jnp.int32),
+        ],
         compiler_params=pltpu.CompilerParams(vmem_limit_bytes=16 * 1024 * 1024),
         name=name,
-    )(*[term for terms in groups for term in terms], *passed)
-    return out[: shape[0]], *out[shape[0] :]
-
-
-def to_relative(block, core, pair, last, rest):
-    groups, members = lax.axis_size("ca"), lax.axis_size("fe")
-    flip = (2 * pair + core) * members + 2 * rest + last
-    return lax.ppermute(block, ("ca", "fe"), [(i, i ^ flip) for i in range(groups * members)])
-
-
-def across_cores(keep, send):
+    )(kept.reshape(shape), received.reshape(shape), own, labels)
+
+
+def plane_sum_kernel(received_ref, label_ref, out_ref, label_out_ref):
+    total = received_ref[0]
+    for source in range(1, received_ref.shape[0]):
+        total = total + received_ref[source]
+    out_ref[...] = total
+    neighbour = (lax.axis_index("ca") // 2 * 2 + (lax.axis_index("fe") & 1)) ^ 1
+    rows = pl.ds(out_ref.shape[1] - 3, 3)
+    out_ref[:, rows, :] = received_ref[neighbour, :, rows, :]
+    label_out_ref[...] = label_ref[...]
+
+
+def plane_sum(received, labels, name):
+    return pl.pallas_call(
+        plane_sum_kernel,
+        out_shape=[
+            jax.ShapeDtypeStruct(received.shape[1:], jnp.float32),
+            jax.ShapeDtypeStruct(labels.shape, jnp.int32),
+        ],
+        compiler_params=pltpu.CompilerParams(vmem_limit_bytes=16 * 1024 * 1024),
+        name=name,
+    )(received, labels)
+
+
+def across_cores(block):
+    groups = lax.axis_size("ca")
+    return lax.ppermute(block, "ca", [(i, i ^ 1) for i in range(groups)])
+
+
+def across(blocks, groups):
+    return lax.all_to_all(
+        blocks, ("ca", "fe"), split_axis=0, concat_axis=0, axis_index_groups=groups, tiled=True
+    )
+
+
+def device_groups():
     pairs, rests = lax.axis_size("ca") // 2, lax.axis_size("fe") // 2
-    split = (2 * pairs, rests) + keep.shape[1:]
-    return [keep.reshape(split), to_relative(send, 1, 0, 0, 0).reshape(split)]
-
-
-def across_plane(parts):
-    return [parts[0]] + [
-        to_relative(parts[index], 0, index // 2, index % 2, 0) for index in range(1, len(parts))
-    ]
-
-
-def across_height(parts):
-    return [parts[0]] + [to_relative(parts[rest], 0, 0, 0, rest) for rest in range(1, len(parts))]
+    number = lambda pair, core, last, rest: ((2 * pair + core) * rests + rest) * 2 + last
+    planes = [
+        [number(pair, core, last, rest) for pair in range(pairs) for last in range(2)]
+        for core in range(2)
+        for rest in range(rests)
+    ]
+    heights = [
+        [number(pair, core, last, rest) for rest in range(rests)]
+        for pair in range(pairs)
+        for core in range(2)
+        for last in range(2)
+    ]
+    return planes, heights
 
 
 def three_parts(value):
@@ -362,12 +405,21 @@
     return total
 
 
-def update_kernel(sources, *refs):
-    own_ref, layers_ref, stress_ref, resistance_ref, weights_ref, table_ref = refs[2 * sources : -2]
-    stress_out_ref, nodal_ref = refs[-2:]
+def update_kernel(
+    first_ref,
+    second_ref,
+    own_ref,
+    stress_ref,
+    resistance_ref,
+    weights_ref,
+    table_ref,
+    stress_out_ref,
+    nodal_ref,
+):
     elements = stress_ref.shape[2]
     gathered = [
-        sum(ref[:, 0:elements] for ref in refs[at : at + sources]) for at in (0, sources)
+        sum(ref[source, :, 0:elements] for source in range(ref.shape[0]))
+        for ref in (first_ref, second_ref)
     ]
     counts = gathered[0][9 * CHUNKS[0][1] : 9 * CHUNKS[0][1] + 1]
     per_brick = 1.0 / (8.0 * jnp.maximum(counts, 1.0))
@@ -393,14 +445,15 @@
     ]
     corner = lax.broadcasted_iota(jnp.int32, (24, 1), 0) & 7
     upper_corner = (corner & 1) == 1
-    above = lax.axis_index("fe") + 1
-    clamped = above == layers_ref.shape[0]
-    above = jnp.minimum(above, layers_ref.shape[0] - 1)
-    free = jnp.where(clamped, 0.0, 1.0)
+    above = lax.axis_index("fe") // 2 + (lax.axis_index("fe") & 1)
+    heights, rows = first_ref.shape[:2]
+    free = jnp.where(above == heights, 0.0, 1.0)
+    above = jnp.minimum(above, heights - 1)
+    upper = first_ref[above, rows - 3 : rows, :] * free
     values = jnp.where(
         upper_corner,
         jnp.concatenate(
-            [jnp.broadcast_to(layers_ref[above, c] * free, (8, COLUMNS)) for c in range(3)], axis=0
+            [jnp.broadcast_to(upper[c : c + 1], (8, COLUMNS)) for c in range(3)], axis=0
         ),
         jnp.concatenate([jnp.broadcast_to(own_ref[c], (8, COLUMNS)) for c in range(3)], axis=0),
     )
@@ -495,7 +548,7 @@
         nodal_ref[1, c] = jnp.sum(above[8 * c : 8 * c + 8], axis=0, keepdims=True)
 
 
-def element_update(gathered, own, layers, stress_old, resistance, quad_weights):
+def element_update(first, second, own, stress_old, resistance, quad_weights):
     grad_table = shape_gradients()
     table = jnp.asarray(
         [
@@ -506,14 +559,14 @@
         dtype=jnp.float32,
     )
     return pl.pallas_call(
-        functools.partial(update_kernel, len(gathered) // 2),
+        update_kernel,
         out_shape=(
             jax.ShapeDtypeStruct(stress_old.shape, jnp.float32),
             jax.ShapeDtypeStruct((2,) + own.shape, jnp.float32),
         ),
         compiler_params=pltpu.CompilerParams(vmem_limit_bytes=8 * 1024 * 1024),
         name="stress_update",
-    )(*gathered, own, layers, stress_old, resistance, quad_weights, table)
+    )(first, second, own, stress_old, resistance, quad_weights, table)
 
 
 def body(
@@ -529,23 +582,27 @@
 ):
     half = lax.axis_size("ca") * lax.axis_size("fe") // 2
     bricks = grain_ids.shape[1]
-    layers = lax.all_gather(displacement, "fe")
     owner = lax.optimization_barrier(brick_owner.reshape(bricks))
     labels = jnp.where(brick_active > 0, owner * COLUMNS + brick_element, -1).reshape(1, bricks)
     (first_a, count_a), (first_b, count_b) = CHUNKS
     split, labels, table = cell_sums(first_a, count_a, grain_ids, labels, euler_angles)
     send, labels = brick_sums(split, labels, half, half)
     keep, labels = brick_sums(split, labels, half, 0)
-    core_a, labels = part_sum([across_cores(keep, send)], [labels], "core_sum_a")
+    planes, heights = device_groups()
+    core_a, labels = core_sum(keep, across_cores(send), displacement, labels, "core_sum_a")
     split, labels = cell_sums(first_b, count_b, grain_ids, labels, table)
-    plane_a, labels, layers = part_sum([across_plane(core_a)], [labels, layers], "plane_sum_a")
+    plane_a, labels = plane_sum(across(core_a, planes), labels, "plane_sum_a")
     send, labels = brick_sums(split, labels, half, half)
     keep, labels = brick_sums(split, labels, half, 0)
-    core_b, labels = part_sum([across_cores(keep, send)], [labels], "core_sum_b")
-    plane_b, labels = part_sum([across_plane(core_b)], [labels], "plane_sum_b")
-    gathered = across_height(plane_a) + across_height(plane_b)
+    core_b, labels = core_sum(keep, across_cores(send), displacement, labels, "core_sum_b")
+    plane_b, labels = plane_sum(across(core_b, planes), labels, "plane_sum_b")
     stress_new, nodal = element_update(
-        gathered, displacement, layers, stress_old, resistance, quad_weights
+        across(plane_a, heights),
+        across(plane_b, heights),
+        displacement,
+        stress_old,
+        resistance,
+        quad_weights,
     )
     forces = nodal[0] + passed_along(nodal[1], "fe", 1)
     return (stress_new, forces)

time: 111 us -> 91.5 us (0.82)
  starting transfers between devices: 21.6 us -> 13.4 us
  blocking collectives: 31.8 us -> 23.7 us
  Pallas kernels: 45.3 us -> 42.2 us
    all_gather x1 -> x0, blocking collectives: 31.8 us -> none  [body(): layers = lax.all_gather(displacement, 'fe')]
    all_to_all x0 -> x2, blocking collectives: none -> 23.7 us  [across(): lax.all_to_all(blocks, ('ca', 'fe'), split_axis=0, concat_axis=0, axis_in...]
    ppermute x14 -> x2, starting transfers between devices: 17.9 us -> 0.59 us  [across_cores(): return lax.ppermute(block, 'ca', [(i, i ^ 1) for i in range(groups)])]
    all_to_all x0 -> x2, starting transfers between devices: none -> 9.95 us  [across(): lax.all_to_all(blocks, ('ca', 'fe'), split_axis=0, concat_axis=0, axis_in...]
    ppermute x14 -> x2, waiting for transfers between devices: 6.66 us -> 0.66 us  [across_cores(): return lax.ppermute(block, 'ca', [(i, i ^ 1) for i in range(groups)])]
    all_to_all x0 -> x2, waiting for transfers between devices: none -> 5.38 us  [across(): lax.all_to_all(blocks, ('ca', 'fe'), split_axis=0, concat_axis=0, axis_in...]
    pallas_call x2, Pallas kernels: 36.4 us -> 31.9 us  [cell_sums(): pl.pallas_call(functools.partial(cell_sum_kernel, first, count), out_shap...]
    pallas_call x5, Pallas kernels: 2.56 us -> 4.09 us  [the longest x1 1.69 us: element_update(): pl.pallas_call(update_kernel, out_shape=(jax.ShapeDtypeStruct(stress_old....]
  transfers between devices with their start and end apart: 15 -> 5, of which waited for: 6 -> 4; matrix products, arithmetic and copies ran while one was open for 0% -> 0% of each run, Pallas kernels for 20% -> 22%
where the time goes in v6:
time: 91.5 us; the launch traced here: 91 us
  Pallas kernels  42.2 us (46%)
  blocking collectives  23.7 us (26%)
  starting transfers between devices  13.4 us (15%)
  waiting for transfers between devices  7.34 us (8%)
  local copies, waits for them, and re-layouts  2.34 us (3%)
  other arithmetic  1.32 us (1%)
    pallas_call x2, Pallas kernels, cell_sums(): pl.pallas_call(functools.partial(cell_sum_kernel, first, count), out_shap...  31.9 us
    all_to_all x2, blocking collectives, across(): lax.all_to_all(blocks, ('ca', 'fe'), split_axis=0, concat_axis=0, axis_in...  23.7 us
    all_to_all x2, starting transfers between devices, across(): lax.all_to_all(blocks, ('ca', 'fe'), split_axis=0, concat_axis=0, axis_in...  9.95 us
    pallas_call x4, Pallas kernels, brick_sums(): pl.pallas_call(functools.partial(brick_sum_kernel, base), out_shape=[jax....  6.25 us
    all_to_all x2, waiting for transfers between devices, across(): lax.all_to_all(blocks, ('ca', 'fe'), split_axis=0, concat_axis=0, axis_in...  5.38 us
    ppermute x1, starting transfers between devices, passed_along(): return lax.ppermute(block, axis, route)  2.82 us
    unnamed x16, local copies, waits for them, and re-layouts  2.34 us
  transfers between devices with their start and end apart: 5, of which 4 were waited for; matrix products, arithmetic and copies ran while one was open for 0% of the time, Pallas kernels for 22%

profile of v6, /device:TPU:0, one launch (start us, length us, event | category | flops | bytes accessed | tf_op | source)
XLA Modules:
  0.0 91.0 jit_solution(6755524658726772152)
XLA Ops:
  0.6 0.7 add_select_fusion
  1.4 1.5 %copy-done.5 = s32[216,2048]{1,0:T(8,128)S(1)} copy-done((s32[216,2048]{1,0:T(8,128)S(1)}, s32[216,2048]{1,0:T(8,128)}, u32[]{:S(2)}) %copy-start.5) | copy-done | bytes 1769496
  2.8 0.8 copy-done.7
  3.7 16.0 %cell_sums.2 = (bf16[80,2048]{1,0:T(8,128)(2,1)S(1)}, s32[1,2048]{1,0:T(1,128)S(1)}, s32[54,8,128]{2,1,0:T(8,128)S(1)}) custom-call(s32[216,2048]{1,0:T(8,128)S(1)} %copy-done.5, s32[1,2048]{1,0:T(1,128)S(1)} %bitcast.14, f32[3,4096]{1,0:T(4,128)S(1)} %copy-done.7), custom_call_target="tpu_custom_call" | custom-call | flops 16000000000 | bytes 40000000 | tf_op jit(solution)/shard_map/cell_sums/pallas_call | solution.py:278
  19.7 1.6 %brick_sums.4 = (f32[16,40,256]{2,1,0:T(8,128)S(1)}, s32[1,2048]{1,0:T(1,128)S(1)}) custom-call(bf16[80,2048]{1,0:T(8,128)(2,1)S(1)} %get-tuple-element.24.split_ref, s32[1,2048]{1,0:T(1,128)S(1)} %get-tuple-element.25.label_ref), custom_call_target="tpu_custom_call" | custom-call | flops 1200000000 | bytes 4000000 | tf_op jit(solution)/shard_map/brick_sums/pallas_call | solution.py:297
  21.3 0.5 collective-permute-start
  21.8 1.6 %brick_sums.5 = (f32[16,40,256]{2,1,0:T(8,128)S(1)}, s32[1,2048]{1,0:T(1,128)S(1)}) custom-call(bf16[80,2048]{1,0:T(8,128)(2,1)S(1)} %get-tuple-element.24.split_ref, s32[1,2048]{1,0:T(1,128)S(1)} %get-tuple-element.26.label_ref), custom_call_target="tpu_custom_call" | custom-call | flops 1200000000 | bytes 4000000 | tf_op jit(solution)/shard_map/brick_sums/pallas_call | solution.py:297
  23.4 0.0 copy-start.6
  23.4 0.1 collective-permute-done
  23.5 0.0 copy-done.2
  23.5 1.0 %core_sum_a.1 = (f32[4,4,40,256]{3,2,1,0:T(8,128)}, s32[1,2048]{1,0:T(1,128)S(1)}) custom-call(f32[4,4,40,256]{3,2,1,0:T(8,128)S(1)} %bitcast.12, f32[4,4,40,256]{3,2,1,0:T(8,128)S(1)} %bitcast.10, f32[3,1,256]{2,1,0:T(1,128)S(1)} %copy-done.2, s32[1,2048]{1,0:T(1,128)S(1)} %get-tuple-element.29.label_ref), custom_call_target="tpu_custom_call" | custom-call | tf_op jit(solution)/shard_map/core_sum_a/pallas_call | solution.py:328
  24.5 5.1 %all-to-all-start = ((f32[4,4,40,256]{3,2,1,0:T(8,128)}), f32[4,4,40,256]{3,2,1,0:T(8,128)S(1)}, u32[]{:S(2)}, u32[]{:S(2)}) async-start(f32[4,4,40,256]{3,2,1,0:T(8,128)} %get-tuple-element.30), calls=%async_computation | async-start | bytes 1310720 | tf_op jit(solution)/shard_map/all_to_all | solution.py:368
  29.6 0.0 copy-done.6
  29.6 15.8 %cell_sums.3 = (bf16[80,2048]{1,0:T(8,128)(2,1)S(1)}, s32[1,2048]{1,0:T(1,128)S(1)}) custom-call(s32[216,2048]{1,0:T(8,128)S(1)} %copy-done.6, s32[1,2048]{1,0:T(1,128)S(1)} %get-tuple-element.31.refs_1_, s32[54,8,128]{2,1,0:T(8,128)S(1)} %get-tuple-element.32.refs_2_), custom_call_target="tpu_custom_call" | custom-call | flops 16000000000 | bytes 40000000 | tf_op jit(solution)/shard_map/cell_sums/pallas_call | solution.py:278
  45.4 0.0 all-to-all-done.received_ref
  45.4 0.7 plane_sum_a.1
  46.1 1.6 %brick_sums.6 = (f32[16,40,256]{2,1,0:T(8,128)S(1)}, s32[1,2048]{1,0:T(1,128)S(1)}) custom-call(bf16[80,2048]{1,0:T(8,128)(2,1)S(1)} %get-tuple-element.35.split_ref, s32[1,2048]{1,0:T(1,128)S(1)} %get-tuple-element.36.label_ref), custom_call_target="tpu_custom_call" | custom-call | flops 1200000000 | bytes 4000000 | tf_op jit(solution)/shard_map/brick_sums/pallas_call | solution.py:297
  47.7 0.1 collective-permute-start.1
  47.8 1.6 %brick_sums.7 = (f32[16,40,256]{2,1,0:T(8,128)S(1)}, s32[1,2048]{1,0:T(1,128)S(1)}) custom-call(bf16[80,2048]{1,0:T(8,128)(2,1)S(1)} %get-tuple-element.35.split_ref, s32[1,2048]{1,0:T(1,128)S(1)} %get-tuple-element.37.label_ref), custom_call_target="tpu_custom_call" | custom-call | flops 1200000000 | bytes 4000000 | tf_op jit(solution)/shard_map/brick_sums/pallas_call | solution.py:297
  49.3 0.5 collective-permute-done.1
  49.9 0.1 core_sum_b.1
  50.0 14.2 %all_to_all.20.received_ref = f32[4,4,40,256]{3,2,1,0:T(8,128)S(1)} all-to-all(f32[4,4,40,256]{3,2,1,0:T(8,128)S(1)} %get-tuple-element.41), channel_id=1, replica_groups={{0,1,16,17},{2,3,18,19},{4,5,20,21},{6,7,22,23},{8,9,24,25},{10,11,26,2..., dimensions={0} | all-to-all | bytes 1310720 | tf_op jit(solution)/shard_map/all_to_all | solution.py:368
  64.2 4.9 %all-to-all-start.1 = ((f32[4,40,256]{2,1,0:T(8,128)}), f32[4,40,256]{2,1,0:T(8,128)S(1)}, u32[]{:S(2)}, u32[]{:S(2)}) async-start(f32[4,40,256]{2,1,0:T(8,128)} %get-tuple-element.34), calls=%async_computation.1 | async-start | bytes 327680 | tf_op jit(solution)/shard_map/all_to_all | solution.py:368
  69.1 0.6 plane_sum_b.1
  69.7 5.4 %all-to-all-done.1.first_ref = f32[4,40,256]{2,1,0:T(8,128)S(1)} async-done(((f32[4,40,256]{2,1,0:T(8,128)}), f32[4,40,256]{2,1,0:T(8,128)S(1)}, u32[]{:S(2)}, u32[]{:S(2)}) %all-to-all-start.1) | async-done | bytes 163872 | tf_op jit(solution)/shard_map/all_to_all | solution.py:368
  75.1 9.5 %all_to_all.21.second_ref = f32[4,40,256]{2,1,0:T(8,128)S(1)} all-to-all(f32[4,40,256]{2,1,0:T(8,128)S(1)} %get-tuple-element.43), channel_id=1, replica_groups={{0,2,4,6},{1,3,5,7},{8,10,12,14},{9,11,13,15},{16,18,20,22},{17,19,21,2..., dimensions={0} | all-to-all | bytes 327680 | tf_op jit(solution)/shard_map/all_to_all | solution.py:368
  84.6 0.0 copy-done
  84.6 0.0 copy-done.1
  84.6 1.7 %stress_update.1 = (f32[6,8,225]{2,1,0:T(8,128)}, f32[2,3,1,256]{3,2,1,0:T(1,128)S(1)}) custom-call(f32[4,40,256]{2,1,0:T(8,128)S(1)} %all-to-all-done.1.first_ref, f32[4,40,256]{2,1,0:T(8,128)S(1)} %all_to_all.21.second_ref, f32[3,1,256]{2,1,0:T(1,128)S(1)} %copy-done.2, f32[6,8,225]{2,1,0:T(8,128)S(1)} %copy-done.1, f32[12,8,225]{2,1,0:T(8,128)S(1)} %copy-done, ...), custom_call_target="tpu_custom_call" | custom-call | tf_op jit(solution)/shard_map/stress_update/pallas_call | solution.py:561
  86.3 2.8 %collective-permute-start.2 = (f32[3,1,256]{2,1,0:T(1,128)S(1)}, f32[3,1,256]{2,1,0:T(1,128)S(1)}, u32[]{:S(2)}, u32[]{:S(2)}) collective-permute-start(f32[3,1,256]{2,1,0:T(1,128)S(1)} %slice_bitcast_fusion), channel_id=1, source_target_pairs={{0,1},{1,2},{2,3},{3,4},{4,5},{5,6},{6,7},{8,9},{9,10},{10,11},{11... | collective-permute-start | bytes 9224 | tf_op jit(solution)/shard_map/ppermute | solution.py:48
  89.2 1.3 %collective-permute-done.2 = f32[3,1,256]{2,1,0:T(1,128)S(1)} collective-permute-done((f32[3,1,256]{2,1,0:T(1,128)S(1)}, f32[3,1,256]{2,1,0:T(1,128)S(1)}, u32[]{:S(2)}, u32[]{:S(2)}) %collective-permute-start.2) | collective-permute-done | bytes 3104 | tf_op jit(solution)/shard_map/ppermute | solution.py:48
  90.5 0.6 bitcast_add_fusion
  (10 shorter events, 0.0 us)
Async XLA Ops:
  1.4 1.5 %copy-start.5 = (s32[216,2048]{1,0:T(8,128)S(1)}, s32[216,2048]{1,0:T(8,128)}, u32[]{:S(2)}) copy-start(s32[216,2048]{1,0:T(8,128)} %refs_0_.3) | copy-start | bytes 5308420
  2.8 0.8 copy-start.7
  21.3 2.2 %collective-permute-start = (f32[16,40,256]{2,1,0:T(8,128)S(1)}, f32[16,40,256]{2,1,0:T(8,128)S(1)}, u32[]{:S(2)}, u32[]{:S(2)}) collective-permute-start(f32[16,40,256]{2,1,0:T(8,128)S(1)} %get-tuple-element.28), channel_id=1, source_target_pairs={{0,8},{8,0},{16,24},{24,16},{1,9},{9,1},{17,25},{25,17},{2,10},{10... | collective-permute-start | bytes 1966088 | tf_op jit(solution)/shard_map/ppermute | solution.py:364
  21.8 1.7 %copy-start.2 = (f32[3,1,256]{2,1,0:T(1,128)S(1)}, f32[3,1,256]{2,1,0:T(1,128)}, u32[]{:S(2)}) copy-start(f32[3,1,256]{2,1,0:T(1,128)} %own_ref.5) | copy-start | bytes 9220
  23.4 6.2 %copy-start.6 = (s32[216,2048]{1,0:T(8,128)S(1)}, s32[216,2048]{1,0:T(8,128)}, u32[]{:S(2)}) copy-start(s32[216,2048]{1,0:T(8,128)} %refs_0_.3) | copy-start | bytes 5308420
  24.5 20.9 %all-to-all-start = ((f32[4,4,40,256]{3,2,1,0:T(8,128)}), f32[4,4,40,256]{3,2,1,0:T(8,128)S(1)}, u32[]{:S(2)}, u32[]{:S(2)}) async-start(f32[4,4,40,256]{3,2,1,0:T(8,128)} %get-tuple-element.30), calls=%async_computation | async-start | bytes 1310720 | tf_op jit(solution)/shard_map/all_to_all | solution.py:368
  47.7 2.2 %collective-permute-start.1 = (f32[16,40,256]{2,1,0:T(8,128)S(1)}, f32[16,40,256]{2,1,0:T(8,128)S(1)}, u32[]{:S(2)}, u32[]{:S(2)}) collective-permute-start(f32[16,40,256]{2,1,0:T(8,128)S(1)} %get-tuple-element.39), channel_id=1, source_target_pairs={{0,8},{8,0},{16,24},{24,16},{1,9},{9,1},{17,25},{25,17},{2,10},{10... | collective-permute-start | bytes 1966088 | tf_op jit(solution)/shard_map/ppermute | solution.py:364
  49.9 34.7 %copy-start = (f32[12,8,225]{2,1,0:T(8,128)S(1)}, f32[12,8,225]{2,1,0:T(8,128)}, u32[]{:S(2)}) copy-start(f32[12,8,225]{2,1,0:T(8,128)} %resistance_ref.1) | copy-start | bytes 259204
  49.9 34.7 %copy-start.1 = (f32[6,8,225]{2,1,0:T(8,128)S(1)}, f32[6,8,225]{2,1,0:T(8,128)}, u32[]{:S(2)}) copy-start(f32[6,8,225]{2,1,0:T(8,128)} %stress_ref.1) | copy-start | bytes 129604
  49.9 34.7 %copy-start.3 = (f32[24,8]{1,0:T(8,128)S(1)}, f32[24,8]{1,0:T(8,128)}, u32[]{:S(2)}) copy-start(f32[24,8]{1,0:T(8,128)} %constant.8.clone.table_ref) | copy-start | bytes 2308
  49.9 34.7 %copy-start.4 = (s32[8,225]{1,0:T(8,128)S(1)}, s32[8,225]{1,0:T(8,128)}, u32[]{:S(2)}) copy-start(s32[8,225]{1,0:T(8,128)} %weights_ref.1) | copy-start | bytes 21604
  64.2 10.9 %all-to-all-start.1 = ((f32[4,40,256]{2,1,0:T(8,128)}), f32[4,40,256]{2,1,0:T(8,128)S(1)}, u32[]{:S(2)}, u32[]{:S(2)}) async-start(f32[4,40,256]{2,1,0:T(8,128)} %get-tuple-element.34), calls=%async_computation.1 | async-start | bytes 327680 | tf_op jit(solution)/shard_map/all_to_all | solution.py:368
  86.3 4.1 %collective-permute-start.2 = (f32[3,1,256]{2,1,0:T(1,128)S(1)}, f32[3,1,256]{2,1,0:T(1,128)S(1)}, u32[]{:S(2)}, u32[]{:S(2)}) collective-permute-start(f32[3,1,256]{2,1,0:T(1,128)S(1)} %slice_bitcast_fusion), channel_id=1, source_target_pairs={{0,1},{1,2},{2,3},{3,4},{4,5},{5,6},{6,7},{8,9},{9,10},{10,11},{11... | collective-permute-start | bytes 9224 | tf_op jit(solution)/shard_map/ppermute | solution.py:48

commit v7 on v6

--- a/solution.py
+++ b/solution.py
@@ -12,7 +12,7 @@
 GX = 15
 LANES = 128
 COLUMNS = 256
-CHUNKS = ((0, 4), (4, 4))
+CHUNKS = ((0, 6), (6, 2))
 QUANTUM = float((1 << 17) - 1)
 
 SLIP_PLANES = [
@@ -179,6 +179,7 @@
         fill_table(table_ref, euler_ref[...])
     groups = tile_ref.shape[0] // 8
     rows_left = count * per_octant - 8 * (groups - 1)
+    turns = count // math.gcd(count, 8)
 
     def tile_sums(tile, carry):
         lanes = pl.ds(pl.multiple_of(tile * LANES, LANES), LANES)
@@ -186,16 +187,19 @@
             tile_ref[pl.ds(octant, per_octant, stride=count), :] = ids_ref[
                 pl.ds((first + octant) * per_octant, per_octant), lanes
             ]
-        sums = [jnp.zeros((8, LANES), jnp.float32) for pair in range(9)]
+        sums = [[jnp.zeros((8, LANES), jnp.float32)] * 9 for turn in range(turns)]
         for group in range(groups):
             ids = tile_ref[pl.ds(8 * group, 8), :]
             products = rotation_products(table_ref, table_rows, ids)
             if group == groups - 1 and rows_left < 8:
                 there = lax.broadcasted_iota(jnp.int32, (8, LANES), 0) < rows_left
                 products = [jnp.where(there, product, 0.0) for product in products]
-            sums = [total + product for total, product in zip(sums, products)]
+            sums[group % turns] = [
+                total + product for total, product in zip(sums[group % turns], products)
+            ]
+        sums = [jnp.concatenate(turned, axis=0) for turned in zip(*sums)]
         sums = [
-            sum(total[count * part : count * (part + 1)] for part in range(8 // count))
+            sum(total[count * part : count * (part + 1)] for part in range(8 * turns // count))
             for total in sums
         ]
         vector = 2.0 / (QUANTUM * QUANTUM)
@@ -220,7 +224,12 @@
         )
         return carry
 
-    lax.fori_loop(0, ids_ref.shape[1] // LANES, tile_sums, 0)
+    lax.fori_loop(0, ids_ref.shape[1] // LANES, tile_sums, 0, unroll=2)
+
+
+def across_cores(block):
+    groups = lax.axis_size("ca")
+    return lax.ppermute(block, "ca", [(i, i ^ 1) for i in range(groups)])
 
 
 def brick_sum_kernel(base, split_ref, label_ref, out_ref, label_out_ref, place_ref, masked_ref):
@@ -257,10 +266,9 @@
 
 def place_of(owner):
     groups, members = lax.axis_size("ca"), lax.axis_size("fe")
-    owner_ca = lax.shift_right_logical(owner, members.bit_length() - 1)
-    owner_fe = owner & (members - 1)
-    place = ((owner_ca ^ lax.axis_index("ca")) & 1) * (groups // 2)
-    place = place + lax.shift_right_logical(owner_ca, 1)
+    owner_ca = lax.shift_right_logical(owner, members.bit_length() - 1) ^ lax.axis_index("ca")
+    owner_fe = (owner & (members - 1)) ^ lax.axis_index("fe")
+    place = (owner_ca & 1) * (groups // 2) + lax.shift_right_logical(owner_ca, 1)
     place = place * 2 + (owner_fe & 1)
     return place * (members // 2) + lax.shift_right_logical(owner_fe, 1)
 
@@ -312,79 +320,82 @@
     )(split, labels)
 
 
-def core_sum_kernel(kept_ref, received_ref, own_ref, label_ref, out_ref, label_out_ref):
-    out_ref[...] = kept_ref[...] + received_ref[...]
-    for c in range(3):
-        row = out_ref.shape[2] - 3 + c
-        out_ref[:, :, row : row + 1, :] = jnp.broadcast_to(
-            own_ref[c][None, None], out_ref.shape[:2] + (1, COLUMNS)
-        )
-    label_out_ref[...] = label_ref[...]
-
-
-def core_sum(kept, received, own, labels, name):
+def core_sum_kernel(spare, kept_ref, received_ref, own_ref, label_ref, *out_refs):
+    for index, out_ref in enumerate(out_refs[:-1]):
+        out_ref[...] = kept_ref[index] + received_ref[index]
+        for c in range(spare):
+            row = out_ref.shape[1] - spare + c
+            out_ref[:, row : row + 1, :] = jnp.broadcast_to(
+                own_ref[c][None], (out_ref.shape[0], 1, COLUMNS)
+            )
+    out_refs[-1][...] = label_ref[...]
+
+
+def core_sum(kept, received, own, labels, spare, name):
     pairs, rests = lax.axis_size("ca") // 2, lax.axis_size("fe") // 2
     shape = (2 * pairs, rests) + kept.shape[1:]
+    *parts, labels = pl.pallas_call(
+        functools.partial(core_sum_kernel, spare),
+        out_shape=[jax.ShapeDtypeStruct(shape[1:], jnp.float32)] * shape[0]
+        + [jax.ShapeDtypeStruct(labels.shape, jnp.int32)],
+        compiler_params=pltpu.CompilerParams(vmem_limit_bytes=16 * 1024 * 1024),
+        name=name,
+    )(kept.reshape(shape), received.reshape(shape), own, labels)
+    return parts, labels
+
+
+def plane_sum_kernel(sources, first_ref, *refs):
+    second, outs = refs[:sources], refs[sources:]
+    rows = first_ref.shape[1]
+    for height, out_ref in enumerate(outs):
+        out_ref[0:rows, :] = first_ref[height]
+        out_ref[rows:, :] = sum(ref[height] for ref in second)
+        out_ref[out_ref.shape[0] - 3 :, :] = second[1][height, second[1].shape[1] - 3 :, :]
+
+
+def plane_sum(first, second):
+    heights, rows, columns = first.shape
+    part = jax.ShapeDtypeStruct((rows + second[0].shape[1], columns), jnp.float32)
     return pl.pallas_call(
-        core_sum_kernel,
+        functools.partial(plane_sum_kernel, len(second)),
+        out_shape=[part] * heights,
+        compiler_params=pltpu.CompilerParams(vmem_limit_bytes=16 * 1024 * 1024),
+        name="plane_sum",
+    )(first, *second)
+
+
+def first_plane_sum_kernel(*refs):
+    *part_refs, label_ref, out_ref, label_out_ref = refs
+    out_ref[...] = sum(ref[...] for ref in part_refs)
+    label_out_ref[...] = label_ref[...]
+
+
+def first_plane_sum(parts, labels):
+    return pl.pallas_call(
+        first_plane_sum_kernel,
         out_shape=[
-            jax.ShapeDtypeStruct(shape, jnp.float32),
+            jax.ShapeDtypeStruct(parts[0].shape, jnp.float32),
             jax.ShapeDtypeStruct(labels.shape, jnp.int32),
         ],
         compiler_params=pltpu.CompilerParams(vmem_limit_bytes=16 * 1024 * 1024),
-        name=name,
-    )(kept.reshape(shape), received.reshape(shape), own, labels)
-
-
-def plane_sum_kernel(received_ref, label_ref, out_ref, label_out_ref):
-    total = received_ref[0]
-    for source in range(1, received_ref.shape[0]):
-        total = total + received_ref[source]
-    out_ref[...] = total
-    neighbour = (lax.axis_index("ca") // 2 * 2 + (lax.axis_index("fe") & 1)) ^ 1
-    rows = pl.ds(out_ref.shape[1] - 3, 3)
-    out_ref[:, rows, :] = received_ref[neighbour, :, rows, :]
-    label_out_ref[...] = label_ref[...]
-
-
-def plane_sum(received, labels, name):
-    return pl.pallas_call(
-        plane_sum_kernel,
-        out_shape=[
-            jax.ShapeDtypeStruct(received.shape[1:], jnp.float32),
-            jax.ShapeDtypeStruct(labels.shape, jnp.int32),
-        ],
-        compiler_params=pltpu.CompilerParams(vmem_limit_bytes=16 * 1024 * 1024),
-        name=name,
-    )(received, labels)
-
-
-def across_cores(block):
-    groups = lax.axis_size("ca")
-    return lax.ppermute(block, "ca", [(i, i ^ 1) for i in range(groups)])
-
-
-def across(blocks, groups):
-    return lax.all_to_all(
-        blocks, ("ca", "fe"), split_axis=0, concat_axis=0, axis_index_groups=groups, tiled=True
-    )
-
-
-def device_groups():
-    pairs, rests = lax.axis_size("ca") // 2, lax.axis_size("fe") // 2
-    number = lambda pair, core, last, rest: ((2 * pair + core) * rests + rest) * 2 + last
-    planes = [
-        [number(pair, core, last, rest) for pair in range(pairs) for last in range(2)]
-        for core in range(2)
-        for rest in range(rests)
-    ]
-    heights = [
-        [number(pair, core, last, rest) for rest in range(rests)]
-        for pair in range(pairs)
-        for core in range(2)
-        for last in range(2)
-    ]
-    return planes, heights
+        name="first_plane_sum",
+    )(*parts, labels)
+
+
+def to_relative(block, core, pair, last, rest):
+    groups, members = lax.axis_size("ca"), lax.axis_size("fe")
+    flip = (2 * pair + core) * members + 2 * rest + last
+    return lax.ppermute(block, ("ca", "fe"), [(i, i ^ flip) for i in range(groups * members)])
+
+
+def across_plane(parts):
+    return [parts[0]] + [
+        to_relative(parts[index], 0, index // 2, index % 2, 0) for index in range(1, len(parts))
+    ]
+
+
+def across_height(parts):
+    return [parts[0]] + [to_relative(parts[rest], 0, 0, 0, rest) for rest in range(1, len(parts))]
 
 
 def three_parts(value):
@@ -405,29 +416,21 @@
     return total
 
 
-def update_kernel(
-    first_ref,
-    second_ref,
-    own_ref,
-    stress_ref,
-    resistance_ref,
-    weights_ref,
-    table_ref,
-    stress_out_ref,
-    nodal_ref,
-):
+def update_kernel(heights, *refs):
+    gathered_refs = refs[:heights]
+    own_ref, stress_ref, resistance_ref, weights_ref, table_ref = refs[heights:-2]
+    stress_out_ref, nodal_ref = refs[-2:]
     elements = stress_ref.shape[2]
-    gathered = [
-        sum(ref[source, :, 0:elements] for source in range(ref.shape[0]))
-        for ref in (first_ref, second_ref)
-    ]
-    counts = gathered[0][9 * CHUNKS[0][1] : 9 * CHUNKS[0][1] + 1]
+    gathered = sum(ref[:, 0:elements] for ref in gathered_refs)
+    starts = [0, padded_rows(CHUNKS[0][1])]
+    counted = starts[1] + 9 * CHUNKS[1][1]
+    counts = gathered[counted : counted + 1]
     per_brick = 1.0 / (8.0 * jnp.maximum(counts, 1.0))
     frames = [
         jnp.concatenate(
             [
-                sums[count * k : count * (k + 1)]
-                for sums, (first, count) in zip(gathered, CHUNKS)
+                gathered[start + count * k : start + count * (k + 1)]
+                for start, (first, count) in zip(starts, CHUNKS)
             ],
             axis=0,
         )
@@ -445,11 +448,12 @@
     ]
     corner = lax.broadcasted_iota(jnp.int32, (24, 1), 0) & 7
     upper_corner = (corner & 1) == 1
-    above = lax.axis_index("fe") // 2 + (lax.axis_index("fe") & 1)
-    heights, rows = first_ref.shape[:2]
-    free = jnp.where(above == heights, 0.0, 1.0)
-    above = jnp.minimum(above, heights - 1)
-    upper = first_ref[above, rows - 3 : rows, :] * free
+    height = lax.axis_index("fe") // 2
+    above = height + (lax.axis_index("fe") & 1)
+    upper = jnp.zeros((3, COLUMNS), jnp.float32)
+    for flip, ref in enumerate(gathered_refs):
+        wanted = (height ^ flip) == above
+        upper = upper + jnp.where(wanted, ref[ref.shape[0] - 3 :, :], 0.0)
     values = jnp.where(
         upper_corner,
         jnp.concatenate(
@@ -548,7 +552,7 @@
         nodal_ref[1, c] = jnp.sum(above[8 * c : 8 * c + 8], axis=0, keepdims=True)
 
 
-def element_update(first, second, own, stress_old, resistance, quad_weights):
+def element_update(gathered, own, stress_old, resistance, quad_weights):
     grad_table = shape_gradients()
     table = jnp.asarray(
         [
@@ -559,14 +563,14 @@
         dtype=jnp.float32,
     )
     return pl.pallas_call(
-        update_kernel,
+        functools.partial(update_kernel, len(gathered)),
         out_shape=(
             jax.ShapeDtypeStruct(stress_old.shape, jnp.float32),
             jax.ShapeDtypeStruct((2,) + own.shape, jnp.float32),
         ),
         compiler_params=pltpu.CompilerParams(vmem_limit_bytes=8 * 1024 * 1024),
         name="stress_update",
-    )(first, second, own, stress_old, resistance, quad_weights, table)
+    )(*gathered, own, stress_old, resistance, quad_weights, table)
 
 
 def body(
@@ -588,21 +592,15 @@
     split, labels, table = cell_sums(first_a, count_a, grain_ids, labels, euler_angles)
     send, labels = brick_sums(split, labels, half, half)
     keep, labels = brick_sums(split, labels, half, 0)
-    planes, heights = device_groups()
-    core_a, labels = core_sum(keep, across_cores(send), displacement, labels, "core_sum_a")
+    core_a, labels = core_sum(keep, across_cores(send), displacement, labels, 0, "core_sum_a")
     split, labels = cell_sums(first_b, count_b, grain_ids, labels, table)
-    plane_a, labels = plane_sum(across(core_a, planes), labels, "plane_sum_a")
+    plane_a, labels = first_plane_sum(across_plane(core_a), labels)
     send, labels = brick_sums(split, labels, half, half)
     keep, labels = brick_sums(split, labels, half, 0)
-    core_b, labels = core_sum(keep, across_cores(send), displacement, labels, "core_sum_b")
-    plane_b, labels = plane_sum(across(core_b, planes), labels, "plane_sum_b")
+    core_b, labels = core_sum(keep, across_cores(send), displacement, labels, 3, "core_sum_b")
+    gathered = plane_sum(plane_a, across_plane(core_b))
     stress_new, nodal = element_update(
-        across(plane_a, heights),
-        across(plane_b, heights),
-        displacement,
-        stress_old,
-        resistance,
-        quad_weights,
+        across_height(gathered), displacement, stress_old, resistance, quad_weights
     )
     forces = nodal[0] + passed_along(nodal[1], "fe", 1)
     return (stress_new, forces)

time: 91.5 us -> 75.3 us (0.82)
  blocking collectives: 23.7 us -> 0 us
  waiting for transfers between devices: 7.34 us -> 15.7 us
  Pallas kernels: 42.2 us -> 38.7 us
  starting transfers between devices: 13.4 us -> 15.8 us
    all_to_all x2 -> x0, blocking collectives: 23.7 us -> none  [across(): lax.all_to_all(blocks, ('ca', 'fe'), split_axis=0, concat_axis=0, axis_in...]
    ppermute x0 -> x9, waiting for transfers between devices: none -> 13.7 us  [to_relative(): lax.ppermute(block, ('ca', 'fe'), [(i, i ^ flip) for i in range(groups *...]
    ppermute x0 -> x9, starting transfers between devices: none -> 12.3 us  [to_relative(): lax.ppermute(block, ('ca', 'fe'), [(i, i ^ flip) for i in range(groups *...]
    all_to_all x2 -> x0, starting transfers between devices: 9.95 us -> none  [across(): lax.all_to_all(blocks, ('ca', 'fe'), split_axis=0, concat_axis=0, axis_in...]
    all_to_all x2 -> x0, waiting for transfers between devices: 5.38 us -> none  [across(): lax.all_to_all(blocks, ('ca', 'fe'), split_axis=0, concat_axis=0, axis_in...]
    pallas_call x2, Pallas kernels: 31.9 us -> 29.8 us  [cell_sums(): pl.pallas_call(functools.partial(cell_sum_kernel, first, count), out_shap...]
    pallas_call x5, Pallas kernels: 4.09 us -> 2.6 us  [the longest x1 1.7 us: element_update(): pl.pallas_call(functools.partial(update_kernel, len(gathered)), out_shape...]
  transfers between devices with their start and end apart: 5 -> 12, of which waited for: 4 -> 8; matrix products, arithmetic and copies ran while one was open for 0% -> 0% of each run, Pallas kernels for 22% -> 15%
where the time goes in v7:
time: 75.3 us; the launch traced here: 74.7 us
  Pallas kernels  38.7 us (51%)
  starting transfers between devices  15.8 us (21%)
  waiting for transfers between devices  15.7 us (21%)
  local copies, waits for them, and re-layouts  2.35 us (3%)
  other arithmetic  1.32 us (2%)
  between operations  0.8 us (1%)
    pallas_call x2, Pallas kernels, cell_sums(): pl.pallas_call(functools.partial(cell_sum_kernel, first, count), out_shap...  29.8 us
    ppermute x9, waiting for transfers between devices, to_relative(): lax.ppermute(block, ('ca', 'fe'), [(i, i ^ flip) for i in range(groups *...  13.7 us
    ppermute x9, starting transfers between devices, to_relative(): lax.ppermute(block, ('ca', 'fe'), [(i, i ^ flip) for i in range(groups *...  12.3 us
    pallas_call x4, Pallas kernels, brick_sums(): pl.pallas_call(functools.partial(brick_sum_kernel, base), out_shape=[jax....  6.33 us
    ppermute x1, starting transfers between devices, passed_along(): return lax.ppermute(block, axis, route)  2.93 us
    unnamed x16, local copies, waits for them, and re-layouts  2.35 us
    pallas_call x1, Pallas kernels, element_update(): pl.pallas_call(functools.partial(update_kernel, len(gathered)), out_shape...  1.7 us
  transfers between devices with their start and end apart: 12, of which 8 were waited for; matrix products, arithmetic and copies ran while one was open for 0% of the time, Pallas kernels for 15%

profile of v7, /device:TPU:0, one launch (start us, length us, event | category | flops | bytes accessed | tf_op | source)
XLA Modules:
  0.0 74.7 jit_solution(14082444913212832627)
XLA Ops:
  0.6 0.7 add_select_fusion
  1.4 1.5 %copy-done.5 = s32[216,2048]{1,0:T(8,128)S(1)} copy-done((s32[216,2048]{1,0:T(8,128)S(1)}, s32[216,2048]{1,0:T(8,128)}, u32[]{:S(2)}) %copy-start.5) | copy-done | bytes 1769496
  2.8 0.8 %copy-done.7 = f32[3,4096]{1,0:T(4,128)S(1)} copy-done((f32[3,4096]{1,0:T(4,128)S(1)}, f32[3,4096]{1,0:T(4,128)}, u32[]{:S(2)}) %copy-start.7) | copy-done | bytes 49176
  3.7 22.1 %cell_sums.2 = (bf16[112,2048]{1,0:T(8,128)(2,1)S(1)}, s32[1,2048]{1,0:T(1,128)S(1)}, s32[54,8,128]{2,1,0:T(8,128)S(1)}) custom-call(s32[216,2048]{1,0:T(8,128)S(1)} %copy-done.5, s32[1,2048]{1,0:T(1,128)S(1)} %bitcast.14, f32[3,4096]{1,0:T(4,128)S(1)} %copy-done.7), custom_call_target="tpu_custom_call" | custom-call | flops 24000000000 | bytes 60000000 | tf_op jit(solution)/shard_map/cell_sums/pallas_call | solution.py:286
  25.8 2.1 %brick_sums.4 = (f32[16,56,256]{2,1,0:T(8,128)S(1)}, s32[1,2048]{1,0:T(1,128)S(1)}) custom-call(bf16[112,2048]{1,0:T(8,128)(2,1)S(1)} %get-tuple-element.32.split_ref, s32[1,2048]{1,0:T(1,128)S(1)} %get-tuple-element.33.label_ref), custom_call_target="tpu_custom_call" | custom-call | flops 1680000000 | bytes 5600000 | tf_op jit(solution)/shard_map/brick_sums/pallas_call | solution.py:305
  28.0 0.5 collective-permute-start
  28.5 2.1 %brick_sums.5 = (f32[16,56,256]{2,1,0:T(8,128)S(1)}, s32[1,2048]{1,0:T(1,128)S(1)}) custom-call(bf16[112,2048]{1,0:T(8,128)(2,1)S(1)} %get-tuple-element.32.split_ref, s32[1,2048]{1,0:T(1,128)S(1)} %get-tuple-element.34.label_ref), custom_call_target="tpu_custom_call" | custom-call | flops 1680000000 | bytes 5600000 | tf_op jit(solution)/shard_map/brick_sums/pallas_call | solution.py:305
  30.7 0.1 core_sum_a.1
  30.8 2.8 %collective-permute-start.1 = (f32[4,56,256]{2,1,0:T(8,128)S(1)}, f32[4,56,256]{2,1,0:T(8,128)S(1)}, u32[]{:S(2)}, u32[]{:S(2)}) collective-permute-start(f32[4,56,256]{2,1,0:T(8,128)S(1)} %get-tuple-element.39), channel_id=1, source_target_pairs={{0,1},{1,0},{2,3},{3,2},{4,5},{5,4},{6,7},{7,6},{8,9},{9,8},{10,11... | collective-permute-start | bytes 688136 | tf_op jit(solution)/shard_map/ppermute | solution.py:388
  33.7 1.5 %collective-permute-start.2 = (f32[4,56,256]{2,1,0:T(8,128)S(1)}, f32[4,56,256]{2,1,0:T(8,128)S(1)}, u32[]{:S(2)}, u32[]{:S(2)}) collective-permute-start(f32[4,56,256]{2,1,0:T(8,128)S(1)} %get-tuple-element.40), channel_id=1, source_target_pairs={{0,16},{1,17},{2,18},{3,19},{4,20},{5,21},{6,22},{7,23},{8,24},{9,... | collective-permute-start | bytes 688136 | tf_op jit(solution)/shard_map/ppermute | solution.py:388
  35.2 7.7 %cell_sums.3 = (bf16[48,2048]{1,0:T(8,128)(2,1)S(1)}, s32[1,2048]{1,0:T(1,128)S(1)}) custom-call(s32[216,2048]{1,0:T(8,128)S(1)} %copy-done.6, s32[1,2048]{1,0:T(1,128)S(1)} %get-tuple-element.42.refs_1_, s32[54,8,128]{2,1,0:T(8,128)S(1)} %get-tuple-element.43.refs_2_), custom_call_target="tpu_custom_call" | custom-call | flops 8000000000 | bytes 20000000 | tf_op jit(solution)/shard_map/cell_sums/pallas_call | solution.py:286
  42.9 3.1 %collective-permute-done.2.refs_2_ = f32[4,56,256]{2,1,0:T(8,128)S(1)} collective-permute-done((f32[4,56,256]{2,1,0:T(8,128)S(1)}, f32[4,56,256]{2,1,0:T(8,128)S(1)}, u32[]{:S(2)}, u32[]{:S(2)}) %collective-permute-start.2) | collective-permute-done | bytes 229408 | tf_op jit(solution)/shard_map/ppermute | solution.py:388
  46.0 0.1 first_plane_sum.1
  46.1 1.0 %brick_sums.6 = (f32[16,24,256]{2,1,0:T(8,128)S(1)}, s32[1,2048]{1,0:T(1,128)S(1)}) custom-call(bf16[48,2048]{1,0:T(8,128)(2,1)S(1)} %get-tuple-element.46.split_ref, s32[1,2048]{1,0:T(1,128)S(1)} %get-tuple-element.47.label_ref), custom_call_target="tpu_custom_call" | custom-call | flops 720000000 | bytes 2400000 | tf_op jit(solution)/shard_map/brick_sums/pallas_call | solution.py:305
  47.3 1.0 %brick_sums.7 = (f32[16,24,256]{2,1,0:T(8,128)S(1)}, s32[1,2048]{1,0:T(1,128)S(1)}) custom-call(bf16[48,2048]{1,0:T(8,128)(2,1)S(1)} %get-tuple-element.46.split_ref, s32[1,2048]{1,0:T(1,128)S(1)} %get-tuple-element.48.label_ref), custom_call_target="tpu_custom_call" | custom-call | flops 720000000 | bytes 2400000 | tf_op jit(solution)/shard_map/brick_sums/pallas_call | solution.py:305
  48.3 0.6 collective-permute-done.4
  48.9 0.7 core_sum_b.1
  49.6 1.2 %collective-permute-start.5 = (f32[4,24,256]{2,1,0:T(8,128)S(1)}, f32[4,24,256]{2,1,0:T(8,128)S(1)}, u32[]{:S(2)}, u32[]{:S(2)}) collective-permute-start(f32[4,24,256]{2,1,0:T(8,128)S(1)} %get-tuple-element.53), channel_id=1, source_target_pairs={{0,1},{1,0},{2,3},{3,2},{4,5},{5,4},{6,7},{7,6},{8,9},{9,8},{10,11... | collective-permute-start | bytes 294920 | tf_op jit(solution)/shard_map/ppermute | solution.py:388
  50.8 0.8 %collective-permute-start.6 = (f32[4,24,256]{2,1,0:T(8,128)S(1)}, f32[4,24,256]{2,1,0:T(8,128)S(1)}, u32[]{:S(2)}, u32[]{:S(2)}) collective-permute-start(f32[4,24,256]{2,1,0:T(8,128)S(1)} %get-tuple-element.54), channel_id=1, source_target_pairs={{0,16},{1,17},{2,18},{3,19},{4,20},{5,21},{6,22},{7,23},{8,24},{9,... | collective-permute-start | bytes 294920 | tf_op jit(solution)/shard_map/ppermute | solution.py:388
  51.6 1.4 %collective-permute-start.7 = (f32[4,24,256]{2,1,0:T(8,128)S(1)}, f32[4,24,256]{2,1,0:T(8,128)S(1)}, u32[]{:S(2)}, u32[]{:S(2)}) collective-permute-start(f32[4,24,256]{2,1,0:T(8,128)S(1)} %get-tuple-element.55), channel_id=1, source_target_pairs={{0,17},{1,16},{2,19},{3,18},{4,21},{5,20},{6,23},{7,22},{8,25},{9,... | collective-permute-start | bytes 294920 | tf_op jit(solution)/shard_map/ppermute | solution.py:388
  53.1 1.3 %collective-permute-done.5.refs_1_ = f32[4,24,256]{2,1,0:T(8,128)S(1)} collective-permute-done((f32[4,24,256]{2,1,0:T(8,128)S(1)}, f32[4,24,256]{2,1,0:T(8,128)S(1)}, u32[]{:S(2)}, u32[]{:S(2)}) %collective-permute-start.5) | collective-permute-done | bytes 98336 | tf_op jit(solution)/shard_map/ppermute | solution.py:388
  54.4 3.1 %collective-permute-done.6.refs_2_ = f32[4,24,256]{2,1,0:T(8,128)S(1)} collective-permute-done((f32[4,24,256]{2,1,0:T(8,128)S(1)}, f32[4,24,256]{2,1,0:T(8,128)S(1)}, u32[]{:S(2)}, u32[]{:S(2)}) %collective-permute-start.6) | collective-permute-done | bytes 98336 | tf_op jit(solution)/shard_map/ppermute | solution.py:388
  57.6 1.6 %collective-permute-start.8 = (f32[80,256]{1,0:T(8,128)S(1)}, f32[80,256]{1,0:T(8,128)S(1)}, u32[]{:S(2)}, u32[]{:S(2)}) collective-permute-start(f32[80,256]{1,0:T(8,128)S(1)} %get-tuple-element.57), channel_id=1, source_target_pairs={{0,2},{1,3},{2,0},{3,1},{4,6},{5,7},{6,4},{7,5},{8,10},{9,11},{10,... | collective-permute-start | bytes 245768 | tf_op jit(solution)/shard_map/ppermute | solution.py:388
  59.2 2.6 %collective-permute-start.9 = (f32[80,256]{1,0:T(8,128)S(1)}, f32[80,256]{1,0:T(8,128)S(1)}, u32[]{:S(2)}, u32[]{:S(2)}) collective-permute-start(f32[80,256]{1,0:T(8,128)S(1)} %get-tuple-element.58), channel_id=1, source_target_pairs={{0,4},{1,5},{2,6},{3,7},{4,0},{5,1},{6,2},{7,3},{8,12},{9,13},{10,... | collective-permute-start | bytes 245768 | tf_op jit(solution)/shard_map/ppermute | solution.py:388
  61.8 0.2 collective-permute-start.10
  62.0 0.9 %collective-permute-done.8.refs_1_ = f32[80,256]{1,0:T(8,128)S(1)} collective-permute-done((f32[80,256]{1,0:T(8,128)S(1)}, f32[80,256]{1,0:T(8,128)S(1)}, u32[]{:S(2)}, u32[]{:S(2)}) %collective-permute-start.8) | collective-permute-done | bytes 81952 | tf_op jit(solution)/shard_map/ppermute | solution.py:388
  62.9 4.1 %collective-permute-done.9.refs_2_ = f32[80,256]{1,0:T(8,128)S(1)} collective-permute-done((f32[80,256]{1,0:T(8,128)S(1)}, f32[80,256]{1,0:T(8,128)S(1)}, u32[]{:S(2)}, u32[]{:S(2)}) %collective-permute-start.9) | collective-permute-done | bytes 81952 | tf_op jit(solution)/shard_map/ppermute | solution.py:388
  67.0 1.1 %collective-permute-done.10.refs_3_ = f32[80,256]{1,0:T(8,128)S(1)} collective-permute-done((f32[80,256]{1,0:T(8,128)S(1)}, f32[80,256]{1,0:T(8,128)S(1)}, u32[]{:S(2)}, u32[]{:S(2)}) %collective-permute-start.10) | collective-permute-done | bytes 81952 | tf_op jit(solution)/shard_map/ppermute | solution.py:388
  68.2 1.7 %stress_update.1 = (f32[6,8,225]{2,1,0:T(8,128)}, f32[2,3,1,256]{3,2,1,0:T(1,128)S(1)}) custom-call(f32[80,256]{1,0:T(8,128)S(1)} %get-tuple-element.56.refs_0_, f32[80,256]{1,0:T(8,128)S(1)} %collective-permute-done.8.refs_1_, f32[80,256]{1,0:T(8,128)S(1)} %collective-permute-done.9.refs_2_, f32[80,256]{1,0:T(8,128)S(1)} %collective-permute-done.10.refs_3_, ...), custom_call_target="tpu_custom_call" | custom-call | tf_op jit(solution)/shard_map/stress_update/pallas_call | solution.py:565
  69.9 2.9 %collective-permute-start.11 = (f32[3,1,256]{2,1,0:T(1,128)S(1)}, f32[3,1,256]{2,1,0:T(1,128)S(1)}, u32[]{:S(2)}, u32[]{:S(2)}) collective-permute-start(f32[3,1,256]{2,1,0:T(1,128)S(1)} %slice_bitcast_fusion), channel_id=1, source_target_pairs={{0,1},{1,2},{2,3},{3,4},{4,5},{5,6},{6,7},{8,9},{9,10},{10,11},{11... | collective-permute-start | bytes 9224 | tf_op jit(solution)/shard_map/ppermute | solution.py:48
  72.8 1.3 %collective-permute-done.11 = f32[3,1,256]{2,1,0:T(1,128)S(1)} collective-permute-done((f32[3,1,256]{2,1,0:T(1,128)S(1)}, f32[3,1,256]{2,1,0:T(1,128)S(1)}, u32[]{:S(2)}, u32[]{:S(2)}) %collective-permute-start.11) | collective-permute-done | bytes 3104 | tf_op jit(solution)/shard_map/ppermute | solution.py:48
  74.1 0.6 bitcast_add_fusion
  (22 shorter events, 0.2 us)
Async XLA Ops:
  1.4 1.5 %copy-start.5 = (s32[216,2048]{1,0:T(8,128)S(1)}, s32[216,2048]{1,0:T(8,128)}, u32[]{:S(2)}) copy-start(s32[216,2048]{1,0:T(8,128)} %refs_0_.3) | copy-start | bytes 5308420
  2.8 0.8 %copy-start.7 = (f32[3,4096]{1,0:T(4,128)S(1)}, f32[3,4096]{1,0:T(4,128)}, u32[]{:S(2)}) copy-start(f32[3,4096]{1,0:T(4,128)} %refs_2_.1) | copy-start | bytes 147460
  28.0 2.7 %collective-permute-start = (f32[16,56,256]{2,1,0:T(8,128)S(1)}, f32[16,56,256]{2,1,0:T(8,128)S(1)}, u32[]{:S(2)}, u32[]{:S(2)}) collective-permute-start(f32[16,56,256]{2,1,0:T(8,128)S(1)} %get-tuple-element.36), channel_id=1, source_target_pairs={{0,8},{8,0},{16,24},{24,16},{1,9},{9,1},{17,25},{25,17},{2,10},{10... | collective-permute-start | bytes 2752520 | tf_op jit(solution)/shard_map/ppermute | solution.py:232
  28.5 2.2 %copy-start.2 = (f32[3,1,256]{2,1,0:T(1,128)S(1)}, f32[3,1,256]{2,1,0:T(1,128)}, u32[]{:S(2)}) copy-start(f32[3,1,256]{2,1,0:T(1,128)} %refs_4_.1) | copy-start | bytes 9220
  30.7 4.5 %copy-start.6 = (s32[216,2048]{1,0:T(8,128)S(1)}, s32[216,2048]{1,0:T(8,128)}, u32[]{:S(2)}) copy-start(s32[216,2048]{1,0:T(8,128)} %refs_0_.3) | copy-start | bytes 5308420
  30.8 12.1 %collective-permute-start.1 = (f32[4,56,256]{2,1,0:T(8,128)S(1)}, f32[4,56,256]{2,1,0:T(8,128)S(1)}, u32[]{:S(2)}, u32[]{:S(2)}) collective-permute-start(f32[4,56,256]{2,1,0:T(8,128)S(1)} %get-tuple-element.39), channel_id=1, source_target_pairs={{0,1},{1,0},{2,3},{3,2},{4,5},{5,4},{6,7},{7,6},{8,9},{9,8},{10,11... | collective-permute-start | bytes 688136 | tf_op jit(solution)/shard_map/ppermute | solution.py:388
  33.7 12.4 %collective-permute-start.2 = (f32[4,56,256]{2,1,0:T(8,128)S(1)}, f32[4,56,256]{2,1,0:T(8,128)S(1)}, u32[]{:S(2)}, u32[]{:S(2)}) collective-permute-start(f32[4,56,256]{2,1,0:T(8,128)S(1)} %get-tuple-element.40), channel_id=1, source_target_pairs={{0,16},{1,17},{2,18},{3,19},{4,20},{5,21},{6,22},{7,23},{8,24},{9,... | collective-permute-start | bytes 688136 | tf_op jit(solution)/shard_map/ppermute | solution.py:388
  35.2 10.9 %collective-permute-start.3 = (f32[4,56,256]{2,1,0:T(8,128)S(1)}, f32[4,56,256]{2,1,0:T(8,128)S(1)}, u32[]{:S(2)}, u32[]{:S(2)}) collective-permute-start(f32[4,56,256]{2,1,0:T(8,128)S(1)} %get-tuple-element.41), channel_id=1, source_target_pairs={{0,17},{1,16},{2,19},{3,18},{4,21},{5,20},{6,23},{7,22},{8,25},{9,... | collective-permute-start | bytes 688136 | tf_op jit(solution)/shard_map/ppermute | solution.py:388
  47.1 1.8 %collective-permute-start.4 = (f32[16,24,256]{2,1,0:T(8,128)S(1)}, f32[16,24,256]{2,1,0:T(8,128)S(1)}, u32[]{:S(2)}, u32[]{:S(2)}) collective-permute-start(f32[16,24,256]{2,1,0:T(8,128)S(1)} %get-tuple-element.50), channel_id=1, source_target_pairs={{0,8},{8,0},{16,24},{24,16},{1,9},{9,1},{17,25},{25,17},{2,10},{10... | collective-permute-start | bytes 1179656 | tf_op jit(solution)/shard_map/ppermute | solution.py:232
  47.2 21.0 %copy-start = (f32[12,8,225]{2,1,0:T(8,128)S(1)}, f32[12,8,225]{2,1,0:T(8,128)}, u32[]{:S(2)}) copy-start(f32[12,8,225]{2,1,0:T(8,128)} %refs_6_.1) | copy-start | bytes 259204
  47.2 20.9 %copy-start.1 = (f32[6,8,225]{2,1,0:T(8,128)S(1)}, f32[6,8,225]{2,1,0:T(8,128)}, u32[]{:S(2)}) copy-start(f32[6,8,225]{2,1,0:T(8,128)} %refs_5_.1) | copy-start | bytes 129604
  47.2 20.9 %copy-start.3 = (f32[24,8]{1,0:T(8,128)S(1)}, f32[24,8]{1,0:T(8,128)}, u32[]{:S(2)}) copy-start(f32[24,8]{1,0:T(8,128)} %constant.8.clone.refs_8_) | copy-start | bytes 2308
  47.2 20.9 %copy-start.4 = (s32[8,225]{1,0:T(8,128)S(1)}, s32[8,225]{1,0:T(8,128)}, u32[]{:S(2)}) copy-start(s32[8,225]{1,0:T(8,128)} %refs_7_.1) | copy-start | bytes 21604
  49.6 4.8 %collective-permute-start.5 = (f32[4,24,256]{2,1,0:T(8,128)S(1)}, f32[4,24,256]{2,1,0:T(8,128)S(1)}, u32[]{:S(2)}, u32[]{:S(2)}) collective-permute-start(f32[4,24,256]{2,1,0:T(8,128)S(1)} %get-tuple-element.53), channel_id=1, source_target_pairs={{0,1},{1,0},{2,3},{3,2},{4,5},{5,4},{6,7},{7,6},{8,9},{9,8},{10,11... | collective-permute-start | bytes 294920 | tf_op jit(solution)/shard_map/ppermute | solution.py:388
  50.8 6.7 %collective-permute-start.6 = (f32[4,24,256]{2,1,0:T(8,128)S(1)}, f32[4,24,256]{2,1,0:T(8,128)S(1)}, u32[]{:S(2)}, u32[]{:S(2)}) collective-permute-start(f32[4,24,256]{2,1,0:T(8,128)S(1)} %get-tuple-element.54), channel_id=1, source_target_pairs={{0,16},{1,17},{2,18},{3,19},{4,20},{5,21},{6,22},{7,23},{8,24},{9,... | collective-permute-start | bytes 294920 | tf_op jit(solution)/shard_map/ppermute | solution.py:388
  51.6 5.9 %collective-permute-start.7 = (f32[4,24,256]{2,1,0:T(8,128)S(1)}, f32[4,24,256]{2,1,0:T(8,128)S(1)}, u32[]{:S(2)}, u32[]{:S(2)}) collective-permute-start(f32[4,24,256]{2,1,0:T(8,128)S(1)} %get-tuple-element.55), channel_id=1, source_target_pairs={{0,17},{1,16},{2,19},{3,18},{4,21},{5,20},{6,23},{7,22},{8,25},{9,... | collective-permute-start | bytes 294920 | tf_op jit(solution)/shard_map/ppermute | solution.py:388
  57.6 5.3 %collective-permute-start.8 = (f32[80,256]{1,0:T(8,128)S(1)}, f32[80,256]{1,0:T(8,128)S(1)}, u32[]{:S(2)}, u32[]{:S(2)}) collective-permute-start(f32[80,256]{1,0:T(8,128)S(1)} %get-tuple-element.57), channel_id=1, source_target_pairs={{0,2},{1,3},{2,0},{3,1},{4,6},{5,7},{6,4},{7,5},{8,10},{9,11},{10,... | collective-permute-start | bytes 245768 | tf_op jit(solution)/shard_map/ppermute | solution.py:388
  59.2 7.8 %collective-permute-start.9 = (f32[80,256]{1,0:T(8,128)S(1)}, f32[80,256]{1,0:T(8,128)S(1)}, u32[]{:S(2)}, u32[]{:S(2)}) collective-permute-start(f32[80,256]{1,0:T(8,128)S(1)} %get-tuple-element.58), channel_id=1, source_target_pairs={{0,4},{1,5},{2,6},{3,7},{4,0},{5,1},{6,2},{7,3},{8,12},{9,13},{10,... | collective-permute-start | bytes 245768 | tf_op jit(solution)/shard_map/ppermute | solution.py:388
  61.8 6.3 %collective-permute-start.10 = (f32[80,256]{1,0:T(8,128)S(1)}, f32[80,256]{1,0:T(8,128)S(1)}, u32[]{:S(2)}, u32[]{:S(2)}) collective-permute-start(f32[80,256]{1,0:T(8,128)S(1)} %get-tuple-element.59), channel_id=1, source_target_pairs={{0,6},{1,7},{2,4},{3,5},{4,2},{5,3},{6,0},{7,1},{8,14},{9,15},{10,... | collective-permute-start | bytes 245768 | tf_op jit(solution)/shard_map/ppermute | solution.py:388
  69.9 4.2 %collective-permute-start.11 = (f32[3,1,256]{2,1,0:T(1,128)S(1)}, f32[3,1,256]{2,1,0:T(1,128)S(1)}, u32[]{:S(2)}, u32[]{:S(2)}) collective-permute-start(f32[3,1,256]{2,1,0:T(1,128)S(1)} %slice_bitcast_fusion), channel_id=1, source_target_pairs={{0,1},{1,2},{2,3},{3,4},{4,5},{5,6},{6,7},{8,9},{9,10},{10,11},{11... | collective-permute-start | bytes 9224 | tf_op jit(solution)/shard_map/ppermute | solution.py:48

commit v8 on v7

--- a/solution.py
+++ b/solution.py
@@ -13,7 +13,8 @@
 LANES = 128
 COLUMNS = 256
 CHUNKS = ((0, 6), (6, 2))
-QUANTUM = float((1 << 17) - 1)
+FIELDS = (32, 16, 2, 1)
+QUANTUM = float((1 << 16) - 1)
 
 SLIP_PLANES = [
     [value / math.sqrt(3.0) for value in row]
@@ -93,16 +94,16 @@
         jnp.clip(jnp.round(value), -QUANTUM, QUANTUM).astype(jnp.int32) for value in (x, y, z)
     ]
     return [
-        (lax.shift_left(x, 14) | (lax.shift_right_arithmetic(y, 4) & 0x3FFF), 32),
-        (lax.shift_left(y & 0xF, 12) | (lax.shift_right_arithmetic(z, 6) & 0xFFF), 16),
-        (lax.shift_right_arithmetic(z, 2) & 0xF, 4),
-        (z & 0x3, 2),
-    ]
-
-
-def fill_table(table_ref, euler):
+        lax.shift_left(x, 15) | (lax.shift_right_arithmetic(y, 2) & 0x7FFF),
+        lax.shift_left(y & 0x3, 14) | (lax.shift_right_arithmetic(z, 3) & 0x3FFF),
+        lax.shift_right_arithmetic(z, 1) & 0x3,
+        z & 0x1,
+    ]
+
+
+def table_kernel(euler_ref, table_ref):
     at = 0
-    for field, width in rotation_words(euler):
+    for field, width in zip(rotation_words(euler_ref[...]), FIELDS):
         rows = field.shape[1] // LANES
         shared = 32 // width
         for first in range(0, rows, shared):
@@ -112,6 +113,16 @@
                 word = word | lax.shift_left(row, other * width)
             table_ref[at] = jnp.broadcast_to(word, (8, LANES))
             at += 1
+
+
+def rotation_table(euler_angles):
+    height = euler_angles.shape[1] // LANES * sum(FIELDS) // 32
+    return pl.pallas_call(
+        table_kernel,
+        out_shape=jax.ShapeDtypeStruct((height, 8, LANES), jnp.int32),
+        compiler_params=pltpu.CompilerParams(vmem_limit_bytes=8 * 1024 * 1024),
+        name="rotation_table",
+    )(euler_angles)
 
 
 def looked_up(table_ref, first_row, rows, lane, bits):
@@ -142,7 +153,7 @@
     bits = [(row & (1 << level)) != 0 for level in range(table_rows.bit_length() - 1)]
     fields = []
     at = 0
-    for width in (32, 16, 4, 2):
+    for width in FIELDS:
         shared = 32 // width
         skipped = shared.bit_length() - 1
         rows = table_rows // shared
@@ -152,12 +163,12 @@
         fields.append(field)
         at += rows
     first, second, third, fourth = fields
-    x = lax.shift_right_arithmetic(first, 14).astype(jnp.float32)
-    y = lax.shift_right_arithmetic(lax.shift_left(first, 18), 14) | (
-        lax.shift_right_logical(second, 12) & 0xF
+    x = lax.shift_right_arithmetic(first, 15).astype(jnp.float32)
+    y = lax.shift_right_arithmetic(lax.shift_left(first, 17), 15) | (
+        lax.shift_right_logical(second, 14) & 0x3
     )
-    z = lax.shift_right_arithmetic(lax.shift_left(second, 20), 14) | (
-        lax.shift_left(third & 0xF, 2) | (fourth & 0x3)
+    z = lax.shift_right_arithmetic(lax.shift_left(second, 18), 15) | (
+        lax.shift_left(third & 0x3, 1) | (fourth & 0x1)
     )
     y, z = y.astype(jnp.float32), z.astype(jnp.float32)
     square = x * x + y * y + z * z
@@ -167,16 +178,22 @@
     return [x * x, y * y, z * z, x * y, x * z, y * z, w * x, w * y, w * z]
 
 
-def cell_sum_kernel(first, count, *refs):
-    if first == 0:
-        ids_ref, label_ref, euler_ref, split_ref, label_out_ref, table_ref, tile_ref = refs
-    else:
-        ids_ref, label_ref, table_ref, split_ref, label_out_ref, tile_ref = refs
+def cell_sum_kernel(
+    first,
+    count,
+    ids_ref,
+    label_ref,
+    table_ref,
+    split_ref,
+    out_ref,
+    label_out_ref,
+    tile_ref,
+    place_ref,
+    masked_ref,
+):
     per_octant = ids_ref.shape[0] // 8
-    table_rows = table_ref.shape[0] * 16 // 27
+    table_rows = table_ref.shape[0] * 32 // sum(FIELDS)
     label_out_ref[...] = label_ref[...]
-    if first == 0:
-        fill_table(table_ref, euler_ref[...])
     groups = tile_ref.shape[0] // 8
     rows_left = count * per_octant - 8 * (groups - 1)
     turns = count // math.gcd(count, 8)
@@ -225,6 +242,7 @@
         return carry
 
     lax.fori_loop(0, ids_ref.shape[1] // LANES, tile_sums, 0, unroll=2)
+    sum_bricks(out_ref.shape[0], split_ref, label_ref, out_ref, place_ref, masked_ref)
 
 
 def across_cores(block):
@@ -232,10 +250,14 @@
     return lax.ppermute(block, "ca", [(i, i ^ 1) for i in range(groups)])
 
 
-def brick_sum_kernel(base, split_ref, label_ref, out_ref, label_out_ref, place_ref, masked_ref):
+def brick_sum_kernel(split_ref, label_ref, out_ref, label_out_ref, place_ref, masked_ref):
+    label_out_ref[...] = label_ref[...]
+    sum_bricks(0, split_ref, label_ref, out_ref, place_ref, masked_ref)
+
+
+def sum_bricks(base, split_ref, label_ref, out_ref, place_ref, masked_ref):
     bricks = split_ref.shape[1]
     labels = label_ref[...]
-    label_out_ref[...] = labels
     place = place_of(lax.shift_right_arithmetic(labels, COLUMNS.bit_length() - 1))
     place_ref[...] = jnp.where(labels < 0, -1, place - base)
     column = lax.broadcasted_iota(jnp.int32, (COLUMNS, bricks), 0)
@@ -273,21 +295,20 @@
     return place * (members // 2) + lax.shift_right_logical(owner_fe, 1)
 
 
-def cell_sums(first, count, grain_ids, labels, table):
+def cell_sums(first, count, grain_ids, labels, table, places):
     bricks = grain_ids.shape[1]
-    per_octant = grain_ids.shape[0] // 8
-    out_shape = [
-        jax.ShapeDtypeStruct((2 * padded_rows(count), bricks), jnp.bfloat16),
-        jax.ShapeDtypeStruct(labels.shape, jnp.int32),
-    ]
-    if first == 0:
-        grains = table.shape[1]
-        out_shape.append(jax.ShapeDtypeStruct((27 * grains // LANES // 16, 8, LANES), jnp.int32))
+    tile_rows = -(-count * (grain_ids.shape[0] // 8) // 8) * 8
+    rows = padded_rows(count)
     return pl.pallas_call(
         functools.partial(cell_sum_kernel, first, count),
-        out_shape=out_shape,
-        scratch_shapes=[pltpu.VMEM((-(-count * per_octant // 8) * 8, LANES), jnp.int32)],
-        compiler_params=pltpu.CompilerParams(vmem_limit_bytes=8 * 1024 * 1024),
+        out_shape=[
+            jax.ShapeDtypeStruct((2 * rows, bricks), jnp.bfloat16),
+            jax.ShapeDtypeStruct((places, rows, COLUMNS), jnp.float32),
+            jax.ShapeDtypeStruct(labels.shape, jnp.int32),
+        ],
+        scratch_shapes=[pltpu.VMEM((tile_rows, LANES), jnp.int32)]
+        + brick_scratch(rows, bricks, places),
+        compiler_params=pltpu.CompilerParams(vmem_limit_bytes=28 * 1024 * 1024),
         cost_estimate=pl.CostEstimate(
             flops=count * 4 * 10**9, bytes_accessed=count * 10**7, transcendentals=0
         ),
@@ -299,19 +320,22 @@
     return -(-9 * count // 8) * 8
 
 
-def brick_sums(split, labels, places, base):
+def brick_scratch(rows, bricks, places):
+    return [
+        pltpu.VMEM((1, bricks), jnp.int32),
+        pltpu.VMEM((min(16, places) * 2 * rows, bricks), jnp.bfloat16),
+    ]
+
+
+def brick_sums(split, labels, places):
     rows, bricks = split.shape
-    members = min(16, places)
     return pl.pallas_call(
-        functools.partial(brick_sum_kernel, base),
+        brick_sum_kernel,
         out_shape=[
             jax.ShapeDtypeStruct((places, rows // 2, COLUMNS), jnp.float32),
             jax.ShapeDtypeStruct(labels.shape, jnp.int32),
         ],
-        scratch_shapes=[
-            pltpu.VMEM((1, bricks), jnp.int32),
-            pltpu.VMEM((members * rows, bricks), jnp.bfloat16),
-        ],
+        scratch_shapes=brick_scratch(rows // 2, bricks, places),
         compiler_params=pltpu.CompilerParams(vmem_limit_bytes=24 * 1024 * 1024),
         cost_estimate=pl.CostEstimate(
             flops=rows * 15 * 10**6, bytes_accessed=rows * 5 * 10**4, transcendentals=0
@@ -344,42 +368,24 @@
     return parts, labels
 
 
-def plane_sum_kernel(sources, first_ref, *refs):
-    second, outs = refs[:sources], refs[sources:]
-    rows = first_ref.shape[1]
-    for height, out_ref in enumerate(outs):
-        out_ref[0:rows, :] = first_ref[height]
-        out_ref[rows:, :] = sum(ref[height] for ref in second)
-        out_ref[out_ref.shape[0] - 3 :, :] = second[1][height, second[1].shape[1] - 3 :, :]
-
-
-def plane_sum(first, second):
-    heights, rows, columns = first.shape
-    part = jax.ShapeDtypeStruct((rows + second[0].shape[1], columns), jnp.float32)
-    return pl.pallas_call(
-        functools.partial(plane_sum_kernel, len(second)),
-        out_shape=[part] * heights,
+def plane_sum_kernel(spare, sources, *refs):
+    for height, out_ref in enumerate(refs[sources + 1 : -1]):
+        out_ref[...] = sum(ref[height] for ref in refs[:sources])
+        if spare:
+            rows = pl.ds(out_ref.shape[0] - spare, spare)
+            out_ref[rows, :] = refs[1][height, rows, :]
+    refs[-1][...] = refs[sources][...]
+
+
+def plane_sum(parts, labels, spare, name):
+    part = jax.ShapeDtypeStruct(parts[0].shape[1:], jnp.float32)
+    *parts, labels = pl.pallas_call(
+        functools.partial(plane_sum_kernel, spare, len(parts)),
+        out_shape=[part] * parts[0].shape[0] + [jax.ShapeDtypeStruct(labels.shape, jnp.int32)],
         compiler_params=pltpu.CompilerParams(vmem_limit_bytes=16 * 1024 * 1024),
-        name="plane_sum",
-    )(first, *second)
-
-
-def first_plane_sum_kernel(*refs):
-    *part_refs, label_ref, out_ref, label_out_ref = refs
-    out_ref[...] = sum(ref[...] for ref in part_refs)
-    label_out_ref[...] = label_ref[...]
-
-
-def first_plane_sum(parts, labels):
-    return pl.pallas_call(
-        first_plane_sum_kernel,
-        out_shape=[
-            jax.ShapeDtypeStruct(parts[0].shape, jnp.float32),
-            jax.ShapeDtypeStruct(labels.shape, jnp.int32),
-        ],
-        compiler_params=pltpu.CompilerParams(vmem_limit_bytes=16 * 1024 * 1024),
-        name="first_plane_sum",
+        name=name,
     )(*parts, labels)
+    return parts, labels
 
 
 def to_relative(block, core, pair, last, rest):
@@ -417,20 +423,21 @@
 
 
 def update_kernel(heights, *refs):
-    gathered_refs = refs[:heights]
-    own_ref, stress_ref, resistance_ref, weights_ref, table_ref = refs[heights:-2]
+    first_refs, second_refs = refs[:heights], refs[heights : 2 * heights]
+    own_ref, stress_ref, resistance_ref, weights_ref, table_ref = refs[2 * heights : -2]
     stress_out_ref, nodal_ref = refs[-2:]
     elements = stress_ref.shape[2]
-    gathered = sum(ref[:, 0:elements] for ref in gathered_refs)
-    starts = [0, padded_rows(CHUNKS[0][1])]
-    counted = starts[1] + 9 * CHUNKS[1][1]
-    counts = gathered[counted : counted + 1]
+    gathered = [
+        sum(ref[:, 0:elements] for ref in chunk_refs) for chunk_refs in (first_refs, second_refs)
+    ]
+    counted = 9 * CHUNKS[1][1]
+    counts = gathered[1][counted : counted + 1]
     per_brick = 1.0 / (8.0 * jnp.maximum(counts, 1.0))
     frames = [
         jnp.concatenate(
             [
-                gathered[start + count * k : start + count * (k + 1)]
-                for start, (first, count) in zip(starts, CHUNKS)
+                sums[count * k : count * (k + 1)]
+                for sums, (first, count) in zip(gathered, CHUNKS)
             ],
             axis=0,
         )
@@ -451,7 +458,7 @@
     height = lax.axis_index("fe") // 2
     above = height + (lax.axis_index("fe") & 1)
     upper = jnp.zeros((3, COLUMNS), jnp.float32)
-    for flip, ref in enumerate(gathered_refs):
+    for flip, ref in enumerate(second_refs):
         wanted = (height ^ flip) == above
         upper = upper + jnp.where(wanted, ref[ref.shape[0] - 3 :, :], 0.0)
     values = jnp.where(
@@ -552,7 +559,7 @@
         nodal_ref[1, c] = jnp.sum(above[8 * c : 8 * c + 8], axis=0, keepdims=True)
 
 
-def element_update(gathered, own, stress_old, resistance, quad_weights):
+def element_update(first, second, own, stress_old, resistance, quad_weights):
     grad_table = shape_gradients()
     table = jnp.asarray(
         [
@@ -563,14 +570,14 @@
         dtype=jnp.float32,
     )
     return pl.pallas_call(
-        functools.partial(update_kernel, len(gathered)),
+        functools.partial(update_kernel, len(first)),
         out_shape=(
             jax.ShapeDtypeStruct(stress_old.shape, jnp.float32),
             jax.ShapeDtypeStruct((2,) + own.shape, jnp.float32),
         ),
         compiler_params=pltpu.CompilerParams(vmem_limit_bytes=8 * 1024 * 1024),
         name="stress_update",
-    )(*gathered, own, stress_old, resistance, quad_weights, table)
+    )(*first, *second, own, stress_old, resistance, quad_weights, table)
 
 
 def body(
@@ -589,18 +596,22 @@
     owner = lax.optimization_barrier(brick_owner.reshape(bricks))
     labels = jnp.where(brick_active > 0, owner * COLUMNS + brick_element, -1).reshape(1, bricks)
     (first_a, count_a), (first_b, count_b) = CHUNKS
-    split, labels, table = cell_sums(first_a, count_a, grain_ids, labels, euler_angles)
-    send, labels = brick_sums(split, labels, half, half)
-    keep, labels = brick_sums(split, labels, half, 0)
+    table = rotation_table(euler_angles)
+    split, send, labels = cell_sums(first_a, count_a, grain_ids, labels, table, half)
+    keep, labels = brick_sums(split, labels, half)
     core_a, labels = core_sum(keep, across_cores(send), displacement, labels, 0, "core_sum_a")
-    split, labels = cell_sums(first_b, count_b, grain_ids, labels, table)
-    plane_a, labels = first_plane_sum(across_plane(core_a), labels)
-    send, labels = brick_sums(split, labels, half, half)
-    keep, labels = brick_sums(split, labels, half, 0)
+    split, send, labels = cell_sums(first_b, count_b, grain_ids, labels, table, half)
+    plane_a, labels = plane_sum(across_plane(core_a), labels, 0, "plane_sum_a")
+    keep, labels = brick_sums(split, labels, half)
     core_b, labels = core_sum(keep, across_cores(send), displacement, labels, 3, "core_sum_b")
-    gathered = plane_sum(plane_a, across_plane(core_b))
+    plane_b, labels = plane_sum(across_plane(core_b), labels, 3, "plane_sum_b")
     stress_new, nodal = element_update(
-        across_height(gathered), displacement, stress_old, resistance, quad_weights
+        across_height(plane_a),
+        across_height(plane_b),
+        displacement,
+        stress_old,
+        resistance,
+        quad_weights,
     )
     forces = nodal[0] + passed_along(nodal[1], "fe", 1)
     return (stress_new, forces)

time: 75.3 us -> 81.9 us (1.088)
  starting transfers between devices: 15.8 us -> 21.6 us
  local copies, waits for them, and re-layouts: 2.35 us -> 3.67 us
    ppermute x9 -> x12, starting transfers between devices: 12.3 us -> 17.9 us  [to_relative(): lax.ppermute(block, ('ca', 'fe'), [(i, i ^ flip) for i in range(groups *...]
    pallas_call x7 -> x6, Pallas kernels: 8.14 us -> 5.77 us  [the longest x2 3.16 us: brick_sums(): pl.pallas_call(brick_sum_kernel, out_shape=[jax.ShapeDtypeStruct((places,...]
    pallas_call x2, Pallas kernels: 29.8 us -> 31.9 us  [cell_sums(): pl.pallas_call(functools.partial(cell_sum_kernel, first, count), out_shap...]
    ppermute x9 -> x12, waiting for transfers between devices: 13.7 us -> 15 us  [to_relative(): lax.ppermute(block, ('ca', 'fe'), [(i, i ^ flip) for i in range(groups *...]
    unnamed x16, local copies, waits for them, and re-layouts: 2.35 us -> 3.66 us
  transfers between devices with their start and end apart: 12 -> 15, of which waited for: 8 -> 5; matrix products, arithmetic and copies ran while one was open for 0% -> 0% of each run, Pallas kernels for 15% -> 5%
where the time goes in v8:
time: 81.9 us; the launch traced here: 81.6 us
  Pallas kernels  37.9 us (46%)
  starting transfers between devices  21.6 us (26%)
  waiting for transfers between devices  16.4 us (20%)
  local copies, waits for them, and re-layouts  3.67 us (4%)
  other arithmetic  1.32 us (2%)
    pallas_call x2, Pallas kernels, cell_sums(): pl.pallas_call(functools.partial(cell_sum_kernel, first, count), out_shap...  31.9 us
    ppermute x12, starting transfers between devices, to_relative(): lax.ppermute(block, ('ca', 'fe'), [(i, i ^ flip) for i in range(groups *...  17.9 us
    ppermute x12, waiting for transfers between devices, to_relative(): lax.ppermute(block, ('ca', 'fe'), [(i, i ^ flip) for i in range(groups *...  15 us
    unnamed x16, local copies, waits for them, and re-layouts  3.66 us
    pallas_call x2, Pallas kernels, brick_sums(): pl.pallas_call(brick_sum_kernel, out_shape=[jax.ShapeDtypeStruct((places,...  3.16 us
    ppermute x1, starting transfers between devices, passed_along(): return lax.ppermute(block, axis, route)  3.14 us
    pallas_call x1, Pallas kernels, element_update(): pl.pallas_call(functools.partial(update_kernel, len(first)), out_shape=(j...  1.7 us
  transfers between devices with their start and end apart: 15, of which 5 were waited for; matrix products, arithmetic and copies ran while one was open for 0% of the time, Pallas kernels for 5%

profile of v8, /device:TPU:0, one launch (start us, length us, event | category | flops | bytes accessed | tf_op | source)
XLA Modules:
  0.0 81.6 jit_solution(14073065789474989800)
XLA Ops:
  0.6 0.8 %copy-done.1 = f32[3,4096]{1,0:T(4,128)S(1)} copy-done((f32[3,4096]{1,0:T(4,128)S(1)}, f32[3,4096]{1,0:T(4,128)}, u32[]{:S(2)}) %copy-start.1) | copy-done | bytes 49176
  1.5 0.2 rotation_table.1.table_ref
  1.7 0.7 add_select_fusion
  2.4 1.5 %copy-done.6 = s32[216,2048]{1,0:T(8,128)S(1)} copy-done((s32[216,2048]{1,0:T(8,128)S(1)}, s32[216,2048]{1,0:T(8,128)}, u32[]{:S(2)}) %copy-start.6) | copy-done | bytes 1769496
  3.9 23.5 %cell_sums.2 = (bf16[112,2048]{1,0:T(8,128)(2,1)S(1)}, f32[16,56,256]{2,1,0:T(8,128)S(1)}, s32[1,2048]{1,0:T(1,128)S(1)}) custom-call(s32[216,2048]{1,0:T(8,128)S(1)} %copy-done.6, s32[1,2048]{1,0:T(1,128)S(1)} %bitcast.14, s32[51,8,128]{2,1,0:T(8,128)S(1)} %rotation_table.1.table_ref), custom_call_target="tpu_custom_call" | custom-call | flops 24000000000 | bytes 60000000 | tf_op jit(solution)/shard_map/cell_sums/pallas_call | solution.py:302
  27.4 0.5 collective-permute-start
  27.9 2.1 %brick_sums.2 = (f32[16,56,256]{2,1,0:T(8,128)S(1)}, s32[1,2048]{1,0:T(1,128)S(1)}) custom-call(bf16[112,2048]{1,0:T(8,128)(2,1)S(1)} %get-tuple-element.33.split_ref, s32[1,2048]{1,0:T(1,128)S(1)} %get-tuple-element.34.label_ref), custom_call_target="tpu_custom_call" | custom-call | flops 1680000000 | bytes 5600000 | tf_op jit(solution)/shard_map/brick_sums/pallas_call | solution.py:332
  30.1 0.1 core_sum_a.1
  30.2 1.3 %copy-done.7 = s32[216,2048]{1,0:T(8,128)S(1)} copy-done((s32[216,2048]{1,0:T(8,128)S(1)}, s32[216,2048]{1,0:T(8,128)}, u32[]{:S(2)}) %copy-start.7) | copy-done | bytes 1769496
  31.6 8.4 %cell_sums.3 = (bf16[48,2048]{1,0:T(8,128)(2,1)S(1)}, f32[16,24,256]{2,1,0:T(8,128)S(1)}, s32[1,2048]{1,0:T(1,128)S(1)}) custom-call(s32[216,2048]{1,0:T(8,128)S(1)} %copy-done.7, s32[1,2048]{1,0:T(1,128)S(1)} %get-tuple-element.42.label_ref, s32[51,8,128]{2,1,0:T(8,128)S(1)} %rotation_table.1.table_ref), custom_call_target="tpu_custom_call" | custom-call | flops 8000000000 | bytes 20000000 | tf_op jit(solution)/shard_map/cell_sums/pallas_call | solution.py:302
  40.0 0.1 collective-permute-start.7
  40.1 3.0 %collective-permute-start.1 = (f32[4,56,256]{2,1,0:T(8,128)S(1)}, f32[4,56,256]{2,1,0:T(8,128)S(1)}, u32[]{:S(2)}, u32[]{:S(2)}) collective-permute-start(f32[4,56,256]{2,1,0:T(8,128)S(1)} %get-tuple-element.39), channel_id=1, source_target_pairs={{0,1},{1,0},{2,3},{3,2},{4,5},{5,4},{6,7},{7,6},{8,9},{9,8},{10,11... | collective-permute-start | bytes 688136 | tf_op jit(solution)/shard_map/ppermute | solution.py:394
  43.0 1.5 %collective-permute-start.2 = (f32[4,56,256]{2,1,0:T(8,128)S(1)}, f32[4,56,256]{2,1,0:T(8,128)S(1)}, u32[]{:S(2)}, u32[]{:S(2)}) collective-permute-start(f32[4,56,256]{2,1,0:T(8,128)S(1)} %get-tuple-element.40), channel_id=1, source_target_pairs={{0,16},{1,17},{2,18},{3,19},{4,20},{5,21},{6,22},{7,23},{8,24},{9,... | collective-permute-start | bytes 688136 | tf_op jit(solution)/shard_map/ppermute | solution.py:394
  44.5 4.9 %collective-permute-done.1.refs_1_ = f32[4,56,256]{2,1,0:T(8,128)S(1)} collective-permute-done((f32[4,56,256]{2,1,0:T(8,128)S(1)}, f32[4,56,256]{2,1,0:T(8,128)S(1)}, u32[]{:S(2)}, u32[]{:S(2)}) %collective-permute-start.1) | collective-permute-done | bytes 229408 | tf_op jit(solution)/shard_map/ppermute | solution.py:394
  49.4 5.8 %collective-permute-done.2.refs_2_ = f32[4,56,256]{2,1,0:T(8,128)S(1)} collective-permute-done((f32[4,56,256]{2,1,0:T(8,128)S(1)}, f32[4,56,256]{2,1,0:T(8,128)S(1)}, u32[]{:S(2)}, u32[]{:S(2)}) %collective-permute-start.2) | collective-permute-done | bytes 229408 | tf_op jit(solution)/shard_map/ppermute | solution.py:394
  55.4 1.0 %brick_sums.3 = (f32[16,24,256]{2,1,0:T(8,128)S(1)}, s32[1,2048]{1,0:T(1,128)S(1)}) custom-call(bf16[48,2048]{1,0:T(8,128)(2,1)S(1)} %get-tuple-element.48.split_ref, s32[1,2048]{1,0:T(1,128)S(1)} %get-tuple-element.49.label_ref), custom_call_target="tpu_custom_call" | custom-call | flops 720000000 | bytes 2400000 | tf_op jit(solution)/shard_map/brick_sums/pallas_call | solution.py:332
  56.5 1.3 %collective-permute-start.8 = (f32[4,24,256]{2,1,0:T(8,128)S(1)}, f32[4,24,256]{2,1,0:T(8,128)S(1)}, u32[]{:S(2)}, u32[]{:S(2)}) collective-permute-start(f32[4,24,256]{2,1,0:T(8,128)S(1)} %get-tuple-element.54), channel_id=1, source_target_pairs={{0,1},{1,0},{2,3},{3,2},{4,5},{5,4},{6,7},{7,6},{8,9},{9,8},{10,11... | collective-permute-start | bytes 294920 | tf_op jit(solution)/shard_map/ppermute | solution.py:394
  57.8 0.8 %collective-permute-start.9 = (f32[4,24,256]{2,1,0:T(8,128)S(1)}, f32[4,24,256]{2,1,0:T(8,128)S(1)}, u32[]{:S(2)}, u32[]{:S(2)}) collective-permute-start(f32[4,24,256]{2,1,0:T(8,128)S(1)} %get-tuple-element.55), channel_id=1, source_target_pairs={{0,16},{1,17},{2,18},{3,19},{4,20},{5,21},{6,22},{7,23},{8,24},{9,... | collective-permute-start | bytes 294920 | tf_op jit(solution)/shard_map/ppermute | solution.py:394
  58.6 1.4 %collective-permute-start.10 = (f32[4,24,256]{2,1,0:T(8,128)S(1)}, f32[4,24,256]{2,1,0:T(8,128)S(1)}, u32[]{:S(2)}, u32[]{:S(2)}) collective-permute-start(f32[4,24,256]{2,1,0:T(8,128)S(1)} %get-tuple-element.56), channel_id=1, source_target_pairs={{0,17},{1,16},{2,19},{3,18},{4,21},{5,20},{6,23},{7,22},{8,25},{9,... | collective-permute-start | bytes 294920 | tf_op jit(solution)/shard_map/ppermute | solution.py:394
  60.0 1.6 %collective-permute-start.4 = (f32[56,256]{1,0:T(8,128)S(1)}, f32[56,256]{1,0:T(8,128)S(1)}, u32[]{:S(2)}, u32[]{:S(2)}) collective-permute-start(f32[56,256]{1,0:T(8,128)S(1)} %get-tuple-element.45), channel_id=1, source_target_pairs={{0,2},{1,3},{2,0},{3,1},{4,6},{5,7},{6,4},{7,5},{8,10},{9,11},{10,... | collective-permute-start | bytes 172040 | tf_op jit(solution)/shard_map/ppermute | solution.py:394
  61.6 2.6 %collective-permute-start.5 = (f32[56,256]{1,0:T(8,128)S(1)}, f32[56,256]{1,0:T(8,128)S(1)}, u32[]{:S(2)}, u32[]{:S(2)}) collective-permute-start(f32[56,256]{1,0:T(8,128)S(1)} %get-tuple-element.46), channel_id=1, source_target_pairs={{0,4},{1,5},{2,6},{3,7},{4,0},{5,1},{6,2},{7,3},{8,12},{9,13},{10,... | collective-permute-start | bytes 172040 | tf_op jit(solution)/shard_map/ppermute | solution.py:394
  64.2 1.3 %collective-permute-start.6 = (f32[56,256]{1,0:T(8,128)S(1)}, f32[56,256]{1,0:T(8,128)S(1)}, u32[]{:S(2)}, u32[]{:S(2)}) collective-permute-start(f32[56,256]{1,0:T(8,128)S(1)} %get-tuple-element.47), channel_id=1, source_target_pairs={{0,6},{1,7},{2,4},{3,5},{4,2},{5,3},{6,0},{7,1},{8,14},{9,15},{10,... | collective-permute-start | bytes 172040 | tf_op jit(solution)/shard_map/ppermute | solution.py:394
  65.5 0.6 plane_sum_b.1
  66.1 0.2 collective-permute-start.11
  66.3 2.9 %collective-permute-start.12 = (f32[24,256]{1,0:T(8,128)S(1)}, f32[24,256]{1,0:T(8,128)S(1)}, u32[]{:S(2)}, u32[]{:S(2)}) collective-permute-start(f32[24,256]{1,0:T(8,128)S(1)} %get-tuple-element.60), channel_id=1, source_target_pairs={{0,4},{1,5},{2,6},{3,7},{4,0},{5,1},{6,2},{7,3},{8,12},{9,13},{10,... | collective-permute-start | bytes 73736 | tf_op jit(solution)/shard_map/ppermute | solution.py:394
  69.2 1.3 %collective-permute-start.13 = (f32[24,256]{1,0:T(8,128)S(1)}, f32[24,256]{1,0:T(8,128)S(1)}, u32[]{:S(2)}, u32[]{:S(2)}) collective-permute-start(f32[24,256]{1,0:T(8,128)S(1)} %get-tuple-element.61), channel_id=1, source_target_pairs={{0,6},{1,7},{2,4},{3,5},{4,2},{5,3},{6,0},{7,1},{8,14},{9,15},{10,... | collective-permute-start | bytes 73736 | tf_op jit(solution)/shard_map/ppermute | solution.py:394
  70.5 0.6 collective-permute-done.12.refs_6_
  71.1 3.7 %collective-permute-done.13.refs_7_ = f32[24,256]{1,0:T(8,128)S(1)} collective-permute-done((f32[24,256]{1,0:T(8,128)S(1)}, f32[24,256]{1,0:T(8,128)S(1)}, u32[]{:S(2)}, u32[]{:S(2)}) %collective-permute-start.13) | collective-permute-done | bytes 24608 | tf_op jit(solution)/shard_map/ppermute | solution.py:394
  74.9 1.7 %stress_update.1 = (f32[6,8,225]{2,1,0:T(8,128)}, f32[2,3,1,256]{3,2,1,0:T(1,128)S(1)}) custom-call(f32[56,256]{1,0:T(8,128)S(1)} %get-tuple-element.44.refs_0_, f32[56,256]{1,0:T(8,128)S(1)} %collective-permute-done.4.refs_1_, f32[56,256]{1,0:T(8,128)S(1)} %collective-permute-done.5.refs_2_, f32[56,256]{1,0:T(8,128)S(1)} %collective-permute-done.6.refs_3_, ...), custom_call_target="tpu_custom_call" | custom-call | tf_op jit(solution)/shard_map/stress_update/pallas_call | solution.py:572
  76.6 3.1 %collective-permute-start.14 = (f32[3,1,256]{2,1,0:T(1,128)S(1)}, f32[3,1,256]{2,1,0:T(1,128)S(1)}, u32[]{:S(2)}, u32[]{:S(2)}) collective-permute-start(f32[3,1,256]{2,1,0:T(1,128)S(1)} %slice_bitcast_fusion), channel_id=1, source_target_pairs={{0,1},{1,2},{2,3},{3,4},{4,5},{5,6},{6,7},{8,9},{9,10},{10,11},{11... | collective-permute-start | bytes 9224 | tf_op jit(solution)/shard_map/ppermute | solution.py:49
  79.7 1.3 %collective-permute-done.14 = f32[3,1,256]{2,1,0:T(1,128)S(1)} collective-permute-done((f32[3,1,256]{2,1,0:T(1,128)S(1)}, f32[3,1,256]{2,1,0:T(1,128)S(1)}, u32[]{:S(2)}, u32[]{:S(2)}) %collective-permute-start.14) | collective-permute-done | bytes 3104 | tf_op jit(solution)/shard_map/ppermute | solution.py:49
  81.0 0.6 bitcast_add_fusion
  (27 shorter events, 0.2 us)
Async XLA Ops:
  0.6 0.8 %copy-start.1 = (f32[3,4096]{1,0:T(4,128)S(1)}, f32[3,4096]{1,0:T(4,128)}, u32[]{:S(2)}) copy-start(f32[3,4096]{1,0:T(4,128)} %euler_ref.1) | copy-start | bytes 147460
  2.4 1.5 %copy-start.6 = (s32[216,2048]{1,0:T(8,128)S(1)}, s32[216,2048]{1,0:T(8,128)}, u32[]{:S(2)}) copy-start(s32[216,2048]{1,0:T(8,128)} %ids_ref.3) | copy-start | bytes 5308420
  27.4 2.7 %collective-permute-start = (f32[16,56,256]{2,1,0:T(8,128)S(1)}, f32[16,56,256]{2,1,0:T(8,128)S(1)}, u32[]{:S(2)}, u32[]{:S(2)}) collective-permute-start(f32[16,56,256]{2,1,0:T(8,128)S(1)} %get-tuple-element.36), channel_id=1, source_target_pairs={{0,8},{8,0},{16,24},{24,16},{1,9},{9,1},{17,25},{25,17},{2,10},{10... | collective-permute-start | bytes 2752520 | tf_op jit(solution)/shard_map/ppermute | solution.py:250
  27.9 2.2 %copy-start.3 = (f32[3,1,256]{2,1,0:T(1,128)S(1)}, f32[3,1,256]{2,1,0:T(1,128)}, u32[]{:S(2)}) copy-start(f32[3,1,256]{2,1,0:T(1,128)} %refs_8_.1) | copy-start | bytes 9220
  30.1 1.5 %copy-start.7 = (s32[216,2048]{1,0:T(8,128)S(1)}, s32[216,2048]{1,0:T(8,128)}, u32[]{:S(2)}) copy-start(s32[216,2048]{1,0:T(8,128)} %ids_ref.3) | copy-start | bytes 5308420
  40.0 16.4 %collective-permute-start.7 = (f32[16,24,256]{2,1,0:T(8,128)S(1)}, f32[16,24,256]{2,1,0:T(8,128)S(1)}, u32[]{:S(2)}, u32[]{:S(2)}) collective-permute-start(f32[16,24,256]{2,1,0:T(8,128)S(1)} %get-tuple-element.51), channel_id=1, source_target_pairs={{0,8},{8,0},{16,24},{24,16},{1,9},{9,1},{17,25},{25,17},{2,10},{10... | collective-permute-start | bytes 1179656 | tf_op jit(solution)/shard_map/ppermute | solution.py:250
  40.1 9.3 %collective-permute-start.1 = (f32[4,56,256]{2,1,0:T(8,128)S(1)}, f32[4,56,256]{2,1,0:T(8,128)S(1)}, u32[]{:S(2)}, u32[]{:S(2)}) collective-permute-start(f32[4,56,256]{2,1,0:T(8,128)S(1)} %get-tuple-element.39), channel_id=1, source_target_pairs={{0,1},{1,0},{2,3},{3,2},{4,5},{5,4},{6,7},{7,6},{8,9},{9,8},{10,11... | collective-permute-start | bytes 688136 | tf_op jit(solution)/shard_map/ppermute | solution.py:394
  43.0 12.2 %collective-permute-start.2 = (f32[4,56,256]{2,1,0:T(8,128)S(1)}, f32[4,56,256]{2,1,0:T(8,128)S(1)}, u32[]{:S(2)}, u32[]{:S(2)}) collective-permute-start(f32[4,56,256]{2,1,0:T(8,128)S(1)} %get-tuple-element.40), channel_id=1, source_target_pairs={{0,16},{1,17},{2,18},{3,19},{4,20},{5,21},{6,22},{7,23},{8,24},{9,... | collective-permute-start | bytes 688136 | tf_op jit(solution)/shard_map/ppermute | solution.py:394
  44.5 10.7 %collective-permute-start.3 = (f32[4,56,256]{2,1,0:T(8,128)S(1)}, f32[4,56,256]{2,1,0:T(8,128)S(1)}, u32[]{:S(2)}, u32[]{:S(2)}) collective-permute-start(f32[4,56,256]{2,1,0:T(8,128)S(1)} %get-tuple-element.41), channel_id=1, source_target_pairs={{0,17},{1,16},{2,19},{3,18},{4,21},{5,20},{6,23},{7,22},{8,25},{9,... | collective-permute-start | bytes 688136 | tf_op jit(solution)/shard_map/ppermute | solution.py:394
  55.3 19.5 %copy-start = (f32[12,8,225]{2,1,0:T(8,128)S(1)}, f32[12,8,225]{2,1,0:T(8,128)}, u32[]{:S(2)}) copy-start(f32[12,8,225]{2,1,0:T(8,128)} %refs_10_.1) | copy-start | bytes 259204
  55.3 19.5 %copy-start.2 = (f32[6,8,225]{2,1,0:T(8,128)S(1)}, f32[6,8,225]{2,1,0:T(8,128)}, u32[]{:S(2)}) copy-start(f32[6,8,225]{2,1,0:T(8,128)} %refs_9_.1) | copy-start | bytes 129604
  55.4 19.5 %copy-start.4 = (f32[24,8]{1,0:T(8,128)S(1)}, f32[24,8]{1,0:T(8,128)}, u32[]{:S(2)}) copy-start(f32[24,8]{1,0:T(8,128)} %constant.8.clone.refs_12_) | copy-start | bytes 2308
  55.4 19.5 %copy-start.5 = (s32[8,225]{1,0:T(8,128)S(1)}, s32[8,225]{1,0:T(8,128)}, u32[]{:S(2)}) copy-start(s32[8,225]{1,0:T(8,128)} %refs_11_.1) | copy-start | bytes 21604
  56.5 7.7 %collective-permute-start.8 = (f32[4,24,256]{2,1,0:T(8,128)S(1)}, f32[4,24,256]{2,1,0:T(8,128)S(1)}, u32[]{:S(2)}, u32[]{:S(2)}) collective-permute-start(f32[4,24,256]{2,1,0:T(8,128)S(1)} %get-tuple-element.54), channel_id=1, source_target_pairs={{0,1},{1,0},{2,3},{3,2},{4,5},{5,4},{6,7},{7,6},{8,9},{9,8},{10,11... | collective-permute-start | bytes 294920 | tf_op jit(solution)/shard_map/ppermute | solution.py:394
  57.8 7.7 %collective-permute-start.9 = (f32[4,24,256]{2,1,0:T(8,128)S(1)}, f32[4,24,256]{2,1,0:T(8,128)S(1)}, u32[]{:S(2)}, u32[]{:S(2)}) collective-permute-start(f32[4,24,256]{2,1,0:T(8,128)S(1)} %get-tuple-element.55), channel_id=1, source_target_pairs={{0,16},{1,17},{2,18},{3,19},{4,20},{5,21},{6,22},{7,23},{8,24},{9,... | collective-permute-start | bytes 294920 | tf_op jit(solution)/shard_map/ppermute | solution.py:394
  58.6 6.9 %collective-permute-start.10 = (f32[4,24,256]{2,1,0:T(8,128)S(1)}, f32[4,24,256]{2,1,0:T(8,128)S(1)}, u32[]{:S(2)}, u32[]{:S(2)}) collective-permute-start(f32[4,24,256]{2,1,0:T(8,128)S(1)} %get-tuple-element.56), channel_id=1, source_target_pairs={{0,17},{1,16},{2,19},{3,18},{4,21},{5,20},{6,23},{7,22},{8,25},{9,... | collective-permute-start | bytes 294920 | tf_op jit(solution)/shard_map/ppermute | solution.py:394
  60.0 9.2 %collective-permute-start.4 = (f32[56,256]{1,0:T(8,128)S(1)}, f32[56,256]{1,0:T(8,128)S(1)}, u32[]{:S(2)}, u32[]{:S(2)}) collective-permute-start(f32[56,256]{1,0:T(8,128)S(1)} %get-tuple-element.45), channel_id=1, source_target_pairs={{0,2},{1,3},{2,0},{3,1},{4,6},{5,7},{6,4},{7,5},{8,10},{9,11},{10,... | collective-permute-start | bytes 172040 | tf_op jit(solution)/shard_map/ppermute | solution.py:394
  61.6 8.9 %collective-permute-start.5 = (f32[56,256]{1,0:T(8,128)S(1)}, f32[56,256]{1,0:T(8,128)S(1)}, u32[]{:S(2)}, u32[]{:S(2)}) collective-permute-start(f32[56,256]{1,0:T(8,128)S(1)} %get-tuple-element.46), channel_id=1, source_target_pairs={{0,4},{1,5},{2,6},{3,7},{4,0},{5,1},{6,2},{7,3},{8,12},{9,13},{10,... | collective-permute-start | bytes 172040 | tf_op jit(solution)/shard_map/ppermute | solution.py:394
  64.2 6.3 %collective-permute-start.6 = (f32[56,256]{1,0:T(8,128)S(1)}, f32[56,256]{1,0:T(8,128)S(1)}, u32[]{:S(2)}, u32[]{:S(2)}) collective-permute-start(f32[56,256]{1,0:T(8,128)S(1)} %get-tuple-element.47), channel_id=1, source_target_pairs={{0,6},{1,7},{2,4},{3,5},{4,2},{5,3},{6,0},{7,1},{8,14},{9,15},{10,... | collective-permute-start | bytes 172040 | tf_op jit(solution)/shard_map/ppermute | solution.py:394
  66.1 4.4 %collective-permute-start.11 = (f32[24,256]{1,0:T(8,128)S(1)}, f32[24,256]{1,0:T(8,128)S(1)}, u32[]{:S(2)}, u32[]{:S(2)}) collective-permute-start(f32[24,256]{1,0:T(8,128)S(1)} %get-tuple-element.59), channel_id=1, source_target_pairs={{0,2},{1,3},{2,0},{3,1},{4,6},{5,7},{6,4},{7,5},{8,10},{9,11},{10,... | collective-permute-start | bytes 73736 | tf_op jit(solution)/shard_map/ppermute | solution.py:394
  66.3 4.8 %collective-permute-start.12 = (f32[24,256]{1,0:T(8,128)S(1)}, f32[24,256]{1,0:T(8,128)S(1)}, u32[]{:S(2)}, u32[]{:S(2)}) collective-permute-start(f32[24,256]{1,0:T(8,128)S(1)} %get-tuple-element.60), channel_id=1, source_target_pairs={{0,4},{1,5},{2,6},{3,7},{4,0},{5,1},{6,2},{7,3},{8,12},{9,13},{10,... | collective-permute-start | bytes 73736 | tf_op jit(solution)/shard_map/ppermute | solution.py:394
  69.2 5.6 %collective-permute-start.13 = (f32[24,256]{1,0:T(8,128)S(1)}, f32[24,256]{1,0:T(8,128)S(1)}, u32[]{:S(2)}, u32[]{:S(2)}) collective-permute-start(f32[24,256]{1,0:T(8,128)S(1)} %get-tuple-element.61), channel_id=1, source_target_pairs={{0,6},{1,7},{2,4},{3,5},{4,2},{5,3},{6,0},{7,1},{8,14},{9,15},{10,... | collective-permute-start | bytes 73736 | tf_op jit(solution)/shard_map/ppermute | solution.py:394
  76.6 4.4 %collective-permute-start.14 = (f32[3,1,256]{2,1,0:T(1,128)S(1)}, f32[3,1,256]{2,1,0:T(1,128)S(1)}, u32[]{:S(2)}, u32[]{:S(2)}) collective-permute-start(f32[3,1,256]{2,1,0:T(1,128)S(1)} %slice_bitcast_fusion), channel_id=1, source_target_pairs={{0,1},{1,2},{2,3},{3,4},{4,5},{5,6},{6,7},{8,9},{9,10},{10,11},{11... | collective-permute-start | bytes 9224 | tf_op jit(solution)/shard_map/ppermute | solution.py:49

commit v9 on v8

--- a/solution.py
+++ b/solution.py
@@ -121,6 +121,7 @@
         table_kernel,
         out_shape=jax.ShapeDtypeStruct((height, 8, LANES), jnp.int32),
         compiler_params=pltpu.CompilerParams(vmem_limit_bytes=8 * 1024 * 1024),
+        cost_estimate=pl.CostEstimate(flops=10**6, bytes_accessed=10**7, transcendentals=0),
         name="rotation_table",
     )(euler_angles)
 
@@ -179,19 +180,21 @@
 
 
 def cell_sum_kernel(
-    first,
-    count,
+    octants,
+    per_octant,
     ids_ref,
     label_ref,
     table_ref,
     split_ref,
     out_ref,
     label_out_ref,
-    tile_ref,
-    place_ref,
-    masked_ref,
+    *refs,
 ):
-    per_octant = ids_ref.shape[0] // 8
+    first, count = octants
+    start = ids_ref.shape[0] - (8 - first) * per_octant
+    tile_ref, place_ref, masked_ref = refs[-3:]
+    if len(refs) > 3:
+        refs[0][...] = ids_ref[pl.ds(ids_ref.shape[0] - refs[0].shape[0], refs[0].shape[0]), :]
     table_rows = table_ref.shape[0] * 32 // sum(FIELDS)
     label_out_ref[...] = label_ref[...]
     groups = tile_ref.shape[0] // 8
@@ -202,7 +205,7 @@
         lanes = pl.ds(pl.multiple_of(tile * LANES, LANES), LANES)
         for octant in range(count):
             tile_ref[pl.ds(octant, per_octant, stride=count), :] = ids_ref[
-                pl.ds((first + octant) * per_octant, per_octant), lanes
+                pl.ds(start + octant * per_octant, per_octant), lanes
             ]
         sums = [[jnp.zeros((8, LANES), jnp.float32)] * 9 for turn in range(turns)]
         for group in range(groups):
@@ -295,25 +298,29 @@
     return place * (members // 2) + lax.shift_right_logical(owner_fe, 1)
 
 
-def cell_sums(first, count, grain_ids, labels, table, places):
-    bricks = grain_ids.shape[1]
-    tile_rows = -(-count * (grain_ids.shape[0] // 8) // 8) * 8
+def cell_sums(octants, per_octant, ids, labels, table, places):
+    first, count = octants
+    bricks = ids.shape[1]
     rows = padded_rows(count)
+    out_shape = [
+        jax.ShapeDtypeStruct((2 * rows, bricks), jnp.bfloat16),
+        jax.ShapeDtypeStruct((places, rows, COLUMNS), jnp.float32),
+        jax.ShapeDtypeStruct(labels.shape, jnp.int32),
+    ]
+    left = 8 - first - count
+    if left:
+        out_shape.append(jax.ShapeDtypeStruct((-(-left * per_octant // 8) * 8, bricks), jnp.int32))
     return pl.pallas_call(
-        functools.partial(cell_sum_kernel, first, count),
-        out_shape=[
-            jax.ShapeDtypeStruct((2 * rows, bricks), jnp.bfloat16),
-            jax.ShapeDtypeStruct((places, rows, COLUMNS), jnp.float32),
-            jax.ShapeDtypeStruct(labels.shape, jnp.int32),
-        ],
-        scratch_shapes=[pltpu.VMEM((tile_rows, LANES), jnp.int32)]
+        functools.partial(cell_sum_kernel, octants, per_octant),
+        out_shape=out_shape,
+        scratch_shapes=[pltpu.VMEM((-(-count * per_octant // 8) * 8, LANES), jnp.int32)]
         + brick_scratch(rows, bricks, places),
         compiler_params=pltpu.CompilerParams(vmem_limit_bytes=28 * 1024 * 1024),
         cost_estimate=pl.CostEstimate(
             flops=count * 4 * 10**9, bytes_accessed=count * 10**7, transcendentals=0
         ),
         name="cell_sums",
-    )(grain_ids, labels, table)
+    )(ids, labels, table)
 
 
 def padded_rows(count):
@@ -368,24 +375,27 @@
     return parts, labels
 
 
-def plane_sum_kernel(spare, sources, *refs):
-    for height, out_ref in enumerate(refs[sources + 1 : -1]):
+def plane_sum_kernel(spare, sources, passed, *refs):
+    outs = refs[sources + passed :]
+    for height, out_ref in enumerate(outs[: len(outs) - passed]):
         out_ref[...] = sum(ref[height] for ref in refs[:sources])
         if spare:
             rows = pl.ds(out_ref.shape[0] - spare, spare)
             out_ref[rows, :] = refs[1][height, rows, :]
-    refs[-1][...] = refs[sources][...]
-
-
-def plane_sum(parts, labels, spare, name):
+    for i in range(passed):
+        outs[len(outs) - passed + i][...] = refs[sources + i][...]
+
+
+def plane_sum(parts, passed, spare, name):
     part = jax.ShapeDtypeStruct(parts[0].shape[1:], jnp.float32)
-    *parts, labels = pl.pallas_call(
-        functools.partial(plane_sum_kernel, spare, len(parts)),
-        out_shape=[part] * parts[0].shape[0] + [jax.ShapeDtypeStruct(labels.shape, jnp.int32)],
+    out = pl.pallas_call(
+        functools.partial(plane_sum_kernel, spare, len(parts), len(passed)),
+        out_shape=[part] * parts[0].shape[0]
+        + [jax.ShapeDtypeStruct(array.shape, array.dtype) for array in passed],
         compiler_params=pltpu.CompilerParams(vmem_limit_bytes=16 * 1024 * 1024),
         name=name,
-    )(*parts, labels)
-    return parts, labels
+    )(*parts, *passed)
+    return out[: parts[0].shape[0]], *out[parts[0].shape[0] :]
 
 
 def to_relative(block, core, pair, last, rest):
@@ -595,16 +605,16 @@
     bricks = grain_ids.shape[1]
     owner = lax.optimization_barrier(brick_owner.reshape(bricks))
     labels = jnp.where(brick_active > 0, owner * COLUMNS + brick_element, -1).reshape(1, bricks)
-    (first_a, count_a), (first_b, count_b) = CHUNKS
+    per_octant = grain_ids.shape[0] // 8
     table = rotation_table(euler_angles)
-    split, send, labels = cell_sums(first_a, count_a, grain_ids, labels, table, half)
+    split, send, labels, ids = cell_sums(CHUNKS[0], per_octant, grain_ids, labels, table, half)
     keep, labels = brick_sums(split, labels, half)
     core_a, labels = core_sum(keep, across_cores(send), displacement, labels, 0, "core_sum_a")
-    split, send, labels = cell_sums(first_b, count_b, grain_ids, labels, table, half)
-    plane_a, labels = plane_sum(across_plane(core_a), labels, 0, "plane_sum_a")
+    split, send, labels = cell_sums(CHUNKS[1], per_octant, ids, labels, table, half)
+    plane_a, labels, send = plane_sum(across_plane(core_a), [labels, send], 0, "plane_sum_a")
     keep, labels = brick_sums(split, labels, half)
     core_b, labels = core_sum(keep, across_cores(send), displacement, labels, 3, "core_sum_b")
-    plane_b, labels = plane_sum(across_plane(core_b), labels, 3, "plane_sum_b")
+    (plane_b,) = plane_sum(across_plane(core_b), [], 3, "plane_sum_b")
     stress_new, nodal = element_update(
         across_height(plane_a),
         across_height(plane_b),

time: 81.9 us -> 72.8 us (0.89)
  waiting for transfers between devices: 16.4 us -> 9.28 us
  local copies, waits for them, and re-layouts: 3.67 us -> 2.34 us
    ppermute x12, waiting for transfers between devices: 15 us -> 7.35 us  [to_relative(): lax.ppermute(block, ('ca', 'fe'), [(i, i ^ flip) for i in range(groups *...]
    unnamed x16 -> x14, local copies, waits for them, and re-layouts: 3.66 us -> 2.34 us
  transfers between devices with their start and end apart: 15 -> 15, of which waited for: 5 -> 6; matrix products, arithmetic and copies ran while one was open for 0% -> 0% of each run, Pallas kernels for 5% -> 16%
where the time goes in v9:
time: 72.8 us; the launch traced here: 72.5 us
  Pallas kernels  37.9 us (52%)
  starting transfers between devices  20.9 us (29%)
  waiting for transfers between devices  9.28 us (13%)
  local copies, waits for them, and re-layouts  2.34 us (3%)
  other arithmetic  1.32 us (2%)
  between operations  0.79 us (1%)
    pallas_call x2, Pallas kernels, cell_sums(): pl.pallas_call(functools.partial(cell_sum_kernel, octants, per_octant), o...  31.9 us
    ppermute x12, starting transfers between devices, to_relative(): lax.ppermute(block, ('ca', 'fe'), [(i, i ^ flip) for i in range(groups *...  17.3 us
    ppermute x12, waiting for transfers between devices, to_relative(): lax.ppermute(block, ('ca', 'fe'), [(i, i ^ flip) for i in range(groups *...  7.35 us
    pallas_call x2, Pallas kernels, brick_sums(): pl.pallas_call(brick_sum_kernel, out_shape=[jax.ShapeDtypeStruct((places,...  3.16 us
    ppermute x1, starting transfers between devices, passed_along(): return lax.ppermute(block, axis, route)  3.07 us
    unnamed x14, local copies, waits for them, and re-layouts  2.34 us
    pallas_call x1, Pallas kernels, element_update(): pl.pallas_call(functools.partial(update_kernel, len(first)), out_shape=(j...  1.7 us
  transfers between devices with their start and end apart: 15, of which 6 were waited for; matrix products, arithmetic and copies ran while one was open for 0% of the time, Pallas kernels for 16%

profile of v9, /device:TPU:0, one launch (start us, length us, event | category | flops | bytes accessed | tf_op | source)
XLA Modules:
  0.0 72.5 jit_solution(13518288470269078602)
XLA Ops:
  0.6 0.8 %copy-done.1 = f32[3,4096]{1,0:T(4,128)S(1)} copy-done((f32[3,4096]{1,0:T(4,128)S(1)}, f32[3,4096]{1,0:T(4,128)}, u32[]{:S(2)}) %copy-start.1) | copy-done | bytes 49176
  1.5 0.2 rotation_table.1.table_ref
  1.7 0.7 %add_select_fusion = s32[2048]{0:T(1024)S(1)} fusion(s32[2048]{0:T(1024)} %param.14, s32[2048]{0:T(1024)} %bitcast.15, s32[2048]{0:T(1024)} %param.12), kind=kLoop, calls=%fused_computation | loop fusion | flops 8192 | bytes 32768 | tf_op jit(solution)/shard_map/jit(_where)/select_n | solution.py:607
  2.4 1.5 %copy-done.6 = s32[216,2048]{1,0:T(8,128)S(1)} copy-done((s32[216,2048]{1,0:T(8,128)S(1)}, s32[216,2048]{1,0:T(8,128)}, u32[]{:S(2)}) %copy-start.6) | copy-done | bytes 1769496
  3.9 23.5 %cell_sums.2 = (bf16[112,2048]{1,0:T(8,128)(2,1)S(1)}, f32[16,56,256]{2,1,0:T(8,128)S(1)}, s32[1,2048]{1,0:T(1,128)S(1)}, s32[56,2048]{1,0:T(8,128)S(1)}) custom-call(s32[216,2048]{1,0:T(8,128)S(1)} %copy-done.6, s32[1,2048]{1,0:T(1,128)S(1)} %bitcast.14, s32[51,8,128]{2,1,0:T(8,128)S(1)} %rotation_table.1.table_ref), custom_call_target="tpu_custom_call" | custom-call | flops 24000000000 | bytes 60000000 | tf_op jit(solution)/shard_map/cell_sums/pallas_call | solution.py:313
  27.4 0.5 collective-permute-start
  28.0 2.1 %brick_sums.2 = (f32[16,56,256]{2,1,0:T(8,128)S(1)}, s32[1,2048]{1,0:T(1,128)S(1)}) custom-call(bf16[112,2048]{1,0:T(8,128)(2,1)S(1)} %get-tuple-element.34.split_ref, s32[1,2048]{1,0:T(1,128)S(1)} %get-tuple-element.35.label_ref), custom_call_target="tpu_custom_call" | custom-call | flops 1680000000 | bytes 5600000 | tf_op jit(solution)/shard_map/brick_sums/pallas_call | solution.py:339
  30.1 0.1 core_sum_a.1
  30.3 2.8 %collective-permute-start.1 = (f32[4,56,256]{2,1,0:T(8,128)S(1)}, f32[4,56,256]{2,1,0:T(8,128)S(1)}, u32[]{:S(2)}, u32[]{:S(2)}) collective-permute-start(f32[4,56,256]{2,1,0:T(8,128)S(1)} %get-tuple-element.40), channel_id=1, source_target_pairs={{0,1},{1,0},{2,3},{3,2},{4,5},{5,4},{6,7},{7,6},{8,9},{9,8},{10,11... | collective-permute-start | bytes 688136 | tf_op jit(solution)/shard_map/ppermute | solution.py:404
  33.1 1.5 %collective-permute-start.2 = (f32[4,56,256]{2,1,0:T(8,128)S(1)}, f32[4,56,256]{2,1,0:T(8,128)S(1)}, u32[]{:S(2)}, u32[]{:S(2)}) collective-permute-start(f32[4,56,256]{2,1,0:T(8,128)S(1)} %get-tuple-element.41), channel_id=1, source_target_pairs={{0,16},{1,17},{2,18},{3,19},{4,20},{5,21},{6,22},{7,23},{8,24},{9,... | collective-permute-start | bytes 688136 | tf_op jit(solution)/shard_map/ppermute | solution.py:404
  34.6 8.4 %cell_sums.3 = (bf16[48,2048]{1,0:T(8,128)(2,1)S(1)}, f32[16,24,256]{2,1,0:T(8,128)S(1)}, s32[1,2048]{1,0:T(1,128)S(1)}) custom-call(s32[56,2048]{1,0:T(8,128)S(1)} %get-tuple-element.43.ids_ref, s32[1,2048]{1,0:T(1,128)S(1)} %get-tuple-element.44.label_ref, s32[51,8,128]{2,1,0:T(8,128)S(1)} %rotation_table.1.table_ref), custom_call_target="tpu_custom_call" | custom-call | flops 8000000000 | bytes 20000000 | tf_op jit(solution)/shard_map/cell_sums/pallas_call | solution.py:313
  43.0 2.4 %collective-permute-done.2.refs_2_ = f32[4,56,256]{2,1,0:T(8,128)S(1)} collective-permute-done((f32[4,56,256]{2,1,0:T(8,128)S(1)}, f32[4,56,256]{2,1,0:T(8,128)S(1)}, u32[]{:S(2)}, u32[]{:S(2)}) %collective-permute-start.2) | collective-permute-done | bytes 229408 | tf_op jit(solution)/shard_map/ppermute | solution.py:404
  45.5 0.1 plane_sum_a.1
  45.7 1.0 %brick_sums.3 = (f32[16,24,256]{2,1,0:T(8,128)S(1)}, s32[1,2048]{1,0:T(1,128)S(1)}) custom-call(bf16[48,2048]{1,0:T(8,128)(2,1)S(1)} %get-tuple-element.51.split_ref, s32[1,2048]{1,0:T(1,128)S(1)} %get-tuple-element.52.label_ref), custom_call_target="tpu_custom_call" | custom-call | flops 720000000 | bytes 2400000 | tf_op jit(solution)/shard_map/brick_sums/pallas_call | solution.py:339
  46.7 0.6 collective-permute-done.7
  47.3 0.7 core_sum_b.1
  48.0 1.2 %collective-permute-start.8 = (f32[4,24,256]{2,1,0:T(8,128)S(1)}, f32[4,24,256]{2,1,0:T(8,128)S(1)}, u32[]{:S(2)}, u32[]{:S(2)}) collective-permute-start(f32[4,24,256]{2,1,0:T(8,128)S(1)} %get-tuple-element.57), channel_id=1, source_target_pairs={{0,1},{1,0},{2,3},{3,2},{4,5},{5,4},{6,7},{7,6},{8,9},{9,8},{10,11... | collective-permute-start | bytes 294920 | tf_op jit(solution)/shard_map/ppermute | solution.py:404
  49.2 0.8 %collective-permute-start.9 = (f32[4,24,256]{2,1,0:T(8,128)S(1)}, f32[4,24,256]{2,1,0:T(8,128)S(1)}, u32[]{:S(2)}, u32[]{:S(2)}) collective-permute-start(f32[4,24,256]{2,1,0:T(8,128)S(1)} %get-tuple-element.58), channel_id=1, source_target_pairs={{0,16},{1,17},{2,18},{3,19},{4,20},{5,21},{6,22},{7,23},{8,24},{9,... | collective-permute-start | bytes 294920 | tf_op jit(solution)/shard_map/ppermute | solution.py:404
  50.0 1.4 %collective-permute-start.10 = (f32[4,24,256]{2,1,0:T(8,128)S(1)}, f32[4,24,256]{2,1,0:T(8,128)S(1)}, u32[]{:S(2)}, u32[]{:S(2)}) collective-permute-start(f32[4,24,256]{2,1,0:T(8,128)S(1)} %get-tuple-element.59), channel_id=1, source_target_pairs={{0,17},{1,16},{2,19},{3,18},{4,21},{5,20},{6,23},{7,22},{8,25},{9,... | collective-permute-start | bytes 294920 | tf_op jit(solution)/shard_map/ppermute | solution.py:404
  51.5 1.6 %collective-permute-start.4 = (f32[56,256]{1,0:T(8,128)S(1)}, f32[56,256]{1,0:T(8,128)S(1)}, u32[]{:S(2)}, u32[]{:S(2)}) collective-permute-start(f32[56,256]{1,0:T(8,128)S(1)} %get-tuple-element.48), channel_id=1, source_target_pairs={{0,2},{1,3},{2,0},{3,1},{4,6},{5,7},{6,4},{7,5},{8,10},{9,11},{10,... | collective-permute-start | bytes 172040 | tf_op jit(solution)/shard_map/ppermute | solution.py:404
  53.1 2.6 %collective-permute-start.5 = (f32[56,256]{1,0:T(8,128)S(1)}, f32[56,256]{1,0:T(8,128)S(1)}, u32[]{:S(2)}, u32[]{:S(2)}) collective-permute-start(f32[56,256]{1,0:T(8,128)S(1)} %get-tuple-element.49), channel_id=1, source_target_pairs={{0,4},{1,5},{2,6},{3,7},{4,0},{5,1},{6,2},{7,3},{8,12},{9,13},{10,... | collective-permute-start | bytes 172040 | tf_op jit(solution)/shard_map/ppermute | solution.py:404
  55.6 0.8 %collective-permute-start.6 = (f32[56,256]{1,0:T(8,128)S(1)}, f32[56,256]{1,0:T(8,128)S(1)}, u32[]{:S(2)}, u32[]{:S(2)}) collective-permute-start(f32[56,256]{1,0:T(8,128)S(1)} %get-tuple-element.50), channel_id=1, source_target_pairs={{0,6},{1,7},{2,4},{3,5},{4,2},{5,3},{6,0},{7,1},{8,14},{9,15},{10,... | collective-permute-start | bytes 172040 | tf_op jit(solution)/shard_map/ppermute | solution.py:404
  56.5 1.2 %collective-permute-start.11 = (f32[24,256]{1,0:T(8,128)S(1)}, f32[24,256]{1,0:T(8,128)S(1)}, u32[]{:S(2)}, u32[]{:S(2)}) collective-permute-start(f32[24,256]{1,0:T(8,128)S(1)} %get-tuple-element.61), channel_id=1, source_target_pairs={{0,2},{1,3},{2,0},{3,1},{4,6},{5,7},{6,4},{7,5},{8,10},{9,11},{10,... | collective-permute-start | bytes 73736 | tf_op jit(solution)/shard_map/ppermute | solution.py:404
  57.6 2.6 %collective-permute-start.12 = (f32[24,256]{1,0:T(8,128)S(1)}, f32[24,256]{1,0:T(8,128)S(1)}, u32[]{:S(2)}, u32[]{:S(2)}) collective-permute-start(f32[24,256]{1,0:T(8,128)S(1)} %get-tuple-element.62), channel_id=1, source_target_pairs={{0,4},{1,5},{2,6},{3,7},{4,0},{5,1},{6,2},{7,3},{8,12},{9,13},{10,... | collective-permute-start | bytes 73736 | tf_op jit(solution)/shard_map/ppermute | solution.py:404
  60.2 0.7 collective-permute-start.13
  60.9 0.7 collective-permute-done.6.refs_3_
  61.6 0.7 collective-permute-done.12.refs_6_
  62.3 3.5 %collective-permute-done.13.refs_7_ = f32[24,256]{1,0:T(8,128)S(1)} collective-permute-done((f32[24,256]{1,0:T(8,128)S(1)}, f32[24,256]{1,0:T(8,128)S(1)}, u32[]{:S(2)}, u32[]{:S(2)}) %collective-permute-start.13) | collective-permute-done | bytes 24608 | tf_op jit(solution)/shard_map/ppermute | solution.py:404
  65.9 1.7 %stress_update.1 = (f32[6,8,225]{2,1,0:T(8,128)}, f32[2,3,1,256]{3,2,1,0:T(1,128)S(1)}) custom-call(f32[56,256]{1,0:T(8,128)S(1)} %get-tuple-element.47.refs_0_, f32[56,256]{1,0:T(8,128)S(1)} %collective-permute-done.4.refs_1_, f32[56,256]{1,0:T(8,128)S(1)} %collective-permute-done.5.refs_2_, f32[56,256]{1,0:T(8,128)S(1)} %collective-permute-done.6.refs_3_, ...), custom_call_target="tpu_custom_call" | custom-call | tf_op jit(solution)/shard_map/stress_update/pallas_call | solution.py:582
  67.6 3.1 %collective-permute-start.14 = (f32[3,1,256]{2,1,0:T(1,128)S(1)}, f32[3,1,256]{2,1,0:T(1,128)S(1)}, u32[]{:S(2)}, u32[]{:S(2)}) collective-permute-start(f32[3,1,256]{2,1,0:T(1,128)S(1)} %slice_bitcast_fusion), channel_id=1, source_target_pairs={{0,1},{1,2},{2,3},{3,4},{4,5},{5,6},{6,7},{8,9},{9,10},{10,11},{11... | collective-permute-start | bytes 9224 | tf_op jit(solution)/shard_map/ppermute | solution.py:49
  70.6 1.3 %collective-permute-done.14 = f32[3,1,256]{2,1,0:T(1,128)S(1)} collective-permute-done((f32[3,1,256]{2,1,0:T(1,128)S(1)}, f32[3,1,256]{2,1,0:T(1,128)S(1)}, u32[]{:S(2)}, u32[]{:S(2)}) %collective-permute-start.14) | collective-permute-done | bytes 3104 | tf_op jit(solution)/shard_map/ppermute | solution.py:49
  71.9 0.6 bitcast_add_fusion
  (25 shorter events, 0.2 us)
Async XLA Ops:
  0.6 0.8 %copy-start.1 = (f32[3,4096]{1,0:T(4,128)S(1)}, f32[3,4096]{1,0:T(4,128)}, u32[]{:S(2)}) copy-start(f32[3,4096]{1,0:T(4,128)} %euler_ref.1) | copy-start | bytes 147460
  2.4 1.5 %copy-start.6 = (s32[216,2048]{1,0:T(8,128)S(1)}, s32[216,2048]{1,0:T(8,128)}, u32[]{:S(2)}) copy-start(s32[216,2048]{1,0:T(8,128)} %ids_ref.1) | copy-start | bytes 5308420
  27.4 2.7 %collective-permute-start = (f32[16,56,256]{2,1,0:T(8,128)S(1)}, f32[16,56,256]{2,1,0:T(8,128)S(1)}, u32[]{:S(2)}, u32[]{:S(2)}) collective-permute-start(f32[16,56,256]{2,1,0:T(8,128)S(1)} %get-tuple-element.37), channel_id=1, source_target_pairs={{0,8},{8,0},{16,24},{24,16},{1,9},{9,1},{17,25},{25,17},{2,10},{10... | collective-permute-start | bytes 2752520 | tf_op jit(solution)/shard_map/ppermute | solution.py:253
  28.0 2.2 %copy-start.3 = (f32[3,1,256]{2,1,0:T(1,128)S(1)}, f32[3,1,256]{2,1,0:T(1,128)}, u32[]{:S(2)}) copy-start(f32[3,1,256]{2,1,0:T(1,128)} %refs_8_.1) | copy-start | bytes 9220
  30.3 12.8 %collective-permute-start.1 = (f32[4,56,256]{2,1,0:T(8,128)S(1)}, f32[4,56,256]{2,1,0:T(8,128)S(1)}, u32[]{:S(2)}, u32[]{:S(2)}) collective-permute-start(f32[4,56,256]{2,1,0:T(8,128)S(1)} %get-tuple-element.40), channel_id=1, source_target_pairs={{0,1},{1,0},{2,3},{3,2},{4,5},{5,4},{6,7},{7,6},{8,9},{9,8},{10,11... | collective-permute-start | bytes 688136 | tf_op jit(solution)/shard_map/ppermute | solution.py:404
  33.1 12.4 %collective-permute-start.2 = (f32[4,56,256]{2,1,0:T(8,128)S(1)}, f32[4,56,256]{2,1,0:T(8,128)S(1)}, u32[]{:S(2)}, u32[]{:S(2)}) collective-permute-start(f32[4,56,256]{2,1,0:T(8,128)S(1)} %get-tuple-element.41), channel_id=1, source_target_pairs={{0,16},{1,17},{2,18},{3,19},{4,20},{5,21},{6,22},{7,23},{8,24},{9,... | collective-permute-start | bytes 688136 | tf_op jit(solution)/shard_map/ppermute | solution.py:404
  34.6 10.8 %collective-permute-start.3 = (f32[4,56,256]{2,1,0:T(8,128)S(1)}, f32[4,56,256]{2,1,0:T(8,128)S(1)}, u32[]{:S(2)}, u32[]{:S(2)}) collective-permute-start(f32[4,56,256]{2,1,0:T(8,128)S(1)} %get-tuple-element.42), channel_id=1, source_target_pairs={{0,17},{1,16},{2,19},{3,18},{4,21},{5,20},{6,23},{7,22},{8,25},{9,... | collective-permute-start | bytes 688136 | tf_op jit(solution)/shard_map/ppermute | solution.py:404
  45.5 1.8 %collective-permute-start.7 = (f32[16,24,256]{2,1,0:T(8,128)S(1)}, f32[16,24,256]{2,1,0:T(8,128)S(1)}, u32[]{:S(2)}, u32[]{:S(2)}) collective-permute-start(f32[16,24,256]{2,1,0:T(8,128)S(1)} %get-tuple-element.54), channel_id=1, source_target_pairs={{0,8},{8,0},{16,24},{24,16},{1,9},{9,1},{17,25},{25,17},{2,10},{10... | collective-permute-start | bytes 1179656 | tf_op jit(solution)/shard_map/ppermute | solution.py:253
  45.6 20.2 %copy-start = (f32[12,8,225]{2,1,0:T(8,128)S(1)}, f32[12,8,225]{2,1,0:T(8,128)}, u32[]{:S(2)}) copy-start(f32[12,8,225]{2,1,0:T(8,128)} %refs_10_.1) | copy-start | bytes 259204
  45.6 20.2 %copy-start.2 = (f32[6,8,225]{2,1,0:T(8,128)S(1)}, f32[6,8,225]{2,1,0:T(8,128)}, u32[]{:S(2)}) copy-start(f32[6,8,225]{2,1,0:T(8,128)} %refs_9_.1) | copy-start | bytes 129604
  45.6 20.2 %copy-start.4 = (f32[24,8]{1,0:T(8,128)S(1)}, f32[24,8]{1,0:T(8,128)}, u32[]{:S(2)}) copy-start(f32[24,8]{1,0:T(8,128)} %constant.8.clone.refs_12_) | copy-start | bytes 2308
  45.7 20.2 %copy-start.5 = (s32[8,225]{1,0:T(8,128)S(1)}, s32[8,225]{1,0:T(8,128)}, u32[]{:S(2)}) copy-start(s32[8,225]{1,0:T(8,128)} %refs_11_.1) | copy-start | bytes 21604
  48.0 7.7 %collective-permute-start.8 = (f32[4,24,256]{2,1,0:T(8,128)S(1)}, f32[4,24,256]{2,1,0:T(8,128)S(1)}, u32[]{:S(2)}, u32[]{:S(2)}) collective-permute-start(f32[4,24,256]{2,1,0:T(8,128)S(1)} %get-tuple-element.57), channel_id=1, source_target_pairs={{0,1},{1,0},{2,3},{3,2},{4,5},{5,4},{6,7},{7,6},{8,9},{9,8},{10,11... | collective-permute-start | bytes 294920 | tf_op jit(solution)/shard_map/ppermute | solution.py:404
  49.2 7.2 %collective-permute-start.9 = (f32[4,24,256]{2,1,0:T(8,128)S(1)}, f32[4,24,256]{2,1,0:T(8,128)S(1)}, u32[]{:S(2)}, u32[]{:S(2)}) collective-permute-start(f32[4,24,256]{2,1,0:T(8,128)S(1)} %get-tuple-element.58), channel_id=1, source_target_pairs={{0,16},{1,17},{2,18},{3,19},{4,20},{5,21},{6,22},{7,23},{8,24},{9,... | collective-permute-start | bytes 294920 | tf_op jit(solution)/shard_map/ppermute | solution.py:404
  50.0 6.4 %collective-permute-start.10 = (f32[4,24,256]{2,1,0:T(8,128)S(1)}, f32[4,24,256]{2,1,0:T(8,128)S(1)}, u32[]{:S(2)}, u32[]{:S(2)}) collective-permute-start(f32[4,24,256]{2,1,0:T(8,128)S(1)} %get-tuple-element.59), channel_id=1, source_target_pairs={{0,17},{1,16},{2,19},{3,18},{4,21},{5,20},{6,23},{7,22},{8,25},{9,... | collective-permute-start | bytes 294920 | tf_op jit(solution)/shard_map/ppermute | solution.py:404
  51.5 8.7 %collective-permute-start.4 = (f32[56,256]{1,0:T(8,128)S(1)}, f32[56,256]{1,0:T(8,128)S(1)}, u32[]{:S(2)}, u32[]{:S(2)}) collective-permute-start(f32[56,256]{1,0:T(8,128)S(1)} %get-tuple-element.48), channel_id=1, source_target_pairs={{0,2},{1,3},{2,0},{3,1},{4,6},{5,7},{6,4},{7,5},{8,10},{9,11},{10,... | collective-permute-start | bytes 172040 | tf_op jit(solution)/shard_map/ppermute | solution.py:404
  53.1 7.9 %collective-permute-start.5 = (f32[56,256]{1,0:T(8,128)S(1)}, f32[56,256]{1,0:T(8,128)S(1)}, u32[]{:S(2)}, u32[]{:S(2)}) collective-permute-start(f32[56,256]{1,0:T(8,128)S(1)} %get-tuple-element.49), channel_id=1, source_target_pairs={{0,4},{1,5},{2,6},{3,7},{4,0},{5,1},{6,2},{7,3},{8,12},{9,13},{10,... | collective-permute-start | bytes 172040 | tf_op jit(solution)/shard_map/ppermute | solution.py:404
  55.6 6.0 %collective-permute-start.6 = (f32[56,256]{1,0:T(8,128)S(1)}, f32[56,256]{1,0:T(8,128)S(1)}, u32[]{:S(2)}, u32[]{:S(2)}) collective-permute-start(f32[56,256]{1,0:T(8,128)S(1)} %get-tuple-element.50), channel_id=1, source_target_pairs={{0,6},{1,7},{2,4},{3,5},{4,2},{5,3},{6,0},{7,1},{8,14},{9,15},{10,... | collective-permute-start | bytes 172040 | tf_op jit(solution)/shard_map/ppermute | solution.py:404
  56.5 5.2 %collective-permute-start.11 = (f32[24,256]{1,0:T(8,128)S(1)}, f32[24,256]{1,0:T(8,128)S(1)}, u32[]{:S(2)}, u32[]{:S(2)}) collective-permute-start(f32[24,256]{1,0:T(8,128)S(1)} %get-tuple-element.61), channel_id=1, source_target_pairs={{0,2},{1,3},{2,0},{3,1},{4,6},{5,7},{6,4},{7,5},{8,10},{9,11},{10,... | collective-permute-start | bytes 73736 | tf_op jit(solution)/shard_map/ppermute | solution.py:404
  57.6 4.7 %collective-permute-start.12 = (f32[24,256]{1,0:T(8,128)S(1)}, f32[24,256]{1,0:T(8,128)S(1)}, u32[]{:S(2)}, u32[]{:S(2)}) collective-permute-start(f32[24,256]{1,0:T(8,128)S(1)} %get-tuple-element.62), channel_id=1, source_target_pairs={{0,4},{1,5},{2,6},{3,7},{4,0},{5,1},{6,2},{7,3},{8,12},{9,13},{10,... | collective-permute-start | bytes 73736 | tf_op jit(solution)/shard_map/ppermute | solution.py:404
  60.2 5.6 %collective-permute-start.13 = (f32[24,256]{1,0:T(8,128)S(1)}, f32[24,256]{1,0:T(8,128)S(1)}, u32[]{:S(2)}, u32[]{:S(2)}) collective-permute-start(f32[24,256]{1,0:T(8,128)S(1)} %get-tuple-element.63), channel_id=1, source_target_pairs={{0,6},{1,7},{2,4},{3,5},{4,2},{5,3},{6,0},{7,1},{8,14},{9,15},{10,... | collective-permute-start | bytes 73736 | tf_op jit(solution)/shard_map/ppermute | solution.py:404
  67.6 4.4 %collective-permute-start.14 = (f32[3,1,256]{2,1,0:T(1,128)S(1)}, f32[3,1,256]{2,1,0:T(1,128)S(1)}, u32[]{:S(2)}, u32[]{:S(2)}) collective-permute-start(f32[3,1,256]{2,1,0:T(1,128)S(1)} %slice_bitcast_fusion), channel_id=1, source_target_pairs={{0,1},{1,2},{2,3},{3,4},{4,5},{5,6},{6,7},{8,9},{9,10},{10,11},{11... | collective-permute-start | bytes 9224 | tf_op jit(solution)/shard_map/ppermute | solution.py:49

commit v10 on v9

--- a/solution.py
+++ b/solution.py
@@ -13,8 +13,7 @@
 LANES = 128
 COLUMNS = 256
 CHUNKS = ((0, 6), (6, 2))
-FIELDS = (32, 16, 2, 1)
-QUANTUM = float((1 << 16) - 1)
+QUANTUM = float((1 << 15) - 1)
 
 SLIP_PLANES = [
     [value / math.sqrt(3.0) for value in row]
@@ -93,30 +92,23 @@
     x, y, z = [
         jnp.clip(jnp.round(value), -QUANTUM, QUANTUM).astype(jnp.int32) for value in (x, y, z)
     ]
-    return [
-        lax.shift_left(x, 15) | (lax.shift_right_arithmetic(y, 2) & 0x7FFF),
-        lax.shift_left(y & 0x3, 14) | (lax.shift_right_arithmetic(z, 3) & 0x3FFF),
-        lax.shift_right_arithmetic(z, 1) & 0x3,
-        z & 0x1,
-    ]
+    return [lax.shift_left(x, 16) | (y & 0xFFFF), z & 0xFFFF]
 
 
 def table_kernel(euler_ref, table_ref):
-    at = 0
-    for field, width in zip(rotation_words(euler_ref[...]), FIELDS):
-        rows = field.shape[1] // LANES
-        shared = 32 // width
-        for first in range(0, rows, shared):
-            word = field[:, first * LANES : (first + 1) * LANES]
-            for other in range(1, shared):
-                row = field[:, (first + other) * LANES : (first + other + 1) * LANES]
-                word = word | lax.shift_left(row, other * width)
-            table_ref[at] = jnp.broadcast_to(word, (8, LANES))
-            at += 1
+    both, third = rotation_words(euler_ref[...])
+    rows = both.shape[1] // LANES
+    for row in range(rows):
+        table_ref[row] = jnp.broadcast_to(both[:, row * LANES : (row + 1) * LANES], (8, LANES))
+    for row in range(0, rows, 2):
+        word = third[:, row * LANES : (row + 1) * LANES] | lax.shift_left(
+            third[:, (row + 1) * LANES : (row + 2) * LANES], 16
+        )
+        table_ref[rows + row // 2] = jnp.broadcast_to(word, (8, LANES))
 
 
 def rotation_table(euler_angles):
-    height = euler_angles.shape[1] // LANES * sum(FIELDS) // 32
+    height = euler_angles.shape[1] // LANES * 3 // 2
     return pl.pallas_call(
         table_kernel,
         out_shape=jax.ShapeDtypeStruct((height, 8, LANES), jnp.int32),
@@ -152,31 +144,34 @@
     lane = (ids & (LANES - 1))[:, :, None]
     row = lax.shift_right_logical(ids, 7)
     bits = [(row & (1 << level)) != 0 for level in range(table_rows.bit_length() - 1)]
-    fields = []
-    at = 0
-    for width in FIELDS:
-        shared = 32 // width
-        skipped = shared.bit_length() - 1
-        rows = table_rows // shared
-        field = looked_up(table_ref, at, rows, lane, bits[skipped:])
-        if shared > 1:
-            field = lax.shift_right_logical(field, (row & (shared - 1)) * width)
-        fields.append(field)
-        at += rows
-    first, second, third, fourth = fields
-    x = lax.shift_right_arithmetic(first, 15).astype(jnp.float32)
-    y = lax.shift_right_arithmetic(lax.shift_left(first, 17), 15) | (
-        lax.shift_right_logical(second, 14) & 0x3
-    )
-    z = lax.shift_right_arithmetic(lax.shift_left(second, 18), 15) | (
-        lax.shift_left(third & 0x3, 1) | (fourth & 0x1)
-    )
-    y, z = y.astype(jnp.float32), z.astype(jnp.float32)
+    both = looked_up(table_ref, 0, table_rows, lane, bits)
+    third = looked_up(table_ref, table_rows, table_rows // 2, lane, bits[1:])
+    third = lax.shift_left(third, lax.shift_left((row & 1) ^ 1, 4))
+    x = lax.shift_right_arithmetic(both, 16).astype(jnp.float32)
+    y = lax.shift_right_arithmetic(lax.shift_left(both, 16), 16).astype(jnp.float32)
+    z = lax.shift_right_arithmetic(third, 16).astype(jnp.float32)
     square = x * x + y * y + z * z
     scale = 2.0 / (1.0 + square * (1.0 / (QUANTUM * QUANTUM)))
     w = scale - 1.0
     x, y, z = x * scale, y * scale, z * scale
     return [x * x, y * y, z * z, x * y, x * z, y * z, w * x, w * y, w * z]
+
+
+ENTRIES = (
+    ((1, -1.0), (2, -1.0)),
+    ((3, 1.0), (8, -1.0)),
+    ((4, 1.0), (7, 1.0)),
+    ((3, 1.0), (8, 1.0)),
+    ((0, -1.0), (2, -1.0)),
+    ((5, 1.0), (6, -1.0)),
+    ((4, 1.0), (7, -1.0)),
+    ((5, 1.0), (6, 1.0)),
+    ((0, -1.0), (1, -1.0)),
+)
+
+
+def remainder(value, divisor):
+    return value - value // divisor * divisor
 
 
 def cell_sum_kernel(
@@ -192,60 +187,116 @@
 ):
     first, count = octants
     start = ids_ref.shape[0] - (8 - first) * per_octant
-    tile_ref, place_ref, masked_ref = refs[-3:]
-    if len(refs) > 3:
+    tile_ref, raw_ref, place_ref, masked_ref = refs[-4:]
+    if len(refs) > 4:
         refs[0][...] = ids_ref[pl.ds(ids_ref.shape[0] - refs[0].shape[0], refs[0].shape[0]), :]
-    table_rows = table_ref.shape[0] * 32 // sum(FIELDS)
+    table_rows = table_ref.shape[0] * 2 // 3
     label_out_ref[...] = label_ref[...]
-    groups = tile_ref.shape[0] // 8
+    groups = tile_ref.shape[1] // 8
     rows_left = count * per_octant - 8 * (groups - 1)
     turns = count // math.gcd(count, 8)
-
-    def tile_sums(tile, carry):
-        lanes = pl.ds(pl.multiple_of(tile * LANES, LANES), LANES)
-        for octant in range(count):
-            tile_ref[pl.ds(octant, per_octant, stride=count), :] = ids_ref[
-                pl.ds(start + octant * per_octant, per_octant), lanes
-            ]
-        sums = [[jnp.zeros((8, LANES), jnp.float32)] * 9 for turn in range(turns)]
-        for group in range(groups):
-            ids = tile_ref[pl.ds(8 * group, 8), :]
-            products = rotation_products(table_ref, table_rows, ids)
-            if group == groups - 1 and rows_left < 8:
-                there = lax.broadcasted_iota(jnp.int32, (8, LANES), 0) < rows_left
-                products = [jnp.where(there, product, 0.0) for product in products]
-            sums[group % turns] = [
-                total + product for total, product in zip(sums[group % turns], products)
-            ]
-        sums = [jnp.concatenate(turned, axis=0) for turned in zip(*sums)]
-        sums = [
-            sum(total[count * part : count * (part + 1)] for part in range(8 * turns // count))
-            for total in sums
-        ]
-        vector = 2.0 / (QUANTUM * QUANTUM)
-        xx, yy, zz, xy, xz, yz = [value * vector for value in sums[:6]]
-        wx, wy, wz = [value * (2.0 / QUANTUM) for value in sums[6:]]
-        entries = [
-            per_octant - (yy + zz),
-            xy - wz,
-            xz + wy,
-            xy + wz,
-            per_octant - (xx + zz),
-            yz - wx,
-            xz - wy,
-            yz + wx,
-            per_octant - (xx + yy),
-            jnp.ones((split_ref.shape[0] // 2 - 9 * count, LANES), jnp.float32),
-        ]
-        stacked = jnp.concatenate(entries, axis=0)
-        leading = stacked.astype(jnp.bfloat16).astype(jnp.float32)
-        split_ref[:, lanes] = jnp.concatenate([leading, stacked - leading], axis=0).astype(
+    rows = out_ref.shape[1]
+    width = masked_ref.shape[1]
+    pairs = ids_ref.shape[1] // width
+
+    out_row = lax.broadcasted_iota(jnp.int32, (rows, raw_ref.shape[0]), 0)
+    raw_row = lax.broadcasted_iota(jnp.int32, (rows, raw_ref.shape[0]), 1)
+    entry, product = out_row // count, raw_row // (8 * turns)
+    fold = jnp.zeros(out_row.shape, jnp.float32)
+    for index, terms in enumerate(ENTRIES):
+        for other, sign in terms:
+            fold = jnp.where((entry == index) & (product == other), sign, fold)
+    fold = jnp.where(remainder(out_row, count) == remainder(raw_row, count), fold, 0.0)
+    fold = fold.astype(jnp.bfloat16)
+    row = lax.broadcasted_iota(jnp.int32, (rows, width), 0)
+    diagonal = (row // count == 0) | (row // count == 4) | (row // count == 8)
+    constant = jnp.where(diagonal, float(per_octant), jnp.where(row < 9 * count, 0.0, 1.0))
+
+    def lanes_of(pair):
+        return pl.ds(pl.multiple_of(pair * width, width), width)
+
+    def look_up(pair):
+        for tile in range(width // LANES):
+            lanes = pl.ds(pl.multiple_of(pair * width + tile * LANES, LANES), LANES)
+            for octant in range(count):
+                tile_ref[tile, pl.ds(octant, per_octant, stride=count), :] = ids_ref[
+                    pl.ds(start + octant * per_octant, per_octant), lanes
+                ]
+            sums = [[jnp.zeros((8, LANES), jnp.float32)] * 9 for turn in range(turns)]
+            for group in range(groups):
+                ids = tile_ref[tile, pl.ds(8 * group, 8), :]
+                products = rotation_products(table_ref, table_rows, ids)
+                if group == groups - 1 and rows_left < 8:
+                    there = lax.broadcasted_iota(jnp.int32, (8, LANES), 0) < rows_left
+                    products = [jnp.where(there, value, 0.0) for value in products]
+                sums[group % turns] = [
+                    total + value for total, value in zip(sums[group % turns], products)
+                ]
+            scales = [2.0 / (QUANTUM * QUANTUM)] * 6 + [2.0 / QUANTUM] * 3
+            raw_ref[:, lanes] = jnp.concatenate(
+                [sums[turn][index] * scales[index] for index in range(9) for turn in range(turns)],
+                axis=0,
+            )
+
+    def fold_entries(pair):
+        lanes = lanes_of(pair)
+        total = constant
+        for part in three_parts(raw_ref[:, lanes]):
+            total = total + jnp.dot(fold, part, preferred_element_type=jnp.float32)
+        leading = total.astype(jnp.bfloat16).astype(jnp.float32)
+        split_ref[:, lanes] = jnp.concatenate([leading, total - leading], axis=0).astype(
             jnp.bfloat16
         )
+
+    def add_bricks(pair, counted):
+        lanes = lanes_of(pair)
+        column = lax.broadcasted_iota(jnp.int32, (COLUMNS, width), 0)
+        chosen = (column == label_ref[:, lanes] & (COLUMNS - 1)).astype(jnp.bfloat16)
+        place = jnp.where(counted, place_ref[:, lanes], -1)
+        add_places(split_ref, lanes, place, chosen, out_ref, masked_ref)
+
+    place_ref[...] = relative_places(label_ref[...], out_ref.shape[0])
+    out_ref[...] = jnp.zeros(out_ref.shape, jnp.float32)
+    raw_ref[:, pl.ds(0, width)] = jnp.zeros((raw_ref.shape[0], width), jnp.float32)
+    split_ref[:, pl.ds(0, width)] = jnp.zeros((split_ref.shape[0], width), jnp.bfloat16)
+
+    def step(pair, carry):
+        add_bricks(jnp.maximum(pair - 2, 0), pair >= 2)
+        fold_entries(jnp.maximum(pair - 1, 0))
+        look_up(pair)
         return carry
 
-    lax.fori_loop(0, ids_ref.shape[1] // LANES, tile_sums, 0, unroll=2)
-    sum_bricks(out_ref.shape[0], split_ref, label_ref, out_ref, place_ref, masked_ref)
+    lax.fori_loop(0, pairs, step, 0)
+    add_bricks(pairs - 2, True)
+    fold_entries(pairs - 1)
+    add_bricks(pairs - 1, True)
+
+
+def relative_places(labels, base):
+    place = place_of(lax.shift_right_arithmetic(labels, COLUMNS.bit_length() - 1))
+    return jnp.where(labels < 0, -1, place - base)
+
+
+def add_places(split_ref, lanes, place, chosen, out_ref, masked_ref):
+    split_rows = split_ref.shape[0]
+    half_rows = split_rows // 2
+    members = masked_ref.shape[0] // split_rows
+    for first in range(0, out_ref.shape[0], members):
+        split = split_ref[:, lanes]
+        for member in range(members):
+            mask = (place == first + member).astype(jnp.bfloat16)
+            masked_ref[pl.ds(member * split_rows, split_rows), :] = split * mask
+        product = lax.dot_general(
+            masked_ref[...],
+            chosen,
+            (((1,), (1,)), ((), ())),
+            preferred_element_type=jnp.float32,
+        )
+        for member in range(members):
+            at = member * split_rows
+            out_ref[first + member] += (
+                product[at : at + half_rows] + product[at + half_rows : at + split_rows]
+            )
 
 
 def across_cores(block):
@@ -254,15 +305,10 @@
 
 
 def brick_sum_kernel(split_ref, label_ref, out_ref, label_out_ref, place_ref, masked_ref):
-    label_out_ref[...] = label_ref[...]
-    sum_bricks(0, split_ref, label_ref, out_ref, place_ref, masked_ref)
-
-
-def sum_bricks(base, split_ref, label_ref, out_ref, place_ref, masked_ref):
+    labels = label_ref[...]
+    label_out_ref[...] = labels
+    place_ref[...] = relative_places(labels, 0)
     bricks = split_ref.shape[1]
-    labels = label_ref[...]
-    place = place_of(lax.shift_right_arithmetic(labels, COLUMNS.bit_length() - 1))
-    place_ref[...] = jnp.where(labels < 0, -1, place - base)
     column = lax.broadcasted_iota(jnp.int32, (COLUMNS, bricks), 0)
     chosen = (column == labels & (COLUMNS - 1)).astype(jnp.bfloat16)
     split_rows = split_ref.shape[0]
@@ -313,8 +359,11 @@
     return pl.pallas_call(
         functools.partial(cell_sum_kernel, octants, per_octant),
         out_shape=out_shape,
-        scratch_shapes=[pltpu.VMEM((-(-count * per_octant // 8) * 8, LANES), jnp.int32)]
-        + brick_scratch(rows, bricks, places),
+        scratch_shapes=[
+            pltpu.VMEM((2, -(-count * per_octant // 8) * 8, LANES), jnp.int32),
+            pltpu.VMEM((72 * (count // math.gcd(count, 8)), bricks), jnp.float32),
+        ]
+        + brick_scratch(rows, bricks, places, 2 * LANES),
         compiler_params=pltpu.CompilerParams(vmem_limit_bytes=28 * 1024 * 1024),
         cost_estimate=pl.CostEstimate(
             flops=count * 4 * 10**9, bytes_accessed=count * 10**7, transcendentals=0
@@ -327,10 +376,10 @@
     return -(-9 * count // 8) * 8
 
 
-def brick_scratch(rows, bricks, places):
+def brick_scratch(rows, bricks, places, width):
     return [
         pltpu.VMEM((1, bricks), jnp.int32),
-        pltpu.VMEM((min(16, places) * 2 * rows, bricks), jnp.bfloat16),
+        pltpu.VMEM((min(16, places) * 2 * rows, width), jnp.bfloat16),
     ]
 
 
@@ -342,7 +391,7 @@
             jax.ShapeDtypeStruct((places, rows // 2, COLUMNS), jnp.float32),
             jax.ShapeDtypeStruct(labels.shape, jnp.int32),
         ],
-        scratch_shapes=brick_scratch(rows // 2, bricks, places),
+        scratch_shapes=brick_scratch(rows // 2, bricks, places, bricks),
         compiler_params=pltpu.CompilerParams(vmem_limit_bytes=24 * 1024 * 1024),
         cost_estimate=pl.CostEstimate(
             flops=rows * 15 * 10**6, bytes_accessed=rows * 5 * 10**4, transcendentals=0
@@ -352,50 +401,57 @@
 
 
 def core_sum_kernel(spare, kept_ref, received_ref, own_ref, label_ref, *out_refs):
-    for index, out_ref in enumerate(out_refs[:-1]):
+    for index, out_ref in enumerate(out_refs[:-2]):
         out_ref[...] = kept_ref[index] + received_ref[index]
         for c in range(spare):
             row = out_ref.shape[1] - spare + c
             out_ref[:, row : row + 1, :] = jnp.broadcast_to(
                 own_ref[c][None], (out_ref.shape[0], 1, COLUMNS)
             )
-    out_refs[-1][...] = label_ref[...]
+    out_refs[-2][...] = label_ref[...]
+    out_refs[-1][...] = own_ref[...]
 
 
 def core_sum(kept, received, own, labels, spare, name):
     pairs, rests = lax.axis_size("ca") // 2, lax.axis_size("fe") // 2
     shape = (2 * pairs, rests) + kept.shape[1:]
-    *parts, labels = pl.pallas_call(
+    *parts, labels, own = pl.pallas_call(
         functools.partial(core_sum_kernel, spare),
         out_shape=[jax.ShapeDtypeStruct(shape[1:], jnp.float32)] * shape[0]
-        + [jax.ShapeDtypeStruct(labels.shape, jnp.int32)],
+        + [
+            jax.ShapeDtypeStruct(labels.shape, jnp.int32),
+            jax.ShapeDtypeStruct(own.shape, jnp.float32),
+        ],
         compiler_params=pltpu.CompilerParams(vmem_limit_bytes=16 * 1024 * 1024),
         name=name,
     )(kept.reshape(shape), received.reshape(shape), own, labels)
-    return parts, labels
+    return parts, labels, own
 
 
 def plane_sum_kernel(spare, sources, passed, *refs):
     outs = refs[sources + passed :]
-    for height, out_ref in enumerate(outs[: len(outs) - passed]):
-        out_ref[...] = sum(ref[height] for ref in refs[:sources])
+    height = 0
+    for out_ref in outs[: len(outs) - passed]:
+        heights = pl.ds(height, out_ref.shape[0])
+        out_ref[...] = sum(ref[heights] for ref in refs[:sources])
         if spare:
-            rows = pl.ds(out_ref.shape[0] - spare, spare)
-            out_ref[rows, :] = refs[1][height, rows, :]
+            rows = pl.ds(out_ref.shape[1] - spare, spare)
+            out_ref[:, rows, :] = refs[1][heights, rows, :]
+        height += out_ref.shape[0]
     for i in range(passed):
         outs[len(outs) - passed + i][...] = refs[sources + i][...]
 
 
-def plane_sum(parts, passed, spare, name):
-    part = jax.ShapeDtypeStruct(parts[0].shape[1:], jnp.float32)
+def plane_sum(parts, passed, spare, cuts, name):
+    rest = parts[0].shape[1:]
     out = pl.pallas_call(
         functools.partial(plane_sum_kernel, spare, len(parts), len(passed)),
-        out_shape=[part] * parts[0].shape[0]
+        out_shape=[jax.ShapeDtypeStruct((cut,) + rest, jnp.float32) for cut in cuts]
         + [jax.ShapeDtypeStruct(array.shape, array.dtype) for array in passed],
         compiler_params=pltpu.CompilerParams(vmem_limit_bytes=16 * 1024 * 1024),
         name=name,
     )(*parts, *passed)
-    return out[: parts[0].shape[0]], *out[parts[0].shape[0] :]
+    return out[: len(cuts)], *out[len(cuts) :]
 
 
 def to_relative(block, core, pair, last, rest):
@@ -432,13 +488,14 @@
     return total
 
 
-def update_kernel(heights, *refs):
-    first_refs, second_refs = refs[:heights], refs[heights : 2 * heights]
-    own_ref, stress_ref, resistance_ref, weights_ref, table_ref = refs[2 * heights : -2]
+def update_kernel(firsts, seconds, *refs):
+    first_refs, second_refs = refs[:firsts], refs[firsts : firsts + seconds]
+    own_ref, stress_ref, resistance_ref, weights_ref, table_ref = refs[firsts + seconds : -2]
     stress_out_ref, nodal_ref = refs[-2:]
     elements = stress_ref.shape[2]
     gathered = [
-        sum(ref[:, 0:elements] for ref in chunk_refs) for chunk_refs in (first_refs, second_refs)
+        sum(ref[0, :, 0:elements] for ref in chunk_refs)
+        for chunk_refs in (first_refs, second_refs)
     ]
     counted = 9 * CHUNKS[1][1]
     counts = gathered[1][counted : counted + 1]
@@ -470,7 +527,7 @@
     upper = jnp.zeros((3, COLUMNS), jnp.float32)
     for flip, ref in enumerate(second_refs):
         wanted = (height ^ flip) == above
-        upper = upper + jnp.where(wanted, ref[ref.shape[0] - 3 :, :], 0.0)
+        upper = upper + jnp.where(wanted, ref[0, ref.shape[1] - 3 :, :], 0.0)
     values = jnp.where(
         upper_corner,
         jnp.concatenate(
@@ -580,7 +637,7 @@
         dtype=jnp.float32,
     )
     return pl.pallas_call(
-        functools.partial(update_kernel, len(first)),
+        functools.partial(update_kernel, len(first), len(second)),
         out_shape=(
             jax.ShapeDtypeStruct(stress_old.shape, jnp.float32),
             jax.ShapeDtypeStruct((2,) + own.shape, jnp.float32),
@@ -609,14 +666,28 @@
     table = rotation_table(euler_angles)
     split, send, labels, ids = cell_sums(CHUNKS[0], per_octant, grain_ids, labels, table, half)
     keep, labels = brick_sums(split, labels, half)
-    core_a, labels = core_sum(keep, across_cores(send), displacement, labels, 0, "core_sum_a")
+    core_a, labels, own = core_sum(
+        keep, across_cores(send), displacement, labels, 0, "core_sum_a"
+    )
     split, send, labels = cell_sums(CHUNKS[1], per_octant, ids, labels, table, half)
-    plane_a, labels, send = plane_sum(across_plane(core_a), [labels, send], 0, "plane_sum_a")
+    heights = lax.axis_size("fe") // 2
+    flip = heights // 2
+    (kept, sent), labels, send = plane_sum(
+        across_plane(core_a), [labels, send], 0, [flip, flip], "plane_sum_a"
+    )
+    received = to_relative(sent, 0, 0, 0, flip)
     keep, labels = brick_sums(split, labels, half)
-    core_b, labels = core_sum(keep, across_cores(send), displacement, labels, 3, "core_sum_b")
-    (plane_b,) = plane_sum(across_plane(core_b), [], 3, "plane_sum_b")
+    core_b, labels, own = core_sum(keep, across_cores(send), own, labels, 3, "core_sum_b")
+    plane_b = across_plane(core_b)
+    while flip > 1:
+        flip //= 2
+        (kept, sent), labels = plane_sum(
+            [kept, received], [labels], 0, [flip, flip], "height_sum_a"
+        )
+        received = to_relative(sent, 0, 0, 0, flip)
+    plane_b, labels = plane_sum(plane_b, [labels], 3, [1] * heights, "plane_sum_b")
     stress_new, nodal = element_update(
-        across_height(plane_a),
+        [kept, received],
         across_height(plane_b),
         displacement,
         stress_old,

time: 72.8 us -> 70.7 us (0.971)
  Pallas kernels: 37.9 us -> 35.1 us
  waiting for transfers between devices: 9.28 us -> 11.6 us
  starting transfers between devices: 20.9 us -> 19.3 us
    pallas_call x2, Pallas kernels: 31.9 us -> 28.6 us  [cell_sums(): pl.pallas_call(functools.partial(cell_sum_kernel, octants, per_octant), o...]
    ppermute x12 -> x11, waiting for transfers between devices: 7.35 us -> 10.3 us  [to_relative(): lax.ppermute(block, ('ca', 'fe'), [(i, i ^ flip) for i in range(groups *...]
    ppermute x12 -> x11, starting transfers between devices: 17.3 us -> 15.7 us  [to_relative(): lax.ppermute(block, ('ca', 'fe'), [(i, i ^ flip) for i in range(groups *...]
  transfers between devices with their start and end apart: 15 -> 14, of which waited for: 6 -> 7; matrix products, arithmetic and copies ran while one was open for 0% -> 0% of each run, Pallas kernels for 16% -> 17%
where the time goes in v10:
time: 70.7 us; the launch traced here: 70.4 us
  Pallas kernels  35.1 us (50%)
  starting transfers between devices  19.3 us (27%)
  waiting for transfers between devices  11.6 us (16%)
  local copies, waits for them, and re-layouts  2.33 us (3%)
  other arithmetic  1.32 us (2%)
  between operations  0.77 us (1%)
    pallas_call x2, Pallas kernels, cell_sums(): pl.pallas_call(functools.partial(cell_sum_kernel, octants, per_octant), o...  28.6 us
    ppermute x11, starting transfers between devices, to_relative(): lax.ppermute(block, ('ca', 'fe'), [(i, i ^ flip) for i in range(groups *...  15.7 us
    ppermute x11, waiting for transfers between devices, to_relative(): lax.ppermute(block, ('ca', 'fe'), [(i, i ^ flip) for i in range(groups *...  10.3 us
    pallas_call x2, Pallas kernels, brick_sums(): pl.pallas_call(brick_sum_kernel, out_shape=[jax.ShapeDtypeStruct((places,...  3.16 us
    ppermute x1, starting transfers between devices, passed_along(): return lax.ppermute(block, axis, route)  3.01 us
    unnamed x14, local copies, waits for them, and re-layouts  2.33 us
    pallas_call x1, Pallas kernels, element_update(): pl.pallas_call(functools.partial(update_kernel, len(first), len(second)),...  1.69 us
  transfers between devices with their start and end apart: 14, of which 7 were waited for; matrix products, arithmetic and copies ran while one was open for 0% of the time, Pallas kernels for 17%

profile of v10, /device:TPU:0, one launch (start us, length us, event | category | flops | bytes accessed | tf_op | source)
XLA Modules:
  0.0 70.4 jit_solution(17784601002540378441)
XLA Ops:
  0.6 0.8 %copy-done.1 = f32[3,4096]{1,0:T(4,128)S(1)} copy-done((f32[3,4096]{1,0:T(4,128)S(1)}, f32[3,4096]{1,0:T(4,128)}, u32[]{:S(2)}) %copy-start.1) | copy-done | bytes 49176
  1.5 0.2 rotation_table.1.table_ref
  1.6 0.7 %add_select_fusion = s32[2048]{0:T(1024)S(1)} fusion(s32[2048]{0:T(1024)} %param.14, s32[2048]{0:T(1024)} %bitcast.15, s32[2048]{0:T(1024)} %param.12), kind=kLoop, calls=%fused_computation | loop fusion | flops 8192 | bytes 32768 | tf_op jit(solution)/shard_map/jit(_where)/select_n | solution.py:664
  2.4 1.5 %copy-done.6 = s32[216,2048]{1,0:T(8,128)S(1)} copy-done((s32[216,2048]{1,0:T(8,128)S(1)}, s32[216,2048]{1,0:T(8,128)}, u32[]{:S(2)}) %copy-start.6) | copy-done | bytes 1769496
  3.9 21.0 %cell_sums.2 = (bf16[112,2048]{1,0:T(8,128)(2,1)S(1)}, f32[16,56,256]{2,1,0:T(8,128)S(1)}, s32[1,2048]{1,0:T(1,128)S(1)}, s32[56,2048]{1,0:T(8,128)S(1)}) custom-call(s32[216,2048]{1,0:T(8,128)S(1)} %copy-done.6, s32[1,2048]{1,0:T(1,128)S(1)} %bitcast.14, s32[48,8,128]{2,1,0:T(8,128)S(1)} %rotation_table.1.table_ref), custom_call_target="tpu_custom_call" | custom-call | flops 24000000000 | bytes 60000000 | tf_op jit(solution)/shard_map/cell_sums/pallas_call | solution.py:359
  24.9 0.5 collective-permute-start
  25.4 2.1 %brick_sums.2 = (f32[16,56,256]{2,1,0:T(8,128)S(1)}, s32[1,2048]{1,0:T(1,128)S(1)}) custom-call(bf16[112,2048]{1,0:T(8,128)(2,1)S(1)} %get-tuple-element.37.split_ref, s32[1,2048]{1,0:T(1,128)S(1)} %get-tuple-element.38.label_ref), custom_call_target="tpu_custom_call" | custom-call | flops 1680000000 | bytes 5600000 | tf_op jit(solution)/shard_map/brick_sums/pallas_call | solution.py:388
  27.6 0.1 core_sum_a.1
  27.7 2.9 %collective-permute-start.1 = (f32[4,56,256]{2,1,0:T(8,128)S(1)}, f32[4,56,256]{2,1,0:T(8,128)S(1)}, u32[]{:S(2)}, u32[]{:S(2)}) collective-permute-start(f32[4,56,256]{2,1,0:T(8,128)S(1)} %get-tuple-element.43), channel_id=1, source_target_pairs={{0,1},{1,0},{2,3},{3,2},{4,5},{5,4},{6,7},{7,6},{8,9},{9,8},{10,11... | collective-permute-start | bytes 688136 | tf_op jit(solution)/shard_map/ppermute | solution.py:460
  30.6 1.5 %collective-permute-start.2 = (f32[4,56,256]{2,1,0:T(8,128)S(1)}, f32[4,56,256]{2,1,0:T(8,128)S(1)}, u32[]{:S(2)}, u32[]{:S(2)}) collective-permute-start(f32[4,56,256]{2,1,0:T(8,128)S(1)} %get-tuple-element.44), channel_id=1, source_target_pairs={{0,16},{1,17},{2,18},{3,19},{4,20},{5,21},{6,22},{7,23},{8,24},{9,... | collective-permute-start | bytes 688136 | tf_op jit(solution)/shard_map/ppermute | solution.py:460
  32.1 7.6 %cell_sums.3 = (bf16[48,2048]{1,0:T(8,128)(2,1)S(1)}, f32[16,24,256]{2,1,0:T(8,128)S(1)}, s32[1,2048]{1,0:T(1,128)S(1)}) custom-call(s32[56,2048]{1,0:T(8,128)S(1)} %get-tuple-element.46.ids_ref, s32[1,2048]{1,0:T(1,128)S(1)} %get-tuple-element.47.label_ref, s32[48,8,128]{2,1,0:T(8,128)S(1)} %rotation_table.1.table_ref), custom_call_target="tpu_custom_call" | custom-call | flops 8000000000 | bytes 20000000 | tf_op jit(solution)/shard_map/cell_sums/pallas_call | solution.py:359
  39.7 3.2 %collective-permute-done.2.refs_2_ = f32[4,56,256]{2,1,0:T(8,128)S(1)} collective-permute-done((f32[4,56,256]{2,1,0:T(8,128)S(1)}, f32[4,56,256]{2,1,0:T(8,128)S(1)}, u32[]{:S(2)}, u32[]{:S(2)}) %collective-permute-start.2) | collective-permute-done | bytes 229408 | tf_op jit(solution)/shard_map/ppermute | solution.py:460
  43.1 2.7 %collective-permute-start.4 = (f32[2,56,256]{2,1,0:T(8,128)S(1)}, f32[2,56,256]{2,1,0:T(8,128)S(1)}, u32[]{:S(2)}, u32[]{:S(2)}) collective-permute-start(f32[2,56,256]{2,1,0:T(8,128)S(1)} %get-tuple-element.51), channel_id=1, source_target_pairs={{0,4},{1,5},{2,6},{3,7},{4,0},{5,1},{6,2},{7,3},{8,12},{9,13},{10,... | collective-permute-start | bytes 344072 | tf_op jit(solution)/shard_map/ppermute | solution.py:460
  45.8 1.0 %brick_sums.3 = (f32[16,24,256]{2,1,0:T(8,128)S(1)}, s32[1,2048]{1,0:T(1,128)S(1)}) custom-call(bf16[48,2048]{1,0:T(8,128)(2,1)S(1)} %get-tuple-element.52.split_ref, s32[1,2048]{1,0:T(1,128)S(1)} %get-tuple-element.53.label_ref), custom_call_target="tpu_custom_call" | custom-call | flops 720000000 | bytes 2400000 | tf_op jit(solution)/shard_map/brick_sums/pallas_call | solution.py:388
  46.8 0.6 core_sum_b.1
  47.4 1.2 %collective-permute-start.7 = (f32[4,24,256]{2,1,0:T(8,128)S(1)}, f32[4,24,256]{2,1,0:T(8,128)S(1)}, u32[]{:S(2)}, u32[]{:S(2)}) collective-permute-start(f32[4,24,256]{2,1,0:T(8,128)S(1)} %get-tuple-element.62), channel_id=1, source_target_pairs={{0,1},{1,0},{2,3},{3,2},{4,5},{5,4},{6,7},{7,6},{8,9},{9,8},{10,11... | collective-permute-start | bytes 294920 | tf_op jit(solution)/shard_map/ppermute | solution.py:460
  48.7 0.8 %collective-permute-start.8 = (f32[4,24,256]{2,1,0:T(8,128)S(1)}, f32[4,24,256]{2,1,0:T(8,128)S(1)}, u32[]{:S(2)}, u32[]{:S(2)}) collective-permute-start(f32[4,24,256]{2,1,0:T(8,128)S(1)} %get-tuple-element.63), channel_id=1, source_target_pairs={{0,16},{1,17},{2,18},{3,19},{4,20},{5,21},{6,22},{7,23},{8,24},{9,... | collective-permute-start | bytes 294920 | tf_op jit(solution)/shard_map/ppermute | solution.py:460
  49.5 1.4 %collective-permute-start.9 = (f32[4,24,256]{2,1,0:T(8,128)S(1)}, f32[4,24,256]{2,1,0:T(8,128)S(1)}, u32[]{:S(2)}, u32[]{:S(2)}) collective-permute-start(f32[4,24,256]{2,1,0:T(8,128)S(1)} %get-tuple-element.64), channel_id=1, source_target_pairs={{0,17},{1,16},{2,19},{3,18},{4,21},{5,20},{6,23},{7,22},{8,25},{9,... | collective-permute-start | bytes 294920 | tf_op jit(solution)/shard_map/ppermute | solution.py:460
  50.9 1.1 %collective-permute-done.4.refs_1_ = f32[2,56,256]{2,1,0:T(8,128)S(1)} collective-permute-done((f32[2,56,256]{2,1,0:T(8,128)S(1)}, f32[2,56,256]{2,1,0:T(8,128)S(1)}, u32[]{:S(2)}, u32[]{:S(2)}) %collective-permute-start.4) | collective-permute-done | bytes 114720 | tf_op jit(solution)/shard_map/ppermute | solution.py:460
  52.0 0.8 %collective-permute-start.6 = (f32[1,56,256]{2,1,0:T(8,128)S(1)}, f32[1,56,256]{2,1,0:T(8,128)S(1)}, u32[]{:S(2)}, u32[]{:S(2)}) collective-permute-start(f32[1,56,256]{2,1,0:T(8,128)S(1)} %get-tuple-element.60), channel_id=1, source_target_pairs={{0,2},{1,3},{2,0},{3,1},{4,6},{5,7},{6,4},{7,5},{8,10},{9,11},{10,... | collective-permute-start | bytes 172040 | tf_op jit(solution)/shard_map/ppermute | solution.py:460
  52.8 1.5 %collective-permute-done.8.refs_2_ = f32[4,24,256]{2,1,0:T(8,128)S(1)} collective-permute-done((f32[4,24,256]{2,1,0:T(8,128)S(1)}, f32[4,24,256]{2,1,0:T(8,128)S(1)}, u32[]{:S(2)}, u32[]{:S(2)}) %collective-permute-start.8) | collective-permute-done | bytes 98336 | tf_op jit(solution)/shard_map/ppermute | solution.py:460
  54.2 1.1 %collective-permute-done.9.refs_3_ = f32[4,24,256]{2,1,0:T(8,128)S(1)} collective-permute-done((f32[4,24,256]{2,1,0:T(8,128)S(1)}, f32[4,24,256]{2,1,0:T(8,128)S(1)}, u32[]{:S(2)}, u32[]{:S(2)}) %collective-permute-start.9) | collective-permute-done | bytes 98336 | tf_op jit(solution)/shard_map/ppermute | solution.py:460
  55.4 0.6 plane_sum_b.1
  56.0 1.6 %collective-permute-start.10 = (f32[1,24,256]{2,1,0:T(8,128)S(1)}, f32[1,24,256]{2,1,0:T(8,128)S(1)}, u32[]{:S(2)}, u32[]{:S(2)}) collective-permute-start(f32[1,24,256]{2,1,0:T(8,128)S(1)} %get-tuple-element.67), channel_id=1, source_target_pairs={{0,2},{1,3},{2,0},{3,1},{4,6},{5,7},{6,4},{7,5},{8,10},{9,11},{10,... | collective-permute-start | bytes 73736 | tf_op jit(solution)/shard_map/ppermute | solution.py:460
  57.6 0.6 collective-permute-start.11
  58.2 2.2 %collective-permute-start.12 = (f32[1,24,256]{2,1,0:T(8,128)S(1)}, f32[1,24,256]{2,1,0:T(8,128)S(1)}, u32[]{:S(2)}, u32[]{:S(2)}) collective-permute-start(f32[1,24,256]{2,1,0:T(8,128)S(1)} %get-tuple-element.69), channel_id=1, source_target_pairs={{0,6},{1,7},{2,4},{3,5},{4,2},{5,3},{6,0},{7,1},{8,14},{9,15},{10,... | collective-permute-start | bytes 73736 | tf_op jit(solution)/shard_map/ppermute | solution.py:460
  60.4 2.1 %collective-permute-done.11.refs_4_ = f32[1,24,256]{2,1,0:T(8,128)S(1)} collective-permute-done((f32[1,24,256]{2,1,0:T(8,128)S(1)}, f32[1,24,256]{2,1,0:T(8,128)S(1)}, u32[]{:S(2)}, u32[]{:S(2)}) %collective-permute-start.11) | collective-permute-done | bytes 24608 | tf_op jit(solution)/shard_map/ppermute | solution.py:460
  62.5 1.3 %collective-permute-done.12.refs_5_ = f32[1,24,256]{2,1,0:T(8,128)S(1)} collective-permute-done((f32[1,24,256]{2,1,0:T(8,128)S(1)}, f32[1,24,256]{2,1,0:T(8,128)S(1)}, u32[]{:S(2)}, u32[]{:S(2)}) %collective-permute-start.12) | collective-permute-done | bytes 24608 | tf_op jit(solution)/shard_map/ppermute | solution.py:460
  63.8 1.7 %stress_update.1 = (f32[6,8,225]{2,1,0:T(8,128)}, f32[2,3,1,256]{3,2,1,0:T(1,128)S(1)}) custom-call(f32[1,56,256]{2,1,0:T(8,128)S(1)} %get-tuple-element.59.refs_0_, f32[1,56,256]{2,1,0:T(8,128)S(1)} %collective-permute-done.6.refs_1_, f32[1,24,256]{2,1,0:T(8,128)S(1)} %get-tuple-element.66.refs_2_, f32[1,24,256]{2,1,0:T(8,128)S(1)} %collective-permute-done.10.refs_3_, ...), custom_call_target="tpu_custom_call" | custom-call | tf_op jit(solution)/shard_map/stress_update/pallas_call | solution.py:639
  65.5 3.0 %collective-permute-start.13 = (f32[3,1,256]{2,1,0:T(1,128)S(1)}, f32[3,1,256]{2,1,0:T(1,128)S(1)}, u32[]{:S(2)}, u32[]{:S(2)}) collective-permute-start(f32[3,1,256]{2,1,0:T(1,128)S(1)} %slice_bitcast_fusion), channel_id=1, source_target_pairs={{0,1},{1,2},{2,3},{3,4},{4,5},{5,6},{6,7},{8,9},{9,10},{10,11},{11... | collective-permute-start | bytes 9224 | tf_op jit(solution)/shard_map/ppermute | solution.py:48
  68.6 1.3 %collective-permute-done.13 = f32[3,1,256]{2,1,0:T(1,128)S(1)} collective-permute-done((f32[3,1,256]{2,1,0:T(1,128)S(1)}, f32[3,1,256]{2,1,0:T(1,128)S(1)}, u32[]{:S(2)}, u32[]{:S(2)}) %collective-permute-start.13) | collective-permute-done | bytes 3104 | tf_op jit(solution)/shard_map/ppermute | solution.py:48
  69.9 0.6 bitcast_add_fusion
  (24 shorter events, 0.2 us)
Async XLA Ops:
  0.6 0.8 %copy-start.1 = (f32[3,4096]{1,0:T(4,128)S(1)}, f32[3,4096]{1,0:T(4,128)}, u32[]{:S(2)}) copy-start(f32[3,4096]{1,0:T(4,128)} %euler_ref.1) | copy-start | bytes 147460
  2.4 1.5 %copy-start.6 = (s32[216,2048]{1,0:T(8,128)S(1)}, s32[216,2048]{1,0:T(8,128)}, u32[]{:S(2)}) copy-start(s32[216,2048]{1,0:T(8,128)} %ids_ref.1) | copy-start | bytes 5308420
  24.9 2.7 %collective-permute-start = (f32[16,56,256]{2,1,0:T(8,128)S(1)}, f32[16,56,256]{2,1,0:T(8,128)S(1)}, u32[]{:S(2)}, u32[]{:S(2)}) collective-permute-start(f32[16,56,256]{2,1,0:T(8,128)S(1)} %get-tuple-element.40), channel_id=1, source_target_pairs={{0,8},{8,0},{16,24},{24,16},{1,9},{9,1},{17,25},{25,17},{2,10},{10... | collective-permute-start | bytes 2752520 | tf_op jit(solution)/shard_map/ppermute | solution.py:304
  25.4 2.2 %copy-start.4 = (f32[3,1,256]{2,1,0:T(1,128)S(1)}, f32[3,1,256]{2,1,0:T(1,128)}, u32[]{:S(2)}) copy-start(f32[3,1,256]{2,1,0:T(1,128)} %refs_6_.1) | copy-start | bytes 9220
  27.7 12.0 %collective-permute-start.1 = (f32[4,56,256]{2,1,0:T(8,128)S(1)}, f32[4,56,256]{2,1,0:T(8,128)S(1)}, u32[]{:S(2)}, u32[]{:S(2)}) collective-permute-start(f32[4,56,256]{2,1,0:T(8,128)S(1)} %get-tuple-element.43), channel_id=1, source_target_pairs={{0,1},{1,0},{2,3},{3,2},{4,5},{5,4},{6,7},{7,6},{8,9},{9,8},{10,11... | collective-permute-start | bytes 688136 | tf_op jit(solution)/shard_map/ppermute | solution.py:460
  30.6 12.4 %collective-permute-start.2 = (f32[4,56,256]{2,1,0:T(8,128)S(1)}, f32[4,56,256]{2,1,0:T(8,128)S(1)}, u32[]{:S(2)}, u32[]{:S(2)}) collective-permute-start(f32[4,56,256]{2,1,0:T(8,128)S(1)} %get-tuple-element.44), channel_id=1, source_target_pairs={{0,16},{1,17},{2,18},{3,19},{4,20},{5,21},{6,22},{7,23},{8,24},{9,... | collective-permute-start | bytes 688136 | tf_op jit(solution)/shard_map/ppermute | solution.py:460
  32.1 10.8 %collective-permute-start.3 = (f32[4,56,256]{2,1,0:T(8,128)S(1)}, f32[4,56,256]{2,1,0:T(8,128)S(1)}, u32[]{:S(2)}, u32[]{:S(2)}) collective-permute-start(f32[4,56,256]{2,1,0:T(8,128)S(1)} %get-tuple-element.45), channel_id=1, source_target_pairs={{0,17},{1,16},{2,19},{3,18},{4,21},{5,20},{6,23},{7,22},{8,25},{9,... | collective-permute-start | bytes 688136 | tf_op jit(solution)/shard_map/ppermute | solution.py:460
  43.0 3.8 %collective-permute-start.5 = (f32[16,24,256]{2,1,0:T(8,128)S(1)}, f32[16,24,256]{2,1,0:T(8,128)S(1)}, u32[]{:S(2)}, u32[]{:S(2)}) collective-permute-start(f32[16,24,256]{2,1,0:T(8,128)S(1)} %get-tuple-element.55), channel_id=1, source_target_pairs={{0,8},{8,0},{16,24},{24,16},{1,9},{9,1},{17,25},{25,17},{2,10},{10... | collective-permute-start | bytes 1179656 | tf_op jit(solution)/shard_map/ppermute | solution.py:304
  43.1 8.9 %collective-permute-start.4 = (f32[2,56,256]{2,1,0:T(8,128)S(1)}, f32[2,56,256]{2,1,0:T(8,128)S(1)}, u32[]{:S(2)}, u32[]{:S(2)}) collective-permute-start(f32[2,56,256]{2,1,0:T(8,128)S(1)} %get-tuple-element.51), channel_id=1, source_target_pairs={{0,4},{1,5},{2,6},{3,7},{4,0},{5,1},{6,2},{7,3},{8,12},{9,13},{10,... | collective-permute-start | bytes 344072 | tf_op jit(solution)/shard_map/ppermute | solution.py:460
  45.7 18.1 %copy-start = (f32[12,8,225]{2,1,0:T(8,128)S(1)}, f32[12,8,225]{2,1,0:T(8,128)}, u32[]{:S(2)}) copy-start(f32[12,8,225]{2,1,0:T(8,128)} %refs_8_.1) | copy-start | bytes 259204
  45.7 18.1 %copy-start.2 = (f32[6,8,225]{2,1,0:T(8,128)S(1)}, f32[6,8,225]{2,1,0:T(8,128)}, u32[]{:S(2)}) copy-start(f32[6,8,225]{2,1,0:T(8,128)} %refs_7_.1) | copy-start | bytes 129604
  45.7 18.1 %copy-start.3 = (f32[24,8]{1,0:T(8,128)S(1)}, f32[24,8]{1,0:T(8,128)}, u32[]{:S(2)}) copy-start(f32[24,8]{1,0:T(8,128)} %constant.8.clone.refs_10_) | copy-start | bytes 2308
  45.7 18.1 %copy-start.5 = (s32[8,225]{1,0:T(8,128)S(1)}, s32[8,225]{1,0:T(8,128)}, u32[]{:S(2)}) copy-start(s32[8,225]{1,0:T(8,128)} %refs_9_.1) | copy-start | bytes 21604
  47.4 5.3 %collective-permute-start.7 = (f32[4,24,256]{2,1,0:T(8,128)S(1)}, f32[4,24,256]{2,1,0:T(8,128)S(1)}, u32[]{:S(2)}, u32[]{:S(2)}) collective-permute-start(f32[4,24,256]{2,1,0:T(8,128)S(1)} %get-tuple-element.62), channel_id=1, source_target_pairs={{0,1},{1,0},{2,3},{3,2},{4,5},{5,4},{6,7},{7,6},{8,9},{9,8},{10,11... | collective-permute-start | bytes 294920 | tf_op jit(solution)/shard_map/ppermute | solution.py:460
  48.7 5.6 %collective-permute-start.8 = (f32[4,24,256]{2,1,0:T(8,128)S(1)}, f32[4,24,256]{2,1,0:T(8,128)S(1)}, u32[]{:S(2)}, u32[]{:S(2)}) collective-permute-start(f32[4,24,256]{2,1,0:T(8,128)S(1)} %get-tuple-element.63), channel_id=1, source_target_pairs={{0,16},{1,17},{2,18},{3,19},{4,20},{5,21},{6,22},{7,23},{8,24},{9,... | collective-permute-start | bytes 294920 | tf_op jit(solution)/shard_map/ppermute | solution.py:460
  49.5 5.9 %collective-permute-start.9 = (f32[4,24,256]{2,1,0:T(8,128)S(1)}, f32[4,24,256]{2,1,0:T(8,128)S(1)}, u32[]{:S(2)}, u32[]{:S(2)}) collective-permute-start(f32[4,24,256]{2,1,0:T(8,128)S(1)} %get-tuple-element.64), channel_id=1, source_target_pairs={{0,17},{1,16},{2,19},{3,18},{4,21},{5,20},{6,23},{7,22},{8,25},{9,... | collective-permute-start | bytes 294920 | tf_op jit(solution)/shard_map/ppermute | solution.py:460
  52.0 8.4 %collective-permute-start.6 = (f32[1,56,256]{2,1,0:T(8,128)S(1)}, f32[1,56,256]{2,1,0:T(8,128)S(1)}, u32[]{:S(2)}, u32[]{:S(2)}) collective-permute-start(f32[1,56,256]{2,1,0:T(8,128)S(1)} %get-tuple-element.60), channel_id=1, source_target_pairs={{0,2},{1,3},{2,0},{3,1},{4,6},{5,7},{6,4},{7,5},{8,10},{9,11},{10,... | collective-permute-start | bytes 172040 | tf_op jit(solution)/shard_map/ppermute | solution.py:460
  56.0 4.4 %collective-permute-start.10 = (f32[1,24,256]{2,1,0:T(8,128)S(1)}, f32[1,24,256]{2,1,0:T(8,128)S(1)}, u32[]{:S(2)}, u32[]{:S(2)}) collective-permute-start(f32[1,24,256]{2,1,0:T(8,128)S(1)} %get-tuple-element.67), channel_id=1, source_target_pairs={{0,2},{1,3},{2,0},{3,1},{4,6},{5,7},{6,4},{7,5},{8,10},{9,11},{10,... | collective-permute-start | bytes 73736 | tf_op jit(solution)/shard_map/ppermute | solution.py:460
  57.6 4.9 %collective-permute-start.11 = (f32[1,24,256]{2,1,0:T(8,128)S(1)}, f32[1,24,256]{2,1,0:T(8,128)S(1)}, u32[]{:S(2)}, u32[]{:S(2)}) collective-permute-start(f32[1,24,256]{2,1,0:T(8,128)S(1)} %get-tuple-element.68), channel_id=1, source_target_pairs={{0,4},{1,5},{2,6},{3,7},{4,0},{5,1},{6,2},{7,3},{8,12},{9,13},{10,... | collective-permute-start | bytes 73736 | tf_op jit(solution)/shard_map/ppermute | solution.py:460
  58.2 5.6 %collective-permute-start.12 = (f32[1,24,256]{2,1,0:T(8,128)S(1)}, f32[1,24,256]{2,1,0:T(8,128)S(1)}, u32[]{:S(2)}, u32[]{:S(2)}) collective-permute-start(f32[1,24,256]{2,1,0:T(8,128)S(1)} %get-tuple-element.69), channel_id=1, source_target_pairs={{0,6},{1,7},{2,4},{3,5},{4,2},{5,3},{6,0},{7,1},{8,14},{9,15},{10,... | collective-permute-start | bytes 73736 | tf_op jit(solution)/shard_map/ppermute | solution.py:460
  65.5 4.3 %collective-permute-start.13 = (f32[3,1,256]{2,1,0:T(1,128)S(1)}, f32[3,1,256]{2,1,0:T(1,128)S(1)}, u32[]{:S(2)}, u32[]{:S(2)}) collective-permute-start(f32[3,1,256]{2,1,0:T(1,128)S(1)} %slice_bitcast_fusion), channel_id=1, source_target_pairs={{0,1},{1,2},{2,3},{3,4},{4,5},{5,6},{6,7},{8,9},{9,10},{10,11},{11... | collective-permute-start | bytes 9224 | tf_op jit(solution)/shard_map/ppermute | solution.py:48

commit v11 on v10

--- a/solution.py
+++ b/solution.py
@@ -140,18 +140,22 @@
     return jnp.where(bits[level], high, low)
 
 
-def rotation_products(table_ref, table_rows, ids):
+def rotation_coordinates(table_ref, table_rows, ids):
     lane = (ids & (LANES - 1))[:, :, None]
     row = lax.shift_right_logical(ids, 7)
     bits = [(row & (1 << level)) != 0 for level in range(table_rows.bit_length() - 1)]
     both = looked_up(table_ref, 0, table_rows, lane, bits)
     third = looked_up(table_ref, table_rows, table_rows // 2, lane, bits[1:])
-    third = lax.shift_left(third, lax.shift_left((row & 1) ^ 1, 4))
+    return both, lax.shift_left(third, lax.shift_left((row & 1) ^ 1, 4))
+
+
+def rotation_products(both, third):
     x = lax.shift_right_arithmetic(both, 16).astype(jnp.float32)
     y = lax.shift_right_arithmetic(lax.shift_left(both, 16), 16).astype(jnp.float32)
     z = lax.shift_right_arithmetic(third, 16).astype(jnp.float32)
-    square = x * x + y * y + z * z
-    scale = 2.0 / (1.0 + square * (1.0 / (QUANTUM * QUANTUM)))
+    length = (x * x + y * y + z * z) * (0.5 / (QUANTUM * QUANTUM)) + 0.5
+    scale = pl.reciprocal(length, approx=True)
+    scale = scale * (2.0 - length * scale)
     w = scale - 1.0
     x, y, z = x * scale, y * scale, z * scale
     return [x * x, y * y, z * z, x * y, x * z, y * z, w * x, w * y, w * z]
@@ -180,22 +184,24 @@
     ids_ref,
     label_ref,
     table_ref,
-    split_ref,
-    out_ref,
-    label_out_ref,
     *refs,
 ):
     first, count = octants
     start = ids_ref.shape[0] - (8 - first) * per_octant
     tile_ref, raw_ref, place_ref, masked_ref = refs[-4:]
-    if len(refs) > 4:
-        refs[0][...] = ids_ref[pl.ds(ids_ref.shape[0] - refs[0].shape[0], refs[0].shape[0]), :]
+    if first + count < 8:
+        label_out_ref, send_ref, split_ref, rest_ref = refs[:-4]
+        label_out_ref[...] = label_ref[...]
+        rest_ref[...] = ids_ref[pl.ds(ids_ref.shape[0] - rest_ref.shape[0], rest_ref.shape[0]), :]
+        targets = [(send_ref.shape[0], send_ref)]
+    else:
+        send_ref, keep_ref, split_ref = refs[:-4]
+        targets = [(send_ref.shape[0], send_ref), (0, keep_ref)]
     table_rows = table_ref.shape[0] * 2 // 3
-    label_out_ref[...] = label_ref[...]
     groups = tile_ref.shape[1] // 8
     rows_left = count * per_octant - 8 * (groups - 1)
     turns = count // math.gcd(count, 8)
-    rows = out_ref.shape[1]
+    rows = send_ref.shape[1]
     width = masked_ref.shape[1]
     pairs = ids_ref.shape[1] // width
 
@@ -223,15 +229,20 @@
                     pl.ds(start + octant * per_octant, per_octant), lanes
                 ]
             sums = [[jnp.zeros((8, LANES), jnp.float32)] * 9 for turn in range(turns)]
-            for group in range(groups):
-                ids = tile_ref[tile, pl.ds(8 * group, 8), :]
-                products = rotation_products(table_ref, table_rows, ids)
-                if group == groups - 1 and rows_left < 8:
+            found = None
+            for group in range(groups + 1):
+                last = found
+                if group < groups:
+                    ids = tile_ref[tile, pl.ds(8 * group, 8), :]
+                    found = rotation_coordinates(table_ref, table_rows, ids)
+                if group == 0:
+                    continue
+                products = rotation_products(*last)
+                if group == groups and rows_left < 8:
                     there = lax.broadcasted_iota(jnp.int32, (8, LANES), 0) < rows_left
                     products = [jnp.where(there, value, 0.0) for value in products]
-                sums[group % turns] = [
-                    total + value for total, value in zip(sums[group % turns], products)
-                ]
+                turn = (group - 1) % turns
+                sums[turn] = [total + value for total, value in zip(sums[turn], products)]
             scales = [2.0 / (QUANTUM * QUANTUM)] * 6 + [2.0 / QUANTUM] * 3
             raw_ref[:, lanes] = jnp.concatenate(
                 [sums[turn][index] * scales[index] for index in range(9) for turn in range(turns)],
@@ -253,10 +264,12 @@
         column = lax.broadcasted_iota(jnp.int32, (COLUMNS, width), 0)
         chosen = (column == label_ref[:, lanes] & (COLUMNS - 1)).astype(jnp.bfloat16)
         place = jnp.where(counted, place_ref[:, lanes], -1)
-        add_places(split_ref, lanes, place, chosen, out_ref, masked_ref)
-
-    place_ref[...] = relative_places(label_ref[...], out_ref.shape[0])
-    out_ref[...] = jnp.zeros(out_ref.shape, jnp.float32)
+        for base, out_ref in targets:
+            add_places(split_ref, lanes, place - base, chosen, out_ref, masked_ref)
+
+    place_ref[...] = relative_places(label_ref[...])
+    for base, out_ref in targets:
+        out_ref[...] = jnp.zeros(out_ref.shape, jnp.float32)
     raw_ref[:, pl.ds(0, width)] = jnp.zeros((raw_ref.shape[0], width), jnp.float32)
     split_ref[:, pl.ds(0, width)] = jnp.zeros((split_ref.shape[0], width), jnp.bfloat16)
 
@@ -266,15 +279,15 @@
         look_up(pair)
         return carry
 
-    lax.fori_loop(0, pairs, step, 0)
+    lax.fori_loop(0, pairs, step, 0, unroll=2)
     add_bricks(pairs - 2, True)
     fold_entries(pairs - 1)
     add_bricks(pairs - 1, True)
 
 
-def relative_places(labels, base):
+def relative_places(labels):
     place = place_of(lax.shift_right_arithmetic(labels, COLUMNS.bit_length() - 1))
-    return jnp.where(labels < 0, -1, place - base)
+    return jnp.where(labels < 0, -1, place)
 
 
 def add_places(split_ref, lanes, place, chosen, out_ref, masked_ref):
@@ -307,7 +320,7 @@
 def brick_sum_kernel(split_ref, label_ref, out_ref, label_out_ref, place_ref, masked_ref):
     labels = label_ref[...]
     label_out_ref[...] = labels
-    place_ref[...] = relative_places(labels, 0)
+    place_ref[...] = relative_places(labels)
     bricks = split_ref.shape[1]
     column = lax.broadcasted_iota(jnp.int32, (COLUMNS, bricks), 0)
     chosen = (column == labels & (COLUMNS - 1)).astype(jnp.bfloat16)
@@ -348,18 +361,25 @@
     first, count = octants
     bricks = ids.shape[1]
     rows = padded_rows(count)
-    out_shape = [
-        jax.ShapeDtypeStruct((2 * rows, bricks), jnp.bfloat16),
-        jax.ShapeDtypeStruct((places, rows, COLUMNS), jnp.float32),
-        jax.ShapeDtypeStruct(labels.shape, jnp.int32),
-    ]
+    half = jax.ShapeDtypeStruct((places, rows, COLUMNS), jnp.float32)
+    split = jax.ShapeDtypeStruct((2 * rows, bricks), jnp.bfloat16)
+    scratch = []
     left = 8 - first - count
     if left:
-        out_shape.append(jax.ShapeDtypeStruct((-(-left * per_octant // 8) * 8, bricks), jnp.int32))
+        out_shape = [
+            jax.ShapeDtypeStruct(labels.shape, jnp.int32),
+            half,
+            split,
+            jax.ShapeDtypeStruct((-(-left * per_octant // 8) * 8, bricks), jnp.int32),
+        ]
+    else:
+        out_shape = [half, half]
+        scratch.append(pltpu.VMEM(split.shape, split.dtype))
     return pl.pallas_call(
         functools.partial(cell_sum_kernel, octants, per_octant),
         out_shape=out_shape,
-        scratch_shapes=[
+        scratch_shapes=scratch
+        + [
             pltpu.VMEM((2, -(-count * per_octant // 8) * 8, LANES), jnp.int32),
             pltpu.VMEM((72 * (count // math.gcd(count, 8)), bricks), jnp.float32),
         ]
@@ -400,52 +420,62 @@
     )(split, labels)
 
 
-def core_sum_kernel(spare, kept_ref, received_ref, own_ref, label_ref, *out_refs):
-    for index, out_ref in enumerate(out_refs[:-2]):
+def core_sum_kernel(passed, kept_ref, received_ref, *refs):
+    outs = refs[passed:]
+    for index, out_ref in enumerate(outs[: len(outs) - passed]):
         out_ref[...] = kept_ref[index] + received_ref[index]
-        for c in range(spare):
-            row = out_ref.shape[1] - spare + c
+    for i in range(passed):
+        outs[len(outs) - passed + i][...] = refs[i][...]
+
+
+def last_core_sum_kernel(kept_ref, received_ref, own_ref, *outs):
+    for index, out_ref in enumerate(outs):
+        out_ref[...] = kept_ref[index] + received_ref[index]
+        for c in range(3):
+            row = out_ref.shape[1] - 3 + c
             out_ref[:, row : row + 1, :] = jnp.broadcast_to(
                 own_ref[c][None], (out_ref.shape[0], 1, COLUMNS)
             )
-    out_refs[-2][...] = label_ref[...]
-    out_refs[-1][...] = own_ref[...]
-
-
-def core_sum(kept, received, own, labels, spare, name):
+
+
+def last_core_sum(kept, received, own):
     pairs, rests = lax.axis_size("ca") // 2, lax.axis_size("fe") // 2
     shape = (2 * pairs, rests) + kept.shape[1:]
-    *parts, labels, own = pl.pallas_call(
-        functools.partial(core_sum_kernel, spare),
+    return pl.pallas_call(
+        last_core_sum_kernel,
+        out_shape=[jax.ShapeDtypeStruct(shape[1:], jnp.float32)] * shape[0],
+        compiler_params=pltpu.CompilerParams(vmem_limit_bytes=16 * 1024 * 1024),
+        name="core_sum_b",
+    )(kept.reshape(shape), received.reshape(shape), own)
+
+
+def core_sum(kept, received, passed, name):
+    pairs, rests = lax.axis_size("ca") // 2, lax.axis_size("fe") // 2
+    shape = (2 * pairs, rests) + kept.shape[1:]
+    out = pl.pallas_call(
+        functools.partial(core_sum_kernel, len(passed)),
         out_shape=[jax.ShapeDtypeStruct(shape[1:], jnp.float32)] * shape[0]
-        + [
-            jax.ShapeDtypeStruct(labels.shape, jnp.int32),
-            jax.ShapeDtypeStruct(own.shape, jnp.float32),
-        ],
+        + [jax.ShapeDtypeStruct(array.shape, array.dtype) for array in passed],
         compiler_params=pltpu.CompilerParams(vmem_limit_bytes=16 * 1024 * 1024),
         name=name,
-    )(kept.reshape(shape), received.reshape(shape), own, labels)
-    return parts, labels, own
-
-
-def plane_sum_kernel(spare, sources, passed, *refs):
+    )(kept.reshape(shape), received.reshape(shape), *passed)
+    return out[: shape[0]], *out[shape[0] :]
+
+
+def plane_sum_kernel(sources, passed, *refs):
     outs = refs[sources + passed :]
     height = 0
     for out_ref in outs[: len(outs) - passed]:
-        heights = pl.ds(height, out_ref.shape[0])
-        out_ref[...] = sum(ref[heights] for ref in refs[:sources])
-        if spare:
-            rows = pl.ds(out_ref.shape[1] - spare, spare)
-            out_ref[:, rows, :] = refs[1][heights, rows, :]
+        out_ref[...] = sum(ref[pl.ds(height, out_ref.shape[0])] for ref in refs[:sources])
         height += out_ref.shape[0]
     for i in range(passed):
         outs[len(outs) - passed + i][...] = refs[sources + i][...]
 
 
-def plane_sum(parts, passed, spare, cuts, name):
+def plane_sum(parts, passed, cuts, name):
     rest = parts[0].shape[1:]
     out = pl.pallas_call(
-        functools.partial(plane_sum_kernel, spare, len(parts), len(passed)),
+        functools.partial(plane_sum_kernel, len(parts), len(passed)),
         out_shape=[jax.ShapeDtypeStruct((cut,) + rest, jnp.float32) for cut in cuts]
         + [jax.ShapeDtypeStruct(array.shape, array.dtype) for array in passed],
         compiler_params=pltpu.CompilerParams(vmem_limit_bytes=16 * 1024 * 1024),
@@ -454,6 +484,30 @@
     return out[: len(cuts)], *out[len(cuts) :]
 
 
+def last_sum_kernel(sources, spare, kept_ref, received_ref, *refs):
+    parts, outs = refs[:sources], refs[sources:]
+    rows = kept_ref.shape[1]
+    outs[0][...] = kept_ref[0] + received_ref[0]
+    outs[2][0:rows, :] = kept_ref[1] + received_ref[1]
+    for height, out_ref in enumerate(outs[1:]):
+        first = out_ref.shape[0] - parts[0].shape[1]
+        out_ref[first:, :] = sum(ref[height] for ref in parts)
+        out_ref[out_ref.shape[0] - spare :, :] = parts[1][height, parts[1].shape[1] - spare :, :]
+
+
+def last_sum(kept, received, parts, spare):
+    heights, rows, columns = parts[0].shape
+    part = jax.ShapeDtypeStruct((rows, columns), jnp.float32)
+    both = jax.ShapeDtypeStruct((kept.shape[1] + rows, columns), jnp.float32)
+    return pl.pallas_call(
+        functools.partial(last_sum_kernel, len(parts), spare),
+        out_shape=[jax.ShapeDtypeStruct(kept.shape[1:], jnp.float32), part, both]
+        + [part] * (heights - 2),
+        compiler_params=pltpu.CompilerParams(vmem_limit_bytes=16 * 1024 * 1024),
+        name="last_sum",
+    )(kept, received, *parts)
+
+
 def to_relative(block, core, pair, last, rest):
     groups, members = lax.axis_size("ca"), lax.axis_size("fe")
     flip = (2 * pair + core) * members + 2 * rest + last
@@ -488,14 +542,15 @@
     return total
 
 
-def update_kernel(firsts, seconds, *refs):
-    first_refs, second_refs = refs[:firsts], refs[firsts : firsts + seconds]
-    own_ref, stress_ref, resistance_ref, weights_ref, table_ref = refs[firsts + seconds : -2]
+def update_kernel(heights, *refs):
+    first_ref, second_refs = refs[0], refs[1 : 1 + heights]
+    own_ref, stress_ref, resistance_ref, weights_ref, table_ref = refs[1 + heights : -2]
     stress_out_ref, nodal_ref = refs[-2:]
     elements = stress_ref.shape[2]
+    rows, second_rows = first_ref.shape[0], second_refs[0].shape[0]
     gathered = [
-        sum(ref[0, :, 0:elements] for ref in chunk_refs)
-        for chunk_refs in (first_refs, second_refs)
+        first_ref[:, 0:elements] + second_refs[1][0:rows, 0:elements],
+        sum(ref[ref.shape[0] - second_rows :, 0:elements] for ref in second_refs),
     ]
     counted = 9 * CHUNKS[1][1]
     counts = gathered[1][counted : counted + 1]
@@ -527,7 +582,7 @@
     upper = jnp.zeros((3, COLUMNS), jnp.float32)
     for flip, ref in enumerate(second_refs):
         wanted = (height ^ flip) == above
-        upper = upper + jnp.where(wanted, ref[0, ref.shape[1] - 3 :, :], 0.0)
+        upper = upper + jnp.where(wanted, ref[ref.shape[0] - 3 :, :], 0.0)
     values = jnp.where(
         upper_corner,
         jnp.concatenate(
@@ -637,14 +692,14 @@
         dtype=jnp.float32,
     )
     return pl.pallas_call(
-        functools.partial(update_kernel, len(first), len(second)),
+        functools.partial(update_kernel, len(second)),
         out_shape=(
             jax.ShapeDtypeStruct(stress_old.shape, jnp.float32),
             jax.ShapeDtypeStruct((2,) + own.shape, jnp.float32),
         ),
         compiler_params=pltpu.CompilerParams(vmem_limit_bytes=8 * 1024 * 1024),
         name="stress_update",
-    )(*first, *second, own, stress_old, resistance, quad_weights, table)
+    )(first, *second, own, stress_old, resistance, quad_weights, table)
 
 
 def body(
@@ -664,35 +719,25 @@
     labels = jnp.where(brick_active > 0, owner * COLUMNS + brick_element, -1).reshape(1, bricks)
     per_octant = grain_ids.shape[0] // 8
     table = rotation_table(euler_angles)
-    split, send, labels, ids = cell_sums(CHUNKS[0], per_octant, grain_ids, labels, table, half)
+    labels, send, split, ids = cell_sums(CHUNKS[0], per_octant, grain_ids, labels, table, half)
     keep, labels = brick_sums(split, labels, half)
     core_a, labels, own = core_sum(
-        keep, across_cores(send), displacement, labels, 0, "core_sum_a"
+        keep, across_cores(send), [labels, displacement], "core_sum_a"
     )
-    split, send, labels = cell_sums(CHUNKS[1], per_octant, ids, labels, table, half)
-    heights = lax.axis_size("fe") // 2
-    flip = heights // 2
-    (kept, sent), labels, send = plane_sum(
-        across_plane(core_a), [labels, send], 0, [flip, flip], "plane_sum_a"
+    send, keep = cell_sums(CHUNKS[1], per_octant, ids, labels, table, half)
+    flip = lax.axis_size("fe") // 4
+    (kept, sent), own, send = plane_sum(
+        across_plane(core_a), [own, send], [flip, flip], "plane_sum_a"
     )
     received = to_relative(sent, 0, 0, 0, flip)
-    keep, labels = brick_sums(split, labels, half)
-    core_b, labels, own = core_sum(keep, across_cores(send), own, labels, 3, "core_sum_b")
-    plane_b = across_plane(core_b)
-    while flip > 1:
+    core_b = last_core_sum(keep, across_cores(send), own)
+    while flip > 2:
         flip //= 2
-        (kept, sent), labels = plane_sum(
-            [kept, received], [labels], 0, [flip, flip], "height_sum_a"
-        )
+        (kept, sent) = plane_sum([kept, received], [], [flip, flip], "height_sum_a")[0]
         received = to_relative(sent, 0, 0, 0, flip)
-    plane_b, labels = plane_sum(plane_b, [labels], 3, [1] * heights, "plane_sum_b")
+    first, *second = last_sum(kept, received, across_plane(core_b), 3)
     stress_new, nodal = element_update(
-        [kept, received],
-        across_height(plane_b),
-        displacement,
-        stress_old,
-        resistance,
-        quad_weights,
+        first, across_height(second), displacement, stress_old, resistance, quad_weights
     )
     forces = nodal[0] + passed_along(nodal[1], "fe", 1)
     return (stress_new, forces)

time: 70.7 us -> 68.9 us (0.975)
  Pallas kernels: 35.1 us -> 32.2 us
  waiting for transfers between devices: 11.6 us -> 13.3 us
    ppermute x11 -> x10, waiting for transfers between devices: 10.3 us -> 12 us  [to_relative(): lax.ppermute(block, ('ca', 'fe'), [(i, i ^ flip) for i in range(groups *...]
    pallas_call x6 -> x5, Pallas kernels: 3.17 us -> 1.99 us  [the longest x1 1.69 us: element_update(): pl.pallas_call(functools.partial(update_kernel, len(second)), out_shape=(...]
    pallas_call x2 -> x1, Pallas kernels: 3.16 us -> 2.11 us  [brick_sums(): pl.pallas_call(brick_sum_kernel, out_shape=[jax.ShapeDtypeStruct((places,...]
    ppermute x11 -> x10, starting transfers between devices: 15.7 us -> 15.1 us  [to_relative(): lax.ppermute(block, ('ca', 'fe'), [(i, i ^ flip) for i in range(groups *...]
  transfers between devices with their start and end apart: 14 -> 13, of which waited for: 7 -> 7; matrix products, arithmetic and copies ran while one was open for 0% -> 0% of each run, Pallas kernels for 17% -> 14%
where the time goes in v11:
time: 68.9 us; the launch traced here: 68.7 us
  Pallas kernels  32.2 us (47%)
  starting transfers between devices  18.7 us (27%)
  waiting for transfers between devices  13.3 us (19%)
  local copies, waits for them, and re-layouts  2.34 us (3%)
  other arithmetic  1.32 us (2%)
  between operations  0.79 us (1%)
    pallas_call x2, Pallas kernels, cell_sums(): pl.pallas_call(functools.partial(cell_sum_kernel, octants, per_octant), o...  28 us
    ppermute x10, starting transfers between devices, to_relative(): lax.ppermute(block, ('ca', 'fe'), [(i, i ^ flip) for i in range(groups *...  15.1 us
    ppermute x10, waiting for transfers between devices, to_relative(): lax.ppermute(block, ('ca', 'fe'), [(i, i ^ flip) for i in range(groups *...  12 us
    ppermute x1, starting transfers between devices, passed_along(): return lax.ppermute(block, axis, route)  3.01 us
    unnamed x14, local copies, waits for them, and re-layouts  2.34 us
    pallas_call x1, Pallas kernels, brick_sums(): pl.pallas_call(brick_sum_kernel, out_shape=[jax.ShapeDtypeStruct((places,...  2.11 us
    pallas_call x1, Pallas kernels, element_update(): pl.pallas_call(functools.partial(update_kernel, len(second)), out_shape=(...  1.69 us
  transfers between devices with their start and end apart: 13, of which 7 were waited for; matrix products, arithmetic and copies ran while one was open for 0% of the time, Pallas kernels for 14%

profile of v11, /device:TPU:0, one launch (start us, length us, event | category | flops | bytes accessed | tf_op | source)
XLA Modules:
  0.0 68.7 jit_solution(11038980970655090762)
XLA Ops:
  0.6 0.8 %copy-done.1 = f32[3,4096]{1,0:T(4,128)S(1)} copy-done((f32[3,4096]{1,0:T(4,128)S(1)}, f32[3,4096]{1,0:T(4,128)}, u32[]{:S(2)}) %copy-start.1) | copy-done | bytes 49176
  1.5 0.2 rotation_table.1.table_ref
  1.6 0.7 %add_select_fusion = s32[2048]{0:T(1024)S(1)} fusion(s32[2048]{0:T(1024)} %param.14, s32[2048]{0:T(1024)} %bitcast.15, s32[2048]{0:T(1024)} %param.12), kind=kLoop, calls=%fused_computation | loop fusion | flops 8192 | bytes 32768 | tf_op jit(solution)/shard_map/jit(_where)/select_n | solution.py:719
  2.4 1.5 %copy-done.6 = s32[216,2048]{1,0:T(8,128)S(1)} copy-done((s32[216,2048]{1,0:T(8,128)S(1)}, s32[216,2048]{1,0:T(8,128)}, u32[]{:S(2)}) %copy-start.6) | copy-done | bytes 1769496
  3.9 20.3 %cell_sums.2 = (s32[1,2048]{1,0:T(1,128)S(1)}, f32[16,56,256]{2,1,0:T(8,128)S(1)}, bf16[112,2048]{1,0:T(8,128)(2,1)S(1)}, s32[56,2048]{1,0:T(8,128)S(1)}) custom-call(s32[216,2048]{1,0:T(8,128)S(1)} %copy-done.6, s32[1,2048]{1,0:T(1,128)S(1)} %bitcast.14, s32[48,8,128]{2,1,0:T(8,128)S(1)} %rotation_table.1.table_ref), custom_call_target="tpu_custom_call" | custom-call | flops 24000000000 | bytes 60000000 | tf_op jit(solution)/shard_map/cell_sums/pallas_call | solution.py:378
  24.2 0.5 collective-permute-start
  24.7 2.1 %brick_sums.1 = (f32[16,56,256]{2,1,0:T(8,128)S(1)}, s32[1,2048]{1,0:T(1,128)S(1)}) custom-call(bf16[112,2048]{1,0:T(8,128)(2,1)S(1)} %get-tuple-element.31.split_ref, s32[1,2048]{1,0:T(1,128)S(1)} %get-tuple-element.32.label_ref), custom_call_target="tpu_custom_call" | custom-call | flops 1680000000 | bytes 5600000 | tf_op jit(solution)/shard_map/brick_sums/pallas_call | solution.py:408
  26.9 0.1 core_sum_a.1
  27.0 2.9 %collective-permute-start.1 = (f32[4,56,256]{2,1,0:T(8,128)S(1)}, f32[4,56,256]{2,1,0:T(8,128)S(1)}, u32[]{:S(2)}, u32[]{:S(2)}) collective-permute-start(f32[4,56,256]{2,1,0:T(8,128)S(1)} %get-tuple-element.37), channel_id=1, source_target_pairs={{0,1},{1,0},{2,3},{3,2},{4,5},{5,4},{6,7},{7,6},{8,9},{9,8},{10,11... | collective-permute-start | bytes 688136 | tf_op jit(solution)/shard_map/ppermute | solution.py:514
  29.9 1.5 %collective-permute-start.2 = (f32[4,56,256]{2,1,0:T(8,128)S(1)}, f32[4,56,256]{2,1,0:T(8,128)S(1)}, u32[]{:S(2)}, u32[]{:S(2)}) collective-permute-start(f32[4,56,256]{2,1,0:T(8,128)S(1)} %get-tuple-element.38), channel_id=1, source_target_pairs={{0,16},{1,17},{2,18},{3,19},{4,20},{5,21},{6,22},{7,23},{8,24},{9,... | collective-permute-start | bytes 688136 | tf_op jit(solution)/shard_map/ppermute | solution.py:514
  31.4 0.0 collective-permute-start.3
  31.4 7.6 %cell_sums.3 = (f32[16,24,256]{2,1,0:T(8,128)S(1)}, f32[16,24,256]{2,1,0:T(8,128)S(1)}) custom-call(s32[56,2048]{1,0:T(8,128)S(1)} %get-tuple-element.41.ids_ref, s32[1,2048]{1,0:T(1,128)S(1)} %get-tuple-element.42.label_ref, s32[48,8,128]{2,1,0:T(8,128)S(1)} %rotation_table.1.table_ref), custom_call_target="tpu_custom_call" | custom-call | flops 8000000000 | bytes 20000000 | tf_op jit(solution)/shard_map/cell_sums/pallas_call | solution.py:378
  39.1 3.1 %collective-permute-done.2.refs_2_ = f32[4,56,256]{2,1,0:T(8,128)S(1)} collective-permute-done((f32[4,56,256]{2,1,0:T(8,128)S(1)}, f32[4,56,256]{2,1,0:T(8,128)S(1)}, u32[]{:S(2)}, u32[]{:S(2)}) %collective-permute-start.2) | collective-permute-done | bytes 229408 | tf_op jit(solution)/shard_map/ppermute | solution.py:514
  42.2 0.1 plane_sum_a.1
  42.3 0.1 collective-permute-start.5
  42.3 2.6 %collective-permute-start.4 = (f32[2,56,256]{2,1,0:T(8,128)S(1)}, f32[2,56,256]{2,1,0:T(8,128)S(1)}, u32[]{:S(2)}, u32[]{:S(2)}) collective-permute-start(f32[2,56,256]{2,1,0:T(8,128)S(1)} %get-tuple-element.45), channel_id=1, source_target_pairs={{0,4},{1,5},{2,6},{3,7},{4,0},{5,1},{6,2},{7,3},{8,12},{9,13},{10,... | collective-permute-start | bytes 344072 | tf_op jit(solution)/shard_map/ppermute | solution.py:514
  45.0 0.1 core_sum_b.1
  45.1 1.3 %collective-permute-start.6 = (f32[4,24,256]{2,1,0:T(8,128)S(1)}, f32[4,24,256]{2,1,0:T(8,128)S(1)}, u32[]{:S(2)}, u32[]{:S(2)}) collective-permute-start(f32[4,24,256]{2,1,0:T(8,128)S(1)} %get-tuple-element.50), channel_id=1, source_target_pairs={{0,1},{1,0},{2,3},{3,2},{4,5},{5,4},{6,7},{7,6},{8,9},{9,8},{10,11... | collective-permute-start | bytes 294920 | tf_op jit(solution)/shard_map/ppermute | solution.py:514
  46.4 0.8 %collective-permute-start.7 = (f32[4,24,256]{2,1,0:T(8,128)S(1)}, f32[4,24,256]{2,1,0:T(8,128)S(1)}, u32[]{:S(2)}, u32[]{:S(2)}) collective-permute-start(f32[4,24,256]{2,1,0:T(8,128)S(1)} %get-tuple-element.51), channel_id=1, source_target_pairs={{0,16},{1,17},{2,18},{3,19},{4,20},{5,21},{6,22},{7,23},{8,24},{9,... | collective-permute-start | bytes 294920 | tf_op jit(solution)/shard_map/ppermute | solution.py:514
  47.2 1.4 %collective-permute-start.8 = (f32[4,24,256]{2,1,0:T(8,128)S(1)}, f32[4,24,256]{2,1,0:T(8,128)S(1)}, u32[]{:S(2)}, u32[]{:S(2)}) collective-permute-start(f32[4,24,256]{2,1,0:T(8,128)S(1)} %get-tuple-element.52), channel_id=1, source_target_pairs={{0,17},{1,16},{2,19},{3,18},{4,21},{5,20},{6,23},{7,22},{8,25},{9,... | collective-permute-start | bytes 294920 | tf_op jit(solution)/shard_map/ppermute | solution.py:514
  48.6 2.6 %collective-permute-done.4.received_ref = f32[2,56,256]{2,1,0:T(8,128)S(1)} collective-permute-done((f32[2,56,256]{2,1,0:T(8,128)S(1)}, f32[2,56,256]{2,1,0:T(8,128)S(1)}, u32[]{:S(2)}, u32[]{:S(2)}) %collective-permute-start.4) | collective-permute-done | bytes 114720 | tf_op jit(solution)/shard_map/ppermute | solution.py:514
  51.3 0.6 collective-permute-done.7.refs_2_
  51.9 1.2 %collective-permute-done.8.refs_3_ = f32[4,24,256]{2,1,0:T(8,128)S(1)} collective-permute-done((f32[4,24,256]{2,1,0:T(8,128)S(1)}, f32[4,24,256]{2,1,0:T(8,128)S(1)}, u32[]{:S(2)}, u32[]{:S(2)}) %collective-permute-start.8) | collective-permute-done | bytes 98336 | tf_op jit(solution)/shard_map/ppermute | solution.py:514
  53.1 1.6 %collective-permute-start.9 = (f32[80,256]{1,0:T(8,128)S(1)}, f32[80,256]{1,0:T(8,128)S(1)}, u32[]{:S(2)}, u32[]{:S(2)}) collective-permute-start(f32[80,256]{1,0:T(8,128)S(1)} %get-tuple-element.55), channel_id=1, source_target_pairs={{0,2},{1,3},{2,0},{3,1},{4,6},{5,7},{6,4},{7,5},{8,10},{9,11},{10,... | collective-permute-start | bytes 245768 | tf_op jit(solution)/shard_map/ppermute | solution.py:514
  54.8 1.6 %collective-permute-start.10 = (f32[24,256]{1,0:T(8,128)S(1)}, f32[24,256]{1,0:T(8,128)S(1)}, u32[]{:S(2)}, u32[]{:S(2)}) collective-permute-start(f32[24,256]{1,0:T(8,128)S(1)} %get-tuple-element.56), channel_id=1, source_target_pairs={{0,4},{1,5},{2,6},{3,7},{4,0},{5,1},{6,2},{7,3},{8,12},{9,13},{10,... | collective-permute-start | bytes 73736 | tf_op jit(solution)/shard_map/ppermute | solution.py:514
  56.4 1.2 %collective-permute-start.11 = (f32[24,256]{1,0:T(8,128)S(1)}, f32[24,256]{1,0:T(8,128)S(1)}, u32[]{:S(2)}, u32[]{:S(2)}) collective-permute-start(f32[24,256]{1,0:T(8,128)S(1)} %get-tuple-element.57), channel_id=1, source_target_pairs={{0,6},{1,7},{2,4},{3,5},{4,2},{5,3},{6,0},{7,1},{8,14},{9,15},{10,... | collective-permute-start | bytes 73736 | tf_op jit(solution)/shard_map/ppermute | solution.py:514
  57.6 2.3 %collective-permute-done.10.refs_3_ = f32[24,256]{1,0:T(8,128)S(1)} collective-permute-done((f32[24,256]{1,0:T(8,128)S(1)}, f32[24,256]{1,0:T(8,128)S(1)}, u32[]{:S(2)}, u32[]{:S(2)}) %collective-permute-start.10) | collective-permute-done | bytes 24608 | tf_op jit(solution)/shard_map/ppermute | solution.py:514
  59.9 2.1 %collective-permute-done.11.refs_4_ = f32[24,256]{1,0:T(8,128)S(1)} collective-permute-done((f32[24,256]{1,0:T(8,128)S(1)}, f32[24,256]{1,0:T(8,128)S(1)}, u32[]{:S(2)}, u32[]{:S(2)}) %collective-permute-start.11) | collective-permute-done | bytes 24608 | tf_op jit(solution)/shard_map/ppermute | solution.py:514
  62.1 1.7 %stress_update.1 = (f32[6,8,225]{2,1,0:T(8,128)}, f32[2,3,1,256]{3,2,1,0:T(1,128)S(1)}) custom-call(f32[56,256]{1,0:T(8,128)S(1)} %get-tuple-element.53.refs_0_, f32[24,256]{1,0:T(8,128)S(1)} %get-tuple-element.54.refs_1_, f32[80,256]{1,0:T(8,128)S(1)} %collective-permute-done.9.refs_2_, f32[24,256]{1,0:T(8,128)S(1)} %collective-permute-done.10.refs_3_, ...), custom_call_target="tpu_custom_call" | custom-call | tf_op jit(solution)/shard_map/stress_update/pallas_call | solution.py:694
  63.8 3.0 %collective-permute-start.12 = (f32[3,1,256]{2,1,0:T(1,128)S(1)}, f32[3,1,256]{2,1,0:T(1,128)S(1)}, u32[]{:S(2)}, u32[]{:S(2)}) collective-permute-start(f32[3,1,256]{2,1,0:T(1,128)S(1)} %slice_bitcast_fusion), channel_id=1, source_target_pairs={{0,1},{1,2},{2,3},{3,4},{4,5},{5,6},{6,7},{8,9},{9,10},{10,11},{11... | collective-permute-start | bytes 9224 | tf_op jit(solution)/shard_map/ppermute | solution.py:48
  66.8 1.3 %collective-permute-done.12 = f32[3,1,256]{2,1,0:T(1,128)S(1)} collective-permute-done((f32[3,1,256]{2,1,0:T(1,128)S(1)}, f32[3,1,256]{2,1,0:T(1,128)S(1)}, u32[]{:S(2)}, u32[]{:S(2)}) %collective-permute-start.12) | collective-permute-done | bytes 3104 | tf_op jit(solution)/shard_map/ppermute | solution.py:48
  68.1 0.6 bitcast_add_fusion
  (20 shorter events, 0.1 us)
Async XLA Ops:
  0.6 0.8 %copy-start.1 = (f32[3,4096]{1,0:T(4,128)S(1)}, f32[3,4096]{1,0:T(4,128)}, u32[]{:S(2)}) copy-start(f32[3,4096]{1,0:T(4,128)} %euler_ref.1) | copy-start | bytes 147460
  2.4 1.5 %copy-start.6 = (s32[216,2048]{1,0:T(8,128)S(1)}, s32[216,2048]{1,0:T(8,128)}, u32[]{:S(2)}) copy-start(s32[216,2048]{1,0:T(8,128)} %ids_ref.1) | copy-start | bytes 5308420
  24.2 2.6 %collective-permute-start = (f32[16,56,256]{2,1,0:T(8,128)S(1)}, f32[16,56,256]{2,1,0:T(8,128)S(1)}, u32[]{:S(2)}, u32[]{:S(2)}) collective-permute-start(f32[16,56,256]{2,1,0:T(8,128)S(1)} %get-tuple-element.34), channel_id=1, source_target_pairs={{0,8},{8,0},{16,24},{24,16},{1,9},{9,1},{17,25},{25,17},{2,10},{10... | collective-permute-start | bytes 2752520 | tf_op jit(solution)/shard_map/ppermute | solution.py:317
  24.7 2.1 %copy-start.4 = (f32[3,1,256]{2,1,0:T(1,128)S(1)}, f32[3,1,256]{2,1,0:T(1,128)}, u32[]{:S(2)}) copy-start(f32[3,1,256]{2,1,0:T(1,128)} %refs_5_.1) | copy-start | bytes 9220
  27.0 12.1 %collective-permute-start.1 = (f32[4,56,256]{2,1,0:T(8,128)S(1)}, f32[4,56,256]{2,1,0:T(8,128)S(1)}, u32[]{:S(2)}, u32[]{:S(2)}) collective-permute-start(f32[4,56,256]{2,1,0:T(8,128)S(1)} %get-tuple-element.37), channel_id=1, source_target_pairs={{0,1},{1,0},{2,3},{3,2},{4,5},{5,4},{6,7},{7,6},{8,9},{9,8},{10,11... | collective-permute-start | bytes 688136 | tf_op jit(solution)/shard_map/ppermute | solution.py:514
  29.9 12.3 %collective-permute-start.2 = (f32[4,56,256]{2,1,0:T(8,128)S(1)}, f32[4,56,256]{2,1,0:T(8,128)S(1)}, u32[]{:S(2)}, u32[]{:S(2)}) collective-permute-start(f32[4,56,256]{2,1,0:T(8,128)S(1)} %get-tuple-element.38), channel_id=1, source_target_pairs={{0,16},{1,17},{2,18},{3,19},{4,20},{5,21},{6,22},{7,23},{8,24},{9,... | collective-permute-start | bytes 688136 | tf_op jit(solution)/shard_map/ppermute | solution.py:514
  31.4 10.8 %collective-permute-start.3 = (f32[4,56,256]{2,1,0:T(8,128)S(1)}, f32[4,56,256]{2,1,0:T(8,128)S(1)}, u32[]{:S(2)}, u32[]{:S(2)}) collective-permute-start(f32[4,56,256]{2,1,0:T(8,128)S(1)} %get-tuple-element.39), channel_id=1, source_target_pairs={{0,17},{1,16},{2,19},{3,18},{4,21},{5,20},{6,23},{7,22},{8,25},{9,... | collective-permute-start | bytes 688136 | tf_op jit(solution)/shard_map/ppermute | solution.py:514
  39.0 23.0 %copy-start = (f32[12,8,225]{2,1,0:T(8,128)S(1)}, f32[12,8,225]{2,1,0:T(8,128)}, u32[]{:S(2)}) copy-start(f32[12,8,225]{2,1,0:T(8,128)} %refs_7_.1) | copy-start | bytes 259204
  39.0 23.0 %copy-start.2 = (f32[6,8,225]{2,1,0:T(8,128)S(1)}, f32[6,8,225]{2,1,0:T(8,128)}, u32[]{:S(2)}) copy-start(f32[6,8,225]{2,1,0:T(8,128)} %refs_6_.1) | copy-start | bytes 129604
  39.1 23.0 %copy-start.3 = (f32[24,8]{1,0:T(8,128)S(1)}, f32[24,8]{1,0:T(8,128)}, u32[]{:S(2)}) copy-start(f32[24,8]{1,0:T(8,128)} %constant.8.clone.refs_9_) | copy-start | bytes 2308
  39.1 23.0 %copy-start.5 = (s32[8,225]{1,0:T(8,128)S(1)}, s32[8,225]{1,0:T(8,128)}, u32[]{:S(2)}) copy-start(s32[8,225]{1,0:T(8,128)} %refs_8_.1) | copy-start | bytes 21604
  42.3 2.7 %collective-permute-start.5 = (f32[16,24,256]{2,1,0:T(8,128)S(1)}, f32[16,24,256]{2,1,0:T(8,128)S(1)}, u32[]{:S(2)}, u32[]{:S(2)}) collective-permute-start(f32[16,24,256]{2,1,0:T(8,128)S(1)} %get-tuple-element.47), channel_id=1, source_target_pairs={{0,8},{8,0},{16,24},{24,16},{1,9},{9,1},{17,25},{25,17},{2,10},{10... | collective-permute-start | bytes 1179656 | tf_op jit(solution)/shard_map/ppermute | solution.py:317
  42.3 8.9 %collective-permute-start.4 = (f32[2,56,256]{2,1,0:T(8,128)S(1)}, f32[2,56,256]{2,1,0:T(8,128)S(1)}, u32[]{:S(2)}, u32[]{:S(2)}) collective-permute-start(f32[2,56,256]{2,1,0:T(8,128)S(1)} %get-tuple-element.45), channel_id=1, source_target_pairs={{0,4},{1,5},{2,6},{3,7},{4,0},{5,1},{6,2},{7,3},{8,12},{9,13},{10,... | collective-permute-start | bytes 344072 | tf_op jit(solution)/shard_map/ppermute | solution.py:514
  45.1 6.2 %collective-permute-start.6 = (f32[4,24,256]{2,1,0:T(8,128)S(1)}, f32[4,24,256]{2,1,0:T(8,128)S(1)}, u32[]{:S(2)}, u32[]{:S(2)}) collective-permute-start(f32[4,24,256]{2,1,0:T(8,128)S(1)} %get-tuple-element.50), channel_id=1, source_target_pairs={{0,1},{1,0},{2,3},{3,2},{4,5},{5,4},{6,7},{7,6},{8,9},{9,8},{10,11... | collective-permute-start | bytes 294920 | tf_op jit(solution)/shard_map/ppermute | solution.py:514
  46.4 5.5 %collective-permute-start.7 = (f32[4,24,256]{2,1,0:T(8,128)S(1)}, f32[4,24,256]{2,1,0:T(8,128)S(1)}, u32[]{:S(2)}, u32[]{:S(2)}) collective-permute-start(f32[4,24,256]{2,1,0:T(8,128)S(1)} %get-tuple-element.51), channel_id=1, source_target_pairs={{0,16},{1,17},{2,18},{3,19},{4,20},{5,21},{6,22},{7,23},{8,24},{9,... | collective-permute-start | bytes 294920 | tf_op jit(solution)/shard_map/ppermute | solution.py:514
  47.2 5.9 %collective-permute-start.8 = (f32[4,24,256]{2,1,0:T(8,128)S(1)}, f32[4,24,256]{2,1,0:T(8,128)S(1)}, u32[]{:S(2)}, u32[]{:S(2)}) collective-permute-start(f32[4,24,256]{2,1,0:T(8,128)S(1)} %get-tuple-element.52), channel_id=1, source_target_pairs={{0,17},{1,16},{2,19},{3,18},{4,21},{5,20},{6,23},{7,22},{8,25},{9,... | collective-permute-start | bytes 294920 | tf_op jit(solution)/shard_map/ppermute | solution.py:514
  53.1 8.9 %collective-permute-start.9 = (f32[80,256]{1,0:T(8,128)S(1)}, f32[80,256]{1,0:T(8,128)S(1)}, u32[]{:S(2)}, u32[]{:S(2)}) collective-permute-start(f32[80,256]{1,0:T(8,128)S(1)} %get-tuple-element.55), channel_id=1, source_target_pairs={{0,2},{1,3},{2,0},{3,1},{4,6},{5,7},{6,4},{7,5},{8,10},{9,11},{10,... | collective-permute-start | bytes 245768 | tf_op jit(solution)/shard_map/ppermute | solution.py:514
  54.8 5.1 %collective-permute-start.10 = (f32[24,256]{1,0:T(8,128)S(1)}, f32[24,256]{1,0:T(8,128)S(1)}, u32[]{:S(2)}, u32[]{:S(2)}) collective-permute-start(f32[24,256]{1,0:T(8,128)S(1)} %get-tuple-element.56), channel_id=1, source_target_pairs={{0,4},{1,5},{2,6},{3,7},{4,0},{5,1},{6,2},{7,3},{8,12},{9,13},{10,... | collective-permute-start | bytes 73736 | tf_op jit(solution)/shard_map/ppermute | solution.py:514
  56.4 5.6 %collective-permute-start.11 = (f32[24,256]{1,0:T(8,128)S(1)}, f32[24,256]{1,0:T(8,128)S(1)}, u32[]{:S(2)}, u32[]{:S(2)}) collective-permute-start(f32[24,256]{1,0:T(8,128)S(1)} %get-tuple-element.57), channel_id=1, source_target_pairs={{0,6},{1,7},{2,4},{3,5},{4,2},{5,3},{6,0},{7,1},{8,14},{9,15},{10,... | collective-permute-start | bytes 73736 | tf_op jit(solution)/shard_map/ppermute | solution.py:514
  63.8 4.3 %collective-permute-start.12 = (f32[3,1,256]{2,1,0:T(1,128)S(1)}, f32[3,1,256]{2,1,0:T(1,128)S(1)}, u32[]{:S(2)}, u32[]{:S(2)}) collective-permute-start(f32[3,1,256]{2,1,0:T(1,128)S(1)} %slice_bitcast_fusion), channel_id=1, source_target_pairs={{0,1},{1,2},{2,3},{3,4},{4,5},{5,6},{6,7},{8,9},{9,10},{10,11},{11... | collective-permute-start | bytes 9224 | tf_op jit(solution)/shard_map/ppermute | solution.py:48

commit v12 on v11

--- a/solution.py
+++ b/solution.py
@@ -80,7 +80,7 @@
     return cosine, sine * angle
 
 
-def rotation_words(euler):
+def rotation_coordinates(euler):
     cos_one, sin_one = cos_sin(0.5 * euler[0 : 0 + 1])
     cos_mid, sin_mid = cos_sin(0.5 * euler[1 : 1 + 1])
     cos_two, sin_two = cos_sin(0.5 * euler[2 : 2 + 1])
@@ -92,19 +92,17 @@
     x, y, z = [
         jnp.clip(jnp.round(value), -QUANTUM, QUANTUM).astype(jnp.int32) for value in (x, y, z)
     ]
-    return [lax.shift_left(x, 16) | (y & 0xFFFF), z & 0xFFFF]
+    return [x, y, z]
 
 
 def table_kernel(euler_ref, table_ref):
-    both, third = rotation_words(euler_ref[...])
-    rows = both.shape[1] // LANES
-    for row in range(rows):
-        table_ref[row] = jnp.broadcast_to(both[:, row * LANES : (row + 1) * LANES], (8, LANES))
-    for row in range(0, rows, 2):
-        word = third[:, row * LANES : (row + 1) * LANES] | lax.shift_left(
-            third[:, (row + 1) * LANES : (row + 2) * LANES], 16
-        )
-        table_ref[rows + row // 2] = jnp.broadcast_to(word, (8, LANES))
+    at = 0
+    for coordinate in rotation_coordinates(euler_ref[...]):
+        for row in range(0, coordinate.shape[1] // LANES, 2):
+            low = coordinate[:, row * LANES : (row + 1) * LANES]
+            high = coordinate[:, (row + 1) * LANES : (row + 2) * LANES]
+            table_ref[at] = jnp.broadcast_to(lax.shift_left(high, 16) | (low & 0xFFFF), (8, LANES))
+            at += 1
 
 
 def rotation_table(euler_angles):
@@ -140,19 +138,20 @@
     return jnp.where(bits[level], high, low)
 
 
-def rotation_coordinates(table_ref, table_rows, ids):
+def looked_up_words(table_ref, ids):
     lane = (ids & (LANES - 1))[:, :, None]
     row = lax.shift_right_logical(ids, 7)
-    bits = [(row & (1 << level)) != 0 for level in range(table_rows.bit_length() - 1)]
-    both = looked_up(table_ref, 0, table_rows, lane, bits)
-    third = looked_up(table_ref, table_rows, table_rows // 2, lane, bits[1:])
-    return both, lax.shift_left(third, lax.shift_left((row & 1) ^ 1, 4))
-
-
-def rotation_products(both, third):
-    x = lax.shift_right_arithmetic(both, 16).astype(jnp.float32)
-    y = lax.shift_right_arithmetic(lax.shift_left(both, 16), 16).astype(jnp.float32)
-    z = lax.shift_right_arithmetic(third, 16).astype(jnp.float32)
+    words = table_ref.shape[0] // 3
+    bits = [(row & (2 << level)) != 0 for level in range(words.bit_length() - 1)]
+    shift = lax.shift_left((row & 1) ^ 1, 4)
+    return [
+        lax.shift_left(looked_up(table_ref, words * axis, words, lane, bits), shift)
+        for axis in range(3)
+    ]
+
+
+def rotation_products(words):
+    x, y, z = [lax.shift_right_arithmetic(word, 16).astype(jnp.float32) for word in words]
     length = (x * x + y * y + z * z) * (0.5 / (QUANTUM * QUANTUM)) + 0.5
     scale = pl.reciprocal(length, approx=True)
     scale = scale * (2.0 - length * scale)
@@ -197,7 +196,6 @@
     else:
         send_ref, keep_ref, split_ref = refs[:-4]
         targets = [(send_ref.shape[0], send_ref), (0, keep_ref)]
-    table_rows = table_ref.shape[0] * 2 // 3
     groups = tile_ref.shape[1] // 8
     rows_left = count * per_octant - 8 * (groups - 1)
     turns = count // math.gcd(count, 8)
@@ -234,10 +232,10 @@
                 last = found
                 if group < groups:
                     ids = tile_ref[tile, pl.ds(8 * group, 8), :]
-                    found = rotation_coordinates(table_ref, table_rows, ids)
+                    found = looked_up_words(table_ref, ids)
                 if group == 0:
                     continue
-                products = rotation_products(*last)
+                products = rotation_products(last)
                 if group == groups and rows_left < 8:
                     there = lax.broadcasted_iota(jnp.int32, (8, LANES), 0) < rows_left
                     products = [jnp.where(there, value, 0.0) for value in products]
@@ -492,7 +490,7 @@
     for height, out_ref in enumerate(outs[1:]):
         first = out_ref.shape[0] - parts[0].shape[1]
         out_ref[first:, :] = sum(ref[height] for ref in parts)
-        out_ref[out_ref.shape[0] - spare :, :] = parts[1][height, parts[1].shape[1] - spare :, :]
+        out_ref[out_ref.shape[0] - spare :, :] = parts[-1][height, -spare:, :]
 
 
 def last_sum(kept, received, parts, spare):
@@ -516,7 +514,8 @@
 
 def across_plane(parts):
     return [parts[0]] + [
-        to_relative(parts[index], 0, index // 2, index % 2, 0) for index in range(1, len(parts))
+        to_relative(parts[index], 0, index // 2, index % 2, 0)
+        for index in range(len(parts) - 1, 0, -1)
     ]
 
 

time: 68.9 us -> 69 us (level)
  transfers between devices with their start and end apart: 13 -> 13, of which waited for: 7 -> 8; matrix products, arithmetic and copies ran while one was open for 0% -> 0% of each run, Pallas kernels for 14% -> 14%
where the time goes in v12:
time: 69 us; the launch traced here: 68.7 us
  Pallas kernels  32.2 us (47%)
  starting transfers between devices  19.1 us (28%)
  waiting for transfers between devices  13 us (19%)
  local copies, waits for them, and re-layouts  2.34 us (3%)
  other arithmetic  1.32 us (2%)
  between operations  0.79 us (1%)
    pallas_call x2, Pallas kernels, cell_sums(): pl.pallas_call(functools.partial(cell_sum_kernel, octants, per_octant), o...  27.9 us
    ppermute x10, starting transfers between devices, to_relative(): lax.ppermute(block, ('ca', 'fe'), [(i, i ^ flip) for i in range(groups *...  15.1 us
    ppermute x10, waiting for transfers between devices, to_relative(): lax.ppermute(block, ('ca', 'fe'), [(i, i ^ flip) for i in range(groups *...  11.7 us
    ppermute x1, starting transfers between devices, passed_along(): return lax.ppermute(block, axis, route)  3.39 us
    unnamed x14, local copies, waits for them, and re-layouts  2.34 us
    pallas_call x1, Pallas kernels, brick_sums(): pl.pallas_call(brick_sum_kernel, out_shape=[jax.ShapeDtypeStruct((places,...  2.11 us
    pallas_call x1, Pallas kernels, element_update(): pl.pallas_call(functools.partial(update_kernel, len(second)), out_shape=(...  1.7 us
  transfers between devices with their start and end apart: 13, of which 8 were waited for; matrix products, arithmetic and copies ran while one was open for 0% of the time, Pallas kernels for 14%

profile of v12, /device:TPU:0, one launch (start us, length us, event | category | flops | bytes accessed | tf_op | source)
XLA Modules:
  0.0 68.7 jit_solution(1533981885406296119)
XLA Ops:
  0.6 0.8 %copy-done.1 = f32[3,4096]{1,0:T(4,128)S(1)} copy-done((f32[3,4096]{1,0:T(4,128)S(1)}, f32[3,4096]{1,0:T(4,128)}, u32[]{:S(2)}) %copy-start.1) | copy-done | bytes 49176
  1.5 0.2 rotation_table.1.table_ref
  1.6 0.7 %add_select_fusion = s32[2048]{0:T(1024)S(1)} fusion(s32[2048]{0:T(1024)} %param.14, s32[2048]{0:T(1024)} %bitcast.15, s32[2048]{0:T(1024)} %param.12), kind=kLoop, calls=%fused_computation | loop fusion | flops 8192 | bytes 32768 | tf_op jit(solution)/shard_map/jit(_where)/select_n | solution.py:718
  2.4 1.5 %copy-done.6 = s32[216,2048]{1,0:T(8,128)S(1)} copy-done((s32[216,2048]{1,0:T(8,128)S(1)}, s32[216,2048]{1,0:T(8,128)}, u32[]{:S(2)}) %copy-start.6) | copy-done | bytes 1769496
  3.9 20.3 %cell_sums.2 = (s32[1,2048]{1,0:T(1,128)S(1)}, f32[16,56,256]{2,1,0:T(8,128)S(1)}, bf16[112,2048]{1,0:T(8,128)(2,1)S(1)}, s32[56,2048]{1,0:T(8,128)S(1)}) custom-call(s32[216,2048]{1,0:T(8,128)S(1)} %copy-done.6, s32[1,2048]{1,0:T(1,128)S(1)} %bitcast.14, s32[48,8,128]{2,1,0:T(8,128)S(1)} %rotation_table.1.table_ref), custom_call_target="tpu_custom_call" | custom-call | flops 24000000000 | bytes 60000000 | tf_op jit(solution)/shard_map/cell_sums/pallas_call | solution.py:376
  24.2 0.5 collective-permute-start
  24.7 2.1 %brick_sums.1 = (f32[16,56,256]{2,1,0:T(8,128)S(1)}, s32[1,2048]{1,0:T(1,128)S(1)}) custom-call(bf16[112,2048]{1,0:T(8,128)(2,1)S(1)} %get-tuple-element.31.split_ref, s32[1,2048]{1,0:T(1,128)S(1)} %get-tuple-element.32.label_ref), custom_call_target="tpu_custom_call" | custom-call | flops 1680000000 | bytes 5600000 | tf_op jit(solution)/shard_map/brick_sums/pallas_call | solution.py:406
  26.8 0.1 core_sum_a.1
  26.9 3.8 %collective-permute-start.1 = (f32[4,56,256]{2,1,0:T(8,128)S(1)}, f32[4,56,256]{2,1,0:T(8,128)S(1)}, u32[]{:S(2)}, u32[]{:S(2)}) collective-permute-start(f32[4,56,256]{2,1,0:T(8,128)S(1)} %get-tuple-element.37), channel_id=1, source_target_pairs={{0,17},{1,16},{2,19},{3,18},{4,21},{5,20},{6,23},{7,22},{8,25},{9,... | collective-permute-start | bytes 688136 | tf_op jit(solution)/shard_map/ppermute | solution.py:512
  30.8 0.5 collective-permute-start.2
  31.3 0.1 collective-permute-start.3
  31.4 7.6 %cell_sums.3 = (f32[16,24,256]{2,1,0:T(8,128)S(1)}, f32[16,24,256]{2,1,0:T(8,128)S(1)}) custom-call(s32[56,2048]{1,0:T(8,128)S(1)} %get-tuple-element.41.ids_ref, s32[1,2048]{1,0:T(1,128)S(1)} %get-tuple-element.42.label_ref, s32[48,8,128]{2,1,0:T(8,128)S(1)} %rotation_table.1.table_ref), custom_call_target="tpu_custom_call" | custom-call | flops 8000000000 | bytes 20000000 | tf_op jit(solution)/shard_map/cell_sums/pallas_call | solution.py:376
  39.1 2.6 %collective-permute-done.2.refs_2_ = f32[4,56,256]{2,1,0:T(8,128)S(1)} collective-permute-done((f32[4,56,256]{2,1,0:T(8,128)S(1)}, f32[4,56,256]{2,1,0:T(8,128)S(1)}, u32[]{:S(2)}, u32[]{:S(2)}) %collective-permute-start.2) | collective-permute-done | bytes 229408 | tf_op jit(solution)/shard_map/ppermute | solution.py:512
  41.6 0.3 collective-permute-done.3.refs_3_
  41.9 0.1 plane_sum_a.1
  42.0 0.1 collective-permute-start.5
  42.1 2.7 %collective-permute-start.4 = (f32[2,56,256]{2,1,0:T(8,128)S(1)}, f32[2,56,256]{2,1,0:T(8,128)S(1)}, u32[]{:S(2)}, u32[]{:S(2)}) collective-permute-start(f32[2,56,256]{2,1,0:T(8,128)S(1)} %get-tuple-element.45), channel_id=1, source_target_pairs={{0,4},{1,5},{2,6},{3,7},{4,0},{5,1},{6,2},{7,3},{8,12},{9,13},{10,... | collective-permute-start | bytes 344072 | tf_op jit(solution)/shard_map/ppermute | solution.py:512
  44.8 1.7 %collective-permute-start.6 = (f32[4,24,256]{2,1,0:T(8,128)S(1)}, f32[4,24,256]{2,1,0:T(8,128)S(1)}, u32[]{:S(2)}, u32[]{:S(2)}) collective-permute-start(f32[4,24,256]{2,1,0:T(8,128)S(1)} %get-tuple-element.50), channel_id=1, source_target_pairs={{0,17},{1,16},{2,19},{3,18},{4,21},{5,20},{6,23},{7,22},{8,25},{9,... | collective-permute-start | bytes 294920 | tf_op jit(solution)/shard_map/ppermute | solution.py:512
  46.5 1.3 %collective-permute-start.7 = (f32[4,24,256]{2,1,0:T(8,128)S(1)}, f32[4,24,256]{2,1,0:T(8,128)S(1)}, u32[]{:S(2)}, u32[]{:S(2)}) collective-permute-start(f32[4,24,256]{2,1,0:T(8,128)S(1)} %get-tuple-element.51), channel_id=1, source_target_pairs={{0,16},{1,17},{2,18},{3,19},{4,20},{5,21},{6,22},{7,23},{8,24},{9,... | collective-permute-start | bytes 294920 | tf_op jit(solution)/shard_map/ppermute | solution.py:512
  47.8 0.5 collective-permute-start.8
  48.4 2.6 %collective-permute-done.4.received_ref = f32[2,56,256]{2,1,0:T(8,128)S(1)} collective-permute-done((f32[2,56,256]{2,1,0:T(8,128)S(1)}, f32[2,56,256]{2,1,0:T(8,128)S(1)}, u32[]{:S(2)}, u32[]{:S(2)}) %collective-permute-start.4) | collective-permute-done | bytes 114720 | tf_op jit(solution)/shard_map/ppermute | solution.py:512
  51.0 0.1 collective-permute-done.6.refs_1_
  51.1 1.6 %collective-permute-done.7.refs_2_ = f32[4,24,256]{2,1,0:T(8,128)S(1)} collective-permute-done((f32[4,24,256]{2,1,0:T(8,128)S(1)}, f32[4,24,256]{2,1,0:T(8,128)S(1)}, u32[]{:S(2)}, u32[]{:S(2)}) %collective-permute-start.7) | collective-permute-done | bytes 98336 | tf_op jit(solution)/shard_map/ppermute | solution.py:512
  52.8 1.6 %collective-permute-start.9 = (f32[80,256]{1,0:T(8,128)S(1)}, f32[80,256]{1,0:T(8,128)S(1)}, u32[]{:S(2)}, u32[]{:S(2)}) collective-permute-start(f32[80,256]{1,0:T(8,128)S(1)} %get-tuple-element.55), channel_id=1, source_target_pairs={{0,2},{1,3},{2,0},{3,1},{4,6},{5,7},{6,4},{7,5},{8,10},{9,11},{10,... | collective-permute-start | bytes 245768 | tf_op jit(solution)/shard_map/ppermute | solution.py:512
  54.4 1.6 %collective-permute-start.10 = (f32[24,256]{1,0:T(8,128)S(1)}, f32[24,256]{1,0:T(8,128)S(1)}, u32[]{:S(2)}, u32[]{:S(2)}) collective-permute-start(f32[24,256]{1,0:T(8,128)S(1)} %get-tuple-element.56), channel_id=1, source_target_pairs={{0,4},{1,5},{2,6},{3,7},{4,0},{5,1},{6,2},{7,3},{8,12},{9,13},{10,... | collective-permute-start | bytes 73736 | tf_op jit(solution)/shard_map/ppermute | solution.py:512
  56.1 1.2 %collective-permute-start.11 = (f32[24,256]{1,0:T(8,128)S(1)}, f32[24,256]{1,0:T(8,128)S(1)}, u32[]{:S(2)}, u32[]{:S(2)}) collective-permute-start(f32[24,256]{1,0:T(8,128)S(1)} %get-tuple-element.57), channel_id=1, source_target_pairs={{0,6},{1,7},{2,4},{3,5},{4,2},{5,3},{6,0},{7,1},{8,14},{9,15},{10,... | collective-permute-start | bytes 73736 | tf_op jit(solution)/shard_map/ppermute | solution.py:512
  57.3 2.1 %collective-permute-done.10.refs_3_ = f32[24,256]{1,0:T(8,128)S(1)} collective-permute-done((f32[24,256]{1,0:T(8,128)S(1)}, f32[24,256]{1,0:T(8,128)S(1)}, u32[]{:S(2)}, u32[]{:S(2)}) %collective-permute-start.10) | collective-permute-done | bytes 24608 | tf_op jit(solution)/shard_map/ppermute | solution.py:512
  59.3 2.4 %collective-permute-done.11.refs_4_ = f32[24,256]{1,0:T(8,128)S(1)} collective-permute-done((f32[24,256]{1,0:T(8,128)S(1)}, f32[24,256]{1,0:T(8,128)S(1)}, u32[]{:S(2)}, u32[]{:S(2)}) %collective-permute-start.11) | collective-permute-done | bytes 24608 | tf_op jit(solution)/shard_map/ppermute | solution.py:512
  61.7 1.7 %stress_update.1 = (f32[6,8,225]{2,1,0:T(8,128)}, f32[2,3,1,256]{3,2,1,0:T(1,128)S(1)}) custom-call(f32[56,256]{1,0:T(8,128)S(1)} %get-tuple-element.53.refs_0_, f32[24,256]{1,0:T(8,128)S(1)} %get-tuple-element.54.refs_1_, f32[80,256]{1,0:T(8,128)S(1)} %collective-permute-done.9.refs_2_, f32[24,256]{1,0:T(8,128)S(1)} %collective-permute-done.10.refs_3_, ...), custom_call_target="tpu_custom_call" | custom-call | tf_op jit(solution)/shard_map/stress_update/pallas_call | solution.py:693
  63.4 3.4 %collective-permute-start.12 = (f32[3,1,256]{2,1,0:T(1,128)S(1)}, f32[3,1,256]{2,1,0:T(1,128)S(1)}, u32[]{:S(2)}, u32[]{:S(2)}) collective-permute-start(f32[3,1,256]{2,1,0:T(1,128)S(1)} %slice_bitcast_fusion), channel_id=1, source_target_pairs={{0,1},{1,2},{2,3},{3,4},{4,5},{5,6},{6,7},{8,9},{9,10},{10,11},{11... | collective-permute-start | bytes 9224 | tf_op jit(solution)/shard_map/ppermute | solution.py:48
  66.8 1.3 %collective-permute-done.12 = f32[3,1,256]{2,1,0:T(1,128)S(1)} collective-permute-done((f32[3,1,256]{2,1,0:T(1,128)S(1)}, f32[3,1,256]{2,1,0:T(1,128)S(1)}, u32[]{:S(2)}, u32[]{:S(2)}) %collective-permute-start.12) | collective-permute-done | bytes 3104 | tf_op jit(solution)/shard_map/ppermute | solution.py:48
  68.1 0.6 bitcast_add_fusion
  (20 shorter events, 0.2 us)
Async XLA Ops:
  0.6 0.8 %copy-start.1 = (f32[3,4096]{1,0:T(4,128)S(1)}, f32[3,4096]{1,0:T(4,128)}, u32[]{:S(2)}) copy-start(f32[3,4096]{1,0:T(4,128)} %euler_ref.1) | copy-start | bytes 147460
  2.4 1.5 %copy-start.6 = (s32[216,2048]{1,0:T(8,128)S(1)}, s32[216,2048]{1,0:T(8,128)}, u32[]{:S(2)}) copy-start(s32[216,2048]{1,0:T(8,128)} %ids_ref.1) | copy-start | bytes 5308420
  24.2 2.6 %collective-permute-start = (f32[16,56,256]{2,1,0:T(8,128)S(1)}, f32[16,56,256]{2,1,0:T(8,128)S(1)}, u32[]{:S(2)}, u32[]{:S(2)}) collective-permute-start(f32[16,56,256]{2,1,0:T(8,128)S(1)} %get-tuple-element.34), channel_id=1, source_target_pairs={{0,8},{8,0},{16,24},{24,16},{1,9},{9,1},{17,25},{25,17},{2,10},{10... | collective-permute-start | bytes 2752520 | tf_op jit(solution)/shard_map/ppermute | solution.py:315
  24.7 2.1 %copy-start.4 = (f32[3,1,256]{2,1,0:T(1,128)S(1)}, f32[3,1,256]{2,1,0:T(1,128)}, u32[]{:S(2)}) copy-start(f32[3,1,256]{2,1,0:T(1,128)} %refs_5_.1) | copy-start | bytes 9220
  26.9 12.1 %collective-permute-start.1 = (f32[4,56,256]{2,1,0:T(8,128)S(1)}, f32[4,56,256]{2,1,0:T(8,128)S(1)}, u32[]{:S(2)}, u32[]{:S(2)}) collective-permute-start(f32[4,56,256]{2,1,0:T(8,128)S(1)} %get-tuple-element.37), channel_id=1, source_target_pairs={{0,17},{1,16},{2,19},{3,18},{4,21},{5,20},{6,23},{7,22},{8,25},{9,... | collective-permute-start | bytes 688136 | tf_op jit(solution)/shard_map/ppermute | solution.py:512
  30.8 10.9 %collective-permute-start.2 = (f32[4,56,256]{2,1,0:T(8,128)S(1)}, f32[4,56,256]{2,1,0:T(8,128)S(1)}, u32[]{:S(2)}, u32[]{:S(2)}) collective-permute-start(f32[4,56,256]{2,1,0:T(8,128)S(1)} %get-tuple-element.38), channel_id=1, source_target_pairs={{0,16},{1,17},{2,18},{3,19},{4,20},{5,21},{6,22},{7,23},{8,24},{9,... | collective-permute-start | bytes 688136 | tf_op jit(solution)/shard_map/ppermute | solution.py:512
  31.3 10.6 %collective-permute-start.3 = (f32[4,56,256]{2,1,0:T(8,128)S(1)}, f32[4,56,256]{2,1,0:T(8,128)S(1)}, u32[]{:S(2)}, u32[]{:S(2)}) collective-permute-start(f32[4,56,256]{2,1,0:T(8,128)S(1)} %get-tuple-element.39), channel_id=1, source_target_pairs={{0,1},{1,0},{2,3},{3,2},{4,5},{5,4},{6,7},{7,6},{8,9},{9,8},{10,11... | collective-permute-start | bytes 688136 | tf_op jit(solution)/shard_map/ppermute | solution.py:512
  39.0 22.7 %copy-start = (f32[12,8,225]{2,1,0:T(8,128)S(1)}, f32[12,8,225]{2,1,0:T(8,128)}, u32[]{:S(2)}) copy-start(f32[12,8,225]{2,1,0:T(8,128)} %refs_7_.1) | copy-start | bytes 259204
  39.0 22.7 %copy-start.2 = (f32[6,8,225]{2,1,0:T(8,128)S(1)}, f32[6,8,225]{2,1,0:T(8,128)}, u32[]{:S(2)}) copy-start(f32[6,8,225]{2,1,0:T(8,128)} %refs_6_.1) | copy-start | bytes 129604
  39.0 22.7 %copy-start.3 = (f32[24,8]{1,0:T(8,128)S(1)}, f32[24,8]{1,0:T(8,128)}, u32[]{:S(2)}) copy-start(f32[24,8]{1,0:T(8,128)} %constant.8.clone.refs_9_) | copy-start | bytes 2308
  39.1 22.6 %copy-start.5 = (s32[8,225]{1,0:T(8,128)S(1)}, s32[8,225]{1,0:T(8,128)}, u32[]{:S(2)}) copy-start(s32[8,225]{1,0:T(8,128)} %refs_8_.1) | copy-start | bytes 21604
  42.0 2.7 %collective-permute-start.5 = (f32[16,24,256]{2,1,0:T(8,128)S(1)}, f32[16,24,256]{2,1,0:T(8,128)S(1)}, u32[]{:S(2)}, u32[]{:S(2)}) collective-permute-start(f32[16,24,256]{2,1,0:T(8,128)S(1)} %get-tuple-element.47), channel_id=1, source_target_pairs={{0,8},{8,0},{16,24},{24,16},{1,9},{9,1},{17,25},{25,17},{2,10},{10... | collective-permute-start | bytes 1179656 | tf_op jit(solution)/shard_map/ppermute | solution.py:315
  42.1 8.9 %collective-permute-start.4 = (f32[2,56,256]{2,1,0:T(8,128)S(1)}, f32[2,56,256]{2,1,0:T(8,128)S(1)}, u32[]{:S(2)}, u32[]{:S(2)}) collective-permute-start(f32[2,56,256]{2,1,0:T(8,128)S(1)} %get-tuple-element.45), channel_id=1, source_target_pairs={{0,4},{1,5},{2,6},{3,7},{4,0},{5,1},{6,2},{7,3},{8,12},{9,13},{10,... | collective-permute-start | bytes 344072 | tf_op jit(solution)/shard_map/ppermute | solution.py:512
  44.8 6.3 %collective-permute-start.6 = (f32[4,24,256]{2,1,0:T(8,128)S(1)}, f32[4,24,256]{2,1,0:T(8,128)S(1)}, u32[]{:S(2)}, u32[]{:S(2)}) collective-permute-start(f32[4,24,256]{2,1,0:T(8,128)S(1)} %get-tuple-element.50), channel_id=1, source_target_pairs={{0,17},{1,16},{2,19},{3,18},{4,21},{5,20},{6,23},{7,22},{8,25},{9,... | collective-permute-start | bytes 294920 | tf_op jit(solution)/shard_map/ppermute | solution.py:512
  46.5 6.2 %collective-permute-start.7 = (f32[4,24,256]{2,1,0:T(8,128)S(1)}, f32[4,24,256]{2,1,0:T(8,128)S(1)}, u32[]{:S(2)}, u32[]{:S(2)}) collective-permute-start(f32[4,24,256]{2,1,0:T(8,128)S(1)} %get-tuple-element.51), channel_id=1, source_target_pairs={{0,16},{1,17},{2,18},{3,19},{4,20},{5,21},{6,22},{7,23},{8,24},{9,... | collective-permute-start | bytes 294920 | tf_op jit(solution)/shard_map/ppermute | solution.py:512
  47.8 4.9 %collective-permute-start.8 = (f32[4,24,256]{2,1,0:T(8,128)S(1)}, f32[4,24,256]{2,1,0:T(8,128)S(1)}, u32[]{:S(2)}, u32[]{:S(2)}) collective-permute-start(f32[4,24,256]{2,1,0:T(8,128)S(1)} %get-tuple-element.52), channel_id=1, source_target_pairs={{0,1},{1,0},{2,3},{3,2},{4,5},{5,4},{6,7},{7,6},{8,9},{9,8},{10,11... | collective-permute-start | bytes 294920 | tf_op jit(solution)/shard_map/ppermute | solution.py:512
  52.8 8.9 %collective-permute-start.9 = (f32[80,256]{1,0:T(8,128)S(1)}, f32[80,256]{1,0:T(8,128)S(1)}, u32[]{:S(2)}, u32[]{:S(2)}) collective-permute-start(f32[80,256]{1,0:T(8,128)S(1)} %get-tuple-element.55), channel_id=1, source_target_pairs={{0,2},{1,3},{2,0},{3,1},{4,6},{5,7},{6,4},{7,5},{8,10},{9,11},{10,... | collective-permute-start | bytes 245768 | tf_op jit(solution)/shard_map/ppermute | solution.py:512
  54.4 4.9 %collective-permute-start.10 = (f32[24,256]{1,0:T(8,128)S(1)}, f32[24,256]{1,0:T(8,128)S(1)}, u32[]{:S(2)}, u32[]{:S(2)}) collective-permute-start(f32[24,256]{1,0:T(8,128)S(1)} %get-tuple-element.56), channel_id=1, source_target_pairs={{0,4},{1,5},{2,6},{3,7},{4,0},{5,1},{6,2},{7,3},{8,12},{9,13},{10,... | collective-permute-start | bytes 73736 | tf_op jit(solution)/shard_map/ppermute | solution.py:512
  56.1 5.6 %collective-permute-start.11 = (f32[24,256]{1,0:T(8,128)S(1)}, f32[24,256]{1,0:T(8,128)S(1)}, u32[]{:S(2)}, u32[]{:S(2)}) collective-permute-start(f32[24,256]{1,0:T(8,128)S(1)} %get-tuple-element.57), channel_id=1, source_target_pairs={{0,6},{1,7},{2,4},{3,5},{4,2},{5,3},{6,0},{7,1},{8,14},{9,15},{10,... | collective-permute-start | bytes 73736 | tf_op jit(solution)/shard_map/ppermute | solution.py:512
  63.4 4.7 %collective-permute-start.12 = (f32[3,1,256]{2,1,0:T(1,128)S(1)}, f32[3,1,256]{2,1,0:T(1,128)S(1)}, u32[]{:S(2)}, u32[]{:S(2)}) collective-permute-start(f32[3,1,256]{2,1,0:T(1,128)S(1)} %slice_bitcast_fusion), channel_id=1, source_target_pairs={{0,1},{1,2},{2,3},{3,4},{4,5},{5,6},{6,7},{8,9},{9,10},{10,11},{11... | collective-permute-start | bytes 9224 | tf_op jit(solution)/shard_map/ppermute | solution.py:48

commit v13 on v12

--- a/solution.py
+++ b/solution.py
@@ -12,7 +12,7 @@
 GX = 15
 LANES = 128
 COLUMNS = 256
-CHUNKS = ((0, 6), (6, 2))
+CHUNKS = ((0, 4), (4, 4))
 QUANTUM = float((1 << 15) - 1)
 
 SLIP_PLANES = [

time: 69 us -> 69.7 us (1.010)
  waiting for transfers between devices: 13 us -> 13.8 us
    ppermute x2, waiting for transfers between devices: 0.01 us -> 2.24 us  [across_cores(): return lax.ppermute(block, 'ca', [(i, i ^ 1) for i in range(groups)])]
    ppermute x10, waiting for transfers between devices: 11.7 us -> 10.3 us  [to_relative(): lax.ppermute(block, ('ca', 'fe'), [(i, i ^ flip) for i in range(groups *...]
  transfers between devices with their start and end apart: 13 -> 13, of which waited for: 8 -> 8; matrix products, arithmetic and copies ran while one was open for 0% -> 0% of each run, Pallas kernels for 14% -> 23%
where the time goes in v13:
time: 69.7 us; the launch traced here: 69.4 us
  Pallas kernels  31.6 us (45%)
  starting transfers between devices  19.5 us (28%)
  waiting for transfers between devices  13.8 us (20%)
  local copies, waits for them, and re-layouts  2.34 us (3%)
  other arithmetic  1.32 us (2%)
  between operations  0.79 us (1%)
    pallas_call x2, Pallas kernels, cell_sums(): pl.pallas_call(functools.partial(cell_sum_kernel, octants, per_octant), o...  27.9 us
    ppermute x10, starting transfers between devices, to_relative(): lax.ppermute(block, ('ca', 'fe'), [(i, i ^ flip) for i in range(groups *...  15.5 us
    ppermute x10, waiting for transfers between devices, to_relative(): lax.ppermute(block, ('ca', 'fe'), [(i, i ^ flip) for i in range(groups *...  10.3 us
    ppermute x1, starting transfers between devices, passed_along(): return lax.ppermute(block, axis, route)  3.4 us
    unnamed x14, local copies, waits for them, and re-layouts  2.34 us
    ppermute x2, waiting for transfers between devices, across_cores(): return lax.ppermute(block, 'ca', [(i, i ^ 1) for i in range(groups)])  2.24 us
    pallas_call x1, Pallas kernels, element_update(): pl.pallas_call(functools.partial(update_kernel, len(second)), out_shape=(...  1.7 us
    pallas_call x1, Pallas kernels, brick_sums(): pl.pallas_call(brick_sum_kernel, out_shape=[jax.ShapeDtypeStruct((places,...  1.56 us
  transfers between devices with their start and end apart: 13, of which 8 were waited for; matrix products, arithmetic and copies ran while one was open for 0% of the time, Pallas kernels for 23%

profile of v13, /device:TPU:0, one launch (start us, length us, event | category | flops | bytes accessed | tf_op | source)
XLA Modules:
  0.0 69.4 jit_solution(3832760020304448447)
XLA Ops:
  0.6 0.8 %copy-done.1 = f32[3,4096]{1,0:T(4,128)S(1)} copy-done((f32[3,4096]{1,0:T(4,128)S(1)}, f32[3,4096]{1,0:T(4,128)}, u32[]{:S(2)}) %copy-start.1) | copy-done | bytes 49176
  1.5 0.2 rotation_table.1.table_ref
  1.6 0.7 %add_select_fusion = s32[2048]{0:T(1024)S(1)} fusion(s32[2048]{0:T(1024)} %param.14, s32[2048]{0:T(1024)} %bitcast.15, s32[2048]{0:T(1024)} %param.12), kind=kLoop, calls=%fused_computation | loop fusion | flops 8192 | bytes 32768 | tf_op jit(solution)/shard_map/jit(_where)/select_n | solution.py:718
  2.4 1.5 %copy-done.6 = s32[216,2048]{1,0:T(8,128)S(1)} copy-done((s32[216,2048]{1,0:T(8,128)S(1)}, s32[216,2048]{1,0:T(8,128)}, u32[]{:S(2)}) %copy-start.6) | copy-done | bytes 1769496
  3.9 13.5 %cell_sums.2 = (s32[1,2048]{1,0:T(1,128)S(1)}, f32[16,40,256]{2,1,0:T(8,128)S(1)}, bf16[80,2048]{1,0:T(8,128)(2,1)S(1)}, s32[112,2048]{1,0:T(8,128)S(1)}) custom-call(s32[216,2048]{1,0:T(8,128)S(1)} %copy-done.6, s32[1,2048]{1,0:T(1,128)S(1)} %bitcast.14, s32[48,8,128]{2,1,0:T(8,128)S(1)} %rotation_table.1.table_ref), custom_call_target="tpu_custom_call" | custom-call | flops 16000000000 | bytes 40000000 | tf_op jit(solution)/shard_map/cell_sums/pallas_call | solution.py:376
  17.4 0.5 collective-permute-start
  17.9 1.6 %brick_sums.1 = (f32[16,40,256]{2,1,0:T(8,128)S(1)}, s32[1,2048]{1,0:T(1,128)S(1)}) custom-call(bf16[80,2048]{1,0:T(8,128)(2,1)S(1)} %get-tuple-element.31.split_ref, s32[1,2048]{1,0:T(1,128)S(1)} %get-tuple-element.32.label_ref), custom_call_target="tpu_custom_call" | custom-call | flops 1200000000 | bytes 4000000 | tf_op jit(solution)/shard_map/brick_sums/pallas_call | solution.py:406
  19.5 0.2 collective-permute-done
  19.6 0.1 core_sum_a.1
  19.7 3.9 %collective-permute-start.1 = (f32[4,40,256]{2,1,0:T(8,128)S(1)}, f32[4,40,256]{2,1,0:T(8,128)S(1)}, u32[]{:S(2)}, u32[]{:S(2)}) collective-permute-start(f32[4,40,256]{2,1,0:T(8,128)S(1)} %get-tuple-element.37), channel_id=1, source_target_pairs={{0,17},{1,16},{2,19},{3,18},{4,21},{5,20},{6,23},{7,22},{8,25},{9,... | collective-permute-start | bytes 491528 | tf_op jit(solution)/shard_map/ppermute | solution.py:512
  23.6 0.5 collective-permute-start.2
  24.1 0.1 collective-permute-start.3
  24.2 14.4 %cell_sums.3 = (f32[16,40,256]{2,1,0:T(8,128)S(1)}, f32[16,40,256]{2,1,0:T(8,128)S(1)}) custom-call(s32[112,2048]{1,0:T(8,128)S(1)} %get-tuple-element.41.ids_ref, s32[1,2048]{1,0:T(1,128)S(1)} %get-tuple-element.42.label_ref, s32[48,8,128]{2,1,0:T(8,128)S(1)} %rotation_table.1.table_ref), custom_call_target="tpu_custom_call" | custom-call | flops 16000000000 | bytes 40000000 | tf_op jit(solution)/shard_map/cell_sums/pallas_call | solution.py:376
  38.7 0.1 plane_sum_a.1
  38.9 2.1 %collective-permute-done.5 = f32[16,40,256]{2,1,0:T(8,128)S(1)} collective-permute-done((f32[16,40,256]{2,1,0:T(8,128)S(1)}, f32[16,40,256]{2,1,0:T(8,128)S(1)}, u32[]{:S(2)}, u32[]{:S(2)}) %collective-permute-start.5) | collective-permute-done | bytes 655392 | tf_op jit(solution)/shard_map/ppermute | solution.py:315
  41.0 0.1 core_sum_b.1
  41.1 2.9 %collective-permute-start.6 = (f32[4,40,256]{2,1,0:T(8,128)S(1)}, f32[4,40,256]{2,1,0:T(8,128)S(1)}, u32[]{:S(2)}, u32[]{:S(2)}) collective-permute-start(f32[4,40,256]{2,1,0:T(8,128)S(1)} %get-tuple-element.50), channel_id=1, source_target_pairs={{0,17},{1,16},{2,19},{3,18},{4,21},{5,20},{6,23},{7,22},{8,25},{9,... | collective-permute-start | bytes 491528 | tf_op jit(solution)/shard_map/ppermute | solution.py:512
  44.0 0.5 collective-permute-start.7
  44.5 0.1 collective-permute-start.8
  44.6 3.0 %collective-permute-start.4 = (f32[2,40,256]{2,1,0:T(8,128)S(1)}, f32[2,40,256]{2,1,0:T(8,128)S(1)}, u32[]{:S(2)}, u32[]{:S(2)}) collective-permute-start(f32[2,40,256]{2,1,0:T(8,128)S(1)} %get-tuple-element.45), channel_id=1, source_target_pairs={{0,4},{1,5},{2,6},{3,7},{4,0},{5,1},{6,2},{7,3},{8,12},{9,13},{10,... | collective-permute-start | bytes 245768 | tf_op jit(solution)/shard_map/ppermute | solution.py:512
  47.6 3.0 %collective-permute-done.4.received_ref = f32[2,40,256]{2,1,0:T(8,128)S(1)} collective-permute-done((f32[2,40,256]{2,1,0:T(8,128)S(1)}, f32[2,40,256]{2,1,0:T(8,128)S(1)}, u32[]{:S(2)}, u32[]{:S(2)}) %collective-permute-start.4) | collective-permute-done | bytes 81952 | tf_op jit(solution)/shard_map/ppermute | solution.py:512
  50.6 1.4 %collective-permute-done.7.refs_2_ = f32[4,40,256]{2,1,0:T(8,128)S(1)} collective-permute-done((f32[4,40,256]{2,1,0:T(8,128)S(1)}, f32[4,40,256]{2,1,0:T(8,128)S(1)}, u32[]{:S(2)}, u32[]{:S(2)}) %collective-permute-start.7) | collective-permute-done | bytes 163872 | tf_op jit(solution)/shard_map/ppermute | solution.py:512
  52.0 0.3 collective-permute-done.8.refs_3_
  52.3 1.6 %collective-permute-start.9 = (f32[80,256]{1,0:T(8,128)S(1)}, f32[80,256]{1,0:T(8,128)S(1)}, u32[]{:S(2)}, u32[]{:S(2)}) collective-permute-start(f32[80,256]{1,0:T(8,128)S(1)} %get-tuple-element.55), channel_id=1, source_target_pairs={{0,2},{1,3},{2,0},{3,1},{4,6},{5,7},{6,4},{7,5},{8,10},{9,11},{10,... | collective-permute-start | bytes 245768 | tf_op jit(solution)/shard_map/ppermute | solution.py:512
  54.0 2.6 %collective-permute-start.10 = (f32[40,256]{1,0:T(8,128)S(1)}, f32[40,256]{1,0:T(8,128)S(1)}, u32[]{:S(2)}, u32[]{:S(2)}) collective-permute-start(f32[40,256]{1,0:T(8,128)S(1)} %get-tuple-element.56), channel_id=1, source_target_pairs={{0,4},{1,5},{2,6},{3,7},{4,0},{5,1},{6,2},{7,3},{8,12},{9,13},{10,... | collective-permute-start | bytes 122888 | tf_op jit(solution)/shard_map/ppermute | solution.py:512
  56.6 0.2 collective-permute-start.11
  56.8 3.0 %collective-permute-done.10.refs_3_ = f32[40,256]{1,0:T(8,128)S(1)} collective-permute-done((f32[40,256]{1,0:T(8,128)S(1)}, f32[40,256]{1,0:T(8,128)S(1)}, u32[]{:S(2)}, u32[]{:S(2)}) %collective-permute-start.10) | collective-permute-done | bytes 40992 | tf_op jit(solution)/shard_map/ppermute | solution.py:512
  59.8 2.6 %collective-permute-done.11.refs_4_ = f32[40,256]{1,0:T(8,128)S(1)} collective-permute-done((f32[40,256]{1,0:T(8,128)S(1)}, f32[40,256]{1,0:T(8,128)S(1)}, u32[]{:S(2)}, u32[]{:S(2)}) %collective-permute-start.11) | collective-permute-done | bytes 40992 | tf_op jit(solution)/shard_map/ppermute | solution.py:512
  62.4 1.7 %stress_update.1 = (f32[6,8,225]{2,1,0:T(8,128)}, f32[2,3,1,256]{3,2,1,0:T(1,128)S(1)}) custom-call(f32[40,256]{1,0:T(8,128)S(1)} %get-tuple-element.53.refs_0_, f32[40,256]{1,0:T(8,128)S(1)} %get-tuple-element.54.refs_1_, f32[80,256]{1,0:T(8,128)S(1)} %collective-permute-done.9.refs_2_, f32[40,256]{1,0:T(8,128)S(1)} %collective-permute-done.10.refs_3_, ...), custom_call_target="tpu_custom_call" | custom-call | tf_op jit(solution)/shard_map/stress_update/pallas_call | solution.py:693
  64.1 3.4 %collective-permute-start.12 = (f32[3,1,256]{2,1,0:T(1,128)S(1)}, f32[3,1,256]{2,1,0:T(1,128)S(1)}, u32[]{:S(2)}, u32[]{:S(2)}) collective-permute-start(f32[3,1,256]{2,1,0:T(1,128)S(1)} %slice_bitcast_fusion), channel_id=1, source_target_pairs={{0,1},{1,2},{2,3},{3,4},{4,5},{5,6},{6,7},{8,9},{9,10},{10,11},{11... | collective-permute-start | bytes 9224 | tf_op jit(solution)/shard_map/ppermute | solution.py:48
  67.5 1.3 %collective-permute-done.12 = f32[3,1,256]{2,1,0:T(1,128)S(1)} collective-permute-done((f32[3,1,256]{2,1,0:T(1,128)S(1)}, f32[3,1,256]{2,1,0:T(1,128)S(1)}, u32[]{:S(2)}, u32[]{:S(2)}) %collective-permute-start.12) | collective-permute-done | bytes 3104 | tf_op jit(solution)/shard_map/ppermute | solution.py:48
  68.8 0.6 bitcast_add_fusion
  (20 shorter events, 0.2 us)
Async XLA Ops:
  0.6 0.8 %copy-start.1 = (f32[3,4096]{1,0:T(4,128)S(1)}, f32[3,4096]{1,0:T(4,128)}, u32[]{:S(2)}) copy-start(f32[3,4096]{1,0:T(4,128)} %euler_ref.1) | copy-start | bytes 147460
  2.4 1.5 %copy-start.6 = (s32[216,2048]{1,0:T(8,128)S(1)}, s32[216,2048]{1,0:T(8,128)}, u32[]{:S(2)}) copy-start(s32[216,2048]{1,0:T(8,128)} %ids_ref.1) | copy-start | bytes 5308420
  17.4 2.2 %collective-permute-start = (f32[16,40,256]{2,1,0:T(8,128)S(1)}, f32[16,40,256]{2,1,0:T(8,128)S(1)}, u32[]{:S(2)}, u32[]{:S(2)}) collective-permute-start(f32[16,40,256]{2,1,0:T(8,128)S(1)} %get-tuple-element.34), channel_id=1, source_target_pairs={{0,8},{8,0},{16,24},{24,16},{1,9},{9,1},{17,25},{25,17},{2,10},{10... | collective-permute-start | bytes 1966088 | tf_op jit(solution)/shard_map/ppermute | solution.py:315
  17.9 1.7 %copy-start.4 = (f32[3,1,256]{2,1,0:T(1,128)S(1)}, f32[3,1,256]{2,1,0:T(1,128)}, u32[]{:S(2)}) copy-start(f32[3,1,256]{2,1,0:T(1,128)} %refs_5_.1) | copy-start | bytes 9220
  19.7 19.0 %collective-permute-start.1 = (f32[4,40,256]{2,1,0:T(8,128)S(1)}, f32[4,40,256]{2,1,0:T(8,128)S(1)}, u32[]{:S(2)}, u32[]{:S(2)}) collective-permute-start(f32[4,40,256]{2,1,0:T(8,128)S(1)} %get-tuple-element.37), channel_id=1, source_target_pairs={{0,17},{1,16},{2,19},{3,18},{4,21},{5,20},{6,23},{7,22},{8,25},{9,... | collective-permute-start | bytes 491528 | tf_op jit(solution)/shard_map/ppermute | solution.py:512
  23.6 15.1 %collective-permute-start.2 = (f32[4,40,256]{2,1,0:T(8,128)S(1)}, f32[4,40,256]{2,1,0:T(8,128)S(1)}, u32[]{:S(2)}, u32[]{:S(2)}) collective-permute-start(f32[4,40,256]{2,1,0:T(8,128)S(1)} %get-tuple-element.38), channel_id=1, source_target_pairs={{0,16},{1,17},{2,18},{3,19},{4,20},{5,21},{6,22},{7,23},{8,24},{9,... | collective-permute-start | bytes 491528 | tf_op jit(solution)/shard_map/ppermute | solution.py:512
  24.1 14.6 %collective-permute-start.3 = (f32[4,40,256]{2,1,0:T(8,128)S(1)}, f32[4,40,256]{2,1,0:T(8,128)S(1)}, u32[]{:S(2)}, u32[]{:S(2)}) collective-permute-start(f32[4,40,256]{2,1,0:T(8,128)S(1)} %get-tuple-element.39), channel_id=1, source_target_pairs={{0,1},{1,0},{2,3},{3,2},{4,5},{5,4},{6,7},{7,6},{8,9},{9,8},{10,11... | collective-permute-start | bytes 491528 | tf_op jit(solution)/shard_map/ppermute | solution.py:512
  38.6 23.7 %copy-start = (f32[12,8,225]{2,1,0:T(8,128)S(1)}, f32[12,8,225]{2,1,0:T(8,128)}, u32[]{:S(2)}) copy-start(f32[12,8,225]{2,1,0:T(8,128)} %refs_7_.1) | copy-start | bytes 259204
  38.6 23.7 %copy-start.2 = (f32[6,8,225]{2,1,0:T(8,128)S(1)}, f32[6,8,225]{2,1,0:T(8,128)}, u32[]{:S(2)}) copy-start(f32[6,8,225]{2,1,0:T(8,128)} %refs_6_.1) | copy-start | bytes 129604
  38.6 23.7 %copy-start.3 = (f32[24,8]{1,0:T(8,128)S(1)}, f32[24,8]{1,0:T(8,128)}, u32[]{:S(2)}) copy-start(f32[24,8]{1,0:T(8,128)} %constant.8.clone.refs_9_) | copy-start | bytes 2308
  38.7 23.7 %copy-start.5 = (s32[8,225]{1,0:T(8,128)S(1)}, s32[8,225]{1,0:T(8,128)}, u32[]{:S(2)}) copy-start(s32[8,225]{1,0:T(8,128)} %refs_8_.1) | copy-start | bytes 21604
  38.8 2.2 %collective-permute-start.5 = (f32[16,40,256]{2,1,0:T(8,128)S(1)}, f32[16,40,256]{2,1,0:T(8,128)S(1)}, u32[]{:S(2)}, u32[]{:S(2)}) collective-permute-start(f32[16,40,256]{2,1,0:T(8,128)S(1)} %get-tuple-element.47), channel_id=1, source_target_pairs={{0,8},{8,0},{16,24},{24,16},{1,9},{9,1},{17,25},{25,17},{2,10},{10... | collective-permute-start | bytes 1966088 | tf_op jit(solution)/shard_map/ppermute | solution.py:315
  41.1 9.5 %collective-permute-start.6 = (f32[4,40,256]{2,1,0:T(8,128)S(1)}, f32[4,40,256]{2,1,0:T(8,128)S(1)}, u32[]{:S(2)}, u32[]{:S(2)}) collective-permute-start(f32[4,40,256]{2,1,0:T(8,128)S(1)} %get-tuple-element.50), channel_id=1, source_target_pairs={{0,17},{1,16},{2,19},{3,18},{4,21},{5,20},{6,23},{7,22},{8,25},{9,... | collective-permute-start | bytes 491528 | tf_op jit(solution)/shard_map/ppermute | solution.py:512
  44.0 8.0 %collective-permute-start.7 = (f32[4,40,256]{2,1,0:T(8,128)S(1)}, f32[4,40,256]{2,1,0:T(8,128)S(1)}, u32[]{:S(2)}, u32[]{:S(2)}) collective-permute-start(f32[4,40,256]{2,1,0:T(8,128)S(1)} %get-tuple-element.51), channel_id=1, source_target_pairs={{0,16},{1,17},{2,18},{3,19},{4,20},{5,21},{6,22},{7,23},{8,24},{9,... | collective-permute-start | bytes 491528 | tf_op jit(solution)/shard_map/ppermute | solution.py:512
  44.5 7.8 %collective-permute-start.8 = (f32[4,40,256]{2,1,0:T(8,128)S(1)}, f32[4,40,256]{2,1,0:T(8,128)S(1)}, u32[]{:S(2)}, u32[]{:S(2)}) collective-permute-start(f32[4,40,256]{2,1,0:T(8,128)S(1)} %get-tuple-element.52), channel_id=1, source_target_pairs={{0,1},{1,0},{2,3},{3,2},{4,5},{5,4},{6,7},{7,6},{8,9},{9,8},{10,11... | collective-permute-start | bytes 491528 | tf_op jit(solution)/shard_map/ppermute | solution.py:512
  44.6 6.0 %collective-permute-start.4 = (f32[2,40,256]{2,1,0:T(8,128)S(1)}, f32[2,40,256]{2,1,0:T(8,128)S(1)}, u32[]{:S(2)}, u32[]{:S(2)}) collective-permute-start(f32[2,40,256]{2,1,0:T(8,128)S(1)} %get-tuple-element.45), channel_id=1, source_target_pairs={{0,4},{1,5},{2,6},{3,7},{4,0},{5,1},{6,2},{7,3},{8,12},{9,13},{10,... | collective-permute-start | bytes 245768 | tf_op jit(solution)/shard_map/ppermute | solution.py:512
  52.3 10.0 %collective-permute-start.9 = (f32[80,256]{1,0:T(8,128)S(1)}, f32[80,256]{1,0:T(8,128)S(1)}, u32[]{:S(2)}, u32[]{:S(2)}) collective-permute-start(f32[80,256]{1,0:T(8,128)S(1)} %get-tuple-element.55), channel_id=1, source_target_pairs={{0,2},{1,3},{2,0},{3,1},{4,6},{5,7},{6,4},{7,5},{8,10},{9,11},{10,... | collective-permute-start | bytes 245768 | tf_op jit(solution)/shard_map/ppermute | solution.py:512
  54.0 5.8 %collective-permute-start.10 = (f32[40,256]{1,0:T(8,128)S(1)}, f32[40,256]{1,0:T(8,128)S(1)}, u32[]{:S(2)}, u32[]{:S(2)}) collective-permute-start(f32[40,256]{1,0:T(8,128)S(1)} %get-tuple-element.56), channel_id=1, source_target_pairs={{0,4},{1,5},{2,6},{3,7},{4,0},{5,1},{6,2},{7,3},{8,12},{9,13},{10,... | collective-permute-start | bytes 122888 | tf_op jit(solution)/shard_map/ppermute | solution.py:512
  56.6 5.8 %collective-permute-start.11 = (f32[40,256]{1,0:T(8,128)S(1)}, f32[40,256]{1,0:T(8,128)S(1)}, u32[]{:S(2)}, u32[]{:S(2)}) collective-permute-start(f32[40,256]{1,0:T(8,128)S(1)} %get-tuple-element.57), channel_id=1, source_target_pairs={{0,6},{1,7},{2,4},{3,5},{4,2},{5,3},{6,0},{7,1},{8,14},{9,15},{10,... | collective-permute-start | bytes 122888 | tf_op jit(solution)/shard_map/ppermute | solution.py:512
  64.1 4.7 %collective-permute-start.12 = (f32[3,1,256]{2,1,0:T(1,128)S(1)}, f32[3,1,256]{2,1,0:T(1,128)S(1)}, u32[]{:S(2)}, u32[]{:S(2)}) collective-permute-start(f32[3,1,256]{2,1,0:T(1,128)S(1)} %slice_bitcast_fusion), channel_id=1, source_target_pairs={{0,1},{1,2},{2,3},{3,4},{4,5},{5,6},{6,7},{8,9},{9,10},{10,11},{11... | collective-permute-start | bytes 9224 | tf_op jit(solution)/shard_map/ppermute | solution.py:48

commit v14 on v13

--- a/solution.py
+++ b/solution.py
@@ -180,6 +180,7 @@
 def cell_sum_kernel(
     octants,
     per_octant,
+    part,
     ids_ref,
     label_ref,
     table_ref,
@@ -192,16 +193,20 @@
         label_out_ref, send_ref, split_ref, rest_ref = refs[:-4]
         label_out_ref[...] = label_ref[...]
         rest_ref[...] = ids_ref[pl.ds(ids_ref.shape[0] - rest_ref.shape[0], rest_ref.shape[0]), :]
-        targets = [(send_ref.shape[0], send_ref)]
+        targets = [(send_ref.shape[0], send_ref, None)]
+    elif part == 0:
+        send_ref, keep_ref, split_ref = refs[:-4]
+        targets = [(send_ref.shape[0], send_ref, None), (0, keep_ref, None)]
     else:
-        send_ref, keep_ref, split_ref = refs[:-4]
-        targets = [(send_ref.shape[0], send_ref), (0, keep_ref)]
+        sent_ref, kept_ref, send_ref, keep_ref, split_ref = refs[:-4]
+        targets = [(send_ref.shape[0], send_ref, sent_ref), (0, keep_ref, kept_ref)]
     groups = tile_ref.shape[1] // 8
     rows_left = count * per_octant - 8 * (groups - 1)
     turns = count // math.gcd(count, 8)
     rows = send_ref.shape[1]
     width = masked_ref.shape[1]
     pairs = ids_ref.shape[1] // width
+    begin, end = (0, pairs) if part is None else (part * pairs // 2, (part + 1) * pairs // 2)
 
     out_row = lax.broadcasted_iota(jnp.int32, (rows, raw_ref.shape[0]), 0)
     raw_row = lax.broadcasted_iota(jnp.int32, (rows, raw_ref.shape[0]), 1)
@@ -217,6 +222,8 @@
     constant = jnp.where(diagonal, float(per_octant), jnp.where(row < 9 * count, 0.0, 1.0))
 
     def lanes_of(pair):
+        if isinstance(pair, int):
+            return pl.ds(pair * width, width)
         return pl.ds(pl.multiple_of(pair * width, width), width)
 
     def look_up(pair):
@@ -262,25 +269,28 @@
         column = lax.broadcasted_iota(jnp.int32, (COLUMNS, width), 0)
         chosen = (column == label_ref[:, lanes] & (COLUMNS - 1)).astype(jnp.bfloat16)
         place = jnp.where(counted, place_ref[:, lanes], -1)
-        for base, out_ref in targets:
+        for base, out_ref, earlier_ref in targets:
             add_places(split_ref, lanes, place - base, chosen, out_ref, masked_ref)
 
     place_ref[...] = relative_places(label_ref[...])
-    for base, out_ref in targets:
-        out_ref[...] = jnp.zeros(out_ref.shape, jnp.float32)
-    raw_ref[:, pl.ds(0, width)] = jnp.zeros((raw_ref.shape[0], width), jnp.float32)
-    split_ref[:, pl.ds(0, width)] = jnp.zeros((split_ref.shape[0], width), jnp.bfloat16)
+    for base, out_ref, earlier_ref in targets:
+        if earlier_ref is None:
+            out_ref[...] = jnp.zeros(out_ref.shape, jnp.float32)
+        else:
+            out_ref[...] = earlier_ref[...]
+    raw_ref[:, lanes_of(begin)] = jnp.zeros((raw_ref.shape[0], width), jnp.float32)
+    split_ref[:, lanes_of(begin)] = jnp.zeros((split_ref.shape[0], width), jnp.bfloat16)
 
     def step(pair, carry):
-        add_bricks(jnp.maximum(pair - 2, 0), pair >= 2)
-        fold_entries(jnp.maximum(pair - 1, 0))
+        add_bricks(jnp.maximum(pair - 2, begin), pair >= begin + 2)
+        fold_entries(jnp.maximum(pair - 1, begin))
         look_up(pair)
         return carry
 
-    lax.fori_loop(0, pairs, step, 0, unroll=2)
-    add_bricks(pairs - 2, True)
-    fold_entries(pairs - 1)
-    add_bricks(pairs - 1, True)
+    lax.fori_loop(begin, end, step, 0, unroll=2)
+    add_bricks(end - 2, True)
+    fold_entries(end - 1)
+    add_bricks(end - 1, True)
 
 
 def relative_places(labels):
@@ -355,7 +365,7 @@
     return place * (members // 2) + lax.shift_right_logical(owner_fe, 1)
 
 
-def cell_sums(octants, per_octant, ids, labels, table, places):
+def cell_sums(octants, per_octant, part, ids, labels, table, places, earlier=()):
     first, count = octants
     bricks = ids.shape[1]
     rows = padded_rows(count)
@@ -374,7 +384,7 @@
         out_shape = [half, half]
         scratch.append(pltpu.VMEM(split.shape, split.dtype))
     return pl.pallas_call(
-        functools.partial(cell_sum_kernel, octants, per_octant),
+        functools.partial(cell_sum_kernel, octants, per_octant, part),
         out_shape=out_shape,
         scratch_shapes=scratch
         + [
@@ -387,7 +397,7 @@
             flops=count * 4 * 10**9, bytes_accessed=count * 10**7, transcendentals=0
         ),
         name="cell_sums",
-    )(ids, labels, table)
+    )(ids, labels, table, *earlier)
 
 
 def padded_rows(count):
@@ -482,28 +492,25 @@
     return out[: len(cuts)], *out[len(cuts) :]
 
 
-def last_sum_kernel(sources, spare, kept_ref, received_ref, *refs):
+def last_sum_kernel(sources, spare, next_ref, *refs):
     parts, outs = refs[:sources], refs[sources:]
-    rows = kept_ref.shape[1]
-    outs[0][...] = kept_ref[0] + received_ref[0]
-    outs[2][0:rows, :] = kept_ref[1] + received_ref[1]
-    for height, out_ref in enumerate(outs[1:]):
+    outs[1][0 : next_ref.shape[1], :] = next_ref[0]
+    for height, out_ref in enumerate(outs):
         first = out_ref.shape[0] - parts[0].shape[1]
         out_ref[first:, :] = sum(ref[height] for ref in parts)
         out_ref[out_ref.shape[0] - spare :, :] = parts[-1][height, -spare:, :]
 
 
-def last_sum(kept, received, parts, spare):
+def last_sum(next_height, parts, spare):
     heights, rows, columns = parts[0].shape
     part = jax.ShapeDtypeStruct((rows, columns), jnp.float32)
-    both = jax.ShapeDtypeStruct((kept.shape[1] + rows, columns), jnp.float32)
+    both = jax.ShapeDtypeStruct((next_height.shape[1] + rows, columns), jnp.float32)
     return pl.pallas_call(
         functools.partial(last_sum_kernel, len(parts), spare),
-        out_shape=[jax.ShapeDtypeStruct(kept.shape[1:], jnp.float32), part, both]
-        + [part] * (heights - 2),
+        out_shape=[part, both] + [part] * (heights - 2),
         compiler_params=pltpu.CompilerParams(vmem_limit_bytes=16 * 1024 * 1024),
         name="last_sum",
-    )(kept, received, *parts)
+    )(next_height, *parts)
 
 
 def to_relative(block, core, pair, last, rest):
@@ -546,9 +553,9 @@
     own_ref, stress_ref, resistance_ref, weights_ref, table_ref = refs[1 + heights : -2]
     stress_out_ref, nodal_ref = refs[-2:]
     elements = stress_ref.shape[2]
-    rows, second_rows = first_ref.shape[0], second_refs[0].shape[0]
+    rows, second_rows = first_ref.shape[1], second_refs[0].shape[0]
     gathered = [
-        first_ref[:, 0:elements] + second_refs[1][0:rows, 0:elements],
+        first_ref[0, :, 0:elements] + second_refs[1][0:rows, 0:elements],
         sum(ref[ref.shape[0] - second_rows :, 0:elements] for ref in second_refs),
     ]
     counted = 9 * CHUNKS[1][1]
@@ -718,25 +725,29 @@
     labels = jnp.where(brick_active > 0, owner * COLUMNS + brick_element, -1).reshape(1, bricks)
     per_octant = grain_ids.shape[0] // 8
     table = rotation_table(euler_angles)
-    labels, send, split, ids = cell_sums(CHUNKS[0], per_octant, grain_ids, labels, table, half)
+    labels, send, split, ids = cell_sums(
+        CHUNKS[0], per_octant, None, grain_ids, labels, table, half
+    )
     keep, labels = brick_sums(split, labels, half)
     core_a, labels, own = core_sum(
         keep, across_cores(send), [labels, displacement], "core_sum_a"
     )
-    send, keep = cell_sums(CHUNKS[1], per_octant, ids, labels, table, half)
+    send, keep = cell_sums(CHUNKS[1], per_octant, 0, ids, labels, table, half)
     flip = lax.axis_size("fe") // 4
     (kept, sent), own, send = plane_sum(
         across_plane(core_a), [own, send], [flip, flip], "plane_sum_a"
     )
     received = to_relative(sent, 0, 0, 0, flip)
+    send, keep = cell_sums(CHUNKS[1], per_octant, 1, ids, labels, table, half, (send, keep))
+    while flip > 1:
+        flip //= 2
+        (kept, sent), send = plane_sum([kept, received], [send], [flip, flip], "height_sum_a")
+        if flip > 1:
+            received = to_relative(sent, 0, 0, 0, flip)
     core_b = last_core_sum(keep, across_cores(send), own)
-    while flip > 2:
-        flip //= 2
-        (kept, sent) = plane_sum([kept, received], [], [flip, flip], "height_sum_a")[0]
-        received = to_relative(sent, 0, 0, 0, flip)
-    first, *second = last_sum(kept, received, across_plane(core_b), 3)
+    second = last_sum(sent, across_plane(core_b), 3)
     stress_new, nodal = element_update(
-        first, across_height(second), displacement, stress_old, resistance, quad_weights
+        kept, across_height(second), displacement, stress_old, resistance, quad_weights
     )
     forces = nodal[0] + passed_along(nodal[1], "fe", 1)
     return (stress_new, forces)

time: 69.7 us -> 71.6 us (1.027)
  Pallas kernels: 31.6 us -> 33.1 us
    pallas_call x2 -> x3, Pallas kernels: 27.9 us -> 29.3 us  [cell_sums(): pl.pallas_call(functools.partial(cell_sum_kernel, octants, per_octant, pa...]
  transfers between devices with their start and end apart: 13 -> 13, of which waited for: 8 -> 8; matrix products, arithmetic and copies ran while one was open for 0% -> 0% of each run, Pallas kernels for 23% -> 24%
where the time goes in v14:
time: 71.6 us; the launch traced here: 71.4 us
  Pallas kernels  33.1 us (46%)
  starting transfers between devices  19.6 us (27%)
  waiting for transfers between devices  14.3 us (20%)
  local copies, waits for them, and re-layouts  2.34 us (3%)
  other arithmetic  1.32 us (2%)
  between operations  0.81 us (1%)
    pallas_call x3, Pallas kernels, cell_sums(): pl.pallas_call(functools.partial(cell_sum_kernel, octants, per_octant, pa...  29.3 us
    ppermute x10, starting transfers between devices, to_relative(): lax.ppermute(block, ('ca', 'fe'), [(i, i ^ flip) for i in range(groups *...  15.6 us
    ppermute x10, waiting for transfers between devices, to_relative(): lax.ppermute(block, ('ca', 'fe'), [(i, i ^ flip) for i in range(groups *...  10.7 us
    ppermute x1, starting transfers between devices, passed_along(): return lax.ppermute(block, axis, route)  3.4 us
    unnamed x14, local copies, waits for them, and re-layouts  2.34 us
    ppermute x2, waiting for transfers between devices, across_cores(): return lax.ppermute(block, 'ca', [(i, i ^ 1) for i in range(groups)])  2.24 us
    pallas_call x1, Pallas kernels, element_update(): pl.pallas_call(functools.partial(update_kernel, len(second)), out_shape=(...  1.7 us
    pallas_call x1, Pallas kernels, brick_sums(): pl.pallas_call(brick_sum_kernel, out_shape=[jax.ShapeDtypeStruct((places,...  1.56 us
  transfers between devices with their start and end apart: 13, of which 8 were waited for; matrix products, arithmetic and copies ran while one was open for 0% of the time, Pallas kernels for 24%

profile of v14, /device:TPU:0, one launch (start us, length us, event | category | flops | bytes accessed | tf_op | source)
XLA Modules:
  0.0 71.4 jit_solution(10979685856682715634)
XLA Ops:
  0.6 0.8 %copy-done.1 = f32[3,4096]{1,0:T(4,128)S(1)} copy-done((f32[3,4096]{1,0:T(4,128)S(1)}, f32[3,4096]{1,0:T(4,128)}, u32[]{:S(2)}) %copy-start.1) | copy-done | bytes 49176
  1.5 0.2 rotation_table.1.table_ref
  1.6 0.7 %add_select_fusion = s32[2048]{0:T(1024)S(1)} fusion(s32[2048]{0:T(1024)} %param.14, s32[2048]{0:T(1024)} %bitcast.15, s32[2048]{0:T(1024)} %param.12), kind=kLoop, calls=%fused_computation | loop fusion | flops 8192 | bytes 32768 | tf_op jit(solution)/shard_map/jit(_where)/select_n | solution.py:725
  2.4 1.5 %copy-done.6 = s32[216,2048]{1,0:T(8,128)S(1)} copy-done((s32[216,2048]{1,0:T(8,128)S(1)}, s32[216,2048]{1,0:T(8,128)}, u32[]{:S(2)}) %copy-start.6) | copy-done | bytes 1769496
  3.9 13.5 %cell_sums.3 = (s32[1,2048]{1,0:T(1,128)S(1)}, f32[16,40,256]{2,1,0:T(8,128)S(1)}, bf16[80,2048]{1,0:T(8,128)(2,1)S(1)}, s32[112,2048]{1,0:T(8,128)S(1)}) custom-call(s32[216,2048]{1,0:T(8,128)S(1)} %copy-done.6, s32[1,2048]{1,0:T(1,128)S(1)} %bitcast.14, s32[48,8,128]{2,1,0:T(8,128)S(1)} %rotation_table.1.table_ref), custom_call_target="tpu_custom_call" | custom-call | flops 16000000000 | bytes 40000000 | tf_op jit(solution)/shard_map/cell_sums/pallas_call | solution.py:386
  17.4 0.5 collective-permute-start
  17.9 1.6 %brick_sums.1 = (f32[16,40,256]{2,1,0:T(8,128)S(1)}, s32[1,2048]{1,0:T(1,128)S(1)}) custom-call(bf16[80,2048]{1,0:T(8,128)(2,1)S(1)} %get-tuple-element.35.split_ref, s32[1,2048]{1,0:T(1,128)S(1)} %get-tuple-element.36.label_ref), custom_call_target="tpu_custom_call" | custom-call | flops 1200000000 | bytes 4000000 | tf_op jit(solution)/shard_map/brick_sums/pallas_call | solution.py:416
  19.5 0.2 collective-permute-done
  19.6 0.1 core_sum_a.1
  19.7 3.9 %collective-permute-start.1 = (f32[4,40,256]{2,1,0:T(8,128)S(1)}, f32[4,40,256]{2,1,0:T(8,128)S(1)}, u32[]{:S(2)}, u32[]{:S(2)}) collective-permute-start(f32[4,40,256]{2,1,0:T(8,128)S(1)} %get-tuple-element.41), channel_id=1, source_target_pairs={{0,17},{1,16},{2,19},{3,18},{4,21},{5,20},{6,23},{7,22},{8,25},{9,... | collective-permute-start | bytes 491528 | tf_op jit(solution)/shard_map/ppermute | solution.py:519
  23.6 0.5 collective-permute-start.2
  24.1 0.1 collective-permute-start.3
  24.2 7.8 %cell_sums.4 = (f32[16,40,256]{2,1,0:T(8,128)S(1)}, f32[16,40,256]{2,1,0:T(8,128)S(1)}) custom-call(s32[112,2048]{1,0:T(8,128)S(1)} %get-tuple-element.45.ids_ref, s32[1,2048]{1,0:T(1,128)S(1)} %get-tuple-element.46.label_ref, s32[48,8,128]{2,1,0:T(8,128)S(1)} %rotation_table.1.table_ref), custom_call_target="tpu_custom_call" | custom-call | flops 16000000000 | bytes 40000000 | tf_op jit(solution)/shard_map/cell_sums/pallas_call | solution.py:386
  32.2 3.1 %collective-permute-start.4 = (f32[2,40,256]{2,1,0:T(8,128)S(1)}, f32[2,40,256]{2,1,0:T(8,128)S(1)}, u32[]{:S(2)}, u32[]{:S(2)}) collective-permute-start(f32[2,40,256]{2,1,0:T(8,128)S(1)} %get-tuple-element.49), channel_id=1, source_target_pairs={{0,4},{1,5},{2,6},{3,7},{4,0},{5,1},{6,2},{7,3},{8,12},{9,13},{10,... | collective-permute-start | bytes 245768 | tf_op jit(solution)/shard_map/ppermute | solution.py:519
  35.2 8.0 %cell_sums.5 = (f32[16,40,256]{2,1,0:T(8,128)S(1)}, f32[16,40,256]{2,1,0:T(8,128)S(1)}) custom-call(s32[112,2048]{1,0:T(8,128)S(1)} %get-tuple-element.45.ids_ref, s32[1,2048]{1,0:T(1,128)S(1)} %get-tuple-element.46.label_ref, s32[48,8,128]{2,1,0:T(8,128)S(1)} %rotation_table.1.table_ref, f32[16,40,256]{2,1,0:T(8,128)S(1)} %get-tuple-element.50.refs_0_, ...), custom_call_target="tpu_custom_call" | custom-call | flops 16000000000 | bytes 40000000 | tf_op jit(solution)/shard_map/cell_sums/pallas_call | solution.py:386
  43.4 2.1 %collective-permute-done.5 = f32[16,40,256]{2,1,0:T(8,128)S(1)} collective-permute-done((f32[16,40,256]{2,1,0:T(8,128)S(1)}, f32[16,40,256]{2,1,0:T(8,128)S(1)}, u32[]{:S(2)}, u32[]{:S(2)}) %collective-permute-start.5) | collective-permute-done | bytes 655392 | tf_op jit(solution)/shard_map/ppermute | solution.py:325
  45.5 0.1 core_sum_b.1
  45.6 2.5 %collective-permute-start.6 = (f32[4,40,256]{2,1,0:T(8,128)S(1)}, f32[4,40,256]{2,1,0:T(8,128)S(1)}, u32[]{:S(2)}, u32[]{:S(2)}) collective-permute-start(f32[4,40,256]{2,1,0:T(8,128)S(1)} %get-tuple-element.59), channel_id=1, source_target_pairs={{0,17},{1,16},{2,19},{3,18},{4,21},{5,20},{6,23},{7,22},{8,25},{9,... | collective-permute-start | bytes 491528 | tf_op jit(solution)/shard_map/ppermute | solution.py:519
  48.1 0.5 collective-permute-start.7
  48.6 0.5 collective-permute-start.8
  49.1 4.5 %collective-permute-done.6.refs_1_ = f32[4,40,256]{2,1,0:T(8,128)S(1)} collective-permute-done((f32[4,40,256]{2,1,0:T(8,128)S(1)}, f32[4,40,256]{2,1,0:T(8,128)S(1)}, u32[]{:S(2)}, u32[]{:S(2)}) %collective-permute-start.6) | collective-permute-done | bytes 163872 | tf_op jit(solution)/shard_map/ppermute | solution.py:519
  53.6 2.7 %collective-permute-done.7.refs_2_ = f32[4,40,256]{2,1,0:T(8,128)S(1)} collective-permute-done((f32[4,40,256]{2,1,0:T(8,128)S(1)}, f32[4,40,256]{2,1,0:T(8,128)S(1)}, u32[]{:S(2)}, u32[]{:S(2)}) %collective-permute-start.7) | collective-permute-done | bytes 163872 | tf_op jit(solution)/shard_map/ppermute | solution.py:519
  56.3 0.1 collective-permute-done.8.refs_3_
  56.4 1.6 %collective-permute-start.9 = (f32[80,256]{1,0:T(8,128)S(1)}, f32[80,256]{1,0:T(8,128)S(1)}, u32[]{:S(2)}, u32[]{:S(2)}) collective-permute-start(f32[80,256]{1,0:T(8,128)S(1)} %get-tuple-element.63), channel_id=1, source_target_pairs={{0,2},{1,3},{2,0},{3,1},{4,6},{5,7},{6,4},{7,5},{8,10},{9,11},{10,... | collective-permute-start | bytes 245768 | tf_op jit(solution)/shard_map/ppermute | solution.py:519
  58.1 0.3 collective-permute-start.10
  58.4 2.5 %collective-permute-start.11 = (f32[40,256]{1,0:T(8,128)S(1)}, f32[40,256]{1,0:T(8,128)S(1)}, u32[]{:S(2)}, u32[]{:S(2)}) collective-permute-start(f32[40,256]{1,0:T(8,128)S(1)} %get-tuple-element.65), channel_id=1, source_target_pairs={{0,6},{1,7},{2,4},{3,5},{4,2},{5,3},{6,0},{7,1},{8,14},{9,15},{10,... | collective-permute-start | bytes 122888 | tf_op jit(solution)/shard_map/ppermute | solution.py:519
  60.9 2.8 %collective-permute-done.10.refs_3_ = f32[40,256]{1,0:T(8,128)S(1)} collective-permute-done((f32[40,256]{1,0:T(8,128)S(1)}, f32[40,256]{1,0:T(8,128)S(1)}, u32[]{:S(2)}, u32[]{:S(2)}) %collective-permute-start.10) | collective-permute-done | bytes 40992 | tf_op jit(solution)/shard_map/ppermute | solution.py:519
  63.7 0.6 collective-permute-done.11.refs_4_
  64.4 1.7 %stress_update.1 = (f32[6,8,225]{2,1,0:T(8,128)}, f32[2,3,1,256]{3,2,1,0:T(1,128)S(1)}) custom-call(f32[1,40,256]{2,1,0:T(8,128)S(1)} %get-tuple-element.53.refs_0_, f32[40,256]{1,0:T(8,128)S(1)} %get-tuple-element.62.refs_1_, f32[80,256]{1,0:T(8,128)S(1)} %collective-permute-done.9.refs_2_, f32[40,256]{1,0:T(8,128)S(1)} %collective-permute-done.10.refs_3_, ...), custom_call_target="tpu_custom_call" | custom-call | tf_op jit(solution)/shard_map/stress_update/pallas_call | solution.py:700
  66.1 3.4 %collective-permute-start.12 = (f32[3,1,256]{2,1,0:T(1,128)S(1)}, f32[3,1,256]{2,1,0:T(1,128)S(1)}, u32[]{:S(2)}, u32[]{:S(2)}) collective-permute-start(f32[3,1,256]{2,1,0:T(1,128)S(1)} %slice_bitcast_fusion), channel_id=1, source_target_pairs={{0,1},{1,2},{2,3},{3,4},{4,5},{5,6},{6,7},{8,9},{9,10},{10,11},{11... | collective-permute-start | bytes 9224 | tf_op jit(solution)/shard_map/ppermute | solution.py:48
  69.5 1.3 %collective-permute-done.12 = f32[3,1,256]{2,1,0:T(1,128)S(1)} collective-permute-done((f32[3,1,256]{2,1,0:T(1,128)S(1)}, f32[3,1,256]{2,1,0:T(1,128)S(1)}, u32[]{:S(2)}, u32[]{:S(2)}) %collective-permute-start.12) | collective-permute-done | bytes 3104 | tf_op jit(solution)/shard_map/ppermute | solution.py:48
  70.8 0.6 bitcast_add_fusion
  (22 shorter events, 0.3 us)
Async XLA Ops:
  0.6 0.8 %copy-start.1 = (f32[3,4096]{1,0:T(4,128)S(1)}, f32[3,4096]{1,0:T(4,128)}, u32[]{:S(2)}) copy-start(f32[3,4096]{1,0:T(4,128)} %euler_ref.1) | copy-start | bytes 147460
  2.4 1.5 %copy-start.6 = (s32[216,2048]{1,0:T(8,128)S(1)}, s32[216,2048]{1,0:T(8,128)}, u32[]{:S(2)}) copy-start(s32[216,2048]{1,0:T(8,128)} %ids_ref.1) | copy-start | bytes 5308420
  17.4 2.2 %collective-permute-start = (f32[16,40,256]{2,1,0:T(8,128)S(1)}, f32[16,40,256]{2,1,0:T(8,128)S(1)}, u32[]{:S(2)}, u32[]{:S(2)}) collective-permute-start(f32[16,40,256]{2,1,0:T(8,128)S(1)} %get-tuple-element.38), channel_id=1, source_target_pairs={{0,8},{8,0},{16,24},{24,16},{1,9},{9,1},{17,25},{25,17},{2,10},{10... | collective-permute-start | bytes 1966088 | tf_op jit(solution)/shard_map/ppermute | solution.py:325
  17.9 1.7 %copy-start.4 = (f32[3,1,256]{2,1,0:T(1,128)S(1)}, f32[3,1,256]{2,1,0:T(1,128)}, u32[]{:S(2)}) copy-start(f32[3,1,256]{2,1,0:T(1,128)} %refs_5_.1) | copy-start | bytes 9220
  19.7 12.3 %collective-permute-start.1 = (f32[4,40,256]{2,1,0:T(8,128)S(1)}, f32[4,40,256]{2,1,0:T(8,128)S(1)}, u32[]{:S(2)}, u32[]{:S(2)}) collective-permute-start(f32[4,40,256]{2,1,0:T(8,128)S(1)} %get-tuple-element.41), channel_id=1, source_target_pairs={{0,17},{1,16},{2,19},{3,18},{4,21},{5,20},{6,23},{7,22},{8,25},{9,... | collective-permute-start | bytes 491528 | tf_op jit(solution)/shard_map/ppermute | solution.py:519
  23.6 8.5 %collective-permute-start.2 = (f32[4,40,256]{2,1,0:T(8,128)S(1)}, f32[4,40,256]{2,1,0:T(8,128)S(1)}, u32[]{:S(2)}, u32[]{:S(2)}) collective-permute-start(f32[4,40,256]{2,1,0:T(8,128)S(1)} %get-tuple-element.42), channel_id=1, source_target_pairs={{0,16},{1,17},{2,18},{3,19},{4,20},{5,21},{6,22},{7,23},{8,24},{9,... | collective-permute-start | bytes 491528 | tf_op jit(solution)/shard_map/ppermute | solution.py:519
  24.1 8.0 %collective-permute-start.3 = (f32[4,40,256]{2,1,0:T(8,128)S(1)}, f32[4,40,256]{2,1,0:T(8,128)S(1)}, u32[]{:S(2)}, u32[]{:S(2)}) collective-permute-start(f32[4,40,256]{2,1,0:T(8,128)S(1)} %get-tuple-element.43), channel_id=1, source_target_pairs={{0,1},{1,0},{2,3},{3,2},{4,5},{5,4},{6,7},{7,6},{8,9},{9,8},{10,11... | collective-permute-start | bytes 491528 | tf_op jit(solution)/shard_map/ppermute | solution.py:519
  32.2 11.1 %collective-permute-start.4 = (f32[2,40,256]{2,1,0:T(8,128)S(1)}, f32[2,40,256]{2,1,0:T(8,128)S(1)}, u32[]{:S(2)}, u32[]{:S(2)}) collective-permute-start(f32[2,40,256]{2,1,0:T(8,128)S(1)} %get-tuple-element.49), channel_id=1, source_target_pairs={{0,4},{1,5},{2,6},{3,7},{4,0},{5,1},{6,2},{7,3},{8,12},{9,13},{10,... | collective-permute-start | bytes 245768 | tf_op jit(solution)/shard_map/ppermute | solution.py:519
  43.2 21.1 %copy-start = (f32[12,8,225]{2,1,0:T(8,128)S(1)}, f32[12,8,225]{2,1,0:T(8,128)}, u32[]{:S(2)}) copy-start(f32[12,8,225]{2,1,0:T(8,128)} %refs_7_.1) | copy-start | bytes 259204
  43.2 21.1 %copy-start.2 = (f32[6,8,225]{2,1,0:T(8,128)S(1)}, f32[6,8,225]{2,1,0:T(8,128)}, u32[]{:S(2)}) copy-start(f32[6,8,225]{2,1,0:T(8,128)} %refs_6_.1) | copy-start | bytes 129604
  43.2 21.1 %copy-start.3 = (f32[24,8]{1,0:T(8,128)S(1)}, f32[24,8]{1,0:T(8,128)}, u32[]{:S(2)}) copy-start(f32[24,8]{1,0:T(8,128)} %constant.8.clone.refs_9_) | copy-start | bytes 2308
  43.2 21.1 %copy-start.5 = (s32[8,225]{1,0:T(8,128)S(1)}, s32[8,225]{1,0:T(8,128)}, u32[]{:S(2)}) copy-start(s32[8,225]{1,0:T(8,128)} %refs_8_.1) | copy-start | bytes 21604
  43.3 2.2 %collective-permute-start.5 = (f32[16,40,256]{2,1,0:T(8,128)S(1)}, f32[16,40,256]{2,1,0:T(8,128)S(1)}, u32[]{:S(2)}, u32[]{:S(2)}) collective-permute-start(f32[16,40,256]{2,1,0:T(8,128)S(1)} %get-tuple-element.56), channel_id=1, source_target_pairs={{0,8},{8,0},{16,24},{24,16},{1,9},{9,1},{17,25},{25,17},{2,10},{10... | collective-permute-start | bytes 1966088 | tf_op jit(solution)/shard_map/ppermute | solution.py:325
  45.6 8.0 %collective-permute-start.6 = (f32[4,40,256]{2,1,0:T(8,128)S(1)}, f32[4,40,256]{2,1,0:T(8,128)S(1)}, u32[]{:S(2)}, u32[]{:S(2)}) collective-permute-start(f32[4,40,256]{2,1,0:T(8,128)S(1)} %get-tuple-element.59), channel_id=1, source_target_pairs={{0,17},{1,16},{2,19},{3,18},{4,21},{5,20},{6,23},{7,22},{8,25},{9,... | collective-permute-start | bytes 491528 | tf_op jit(solution)/shard_map/ppermute | solution.py:519
  48.1 8.2 %collective-permute-start.7 = (f32[4,40,256]{2,1,0:T(8,128)S(1)}, f32[4,40,256]{2,1,0:T(8,128)S(1)}, u32[]{:S(2)}, u32[]{:S(2)}) collective-permute-start(f32[4,40,256]{2,1,0:T(8,128)S(1)} %get-tuple-element.60), channel_id=1, source_target_pairs={{0,16},{1,17},{2,18},{3,19},{4,20},{5,21},{6,22},{7,23},{8,24},{9,... | collective-permute-start | bytes 491528 | tf_op jit(solution)/shard_map/ppermute | solution.py:519
  48.6 7.8 %collective-permute-start.8 = (f32[4,40,256]{2,1,0:T(8,128)S(1)}, f32[4,40,256]{2,1,0:T(8,128)S(1)}, u32[]{:S(2)}, u32[]{:S(2)}) collective-permute-start(f32[4,40,256]{2,1,0:T(8,128)S(1)} %get-tuple-element.61), channel_id=1, source_target_pairs={{0,1},{1,0},{2,3},{3,2},{4,5},{5,4},{6,7},{7,6},{8,9},{9,8},{10,11... | collective-permute-start | bytes 491528 | tf_op jit(solution)/shard_map/ppermute | solution.py:519
  56.4 7.9 %collective-permute-start.9 = (f32[80,256]{1,0:T(8,128)S(1)}, f32[80,256]{1,0:T(8,128)S(1)}, u32[]{:S(2)}, u32[]{:S(2)}) collective-permute-start(f32[80,256]{1,0:T(8,128)S(1)} %get-tuple-element.63), channel_id=1, source_target_pairs={{0,2},{1,3},{2,0},{3,1},{4,6},{5,7},{6,4},{7,5},{8,10},{9,11},{10,... | collective-permute-start | bytes 245768 | tf_op jit(solution)/shard_map/ppermute | solution.py:519
  58.1 5.7 %collective-permute-start.10 = (f32[40,256]{1,0:T(8,128)S(1)}, f32[40,256]{1,0:T(8,128)S(1)}, u32[]{:S(2)}, u32[]{:S(2)}) collective-permute-start(f32[40,256]{1,0:T(8,128)S(1)} %get-tuple-element.64), channel_id=1, source_target_pairs={{0,4},{1,5},{2,6},{3,7},{4,0},{5,1},{6,2},{7,3},{8,12},{9,13},{10,... | collective-permute-start | bytes 122888 | tf_op jit(solution)/shard_map/ppermute | solution.py:519
  58.4 5.9 %collective-permute-start.11 = (f32[40,256]{1,0:T(8,128)S(1)}, f32[40,256]{1,0:T(8,128)S(1)}, u32[]{:S(2)}, u32[]{:S(2)}) collective-permute-start(f32[40,256]{1,0:T(8,128)S(1)} %get-tuple-element.65), channel_id=1, source_target_pairs={{0,6},{1,7},{2,4},{3,5},{4,2},{5,3},{6,0},{7,1},{8,14},{9,15},{10,... | collective-permute-start | bytes 122888 | tf_op jit(solution)/shard_map/ppermute | solution.py:519
  66.1 4.7 %collective-permute-start.12 = (f32[3,1,256]{2,1,0:T(1,128)S(1)}, f32[3,1,256]{2,1,0:T(1,128)S(1)}, u32[]{:S(2)}, u32[]{:S(2)}) collective-permute-start(f32[3,1,256]{2,1,0:T(1,128)S(1)} %slice_bitcast_fusion), channel_id=1, source_target_pairs={{0,1},{1,2},{2,3},{3,4},{4,5},{5,6},{6,7},{8,9},{9,10},{10,11},{11... | collective-permute-start | bytes 9224 | tf_op jit(solution)/shard_map/ppermute | solution.py:48

commit v15 on v13

--- a/solution.py
+++ b/solution.py
@@ -12,7 +12,7 @@
 GX = 15
 LANES = 128
 COLUMNS = 256
-CHUNKS = ((0, 4), (4, 4))
+CHUNKS = ((0, 5), (5, 3))
 QUANTUM = float((1 << 15) - 1)
 
 SLIP_PLANES = [

time: 69.7 us -> 69.6 us (level)
  waiting for transfers between devices: 13.8 us -> 13.1 us
  Pallas kernels: 31.6 us -> 32.3 us
  transfers between devices with their start and end apart: 13 -> 13, of which waited for: 8 -> 6; matrix products, arithmetic and copies ran while one was open for 0% -> 0% of each run, Pallas kernels for 23% -> 19%
where the time goes in v15:
time: 69.6 us; the launch traced here: 69.4 us
  Pallas kernels  32.3 us (46%)
  starting transfers between devices  19.5 us (28%)
  waiting for transfers between devices  13.1 us (19%)
  local copies, waits for them, and re-layouts  2.34 us (3%)
  other arithmetic  1.32 us (2%)
  between operations  0.8 us (1%)
    pallas_call x2, Pallas kernels, cell_sums(): pl.pallas_call(functools.partial(cell_sum_kernel, octants, per_octant), o...  28.3 us
    ppermute x10, starting transfers between devices, to_relative(): lax.ppermute(block, ('ca', 'fe'), [(i, i ^ flip) for i in range(groups *...  15.5 us
    ppermute x10, waiting for transfers between devices, to_relative(): lax.ppermute(block, ('ca', 'fe'), [(i, i ^ flip) for i in range(groups *...  9.81 us
    ppermute x1, starting transfers between devices, passed_along(): return lax.ppermute(block, axis, route)  3.4 us
    unnamed x14, local copies, waits for them, and re-layouts  2.34 us
    ppermute x2, waiting for transfers between devices, across_cores(): return lax.ppermute(block, 'ca', [(i, i ^ 1) for i in range(groups)])  1.98 us
    pallas_call x1, Pallas kernels, brick_sums(): pl.pallas_call(brick_sum_kernel, out_shape=[jax.ShapeDtypeStruct((places,...  1.82 us
    pallas_call x1, Pallas kernels, element_update(): pl.pallas_call(functools.partial(update_kernel, len(second)), out_shape=(...  1.7 us
  transfers between devices with their start and end apart: 13, of which 6 were waited for; matrix products, arithmetic and copies ran while one was open for 0% of the time, Pallas kernels for 19%

profile of v15, /device:TPU:0, one launch (start us, length us, event | category | flops | bytes accessed | tf_op | source)
XLA Modules:
  0.0 69.4 jit_solution(9658077825869767099)
XLA Ops:
  0.6 0.8 %copy-done.1 = f32[3,4096]{1,0:T(4,128)S(1)} copy-done((f32[3,4096]{1,0:T(4,128)S(1)}, f32[3,4096]{1,0:T(4,128)}, u32[]{:S(2)}) %copy-start.1) | copy-done | bytes 49176
  1.5 0.2 rotation_table.1.table_ref
  1.6 0.7 %add_select_fusion = s32[2048]{0:T(1024)S(1)} fusion(s32[2048]{0:T(1024)} %param.14, s32[2048]{0:T(1024)} %bitcast.15, s32[2048]{0:T(1024)} %param.12), kind=kLoop, calls=%fused_computation | loop fusion | flops 8192 | bytes 32768 | tf_op jit(solution)/shard_map/jit(_where)/select_n | solution.py:718
  2.4 1.5 %copy-done.6 = s32[216,2048]{1,0:T(8,128)S(1)} copy-done((s32[216,2048]{1,0:T(8,128)S(1)}, s32[216,2048]{1,0:T(8,128)}, u32[]{:S(2)}) %copy-start.6) | copy-done | bytes 1769496
  3.9 17.0 %cell_sums.2 = (s32[1,2048]{1,0:T(1,128)S(1)}, f32[16,48,256]{2,1,0:T(8,128)S(1)}, bf16[96,2048]{1,0:T(8,128)(2,1)S(1)}, s32[88,2048]{1,0:T(8,128)S(1)}) custom-call(s32[216,2048]{1,0:T(8,128)S(1)} %copy-done.6, s32[1,2048]{1,0:T(1,128)S(1)} %bitcast.14, s32[48,8,128]{2,1,0:T(8,128)S(1)} %rotation_table.1.table_ref), custom_call_target="tpu_custom_call" | custom-call | flops 20000000000 | bytes 50000000 | tf_op jit(solution)/shard_map/cell_sums/pallas_call | solution.py:376
  20.9 0.5 collective-permute-start
  21.4 1.8 %brick_sums.1 = (f32[16,48,256]{2,1,0:T(8,128)S(1)}, s32[1,2048]{1,0:T(1,128)S(1)}) custom-call(bf16[96,2048]{1,0:T(8,128)(2,1)S(1)} %get-tuple-element.31.split_ref, s32[1,2048]{1,0:T(1,128)S(1)} %get-tuple-element.32.label_ref), custom_call_target="tpu_custom_call" | custom-call | flops 1440000000 | bytes 4800000 | tf_op jit(solution)/shard_map/brick_sums/pallas_call | solution.py:406
  23.2 0.1 collective-permute-done
  23.3 0.1 core_sum_a.1
  23.4 3.9 %collective-permute-start.1 = (f32[4,48,256]{2,1,0:T(8,128)S(1)}, f32[4,48,256]{2,1,0:T(8,128)S(1)}, u32[]{:S(2)}, u32[]{:S(2)}) collective-permute-start(f32[4,48,256]{2,1,0:T(8,128)S(1)} %get-tuple-element.37), channel_id=1, source_target_pairs={{0,17},{1,16},{2,19},{3,18},{4,21},{5,20},{6,23},{7,22},{8,25},{9,... | collective-permute-start | bytes 589832 | tf_op jit(solution)/shard_map/ppermute | solution.py:512
  27.3 0.5 collective-permute-start.2
  27.8 0.1 collective-permute-start.3
  27.9 11.3 %cell_sums.3 = (f32[16,32,256]{2,1,0:T(8,128)S(1)}, f32[16,32,256]{2,1,0:T(8,128)S(1)}) custom-call(s32[88,2048]{1,0:T(8,128)S(1)} %get-tuple-element.41.ids_ref, s32[1,2048]{1,0:T(1,128)S(1)} %get-tuple-element.42.label_ref, s32[48,8,128]{2,1,0:T(8,128)S(1)} %rotation_table.1.table_ref), custom_call_target="tpu_custom_call" | custom-call | flops 12000000000 | bytes 30000000 | tf_op jit(solution)/shard_map/cell_sums/pallas_call | solution.py:376
  39.3 0.0 copy-start
  39.3 0.1 plane_sum_a.1
  39.4 0.1 collective-permute-start.5
  39.5 1.9 %collective-permute-done.5 = f32[16,32,256]{2,1,0:T(8,128)S(1)} collective-permute-done((f32[16,32,256]{2,1,0:T(8,128)S(1)}, f32[16,32,256]{2,1,0:T(8,128)S(1)}, u32[]{:S(2)}, u32[]{:S(2)}) %collective-permute-start.5) | collective-permute-done | bytes 524320 | tf_op jit(solution)/shard_map/ppermute | solution.py:315
  41.4 0.1 core_sum_b.1
  41.5 2.9 %collective-permute-start.6 = (f32[4,32,256]{2,1,0:T(8,128)S(1)}, f32[4,32,256]{2,1,0:T(8,128)S(1)}, u32[]{:S(2)}, u32[]{:S(2)}) collective-permute-start(f32[4,32,256]{2,1,0:T(8,128)S(1)} %get-tuple-element.50), channel_id=1, source_target_pairs={{0,17},{1,16},{2,19},{3,18},{4,21},{5,20},{6,23},{7,22},{8,25},{9,... | collective-permute-start | bytes 393224 | tf_op jit(solution)/shard_map/ppermute | solution.py:512
  44.4 0.5 collective-permute-start.7
  44.9 0.1 collective-permute-start.8
  45.1 3.0 %collective-permute-start.4 = (f32[2,48,256]{2,1,0:T(8,128)S(1)}, f32[2,48,256]{2,1,0:T(8,128)S(1)}, u32[]{:S(2)}, u32[]{:S(2)}) collective-permute-start(f32[2,48,256]{2,1,0:T(8,128)S(1)} %get-tuple-element.45), channel_id=1, source_target_pairs={{0,4},{1,5},{2,6},{3,7},{4,0},{5,1},{6,2},{7,3},{8,12},{9,13},{10,... | collective-permute-start | bytes 294920 | tf_op jit(solution)/shard_map/ppermute | solution.py:512
  48.0 4.4 %collective-permute-done.4.received_ref = f32[2,48,256]{2,1,0:T(8,128)S(1)} collective-permute-done((f32[2,48,256]{2,1,0:T(8,128)S(1)}, f32[2,48,256]{2,1,0:T(8,128)S(1)}, u32[]{:S(2)}, u32[]{:S(2)}) %collective-permute-start.4) | collective-permute-done | bytes 98336 | tf_op jit(solution)/shard_map/ppermute | solution.py:512
  52.5 0.8 %collective-permute-start.9 = (f32[80,256]{1,0:T(8,128)S(1)}, f32[80,256]{1,0:T(8,128)S(1)}, u32[]{:S(2)}, u32[]{:S(2)}) collective-permute-start(f32[80,256]{1,0:T(8,128)S(1)} %get-tuple-element.55), channel_id=1, source_target_pairs={{0,2},{1,3},{2,0},{3,1},{4,6},{5,7},{6,4},{7,5},{8,10},{9,11},{10,... | collective-permute-start | bytes 245768 | tf_op jit(solution)/shard_map/ppermute | solution.py:512
  53.2 3.4 %collective-permute-start.10 = (f32[32,256]{1,0:T(8,128)S(1)}, f32[32,256]{1,0:T(8,128)S(1)}, u32[]{:S(2)}, u32[]{:S(2)}) collective-permute-start(f32[32,256]{1,0:T(8,128)S(1)} %get-tuple-element.56), channel_id=1, source_target_pairs={{0,4},{1,5},{2,6},{3,7},{4,0},{5,1},{6,2},{7,3},{8,12},{9,13},{10,... | collective-permute-start | bytes 98312 | tf_op jit(solution)/shard_map/ppermute | solution.py:512
  56.6 0.3 collective-permute-start.11
  56.9 1.6 %collective-permute-done.10.refs_3_ = f32[32,256]{1,0:T(8,128)S(1)} collective-permute-done((f32[32,256]{1,0:T(8,128)S(1)}, f32[32,256]{1,0:T(8,128)S(1)}, u32[]{:S(2)}, u32[]{:S(2)}) %collective-permute-start.10) | collective-permute-done | bytes 32800 | tf_op jit(solution)/shard_map/ppermute | solution.py:512
  58.5 3.8 %collective-permute-done.11.refs_4_ = f32[32,256]{1,0:T(8,128)S(1)} collective-permute-done((f32[32,256]{1,0:T(8,128)S(1)}, f32[32,256]{1,0:T(8,128)S(1)}, u32[]{:S(2)}, u32[]{:S(2)}) %collective-permute-start.11) | collective-permute-done | bytes 32800 | tf_op jit(solution)/shard_map/ppermute | solution.py:512
  62.4 1.7 %stress_update.1 = (f32[6,8,225]{2,1,0:T(8,128)}, f32[2,3,1,256]{3,2,1,0:T(1,128)S(1)}) custom-call(f32[48,256]{1,0:T(8,128)S(1)} %get-tuple-element.53.refs_0_, f32[32,256]{1,0:T(8,128)S(1)} %get-tuple-element.54.refs_1_, f32[80,256]{1,0:T(8,128)S(1)} %collective-permute-done.9.refs_2_, f32[32,256]{1,0:T(8,128)S(1)} %collective-permute-done.10.refs_3_, ...), custom_call_target="tpu_custom_call" | custom-call | tf_op jit(solution)/shard_map/stress_update/pallas_call | solution.py:693
  64.1 3.4 %collective-permute-start.12 = (f32[3,1,256]{2,1,0:T(1,128)S(1)}, f32[3,1,256]{2,1,0:T(1,128)S(1)}, u32[]{:S(2)}, u32[]{:S(2)}) collective-permute-start(f32[3,1,256]{2,1,0:T(1,128)S(1)} %slice_bitcast_fusion), channel_id=1, source_target_pairs={{0,1},{1,2},{2,3},{3,4},{4,5},{5,6},{6,7},{8,9},{9,10},{10,11},{11... | collective-permute-start | bytes 9224 | tf_op jit(solution)/shard_map/ppermute | solution.py:48
  67.5 1.3 %collective-permute-done.12 = f32[3,1,256]{2,1,0:T(1,128)S(1)} collective-permute-done((f32[3,1,256]{2,1,0:T(1,128)S(1)}, f32[3,1,256]{2,1,0:T(1,128)S(1)}, u32[]{:S(2)}, u32[]{:S(2)}) %collective-permute-start.12) | collective-permute-done | bytes 3104 | tf_op jit(solution)/shard_map/ppermute | solution.py:48
  68.8 0.6 bitcast_add_fusion
  (20 shorter events, 0.1 us)
Async XLA Ops:
  0.6 0.8 %copy-start.1 = (f32[3,4096]{1,0:T(4,128)S(1)}, f32[3,4096]{1,0:T(4,128)}, u32[]{:S(2)}) copy-start(f32[3,4096]{1,0:T(4,128)} %euler_ref.1) | copy-start | bytes 147460
  2.4 1.5 %copy-start.6 = (s32[216,2048]{1,0:T(8,128)S(1)}, s32[216,2048]{1,0:T(8,128)}, u32[]{:S(2)}) copy-start(s32[216,2048]{1,0:T(8,128)} %ids_ref.1) | copy-start | bytes 5308420
  20.9 2.4 %collective-permute-start = (f32[16,48,256]{2,1,0:T(8,128)S(1)}, f32[16,48,256]{2,1,0:T(8,128)S(1)}, u32[]{:S(2)}, u32[]{:S(2)}) collective-permute-start(f32[16,48,256]{2,1,0:T(8,128)S(1)} %get-tuple-element.34), channel_id=1, source_target_pairs={{0,8},{8,0},{16,24},{24,16},{1,9},{9,1},{17,25},{25,17},{2,10},{10... | collective-permute-start | bytes 2359304 | tf_op jit(solution)/shard_map/ppermute | solution.py:315
  21.4 1.9 %copy-start.4 = (f32[3,1,256]{2,1,0:T(1,128)S(1)}, f32[3,1,256]{2,1,0:T(1,128)}, u32[]{:S(2)}) copy-start(f32[3,1,256]{2,1,0:T(1,128)} %refs_5_.1) | copy-start | bytes 9220
  23.4 15.9 %collective-permute-start.1 = (f32[4,48,256]{2,1,0:T(8,128)S(1)}, f32[4,48,256]{2,1,0:T(8,128)S(1)}, u32[]{:S(2)}, u32[]{:S(2)}) collective-permute-start(f32[4,48,256]{2,1,0:T(8,128)S(1)} %get-tuple-element.37), channel_id=1, source_target_pairs={{0,17},{1,16},{2,19},{3,18},{4,21},{5,20},{6,23},{7,22},{8,25},{9,... | collective-permute-start | bytes 589832 | tf_op jit(solution)/shard_map/ppermute | solution.py:512
  27.3 12.0 %collective-permute-start.2 = (f32[4,48,256]{2,1,0:T(8,128)S(1)}, f32[4,48,256]{2,1,0:T(8,128)S(1)}, u32[]{:S(2)}, u32[]{:S(2)}) collective-permute-start(f32[4,48,256]{2,1,0:T(8,128)S(1)} %get-tuple-element.38), channel_id=1, source_target_pairs={{0,16},{1,17},{2,18},{3,19},{4,20},{5,21},{6,22},{7,23},{8,24},{9,... | collective-permute-start | bytes 589832 | tf_op jit(solution)/shard_map/ppermute | solution.py:512
  27.8 11.5 %collective-permute-start.3 = (f32[4,48,256]{2,1,0:T(8,128)S(1)}, f32[4,48,256]{2,1,0:T(8,128)S(1)}, u32[]{:S(2)}, u32[]{:S(2)}) collective-permute-start(f32[4,48,256]{2,1,0:T(8,128)S(1)} %get-tuple-element.39), channel_id=1, source_target_pairs={{0,1},{1,0},{2,3},{3,2},{4,5},{5,4},{6,7},{7,6},{8,9},{9,8},{10,11... | collective-permute-start | bytes 589832 | tf_op jit(solution)/shard_map/ppermute | solution.py:512
  39.3 23.1 %copy-start = (f32[12,8,225]{2,1,0:T(8,128)S(1)}, f32[12,8,225]{2,1,0:T(8,128)}, u32[]{:S(2)}) copy-start(f32[12,8,225]{2,1,0:T(8,128)} %refs_7_.1) | copy-start | bytes 259204
  39.3 23.1 %copy-start.2 = (f32[6,8,225]{2,1,0:T(8,128)S(1)}, f32[6,8,225]{2,1,0:T(8,128)}, u32[]{:S(2)}) copy-start(f32[6,8,225]{2,1,0:T(8,128)} %refs_6_.1) | copy-start | bytes 129604
  39.3 23.1 %copy-start.3 = (f32[24,8]{1,0:T(8,128)S(1)}, f32[24,8]{1,0:T(8,128)}, u32[]{:S(2)}) copy-start(f32[24,8]{1,0:T(8,128)} %constant.8.clone.refs_9_) | copy-start | bytes 2308
  39.3 23.1 %copy-start.5 = (s32[8,225]{1,0:T(8,128)S(1)}, s32[8,225]{1,0:T(8,128)}, u32[]{:S(2)}) copy-start(s32[8,225]{1,0:T(8,128)} %refs_8_.1) | copy-start | bytes 21604
  39.4 2.0 %collective-permute-start.5 = (f32[16,32,256]{2,1,0:T(8,128)S(1)}, f32[16,32,256]{2,1,0:T(8,128)S(1)}, u32[]{:S(2)}, u32[]{:S(2)}) collective-permute-start(f32[16,32,256]{2,1,0:T(8,128)S(1)} %get-tuple-element.47), channel_id=1, source_target_pairs={{0,8},{8,0},{16,24},{24,16},{1,9},{9,1},{17,25},{25,17},{2,10},{10... | collective-permute-start | bytes 1572872 | tf_op jit(solution)/shard_map/ppermute | solution.py:315
  41.5 10.9 %collective-permute-start.6 = (f32[4,32,256]{2,1,0:T(8,128)S(1)}, f32[4,32,256]{2,1,0:T(8,128)S(1)}, u32[]{:S(2)}, u32[]{:S(2)}) collective-permute-start(f32[4,32,256]{2,1,0:T(8,128)S(1)} %get-tuple-element.50), channel_id=1, source_target_pairs={{0,17},{1,16},{2,19},{3,18},{4,21},{5,20},{6,23},{7,22},{8,25},{9,... | collective-permute-start | bytes 393224 | tf_op jit(solution)/shard_map/ppermute | solution.py:512
  44.4 8.0 %collective-permute-start.7 = (f32[4,32,256]{2,1,0:T(8,128)S(1)}, f32[4,32,256]{2,1,0:T(8,128)S(1)}, u32[]{:S(2)}, u32[]{:S(2)}) collective-permute-start(f32[4,32,256]{2,1,0:T(8,128)S(1)} %get-tuple-element.51), channel_id=1, source_target_pairs={{0,16},{1,17},{2,18},{3,19},{4,20},{5,21},{6,22},{7,23},{8,24},{9,... | collective-permute-start | bytes 393224 | tf_op jit(solution)/shard_map/ppermute | solution.py:512
  44.9 7.5 %collective-permute-start.8 = (f32[4,32,256]{2,1,0:T(8,128)S(1)}, f32[4,32,256]{2,1,0:T(8,128)S(1)}, u32[]{:S(2)}, u32[]{:S(2)}) collective-permute-start(f32[4,32,256]{2,1,0:T(8,128)S(1)} %get-tuple-element.52), channel_id=1, source_target_pairs={{0,1},{1,0},{2,3},{3,2},{4,5},{5,4},{6,7},{7,6},{8,9},{9,8},{10,11... | collective-permute-start | bytes 393224 | tf_op jit(solution)/shard_map/ppermute | solution.py:512
  45.1 7.4 %collective-permute-start.4 = (f32[2,48,256]{2,1,0:T(8,128)S(1)}, f32[2,48,256]{2,1,0:T(8,128)S(1)}, u32[]{:S(2)}, u32[]{:S(2)}) collective-permute-start(f32[2,48,256]{2,1,0:T(8,128)S(1)} %get-tuple-element.45), channel_id=1, source_target_pairs={{0,4},{1,5},{2,6},{3,7},{4,0},{5,1},{6,2},{7,3},{8,12},{9,13},{10,... | collective-permute-start | bytes 294920 | tf_op jit(solution)/shard_map/ppermute | solution.py:512
  52.5 9.9 %collective-permute-start.9 = (f32[80,256]{1,0:T(8,128)S(1)}, f32[80,256]{1,0:T(8,128)S(1)}, u32[]{:S(2)}, u32[]{:S(2)}) collective-permute-start(f32[80,256]{1,0:T(8,128)S(1)} %get-tuple-element.55), channel_id=1, source_target_pairs={{0,2},{1,3},{2,0},{3,1},{4,6},{5,7},{6,4},{7,5},{8,10},{9,11},{10,... | collective-permute-start | bytes 245768 | tf_op jit(solution)/shard_map/ppermute | solution.py:512
  53.2 5.3 %collective-permute-start.10 = (f32[32,256]{1,0:T(8,128)S(1)}, f32[32,256]{1,0:T(8,128)S(1)}, u32[]{:S(2)}, u32[]{:S(2)}) collective-permute-start(f32[32,256]{1,0:T(8,128)S(1)} %get-tuple-element.56), channel_id=1, source_target_pairs={{0,4},{1,5},{2,6},{3,7},{4,0},{5,1},{6,2},{7,3},{8,12},{9,13},{10,... | collective-permute-start | bytes 98312 | tf_op jit(solution)/shard_map/ppermute | solution.py:512
  56.6 5.7 %collective-permute-start.11 = (f32[32,256]{1,0:T(8,128)S(1)}, f32[32,256]{1,0:T(8,128)S(1)}, u32[]{:S(2)}, u32[]{:S(2)}) collective-permute-start(f32[32,256]{1,0:T(8,128)S(1)} %get-tuple-element.57), channel_id=1, source_target_pairs={{0,6},{1,7},{2,4},{3,5},{4,2},{5,3},{6,0},{7,1},{8,14},{9,15},{10,... | collective-permute-start | bytes 98312 | tf_op jit(solution)/shard_map/ppermute | solution.py:512
  64.1 4.7 %collective-permute-start.12 = (f32[3,1,256]{2,1,0:T(1,128)S(1)}, f32[3,1,256]{2,1,0:T(1,128)S(1)}, u32[]{:S(2)}, u32[]{:S(2)}) collective-permute-start(f32[3,1,256]{2,1,0:T(1,128)S(1)} %slice_bitcast_fusion), channel_id=1, source_target_pairs={{0,1},{1,2},{2,3},{3,4},{4,5},{5,6},{6,7},{8,9},{9,10},{10,11},{11... | collective-permute-start | bytes 9224 | tf_op jit(solution)/shard_map/ppermute | solution.py:48

commit v16 on v12

--- a/solution.py
+++ b/solution.py
@@ -186,12 +186,15 @@
     *refs,
 ):
     first, count = octants
-    start = ids_ref.shape[0] - (8 - first) * per_octant
+    cells = ids_ref.shape[0] if label_ref is not None else ids_ref.shape[0] - 1
+    start = cells - (8 - first) * per_octant
+    if label_ref is None:
+        label_ref = ids_ref.at[pl.ds(cells, 1), :]
     tile_ref, raw_ref, place_ref, masked_ref = refs[-4:]
     if first + count < 8:
         label_out_ref, send_ref, split_ref, rest_ref = refs[:-4]
         label_out_ref[...] = label_ref[...]
-        rest_ref[...] = ids_ref[pl.ds(ids_ref.shape[0] - rest_ref.shape[0], rest_ref.shape[0]), :]
+        rest_ref[...] = ids_ref[pl.ds(cells - rest_ref.shape[0], rest_ref.shape[0]), :]
         targets = [(send_ref.shape[0], send_ref)]
     else:
         send_ref, keep_ref, split_ref = refs[:-4]
@@ -269,16 +272,14 @@
     for base, out_ref in targets:
         out_ref[...] = jnp.zeros(out_ref.shape, jnp.float32)
     raw_ref[:, pl.ds(0, width)] = jnp.zeros((raw_ref.shape[0], width), jnp.float32)
-    split_ref[:, pl.ds(0, width)] = jnp.zeros((split_ref.shape[0], width), jnp.bfloat16)
 
     def step(pair, carry):
-        add_bricks(jnp.maximum(pair - 2, 0), pair >= 2)
         fold_entries(jnp.maximum(pair - 1, 0))
+        add_bricks(jnp.maximum(pair - 1, 0), pair >= 1)
         look_up(pair)
         return carry
 
     lax.fori_loop(0, pairs, step, 0, unroll=2)
-    add_bricks(pairs - 2, True)
     fold_entries(pairs - 1)
     add_bricks(pairs - 1, True)
 
@@ -365,7 +366,7 @@
     left = 8 - first - count
     if left:
         out_shape = [
-            jax.ShapeDtypeStruct(labels.shape, jnp.int32),
+            jax.ShapeDtypeStruct((1, bricks), jnp.int32),
             half,
             split,
             jax.ShapeDtypeStruct((-(-left * per_octant // 8) * 8, bricks), jnp.int32),
@@ -373,8 +374,13 @@
     else:
         out_shape = [half, half]
         scratch.append(pltpu.VMEM(split.shape, split.dtype))
+    kernel = functools.partial(cell_sum_kernel, octants, per_octant)
+    inputs = (ids, labels, table)
+    if labels is None:
+        kernel = lambda ids_ref, *refs: cell_sum_kernel(octants, per_octant, ids_ref, None, *refs)
+        inputs = (ids, table)
     return pl.pallas_call(
-        functools.partial(cell_sum_kernel, octants, per_octant),
+        kernel,
         out_shape=out_shape,
         scratch_shapes=scratch
         + [
@@ -387,7 +393,7 @@
             flops=count * 4 * 10**9, bytes_accessed=count * 10**7, transcendentals=0
         ),
         name="cell_sums",
-    )(ids, labels, table)
+    )(*inputs)
 
 
 def padded_rows(count):
@@ -716,9 +722,10 @@
     bricks = grain_ids.shape[1]
     owner = lax.optimization_barrier(brick_owner.reshape(bricks))
     labels = jnp.where(brick_active > 0, owner * COLUMNS + brick_element, -1).reshape(1, bricks)
+    ids = jnp.concatenate([grain_ids, labels], axis=0)
     per_octant = grain_ids.shape[0] // 8
     table = rotation_table(euler_angles)
-    labels, send, split, ids = cell_sums(CHUNKS[0], per_octant, grain_ids, labels, table, half)
+    labels, send, split, ids = cell_sums(CHUNKS[0], per_octant, ids, None, table, half)
     keep, labels = brick_sums(split, labels, half)
     core_a, labels, own = core_sum(
         keep, across_cores(send), [labels, displacement], "core_sum_a"

time: 69 us -> 69.5 us (level)
  other arithmetic: 1.32 us -> 2.99 us
  local copies, waits for them, and re-layouts: 2.34 us -> 0.86 us
    concatenate x0 -> x1, other arithmetic: none -> 1.67 us  [body(): ids = jnp.concatenate([grain_ids, labels], axis=0)]
    unnamed x14 -> x12, local copies, waits for them, and re-layouts: 2.34 us -> 0.86 us
where the time goes in v16:
time: 69.5 us; the launch traced here: 69.3 us
  Pallas kernels  32.4 us (47%)
  starting transfers between devices  19.1 us (27%)
  waiting for transfers between devices  13.1 us (19%)
  other arithmetic  2.99 us (4%)
  local copies, waits for them, and re-layouts  0.86 us (1%)
  between operations  0.8 us (1%)
    pallas_call x2, Pallas kernels, cell_sums(): pl.pallas_call(kernel, out_shape=out_shape, scratch_shapes=scratch + [plt...  28.1 us
    ppermute x10, starting transfers between devices, to_relative(): lax.ppermute(block, ('ca', 'fe'), [(i, i ^ flip) for i in range(groups *...  15.1 us
    ppermute x10, waiting for transfers between devices, to_relative(): lax.ppermute(block, ('ca', 'fe'), [(i, i ^ flip) for i in range(groups *...  11.8 us
    ppermute x1, starting transfers between devices, passed_along(): return lax.ppermute(block, axis, route)  3.4 us
    pallas_call x1, Pallas kernels, brick_sums(): pl.pallas_call(brick_sum_kernel, out_shape=[jax.ShapeDtypeStruct((places,...  2.14 us
    pallas_call x1, Pallas kernels, element_update(): pl.pallas_call(functools.partial(update_kernel, len(second)), out_shape=(...  1.69 us
    concatenate x1, other arithmetic, body(): ids = jnp.concatenate([grain_ids, labels], axis=0)  1.67 us
  transfers between devices with their start and end apart: 13, of which 8 were waited for; matrix products, arithmetic and copies ran while one was open for 0% of the time, Pallas kernels for 14%

profile of v16, /device:TPU:0, one launch (start us, length us, event | category | flops | bytes accessed | tf_op | source)
XLA Modules:
  0.0 69.3 jit_solution(13608650013504584440)
XLA Ops:
  0.6 0.8 %copy-done.1 = f32[3,4096]{1,0:T(4,128)S(1)} copy-done((f32[3,4096]{1,0:T(4,128)S(1)}, f32[3,4096]{1,0:T(4,128)}, u32[]{:S(2)}) %copy-start.1) | copy-done | bytes 49176
  1.5 0.2 rotation_table.1.refs_0_.table_ref
  1.6 0.7 %add_select_fusion = s32[2048]{0:T(1024)S(1)} fusion(s32[2048]{0:T(1024)} %param.14, s32[2048]{0:T(1024)} %bitcast.15, s32[2048]{0:T(1024)} %param.12), kind=kLoop, calls=%fused_computation.1 | loop fusion | flops 8192 | bytes 32768 | tf_op jit(solution)/shard_map/jit(_where)/select_n | solution.py:724
  2.4 1.7 %pad_add_fusion.ids_ref = s32[217,2048]{1,0:T(8,128)S(1)} fusion(s32[1,2048]{1,0:T(1,128)S(1)} %bitcast.14, s32[216,2048]{1,0:T(8,128)} %param.10), kind=kLoop, calls=%fused_computation | loop fusion | flops 444416 | bytes 3555328 | tf_op jit(solution)/shard_map/concatenate | solution.py:725
  4.1 20.6 %cell_sums.2 = (s32[1,2048]{1,0:T(1,128)S(1)}, f32[16,56,256]{2,1,0:T(8,128)S(1)}, bf16[112,2048]{1,0:T(8,128)(2,1)S(1)}, s32[56,2048]{1,0:T(8,128)S(1)}) custom-call(s32[217,2048]{1,0:T(8,128)S(1)} %pad_add_fusion.ids_ref, s32[48,8,128]{2,1,0:T(8,128)S(1)} %rotation_table.1.refs_0_.table_ref), custom_call_target="tpu_custom_call" | custom-call | flops 24000000000 | bytes 60000000 | tf_op jit(solution)/shard_map/cell_sums/pallas_call | solution.py:382
  24.7 0.5 collective-permute-start
  25.2 2.1 %brick_sums.1 = (f32[16,56,256]{2,1,0:T(8,128)S(1)}, s32[1,2048]{1,0:T(1,128)S(1)}) custom-call(bf16[112,2048]{1,0:T(8,128)(2,1)S(1)} %get-tuple-element.31.split_ref, s32[1,2048]{1,0:T(1,128)S(1)} %get-tuple-element.32.label_ref), custom_call_target="tpu_custom_call" | custom-call | flops 1680000000 | bytes 5600000 | tf_op jit(solution)/shard_map/brick_sums/pallas_call | solution.py:412
  27.4 0.1 core_sum_a.1
  27.5 3.8 %collective-permute-start.1 = (f32[4,56,256]{2,1,0:T(8,128)S(1)}, f32[4,56,256]{2,1,0:T(8,128)S(1)}, u32[]{:S(2)}, u32[]{:S(2)}) collective-permute-start(f32[4,56,256]{2,1,0:T(8,128)S(1)} %get-tuple-element.37), channel_id=1, source_target_pairs={{0,17},{1,16},{2,19},{3,18},{4,21},{5,20},{6,23},{7,22},{8,25},{9,... | collective-permute-start | bytes 688136 | tf_op jit(solution)/shard_map/ppermute | solution.py:518
  31.3 0.5 collective-permute-start.2
  31.8 0.1 collective-permute-start.3
  31.9 7.5 %cell_sums.3 = (f32[16,24,256]{2,1,0:T(8,128)S(1)}, f32[16,24,256]{2,1,0:T(8,128)S(1)}) custom-call(s32[56,2048]{1,0:T(8,128)S(1)} %get-tuple-element.41.ids_ref, s32[1,2048]{1,0:T(1,128)S(1)} %get-tuple-element.42.label_ref, s32[48,8,128]{2,1,0:T(8,128)S(1)} %rotation_table.1.refs_0_.table_ref), custom_call_target="tpu_custom_call" | custom-call | flops 8000000000 | bytes 20000000 | tf_op jit(solution)/shard_map/cell_sums/pallas_call | solution.py:382
  39.5 2.7 %collective-permute-done.2.refs_2_ = f32[4,56,256]{2,1,0:T(8,128)S(1)} collective-permute-done((f32[4,56,256]{2,1,0:T(8,128)S(1)}, f32[4,56,256]{2,1,0:T(8,128)S(1)}, u32[]{:S(2)}, u32[]{:S(2)}) %collective-permute-start.2) | collective-permute-done | bytes 229408 | tf_op jit(solution)/shard_map/ppermute | solution.py:518
  42.2 0.3 collective-permute-done.3.refs_3_
  42.5 0.1 plane_sum_a.1
  42.6 0.1 collective-permute-start.5
  42.6 2.7 %collective-permute-start.4 = (f32[2,56,256]{2,1,0:T(8,128)S(1)}, f32[2,56,256]{2,1,0:T(8,128)S(1)}, u32[]{:S(2)}, u32[]{:S(2)}) collective-permute-start(f32[2,56,256]{2,1,0:T(8,128)S(1)} %get-tuple-element.45), channel_id=1, source_target_pairs={{0,4},{1,5},{2,6},{3,7},{4,0},{5,1},{6,2},{7,3},{8,12},{9,13},{10,... | collective-permute-start | bytes 344072 | tf_op jit(solution)/shard_map/ppermute | solution.py:518
  45.4 1.7 %collective-permute-start.6 = (f32[4,24,256]{2,1,0:T(8,128)S(1)}, f32[4,24,256]{2,1,0:T(8,128)S(1)}, u32[]{:S(2)}, u32[]{:S(2)}) collective-permute-start(f32[4,24,256]{2,1,0:T(8,128)S(1)} %get-tuple-element.50), channel_id=1, source_target_pairs={{0,17},{1,16},{2,19},{3,18},{4,21},{5,20},{6,23},{7,22},{8,25},{9,... | collective-permute-start | bytes 294920 | tf_op jit(solution)/shard_map/ppermute | solution.py:518
  47.1 1.3 %collective-permute-start.7 = (f32[4,24,256]{2,1,0:T(8,128)S(1)}, f32[4,24,256]{2,1,0:T(8,128)S(1)}, u32[]{:S(2)}, u32[]{:S(2)}) collective-permute-start(f32[4,24,256]{2,1,0:T(8,128)S(1)} %get-tuple-element.51), channel_id=1, source_target_pairs={{0,16},{1,17},{2,18},{3,19},{4,20},{5,21},{6,22},{7,23},{8,24},{9,... | collective-permute-start | bytes 294920 | tf_op jit(solution)/shard_map/ppermute | solution.py:518
  48.4 0.5 collective-permute-start.8
  48.9 2.6 %collective-permute-done.4.received_ref = f32[2,56,256]{2,1,0:T(8,128)S(1)} collective-permute-done((f32[2,56,256]{2,1,0:T(8,128)S(1)}, f32[2,56,256]{2,1,0:T(8,128)S(1)}, u32[]{:S(2)}, u32[]{:S(2)}) %collective-permute-start.4) | collective-permute-done | bytes 114720 | tf_op jit(solution)/shard_map/ppermute | solution.py:518
  51.6 0.1 collective-permute-done.6.refs_1_
  51.7 1.6 %collective-permute-done.7.refs_2_ = f32[4,24,256]{2,1,0:T(8,128)S(1)} collective-permute-done((f32[4,24,256]{2,1,0:T(8,128)S(1)}, f32[4,24,256]{2,1,0:T(8,128)S(1)}, u32[]{:S(2)}, u32[]{:S(2)}) %collective-permute-start.7) | collective-permute-done | bytes 98336 | tf_op jit(solution)/shard_map/ppermute | solution.py:518
  53.4 1.6 %collective-permute-start.9 = (f32[80,256]{1,0:T(8,128)S(1)}, f32[80,256]{1,0:T(8,128)S(1)}, u32[]{:S(2)}, u32[]{:S(2)}) collective-permute-start(f32[80,256]{1,0:T(8,128)S(1)} %get-tuple-element.55), channel_id=1, source_target_pairs={{0,2},{1,3},{2,0},{3,1},{4,6},{5,7},{6,4},{7,5},{8,10},{9,11},{10,... | collective-permute-start | bytes 245768 | tf_op jit(solution)/shard_map/ppermute | solution.py:518
  55.0 1.6 %collective-permute-start.10 = (f32[24,256]{1,0:T(8,128)S(1)}, f32[24,256]{1,0:T(8,128)S(1)}, u32[]{:S(2)}, u32[]{:S(2)}) collective-permute-start(f32[24,256]{1,0:T(8,128)S(1)} %get-tuple-element.56), channel_id=1, source_target_pairs={{0,4},{1,5},{2,6},{3,7},{4,0},{5,1},{6,2},{7,3},{8,12},{9,13},{10,... | collective-permute-start | bytes 73736 | tf_op jit(solution)/shard_map/ppermute | solution.py:518
  56.6 1.2 %collective-permute-start.11 = (f32[24,256]{1,0:T(8,128)S(1)}, f32[24,256]{1,0:T(8,128)S(1)}, u32[]{:S(2)}, u32[]{:S(2)}) collective-permute-start(f32[24,256]{1,0:T(8,128)S(1)} %get-tuple-element.57), channel_id=1, source_target_pairs={{0,6},{1,7},{2,4},{3,5},{4,2},{5,3},{6,0},{7,1},{8,14},{9,15},{10,... | collective-permute-start | bytes 73736 | tf_op jit(solution)/shard_map/ppermute | solution.py:518
  57.8 2.1 %collective-permute-done.10.refs_3_ = f32[24,256]{1,0:T(8,128)S(1)} collective-permute-done((f32[24,256]{1,0:T(8,128)S(1)}, f32[24,256]{1,0:T(8,128)S(1)}, u32[]{:S(2)}, u32[]{:S(2)}) %collective-permute-start.10) | collective-permute-done | bytes 24608 | tf_op jit(solution)/shard_map/ppermute | solution.py:518
  59.9 2.4 %collective-permute-done.11.refs_4_ = f32[24,256]{1,0:T(8,128)S(1)} collective-permute-done((f32[24,256]{1,0:T(8,128)S(1)}, f32[24,256]{1,0:T(8,128)S(1)}, u32[]{:S(2)}, u32[]{:S(2)}) %collective-permute-start.11) | collective-permute-done | bytes 24608 | tf_op jit(solution)/shard_map/ppermute | solution.py:518
  62.3 1.7 %stress_update.1 = (f32[6,8,225]{2,1,0:T(8,128)}, f32[2,3,1,256]{3,2,1,0:T(1,128)S(1)}) custom-call(f32[56,256]{1,0:T(8,128)S(1)} %get-tuple-element.53.refs_0_, f32[24,256]{1,0:T(8,128)S(1)} %get-tuple-element.54.refs_1_, f32[80,256]{1,0:T(8,128)S(1)} %collective-permute-done.9.refs_2_, f32[24,256]{1,0:T(8,128)S(1)} %collective-permute-done.10.refs_3_, ...), custom_call_target="tpu_custom_call" | custom-call | tf_op jit(solution)/shard_map/stress_update/pallas_call | solution.py:699
  64.0 3.4 %collective-permute-start.12 = (f32[3,1,256]{2,1,0:T(1,128)S(1)}, f32[3,1,256]{2,1,0:T(1,128)S(1)}, u32[]{:S(2)}, u32[]{:S(2)}) collective-permute-start(f32[3,1,256]{2,1,0:T(1,128)S(1)} %slice_bitcast_fusion), channel_id=1, source_target_pairs={{0,1},{1,2},{2,3},{3,4},{4,5},{5,6},{6,7},{8,9},{9,10},{10,11},{11... | collective-permute-start | bytes 9224 | tf_op jit(solution)/shard_map/ppermute | solution.py:48
  67.4 1.3 %collective-permute-done.12 = f32[3,1,256]{2,1,0:T(1,128)S(1)} collective-permute-done((f32[3,1,256]{2,1,0:T(1,128)S(1)}, f32[3,1,256]{2,1,0:T(1,128)S(1)}, u32[]{:S(2)}, u32[]{:S(2)}) %collective-permute-start.12) | collective-permute-done | bytes 3104 | tf_op jit(solution)/shard_map/ppermute | solution.py:48
  68.7 0.6 bitcast_add_fusion
  (19 shorter events, 0.2 us)
Async XLA Ops:
  0.6 0.8 %copy-start.1 = (f32[3,4096]{1,0:T(4,128)S(1)}, f32[3,4096]{1,0:T(4,128)}, u32[]{:S(2)}) copy-start(f32[3,4096]{1,0:T(4,128)} %euler_ref.1) | copy-start | bytes 147460
  24.7 2.7 %collective-permute-start = (f32[16,56,256]{2,1,0:T(8,128)S(1)}, f32[16,56,256]{2,1,0:T(8,128)S(1)}, u32[]{:S(2)}, u32[]{:S(2)}) collective-permute-start(f32[16,56,256]{2,1,0:T(8,128)S(1)} %get-tuple-element.34), channel_id=1, source_target_pairs={{0,8},{8,0},{16,24},{24,16},{1,9},{9,1},{17,25},{25,17},{2,10},{10... | collective-permute-start | bytes 2752520 | tf_op jit(solution)/shard_map/ppermute | solution.py:316
  25.2 2.2 %copy-start.4 = (f32[3,1,256]{2,1,0:T(1,128)S(1)}, f32[3,1,256]{2,1,0:T(1,128)}, u32[]{:S(2)}) copy-start(f32[3,1,256]{2,1,0:T(1,128)} %refs_5_.1) | copy-start | bytes 9220
  27.5 12.0 %collective-permute-start.1 = (f32[4,56,256]{2,1,0:T(8,128)S(1)}, f32[4,56,256]{2,1,0:T(8,128)S(1)}, u32[]{:S(2)}, u32[]{:S(2)}) collective-permute-start(f32[4,56,256]{2,1,0:T(8,128)S(1)} %get-tuple-element.37), channel_id=1, source_target_pairs={{0,17},{1,16},{2,19},{3,18},{4,21},{5,20},{6,23},{7,22},{8,25},{9,... | collective-permute-start | bytes 688136 | tf_op jit(solution)/shard_map/ppermute | solution.py:518
  31.3 10.9 %collective-permute-start.2 = (f32[4,56,256]{2,1,0:T(8,128)S(1)}, f32[4,56,256]{2,1,0:T(8,128)S(1)}, u32[]{:S(2)}, u32[]{:S(2)}) collective-permute-start(f32[4,56,256]{2,1,0:T(8,128)S(1)} %get-tuple-element.38), channel_id=1, source_target_pairs={{0,16},{1,17},{2,18},{3,19},{4,20},{5,21},{6,22},{7,23},{8,24},{9,... | collective-permute-start | bytes 688136 | tf_op jit(solution)/shard_map/ppermute | solution.py:518
  31.8 10.7 %collective-permute-start.3 = (f32[4,56,256]{2,1,0:T(8,128)S(1)}, f32[4,56,256]{2,1,0:T(8,128)S(1)}, u32[]{:S(2)}, u32[]{:S(2)}) collective-permute-start(f32[4,56,256]{2,1,0:T(8,128)S(1)} %get-tuple-element.39), channel_id=1, source_target_pairs={{0,1},{1,0},{2,3},{3,2},{4,5},{5,4},{6,7},{7,6},{8,9},{9,8},{10,11... | collective-permute-start | bytes 688136 | tf_op jit(solution)/shard_map/ppermute | solution.py:518
  39.5 22.8 %copy-start = (f32[12,8,225]{2,1,0:T(8,128)S(1)}, f32[12,8,225]{2,1,0:T(8,128)}, u32[]{:S(2)}) copy-start(f32[12,8,225]{2,1,0:T(8,128)} %refs_7_.1) | copy-start | bytes 259204
  39.5 22.8 %copy-start.2 = (f32[6,8,225]{2,1,0:T(8,128)S(1)}, f32[6,8,225]{2,1,0:T(8,128)}, u32[]{:S(2)}) copy-start(f32[6,8,225]{2,1,0:T(8,128)} %refs_6_.1) | copy-start | bytes 129604
  39.5 22.7 %copy-start.3 = (f32[24,8]{1,0:T(8,128)S(1)}, f32[24,8]{1,0:T(8,128)}, u32[]{:S(2)}) copy-start(f32[24,8]{1,0:T(8,128)} %constant.8.clone.refs_9_) | copy-start | bytes 2308
  39.5 22.7 %copy-start.5 = (s32[8,225]{1,0:T(8,128)S(1)}, s32[8,225]{1,0:T(8,128)}, u32[]{:S(2)}) copy-start(s32[8,225]{1,0:T(8,128)} %refs_8_.1) | copy-start | bytes 21604
  42.6 2.7 %collective-permute-start.5 = (f32[16,24,256]{2,1,0:T(8,128)S(1)}, f32[16,24,256]{2,1,0:T(8,128)S(1)}, u32[]{:S(2)}, u32[]{:S(2)}) collective-permute-start(f32[16,24,256]{2,1,0:T(8,128)S(1)} %get-tuple-element.47), channel_id=1, source_target_pairs={{0,8},{8,0},{16,24},{24,16},{1,9},{9,1},{17,25},{25,17},{2,10},{10... | collective-permute-start | bytes 1179656 | tf_op jit(solution)/shard_map/ppermute | solution.py:316
  42.6 8.9 %collective-permute-start.4 = (f32[2,56,256]{2,1,0:T(8,128)S(1)}, f32[2,56,256]{2,1,0:T(8,128)S(1)}, u32[]{:S(2)}, u32[]{:S(2)}) collective-permute-start(f32[2,56,256]{2,1,0:T(8,128)S(1)} %get-tuple-element.45), channel_id=1, source_target_pairs={{0,4},{1,5},{2,6},{3,7},{4,0},{5,1},{6,2},{7,3},{8,12},{9,13},{10,... | collective-permute-start | bytes 344072 | tf_op jit(solution)/shard_map/ppermute | solution.py:518
  45.4 6.3 %collective-permute-start.6 = (f32[4,24,256]{2,1,0:T(8,128)S(1)}, f32[4,24,256]{2,1,0:T(8,128)S(1)}, u32[]{:S(2)}, u32[]{:S(2)}) collective-permute-start(f32[4,24,256]{2,1,0:T(8,128)S(1)} %get-tuple-element.50), channel_id=1, source_target_pairs={{0,17},{1,16},{2,19},{3,18},{4,21},{5,20},{6,23},{7,22},{8,25},{9,... | collective-permute-start | bytes 294920 | tf_op jit(solution)/shard_map/ppermute | solution.py:518
  47.1 6.2 %collective-permute-start.7 = (f32[4,24,256]{2,1,0:T(8,128)S(1)}, f32[4,24,256]{2,1,0:T(8,128)S(1)}, u32[]{:S(2)}, u32[]{:S(2)}) collective-permute-start(f32[4,24,256]{2,1,0:T(8,128)S(1)} %get-tuple-element.51), channel_id=1, source_target_pairs={{0,16},{1,17},{2,18},{3,19},{4,20},{5,21},{6,22},{7,23},{8,24},{9,... | collective-permute-start | bytes 294920 | tf_op jit(solution)/shard_map/ppermute | solution.py:518
  48.4 4.9 %collective-permute-start.8 = (f32[4,24,256]{2,1,0:T(8,128)S(1)}, f32[4,24,256]{2,1,0:T(8,128)S(1)}, u32[]{:S(2)}, u32[]{:S(2)}) collective-permute-start(f32[4,24,256]{2,1,0:T(8,128)S(1)} %get-tuple-element.52), channel_id=1, source_target_pairs={{0,1},{1,0},{2,3},{3,2},{4,5},{5,4},{6,7},{7,6},{8,9},{9,8},{10,11... | collective-permute-start | bytes 294920 | tf_op jit(solution)/shard_map/ppermute | solution.py:518
  53.4 8.9 %collective-permute-start.9 = (f32[80,256]{1,0:T(8,128)S(1)}, f32[80,256]{1,0:T(8,128)S(1)}, u32[]{:S(2)}, u32[]{:S(2)}) collective-permute-start(f32[80,256]{1,0:T(8,128)S(1)} %get-tuple-element.55), channel_id=1, source_target_pairs={{0,2},{1,3},{2,0},{3,1},{4,6},{5,7},{6,4},{7,5},{8,10},{9,11},{10,... | collective-permute-start | bytes 245768 | tf_op jit(solution)/shard_map/ppermute | solution.py:518
  55.0 4.9 %collective-permute-start.10 = (f32[24,256]{1,0:T(8,128)S(1)}, f32[24,256]{1,0:T(8,128)S(1)}, u32[]{:S(2)}, u32[]{:S(2)}) collective-permute-start(f32[24,256]{1,0:T(8,128)S(1)} %get-tuple-element.56), channel_id=1, source_target_pairs={{0,4},{1,5},{2,6},{3,7},{4,0},{5,1},{6,2},{7,3},{8,12},{9,13},{10,... | collective-permute-start | bytes 73736 | tf_op jit(solution)/shard_map/ppermute | solution.py:518
  56.6 5.6 %collective-permute-start.11 = (f32[24,256]{1,0:T(8,128)S(1)}, f32[24,256]{1,0:T(8,128)S(1)}, u32[]{:S(2)}, u32[]{:S(2)}) collective-permute-start(f32[24,256]{1,0:T(8,128)S(1)} %get-tuple-element.57), channel_id=1, source_target_pairs={{0,6},{1,7},{2,4},{3,5},{4,2},{5,3},{6,0},{7,1},{8,14},{9,15},{10,... | collective-permute-start | bytes 73736 | tf_op jit(solution)/shard_map/ppermute | solution.py:518
  64.0 4.7 %collective-permute-start.12 = (f32[3,1,256]{2,1,0:T(1,128)S(1)}, f32[3,1,256]{2,1,0:T(1,128)S(1)}, u32[]{:S(2)}, u32[]{:S(2)}) collective-permute-start(f32[3,1,256]{2,1,0:T(1,128)S(1)} %slice_bitcast_fusion), channel_id=1, source_target_pairs={{0,1},{1,2},{2,3},{3,4},{4,5},{5,6},{6,7},{8,9},{9,10},{10,11},{11... | collective-permute-start | bytes 9224 | tf_op jit(solution)/shard_map/ppermute | solution.py:48

commit v17 on v12

--- a/solution.py
+++ b/solution.py
@@ -4,6 +4,8 @@
 
 import jax
 import jax.numpy as jnp
+import ml_dtypes
+import numpy as np
 from jax import lax
 from jax.experimental import pallas as pl
 from jax.experimental.pallas import tpu as pltpu
@@ -531,19 +533,39 @@
     return first, second, third
 
 
+def joined(parts, axis):
+    whole = jnp.concatenate([part.astype(jnp.float32) for part in parts], axis=axis)
+    return whole.astype(jnp.bfloat16)
+
+
+def six_terms(value):
+    first, second, third = three_parts(value)
+    return joined([first, second, third, first, second, first], 0)
+
+
+def six_terms_of(table):
+    first = table.astype(ml_dtypes.bfloat16)
+    rest = table - first.astype(np.float32)
+    second = rest.astype(ml_dtypes.bfloat16)
+    third = (rest - second.astype(np.float32)).astype(ml_dtypes.bfloat16)
+    terms = np.concatenate([first, first, first, second, second, third], axis=1)
+    return np.pad(terms, ((0, -terms.shape[0] % 16), (0, 0)))
+
+
 def dot_selected(value, selector, contract):
-    total = None
-    for part in three_parts(value):
-        term = lax.dot_general(
-            part, selector, (((1,), (contract,)), ((), ())), preferred_element_type=jnp.float32
-        )
-        total = term if total is None else total + term
-    return total
+    rows = value.shape[0]
+    product = lax.dot_general(
+        joined(three_parts(value), 0),
+        selector,
+        (((1,), (contract,)), ((), ())),
+        preferred_element_type=jnp.float32,
+    )
+    return product[:rows] + product[rows : 2 * rows] + product[2 * rows :]
 
 
 def update_kernel(heights, *refs):
     first_ref, second_refs = refs[0], refs[1 : 1 + heights]
-    own_ref, stress_ref, resistance_ref, weights_ref, table_ref = refs[1 + heights : -2]
+    own_ref, stress_ref, resistance_ref, weights_ref, table_ref, turned_ref = refs[1 + heights : -2]
     stress_out_ref, nodal_ref = refs[-2:]
     elements = stress_ref.shape[2]
     rows, second_rows = first_ref.shape[0], second_refs[0].shape[0]
@@ -589,16 +611,18 @@
         ),
         jnp.concatenate([jnp.broadcast_to(own_ref[c], (8, COLUMNS)) for c in range(3)], axis=0),
     )
-    corners = jnp.zeros((24, elements), jnp.float32)
-    for step in range(4):
-        part = jnp.where(corner >> 1 == step, values, 0.0)
-        corners = corners + dot_selected(part, selectors[step], 0)
+    corners = dot_selected(
+        jnp.concatenate(
+            [jnp.where(corner >> 1 == step, values, 0.0) for step in range(4)], axis=1
+        ),
+        jnp.concatenate(selectors, axis=0),
+        0,
+    )
     gradients = []
     for c in range(3):
         product = jnp.dot(
             table_ref[...],
-            corners[8 * c : 8 * c + 8],
-            precision=lax.Precision.HIGHEST,
+            six_terms(corners[8 * c : 8 * c + 8]),
             preferred_element_type=jnp.float32,
         )
         gradients.append([product[8 * d : 8 * d + 8] for d in range(3)])
@@ -660,13 +684,11 @@
     forces = []
     for rows in [(0, 5, 4), (5, 1, 3), (4, 3, 2)]:
         forces.append(
-            lax.dot_general(
-                table_ref[...],
-                jnp.concatenate([scaled[row] for row in rows], axis=0),
-                (((0,), (0,)), ((), ())),
-                precision=lax.Precision.HIGHEST,
+            jnp.dot(
+                turned_ref[...],
+                six_terms(jnp.concatenate([scaled[row] for row in rows], axis=0)),
                 preferred_element_type=jnp.float32,
-            )
+            )[:8]
         )
     forces = jnp.concatenate(forces, axis=0)
     nodal = jnp.zeros((24, COLUMNS), jnp.float32)
@@ -682,14 +704,15 @@
 
 def element_update(first, second, own, stress_old, resistance, quad_weights):
     grad_table = shape_gradients()
-    table = jnp.asarray(
+    table = np.asarray(
         [
             [grad_table[quadrature][corner][direction] for corner in range(8)]
             for direction in range(3)
             for quadrature in range(8)
         ],
-        dtype=jnp.float32,
-    )
+        dtype=np.float32,
+    )
+    tables = [jnp.asarray(six_terms_of(part)) for part in (table, table.T)]
     return pl.pallas_call(
         functools.partial(update_kernel, len(second)),
         out_shape=(
@@ -698,7 +721,7 @@
         ),
         compiler_params=pltpu.CompilerParams(vmem_limit_bytes=8 * 1024 * 1024),
         name="stress_update",
-    )(first, *second, own, stress_old, resistance, quad_weights, table)
+    )(first, *second, own, stress_old, resistance, quad_weights, *tables)
 
 
 def body(

time: 69 us -> 68.5 us (level)
    unnamed x14 -> x16, local copies, waits for them, and re-layouts: 2.34 us -> 2.34 us
where the time goes in v17:
time: 68.5 us; the launch traced here: 68.3 us
  Pallas kernels  31.7 us (46%)
  starting transfers between devices  19.1 us (28%)
  waiting for transfers between devices  13 us (19%)
  local copies, waits for them, and re-layouts  2.35 us (3%)
  other arithmetic  1.32 us (2%)
  between operations  0.79 us (1%)
    pallas_call x2, Pallas kernels, cell_sums(): pl.pallas_call(functools.partial(cell_sum_kernel, octants, per_octant), o...  27.9 us
    ppermute x10, starting transfers between devices, to_relative(): lax.ppermute(block, ('ca', 'fe'), [(i, i ^ flip) for i in range(groups *...  15.1 us
    ppermute x10, waiting for transfers between devices, to_relative(): lax.ppermute(block, ('ca', 'fe'), [(i, i ^ flip) for i in range(groups *...  11.7 us
    ppermute x1, starting transfers between devices, passed_along(): return lax.ppermute(block, axis, route)  3.38 us
    unnamed x16, local copies, waits for them, and re-layouts  2.34 us
    pallas_call x1, Pallas kernels, brick_sums(): pl.pallas_call(brick_sum_kernel, out_shape=[jax.ShapeDtypeStruct((places,...  2.11 us
  transfers between devices with their start and end apart: 13, of which 8 were waited for; matrix products, arithmetic and copies ran while one was open for 0% of the time, Pallas kernels for 14%

profile of v17, /device:TPU:0, one launch (start us, length us, event | category | flops | bytes accessed | tf_op | source)
XLA Modules:
  0.0 68.3 jit_solution(16645665907456344589)
XLA Ops:
  0.6 0.8 %copy-done.1 = f32[3,4096]{1,0:T(4,128)S(1)} copy-done((f32[3,4096]{1,0:T(4,128)S(1)}, f32[3,4096]{1,0:T(4,128)}, u32[]{:S(2)}) %copy-start.1) | copy-done | bytes 49176
  1.5 0.2 rotation_table.1.table_ref
  1.6 0.7 %add_select_fusion = s32[2048]{0:T(1024)S(1)} fusion(s32[2048]{0:T(1024)} %param.15, s32[2048]{0:T(1024)} %bitcast.15, s32[2048]{0:T(1024)} %param.13), kind=kLoop, calls=%fused_computation | loop fusion | flops 8192 | bytes 32768 | tf_op jit(solution)/shard_map/jit(_where)/select_n | solution.py:741
  2.4 1.5 %copy-done.7 = s32[216,2048]{1,0:T(8,128)S(1)} copy-done((s32[216,2048]{1,0:T(8,128)S(1)}, s32[216,2048]{1,0:T(8,128)}, u32[]{:S(2)}) %copy-start.7) | copy-done | bytes 1769496
  3.9 20.3 %cell_sums.2 = (s32[1,2048]{1,0:T(1,128)S(1)}, f32[16,56,256]{2,1,0:T(8,128)S(1)}, bf16[112,2048]{1,0:T(8,128)(2,1)S(1)}, s32[56,2048]{1,0:T(8,128)S(1)}) custom-call(s32[216,2048]{1,0:T(8,128)S(1)} %copy-done.7, s32[1,2048]{1,0:T(1,128)S(1)} %bitcast.14, s32[48,8,128]{2,1,0:T(8,128)S(1)} %rotation_table.1.table_ref), custom_call_target="tpu_custom_call" | custom-call | flops 24000000000 | bytes 60000000 | tf_op jit(solution)/shard_map/cell_sums/pallas_call | solution.py:378
  24.2 0.5 collective-permute-start
  24.7 2.1 %brick_sums.1 = (f32[16,56,256]{2,1,0:T(8,128)S(1)}, s32[1,2048]{1,0:T(1,128)S(1)}) custom-call(bf16[112,2048]{1,0:T(8,128)(2,1)S(1)} %get-tuple-element.31.split_ref, s32[1,2048]{1,0:T(1,128)S(1)} %get-tuple-element.32.label_ref), custom_call_target="tpu_custom_call" | custom-call | flops 1680000000 | bytes 5600000 | tf_op jit(solution)/shard_map/brick_sums/pallas_call | solution.py:408
  26.8 0.1 core_sum_a.1
  26.9 3.8 %collective-permute-start.1 = (f32[4,56,256]{2,1,0:T(8,128)S(1)}, f32[4,56,256]{2,1,0:T(8,128)S(1)}, u32[]{:S(2)}, u32[]{:S(2)}) collective-permute-start(f32[4,56,256]{2,1,0:T(8,128)S(1)} %get-tuple-element.37), channel_id=1, source_target_pairs={{0,17},{1,16},{2,19},{3,18},{4,21},{5,20},{6,23},{7,22},{8,25},{9,... | collective-permute-start | bytes 688136 | tf_op jit(solution)/shard_map/ppermute | solution.py:514
  30.8 0.5 collective-permute-start.2
  31.3 0.1 collective-permute-start.3
  31.4 7.6 %cell_sums.3 = (f32[16,24,256]{2,1,0:T(8,128)S(1)}, f32[16,24,256]{2,1,0:T(8,128)S(1)}) custom-call(s32[56,2048]{1,0:T(8,128)S(1)} %get-tuple-element.41.ids_ref, s32[1,2048]{1,0:T(1,128)S(1)} %get-tuple-element.42.label_ref, s32[48,8,128]{2,1,0:T(8,128)S(1)} %rotation_table.1.table_ref), custom_call_target="tpu_custom_call" | custom-call | flops 8000000000 | bytes 20000000 | tf_op jit(solution)/shard_map/cell_sums/pallas_call | solution.py:378
  39.1 2.6 %collective-permute-done.2.refs_2_ = f32[4,56,256]{2,1,0:T(8,128)S(1)} collective-permute-done((f32[4,56,256]{2,1,0:T(8,128)S(1)}, f32[4,56,256]{2,1,0:T(8,128)S(1)}, u32[]{:S(2)}, u32[]{:S(2)}) %collective-permute-start.2) | collective-permute-done | bytes 229408 | tf_op jit(solution)/shard_map/ppermute | solution.py:514
  41.6 0.3 collective-permute-done.3.refs_3_
  41.9 0.1 plane_sum_a.1
  42.0 0.1 collective-permute-start.5
  42.1 2.7 %collective-permute-start.4 = (f32[2,56,256]{2,1,0:T(8,128)S(1)}, f32[2,56,256]{2,1,0:T(8,128)S(1)}, u32[]{:S(2)}, u32[]{:S(2)}) collective-permute-start(f32[2,56,256]{2,1,0:T(8,128)S(1)} %get-tuple-element.45), channel_id=1, source_target_pairs={{0,4},{1,5},{2,6},{3,7},{4,0},{5,1},{6,2},{7,3},{8,12},{9,13},{10,... | collective-permute-start | bytes 344072 | tf_op jit(solution)/shard_map/ppermute | solution.py:514
  44.8 1.7 %collective-permute-start.6 = (f32[4,24,256]{2,1,0:T(8,128)S(1)}, f32[4,24,256]{2,1,0:T(8,128)S(1)}, u32[]{:S(2)}, u32[]{:S(2)}) collective-permute-start(f32[4,24,256]{2,1,0:T(8,128)S(1)} %get-tuple-element.50), channel_id=1, source_target_pairs={{0,17},{1,16},{2,19},{3,18},{4,21},{5,20},{6,23},{7,22},{8,25},{9,... | collective-permute-start | bytes 294920 | tf_op jit(solution)/shard_map/ppermute | solution.py:514
  46.5 1.3 %collective-permute-start.7 = (f32[4,24,256]{2,1,0:T(8,128)S(1)}, f32[4,24,256]{2,1,0:T(8,128)S(1)}, u32[]{:S(2)}, u32[]{:S(2)}) collective-permute-start(f32[4,24,256]{2,1,0:T(8,128)S(1)} %get-tuple-element.51), channel_id=1, source_target_pairs={{0,16},{1,17},{2,18},{3,19},{4,20},{5,21},{6,22},{7,23},{8,24},{9,... | collective-permute-start | bytes 294920 | tf_op jit(solution)/shard_map/ppermute | solution.py:514
  47.8 0.5 collective-permute-start.8
  48.4 2.6 %collective-permute-done.4.received_ref = f32[2,56,256]{2,1,0:T(8,128)S(1)} collective-permute-done((f32[2,56,256]{2,1,0:T(8,128)S(1)}, f32[2,56,256]{2,1,0:T(8,128)S(1)}, u32[]{:S(2)}, u32[]{:S(2)}) %collective-permute-start.4) | collective-permute-done | bytes 114720 | tf_op jit(solution)/shard_map/ppermute | solution.py:514
  51.0 0.1 collective-permute-done.6.refs_1_
  51.1 1.6 %collective-permute-done.7.refs_2_ = f32[4,24,256]{2,1,0:T(8,128)S(1)} collective-permute-done((f32[4,24,256]{2,1,0:T(8,128)S(1)}, f32[4,24,256]{2,1,0:T(8,128)S(1)}, u32[]{:S(2)}, u32[]{:S(2)}) %collective-permute-start.7) | collective-permute-done | bytes 98336 | tf_op jit(solution)/shard_map/ppermute | solution.py:514
  52.8 1.6 %collective-permute-start.9 = (f32[80,256]{1,0:T(8,128)S(1)}, f32[80,256]{1,0:T(8,128)S(1)}, u32[]{:S(2)}, u32[]{:S(2)}) collective-permute-start(f32[80,256]{1,0:T(8,128)S(1)} %get-tuple-element.55), channel_id=1, source_target_pairs={{0,2},{1,3},{2,0},{3,1},{4,6},{5,7},{6,4},{7,5},{8,10},{9,11},{10,... | collective-permute-start | bytes 245768 | tf_op jit(solution)/shard_map/ppermute | solution.py:514
  54.4 1.6 %collective-permute-start.10 = (f32[24,256]{1,0:T(8,128)S(1)}, f32[24,256]{1,0:T(8,128)S(1)}, u32[]{:S(2)}, u32[]{:S(2)}) collective-permute-start(f32[24,256]{1,0:T(8,128)S(1)} %get-tuple-element.56), channel_id=1, source_target_pairs={{0,4},{1,5},{2,6},{3,7},{4,0},{5,1},{6,2},{7,3},{8,12},{9,13},{10,... | collective-permute-start | bytes 73736 | tf_op jit(solution)/shard_map/ppermute | solution.py:514
  56.1 1.2 %collective-permute-start.11 = (f32[24,256]{1,0:T(8,128)S(1)}, f32[24,256]{1,0:T(8,128)S(1)}, u32[]{:S(2)}, u32[]{:S(2)}) collective-permute-start(f32[24,256]{1,0:T(8,128)S(1)} %get-tuple-element.57), channel_id=1, source_target_pairs={{0,6},{1,7},{2,4},{3,5},{4,2},{5,3},{6,0},{7,1},{8,14},{9,15},{10,... | collective-permute-start | bytes 73736 | tf_op jit(solution)/shard_map/ppermute | solution.py:514
  57.3 2.1 %collective-permute-done.10.refs_3_ = f32[24,256]{1,0:T(8,128)S(1)} collective-permute-done((f32[24,256]{1,0:T(8,128)S(1)}, f32[24,256]{1,0:T(8,128)S(1)}, u32[]{:S(2)}, u32[]{:S(2)}) %collective-permute-start.10) | collective-permute-done | bytes 24608 | tf_op jit(solution)/shard_map/ppermute | solution.py:514
  59.3 2.4 %collective-permute-done.11.refs_4_ = f32[24,256]{1,0:T(8,128)S(1)} collective-permute-done((f32[24,256]{1,0:T(8,128)S(1)}, f32[24,256]{1,0:T(8,128)S(1)}, u32[]{:S(2)}, u32[]{:S(2)}) %collective-permute-start.11) | collective-permute-done | bytes 24608 | tf_op jit(solution)/shard_map/ppermute | solution.py:514
  61.7 1.3 %stress_update.1 = (f32[6,8,225]{2,1,0:T(8,128)}, f32[2,3,1,256]{3,2,1,0:T(1,128)S(1)}) custom-call(f32[56,256]{1,0:T(8,128)S(1)} %get-tuple-element.53.refs_0_, f32[24,256]{1,0:T(8,128)S(1)} %get-tuple-element.54.refs_1_, f32[80,256]{1,0:T(8,128)S(1)} %collective-permute-done.9.refs_2_, f32[24,256]{1,0:T(8,128)S(1)} %collective-permute-done.10.refs_3_, ...), custom_call_target="tpu_custom_call" | custom-call | tf_op jit(solution)/shard_map/stress_update/pallas_call | solution.py:716
  63.0 3.4 %collective-permute-start.12 = (f32[3,1,256]{2,1,0:T(1,128)S(1)}, f32[3,1,256]{2,1,0:T(1,128)S(1)}, u32[]{:S(2)}, u32[]{:S(2)}) collective-permute-start(f32[3,1,256]{2,1,0:T(1,128)S(1)} %slice_bitcast_fusion), channel_id=1, source_target_pairs={{0,1},{1,2},{2,3},{3,4},{4,5},{5,6},{6,7},{8,9},{9,10},{10,11},{11... | collective-permute-start | bytes 9224 | tf_op jit(solution)/shard_map/ppermute | solution.py:50
  66.4 1.3 %collective-permute-done.12 = f32[3,1,256]{2,1,0:T(1,128)S(1)} collective-permute-done((f32[3,1,256]{2,1,0:T(1,128)S(1)}, f32[3,1,256]{2,1,0:T(1,128)S(1)}, u32[]{:S(2)}, u32[]{:S(2)}) %collective-permute-start.12) | collective-permute-done | bytes 3104 | tf_op jit(solution)/shard_map/ppermute | solution.py:50
  67.7 0.6 bitcast_add_fusion
  (22 shorter events, 0.2 us)
Async XLA Ops:
  0.6 0.8 %copy-start.1 = (f32[3,4096]{1,0:T(4,128)S(1)}, f32[3,4096]{1,0:T(4,128)}, u32[]{:S(2)}) copy-start(f32[3,4096]{1,0:T(4,128)} %euler_ref.1) | copy-start | bytes 147460
  2.4 1.5 %copy-start.7 = (s32[216,2048]{1,0:T(8,128)S(1)}, s32[216,2048]{1,0:T(8,128)}, u32[]{:S(2)}) copy-start(s32[216,2048]{1,0:T(8,128)} %ids_ref.1) | copy-start | bytes 5308420
  24.2 2.6 %collective-permute-start = (f32[16,56,256]{2,1,0:T(8,128)S(1)}, f32[16,56,256]{2,1,0:T(8,128)S(1)}, u32[]{:S(2)}, u32[]{:S(2)}) collective-permute-start(f32[16,56,256]{2,1,0:T(8,128)S(1)} %get-tuple-element.34), channel_id=1, source_target_pairs={{0,8},{8,0},{16,24},{24,16},{1,9},{9,1},{17,25},{25,17},{2,10},{10... | collective-permute-start | bytes 2752520 | tf_op jit(solution)/shard_map/ppermute | solution.py:317
  24.7 2.1 %copy-start.3 = (f32[3,1,256]{2,1,0:T(1,128)S(1)}, f32[3,1,256]{2,1,0:T(1,128)}, u32[]{:S(2)}) copy-start(f32[3,1,256]{2,1,0:T(1,128)} %refs_5_.1) | copy-start | bytes 9220
  26.9 12.1 %collective-permute-start.1 = (f32[4,56,256]{2,1,0:T(8,128)S(1)}, f32[4,56,256]{2,1,0:T(8,128)S(1)}, u32[]{:S(2)}, u32[]{:S(2)}) collective-permute-start(f32[4,56,256]{2,1,0:T(8,128)S(1)} %get-tuple-element.37), channel_id=1, source_target_pairs={{0,17},{1,16},{2,19},{3,18},{4,21},{5,20},{6,23},{7,22},{8,25},{9,... | collective-permute-start | bytes 688136 | tf_op jit(solution)/shard_map/ppermute | solution.py:514
  30.8 10.9 %collective-permute-start.2 = (f32[4,56,256]{2,1,0:T(8,128)S(1)}, f32[4,56,256]{2,1,0:T(8,128)S(1)}, u32[]{:S(2)}, u32[]{:S(2)}) collective-permute-start(f32[4,56,256]{2,1,0:T(8,128)S(1)} %get-tuple-element.38), channel_id=1, source_target_pairs={{0,16},{1,17},{2,18},{3,19},{4,20},{5,21},{6,22},{7,23},{8,24},{9,... | collective-permute-start | bytes 688136 | tf_op jit(solution)/shard_map/ppermute | solution.py:514
  31.3 10.6 %collective-permute-start.3 = (f32[4,56,256]{2,1,0:T(8,128)S(1)}, f32[4,56,256]{2,1,0:T(8,128)S(1)}, u32[]{:S(2)}, u32[]{:S(2)}) collective-permute-start(f32[4,56,256]{2,1,0:T(8,128)S(1)} %get-tuple-element.39), channel_id=1, source_target_pairs={{0,1},{1,0},{2,3},{3,2},{4,5},{5,4},{6,7},{7,6},{8,9},{9,8},{10,11... | collective-permute-start | bytes 688136 | tf_op jit(solution)/shard_map/ppermute | solution.py:514
  39.0 22.7 %copy-start = (f32[12,8,225]{2,1,0:T(8,128)S(1)}, f32[12,8,225]{2,1,0:T(8,128)}, u32[]{:S(2)}) copy-start(f32[12,8,225]{2,1,0:T(8,128)} %refs_7_.1) | copy-start | bytes 259204
  39.0 22.7 %copy-start.2 = (f32[6,8,225]{2,1,0:T(8,128)S(1)}, f32[6,8,225]{2,1,0:T(8,128)}, u32[]{:S(2)}) copy-start(f32[6,8,225]{2,1,0:T(8,128)} %refs_6_.1) | copy-start | bytes 129604
  39.0 22.7 %copy-start.4 = (s32[8,225]{1,0:T(8,128)S(1)}, s32[8,225]{1,0:T(8,128)}, u32[]{:S(2)}) copy-start(s32[8,225]{1,0:T(8,128)} %refs_8_.1) | copy-start | bytes 21604
  39.1 22.6 %copy-start.5 = (bf16[16,144]{1,0:T(8,128)(2,1)S(1)}, bf16[16,144]{1,0:T(8,128)(2,1)}, u32[]{:S(2)}) copy-start(bf16[16,144]{1,0:T(8,128)(2,1)} %constant.11.clone.refs_10_) | copy-start | bytes 13828
  39.1 22.6 %copy-start.6 = (bf16[32,48]{1,0:T(8,128)(2,1)S(1)}, bf16[32,48]{1,0:T(8,128)(2,1)}, u32[]{:S(2)}) copy-start(bf16[32,48]{1,0:T(8,128)(2,1)} %constant.10.clone.refs_9_) | copy-start | bytes 9220
  42.0 2.7 %collective-permute-start.5 = (f32[16,24,256]{2,1,0:T(8,128)S(1)}, f32[16,24,256]{2,1,0:T(8,128)S(1)}, u32[]{:S(2)}, u32[]{:S(2)}) collective-permute-start(f32[16,24,256]{2,1,0:T(8,128)S(1)} %get-tuple-element.47), channel_id=1, source_target_pairs={{0,8},{8,0},{16,24},{24,16},{1,9},{9,1},{17,25},{25,17},{2,10},{10... | collective-permute-start | bytes 1179656 | tf_op jit(solution)/shard_map/ppermute | solution.py:317
  42.1 8.9 %collective-permute-start.4 = (f32[2,56,256]{2,1,0:T(8,128)S(1)}, f32[2,56,256]{2,1,0:T(8,128)S(1)}, u32[]{:S(2)}, u32[]{:S(2)}) collective-permute-start(f32[2,56,256]{2,1,0:T(8,128)S(1)} %get-tuple-element.45), channel_id=1, source_target_pairs={{0,4},{1,5},{2,6},{3,7},{4,0},{5,1},{6,2},{7,3},{8,12},{9,13},{10,... | collective-permute-start | bytes 344072 | tf_op jit(solution)/shard_map/ppermute | solution.py:514
  44.8 6.3 %collective-permute-start.6 = (f32[4,24,256]{2,1,0:T(8,128)S(1)}, f32[4,24,256]{2,1,0:T(8,128)S(1)}, u32[]{:S(2)}, u32[]{:S(2)}) collective-permute-start(f32[4,24,256]{2,1,0:T(8,128)S(1)} %get-tuple-element.50), channel_id=1, source_target_pairs={{0,17},{1,16},{2,19},{3,18},{4,21},{5,20},{6,23},{7,22},{8,25},{9,... | collective-permute-start | bytes 294920 | tf_op jit(solution)/shard_map/ppermute | solution.py:514
  46.5 6.2 %collective-permute-start.7 = (f32[4,24,256]{2,1,0:T(8,128)S(1)}, f32[4,24,256]{2,1,0:T(8,128)S(1)}, u32[]{:S(2)}, u32[]{:S(2)}) collective-permute-start(f32[4,24,256]{2,1,0:T(8,128)S(1)} %get-tuple-element.51), channel_id=1, source_target_pairs={{0,16},{1,17},{2,18},{3,19},{4,20},{5,21},{6,22},{7,23},{8,24},{9,... | collective-permute-start | bytes 294920 | tf_op jit(solution)/shard_map/ppermute | solution.py:514
  47.8 4.9 %collective-permute-start.8 = (f32[4,24,256]{2,1,0:T(8,128)S(1)}, f32[4,24,256]{2,1,0:T(8,128)S(1)}, u32[]{:S(2)}, u32[]{:S(2)}) collective-permute-start(f32[4,24,256]{2,1,0:T(8,128)S(1)} %get-tuple-element.52), channel_id=1, source_target_pairs={{0,1},{1,0},{2,3},{3,2},{4,5},{5,4},{6,7},{7,6},{8,9},{9,8},{10,11... | collective-permute-start | bytes 294920 | tf_op jit(solution)/shard_map/ppermute | solution.py:514
  52.8 8.9 %collective-permute-start.9 = (f32[80,256]{1,0:T(8,128)S(1)}, f32[80,256]{1,0:T(8,128)S(1)}, u32[]{:S(2)}, u32[]{:S(2)}) collective-permute-start(f32[80,256]{1,0:T(8,128)S(1)} %get-tuple-element.55), channel_id=1, source_target_pairs={{0,2},{1,3},{2,0},{3,1},{4,6},{5,7},{6,4},{7,5},{8,10},{9,11},{10,... | collective-permute-start | bytes 245768 | tf_op jit(solution)/shard_map/ppermute | solution.py:514
  54.4 4.9 %collective-permute-start.10 = (f32[24,256]{1,0:T(8,128)S(1)}, f32[24,256]{1,0:T(8,128)S(1)}, u32[]{:S(2)}, u32[]{:S(2)}) collective-permute-start(f32[24,256]{1,0:T(8,128)S(1)} %get-tuple-element.56), channel_id=1, source_target_pairs={{0,4},{1,5},{2,6},{3,7},{4,0},{5,1},{6,2},{7,3},{8,12},{9,13},{10,... | collective-permute-start | bytes 73736 | tf_op jit(solution)/shard_map/ppermute | solution.py:514
  56.1 5.6 %collective-permute-start.11 = (f32[24,256]{1,0:T(8,128)S(1)}, f32[24,256]{1,0:T(8,128)S(1)}, u32[]{:S(2)}, u32[]{:S(2)}) collective-permute-start(f32[24,256]{1,0:T(8,128)S(1)} %get-tuple-element.57), channel_id=1, source_target_pairs={{0,6},{1,7},{2,4},{3,5},{4,2},{5,3},{6,0},{7,1},{8,14},{9,15},{10,... | collective-permute-start | bytes 73736 | tf_op jit(solution)/shard_map/ppermute | solution.py:514
  63.0 4.7 %collective-permute-start.12 = (f32[3,1,256]{2,1,0:T(1,128)S(1)}, f32[3,1,256]{2,1,0:T(1,128)S(1)}, u32[]{:S(2)}, u32[]{:S(2)}) collective-permute-start(f32[3,1,256]{2,1,0:T(1,128)S(1)} %slice_bitcast_fusion), channel_id=1, source_target_pairs={{0,1},{1,2},{2,3},{3,4},{4,5},{5,6},{6,7},{8,9},{9,10},{10,11},{11... | collective-permute-start | bytes 9224 | tf_op jit(solution)/shard_map/ppermute | solution.py:50

commit v18 on v17

--- a/solution.py
+++ b/solution.py
@@ -422,51 +422,53 @@
 
 def core_sum_kernel(passed, kept_ref, received_ref, *refs):
     outs = refs[passed:]
-    for index, out_ref in enumerate(outs[: len(outs) - passed]):
-        out_ref[...] = kept_ref[index] + received_ref[index]
+    for last in range(2):
+        outs[last][...] = kept_ref[:, last] + received_ref[:, last]
     for i in range(passed):
-        outs[len(outs) - passed + i][...] = refs[i][...]
+        outs[2 + i][...] = refs[i][...]
 
 
 def last_core_sum_kernel(kept_ref, received_ref, own_ref, *outs):
-    for index, out_ref in enumerate(outs):
-        out_ref[...] = kept_ref[index] + received_ref[index]
-        for c in range(3):
-            row = out_ref.shape[1] - 3 + c
-            out_ref[:, row : row + 1, :] = jnp.broadcast_to(
-                own_ref[c][None], (out_ref.shape[0], 1, COLUMNS)
-            )
-
-
-def last_core_sum(kept, received, own):
-    pairs, rests = lax.axis_size("ca") // 2, lax.axis_size("fe") // 2
-    shape = (2 * pairs, rests) + kept.shape[1:]
-    return pl.pallas_call(
-        last_core_sum_kernel,
-        out_shape=[jax.ShapeDtypeStruct(shape[1:], jnp.float32)] * shape[0],
-        compiler_params=pltpu.CompilerParams(vmem_limit_bytes=16 * 1024 * 1024),
-        name="core_sum_b",
-    )(kept.reshape(shape), received.reshape(shape), own)
+    for last, out_ref in enumerate(outs):
+        out_ref[...] = kept_ref[:, last] + received_ref[:, last]
+        pairs, rests, rows, columns = out_ref.shape
+        out_ref[:, :, rows - 3 : rows, :] = jnp.zeros((pairs, rests, 3, columns), jnp.float32)
+    for c in range(3):
+        row = rows - 3 + c
+        outs[1][0, :, row : row + 1, :] = jnp.broadcast_to(own_ref[c][None], (rests, 1, columns))
 
 
 def core_sum(kept, received, passed, name):
     pairs, rests = lax.axis_size("ca") // 2, lax.axis_size("fe") // 2
-    shape = (2 * pairs, rests) + kept.shape[1:]
-    out = pl.pallas_call(
+    shape = (pairs, 2, rests) + kept.shape[1:]
+    half = jax.ShapeDtypeStruct((pairs, rests) + kept.shape[1:], jnp.float32)
+    return pl.pallas_call(
         functools.partial(core_sum_kernel, len(passed)),
-        out_shape=[jax.ShapeDtypeStruct(shape[1:], jnp.float32)] * shape[0]
+        out_shape=[half, half]
         + [jax.ShapeDtypeStruct(array.shape, array.dtype) for array in passed],
         compiler_params=pltpu.CompilerParams(vmem_limit_bytes=16 * 1024 * 1024),
         name=name,
     )(kept.reshape(shape), received.reshape(shape), *passed)
-    return out[: shape[0]], *out[shape[0] :]
+
+
+def last_core_sum(kept, received, own):
+    pairs, rests = lax.axis_size("ca") // 2, lax.axis_size("fe") // 2
+    shape = (pairs, 2, rests) + kept.shape[1:]
+    half = jax.ShapeDtypeStruct((pairs, rests) + kept.shape[1:], jnp.float32)
+    return pl.pallas_call(
+        last_core_sum_kernel,
+        out_shape=[half, half],
+        compiler_params=pltpu.CompilerParams(vmem_limit_bytes=16 * 1024 * 1024),
+        name="core_sum_b",
+    )(kept.reshape(shape), received.reshape(shape), own)
 
 
 def plane_sum_kernel(sources, passed, *refs):
     outs = refs[sources + passed :]
     height = 0
     for out_ref in outs[: len(outs) - passed]:
-        out_ref[...] = sum(ref[pl.ds(height, out_ref.shape[0])] for ref in refs[:sources])
+        total = sum(ref[pl.ds(height, out_ref.shape[0])] for ref in refs[:sources])
+        out_ref[...] = total
         height += out_ref.shape[0]
     for i in range(passed):
         outs[len(outs) - passed + i][...] = refs[sources + i][...]
@@ -484,23 +486,22 @@
     return out[: len(cuts)], *out[len(cuts) :]
 
 
-def last_sum_kernel(sources, spare, kept_ref, received_ref, *refs):
+def last_sum_kernel(sources, kept_ref, received_ref, *refs):
     parts, outs = refs[:sources], refs[sources:]
     rows = kept_ref.shape[1]
     outs[0][...] = kept_ref[0] + received_ref[0]
     outs[2][0:rows, :] = kept_ref[1] + received_ref[1]
     for height, out_ref in enumerate(outs[1:]):
-        first = out_ref.shape[0] - parts[0].shape[1]
-        out_ref[first:, :] = sum(ref[height] for ref in parts)
-        out_ref[out_ref.shape[0] - spare :, :] = parts[-1][height, -spare:, :]
-
-
-def last_sum(kept, received, parts, spare):
-    heights, rows, columns = parts[0].shape
+        first = out_ref.shape[0] - parts[0].shape[2]
+        out_ref[first:, :] = sum(ref[0, height] for ref in parts)
+
+
+def last_sum(kept, received, parts):
+    heights, rows, columns = parts[0].shape[1:]
     part = jax.ShapeDtypeStruct((rows, columns), jnp.float32)
     both = jax.ShapeDtypeStruct((kept.shape[1] + rows, columns), jnp.float32)
     return pl.pallas_call(
-        functools.partial(last_sum_kernel, len(parts), spare),
+        functools.partial(last_sum_kernel, len(parts)),
         out_shape=[jax.ShapeDtypeStruct(kept.shape[1:], jnp.float32), part, both]
         + [part] * (heights - 2),
         compiler_params=pltpu.CompilerParams(vmem_limit_bytes=16 * 1024 * 1024),
@@ -514,11 +515,8 @@
     return lax.ppermute(block, ("ca", "fe"), [(i, i ^ flip) for i in range(groups * members)])
 
 
-def across_plane(parts):
-    return [parts[0]] + [
-        to_relative(parts[index], 0, index // 2, index % 2, 0)
-        for index in range(len(parts) - 1, 0, -1)
-    ]
+def across_pairs(parts):
+    return [parts[0]] + [to_relative(parts[pair], 0, pair, 0, 0) for pair in range(1, len(parts))]
 
 
 def across_height(parts):
@@ -743,21 +741,25 @@
     table = rotation_table(euler_angles)
     labels, send, split, ids = cell_sums(CHUNKS[0], per_octant, grain_ids, labels, table, half)
     keep, labels = brick_sums(split, labels, half)
-    core_a, labels, own = core_sum(
+    kept, sent, labels, own = core_sum(
         keep, across_cores(send), [labels, displacement], "core_sum_a"
     )
+    received = to_relative(sent, 0, 0, 1, 0)
     send, keep = cell_sums(CHUNKS[1], per_octant, ids, labels, table, half)
-    flip = lax.axis_size("fe") // 4
-    (kept, sent), own, send = plane_sum(
-        across_plane(core_a), [own, send], [flip, flip], "plane_sum_a"
-    )
+    pairs, heights = lax.axis_size("ca") // 2, lax.axis_size("fe") // 2
+    plane_a, own, send = plane_sum([kept, received], [own, send], [1] * pairs, "x_sum_a")
+    plane_a = [part.reshape(part.shape[1:]) for part in across_pairs(plane_a)]
+    kept_b, sent_b = last_core_sum(keep, across_cores(send), own)
+    received_b = to_relative(sent_b, 0, 0, 1, 0)
+    flip = heights // 2
+    (kept, sent), kept_b = plane_sum(plane_a, [kept_b], [flip, flip], "y_sum_a")
     received = to_relative(sent, 0, 0, 0, flip)
-    core_b = last_core_sum(keep, across_cores(send), own)
     while flip > 2:
         flip //= 2
         (kept, sent) = plane_sum([kept, received], [], [flip, flip], "height_sum_a")[0]
         received = to_relative(sent, 0, 0, 0, flip)
-    first, *second = last_sum(kept, received, across_plane(core_b), 3)
+    plane_b = across_pairs(plane_sum([kept_b, received_b], [], [1] * pairs, "x_sum_b")[0])
+    first, *second = last_sum(kept, received, plane_b)
     stress_new, nodal = element_update(
         first, across_height(second), displacement, stress_old, resistance, quad_weights
     )

time: 68.5 us -> 73.9 us (1.079)
  waiting for transfers between devices: 13 us -> 18.2 us
    ppermute x10 -> x8, waiting for transfers between devices: 11.7 us -> 16.9 us  [to_relative(): lax.ppermute(block, ('ca', 'fe'), [(i, i ^ flip) for i in range(groups *...]
    ppermute x10 -> x8, starting transfers between devices: 15.1 us -> 15.3 us  [to_relative(): lax.ppermute(block, ('ca', 'fe'), [(i, i ^ flip) for i in range(groups *...]
  transfers between devices with their start and end apart: 13 -> 11, of which waited for: 8 -> 6; matrix products, arithmetic and copies ran while one was open for 0% -> 0% of each run, Pallas kernels for 14% -> 13%
where the time goes in v18:
time: 73.9 us; the launch traced here: 73.7 us
  Pallas kernels  31.8 us (43%)
  starting transfers between devices  19.3 us (26%)
  waiting for transfers between devices  18.2 us (25%)
  local copies, waits for them, and re-layouts  2.34 us (3%)
  other arithmetic  1.32 us (2%)
  between operations  0.77 us (1%)
    pallas_call x2, Pallas kernels, cell_sums(): pl.pallas_call(functools.partial(cell_sum_kernel, octants, per_octant), o...  27.9 us
    ppermute x8, waiting for transfers between devices, to_relative(): lax.ppermute(block, ('ca', 'fe'), [(i, i ^ flip) for i in range(groups *...  16.9 us
    ppermute x8, starting transfers between devices, to_relative(): lax.ppermute(block, ('ca', 'fe'), [(i, i ^ flip) for i in range(groups *...  15.3 us
    ppermute x1, starting transfers between devices, passed_along(): return lax.ppermute(block, axis, route)  3.38 us
    unnamed x16, local copies, waits for them, and re-layouts  2.33 us
    pallas_call x1, Pallas kernels, brick_sums(): pl.pallas_call(brick_sum_kernel, out_shape=[jax.ShapeDtypeStruct((places,...  2.11 us
  transfers between devices with their start and end apart: 11, of which 6 were waited for; matrix products, arithmetic and copies ran while one was open for 0% of the time, Pallas kernels for 13%

profile of v18, /device:TPU:0, one launch (start us, length us, event | category | flops | bytes accessed | tf_op | source)
XLA Modules:
  0.0 73.7 jit_solution(15175480416802986416)
XLA Ops:
  0.6 0.8 %copy-done.1 = f32[3,4096]{1,0:T(4,128)S(1)} copy-done((f32[3,4096]{1,0:T(4,128)S(1)}, f32[3,4096]{1,0:T(4,128)}, u32[]{:S(2)}) %copy-start.1) | copy-done | bytes 49176
  1.5 0.2 rotation_table.1.table_ref
  1.6 0.7 %add_select_fusion = s32[2048]{0:T(1024)S(1)} fusion(s32[2048]{0:T(1024)} %param.15, s32[2048]{0:T(1024)} %bitcast.19, s32[2048]{0:T(1024)} %param.13), kind=kLoop, calls=%fused_computation | loop fusion | flops 8192 | bytes 32768 | tf_op jit(solution)/shard_map/jit(_where)/select_n | solution.py:739
  2.4 1.5 %copy-done.7 = s32[216,2048]{1,0:T(8,128)S(1)} copy-done((s32[216,2048]{1,0:T(8,128)S(1)}, s32[216,2048]{1,0:T(8,128)}, u32[]{:S(2)}) %copy-start.7) | copy-done | bytes 1769496
  3.9 20.3 %cell_sums.2 = (s32[1,2048]{1,0:T(1,128)S(1)}, f32[16,56,256]{2,1,0:T(8,128)S(1)}, bf16[112,2048]{1,0:T(8,128)(2,1)S(1)}, s32[56,2048]{1,0:T(8,128)S(1)}) custom-call(s32[216,2048]{1,0:T(8,128)S(1)} %copy-done.7, s32[1,2048]{1,0:T(1,128)S(1)} %bitcast.18, s32[48,8,128]{2,1,0:T(8,128)S(1)} %rotation_table.1.table_ref), custom_call_target="tpu_custom_call" | custom-call | flops 24000000000 | bytes 60000000 | tf_op jit(solution)/shard_map/cell_sums/pallas_call | solution.py:378
  24.2 0.5 collective-permute-start
  24.7 2.1 %brick_sums.1 = (f32[16,56,256]{2,1,0:T(8,128)S(1)}, s32[1,2048]{1,0:T(1,128)S(1)}) custom-call(bf16[112,2048]{1,0:T(8,128)(2,1)S(1)} %get-tuple-element.32.split_ref, s32[1,2048]{1,0:T(1,128)S(1)} %get-tuple-element.33.label_ref), custom_call_target="tpu_custom_call" | custom-call | flops 1680000000 | bytes 5600000 | tf_op jit(solution)/shard_map/brick_sums/pallas_call | solution.py:408
  26.8 0.0 collective-permute-done
  26.8 0.1 core_sum_a.1
  26.9 2.9 %collective-permute-start.1 = (f32[2,4,56,256]{3,2,1,0:T(8,128)S(1)}, f32[2,4,56,256]{3,2,1,0:T(8,128)S(1)}, u32[]{:S(2)}, u32[]{:S(2)}) collective-permute-start(f32[2,4,56,256]{3,2,1,0:T(8,128)S(1)} %get-tuple-element.38), channel_id=1, source_target_pairs={{0,1},{1,0},{2,3},{3,2},{4,5},{5,4},{6,7},{7,6},{8,9},{9,8},{10,11... | collective-permute-start | bytes 1376264 | tf_op jit(solution)/shard_map/ppermute | solution.py:515
  29.8 7.6 %cell_sums.3 = (f32[16,24,256]{2,1,0:T(8,128)S(1)}, f32[16,24,256]{2,1,0:T(8,128)S(1)}) custom-call(s32[56,2048]{1,0:T(8,128)S(1)} %get-tuple-element.40.ids_ref, s32[1,2048]{1,0:T(1,128)S(1)} %get-tuple-element.41.label_ref, s32[48,8,128]{2,1,0:T(8,128)S(1)} %rotation_table.1.table_ref), custom_call_target="tpu_custom_call" | custom-call | flops 8000000000 | bytes 20000000 | tf_op jit(solution)/shard_map/cell_sums/pallas_call | solution.py:378
  37.4 3.3 %collective-permute-done.1.refs_1_ = f32[2,4,56,256]{3,2,1,0:T(8,128)S(1)} collective-permute-done((f32[2,4,56,256]{3,2,1,0:T(8,128)S(1)}, f32[2,4,56,256]{3,2,1,0:T(8,128)S(1)}, u32[]{:S(2)}, u32[]{:S(2)}) %collective-permute-start.1) | collective-permute-done | bytes 458784 | tf_op jit(solution)/shard_map/ppermute | solution.py:515
  40.7 0.0 copy-start.6
  40.7 0.1 x_sum_a.1
  40.8 0.1 collective-permute-start.3
  40.9 1.8 %collective-permute-start.2 = (f32[1,4,56,256]{3,2,1,0:T(8,128)S(1)}, f32[1,4,56,256]{3,2,1,0:T(8,128)S(1)}, u32[]{:S(2)}, u32[]{:S(2)}) collective-permute-start(f32[1,4,56,256]{3,2,1,0:T(8,128)S(1)} %get-tuple-element.44), channel_id=1, source_target_pairs={{0,16},{1,17},{2,18},{3,19},{4,20},{5,21},{6,22},{7,23},{8,24},{9,... | collective-permute-start | bytes 688136 | tf_op jit(solution)/shard_map/ppermute | solution.py:515
  42.7 0.1 core_sum_b.1
  42.8 1.7 %collective-permute-start.5 = (f32[2,4,24,256]{3,2,1,0:T(8,128)S(1)}, f32[2,4,24,256]{3,2,1,0:T(8,128)S(1)}, u32[]{:S(2)}, u32[]{:S(2)}) collective-permute-start(f32[2,4,24,256]{3,2,1,0:T(8,128)S(1)} %get-tuple-element.52), channel_id=1, source_target_pairs={{0,1},{1,0},{2,3},{3,2},{4,5},{5,4},{6,7},{7,6},{8,9},{9,8},{10,11... | collective-permute-start | bytes 589832 | tf_op jit(solution)/shard_map/ppermute | solution.py:515
  44.4 4.5 %collective-permute-done.2 = f32[1,4,56,256]{3,2,1,0:T(8,128)S(1)} collective-permute-done((f32[1,4,56,256]{3,2,1,0:T(8,128)S(1)}, f32[1,4,56,256]{3,2,1,0:T(8,128)S(1)}, u32[]{:S(2)}, u32[]{:S(2)}) %collective-permute-start.2) | collective-permute-done | bytes 229408 | tf_op jit(solution)/shard_map/ppermute | solution.py:515
  49.0 2.9 %collective-permute-start.4 = (f32[2,56,256]{2,1,0:T(8,128)S(1)}, f32[2,56,256]{2,1,0:T(8,128)S(1)}, u32[]{:S(2)}, u32[]{:S(2)}) collective-permute-start(f32[2,56,256]{2,1,0:T(8,128)S(1)} %get-tuple-element.50), channel_id=1, source_target_pairs={{0,4},{1,5},{2,6},{3,7},{4,0},{5,1},{6,2},{7,3},{8,12},{9,13},{10,... | collective-permute-start | bytes 344072 | tf_op jit(solution)/shard_map/ppermute | solution.py:515
  51.8 0.0 collective-permute-done.5.refs_1_
  51.9 1.6 %collective-permute-start.6 = (f32[1,4,24,256]{3,2,1,0:T(8,128)S(1)}, f32[1,4,24,256]{3,2,1,0:T(8,128)S(1)}, u32[]{:S(2)}, u32[]{:S(2)}) collective-permute-start(f32[1,4,24,256]{3,2,1,0:T(8,128)S(1)} %get-tuple-element.54), channel_id=1, source_target_pairs={{0,16},{1,17},{2,18},{3,19},{4,20},{5,21},{6,22},{7,23},{8,24},{9,... | collective-permute-start | bytes 294920 | tf_op jit(solution)/shard_map/ppermute | solution.py:515
  53.5 3.8 %collective-permute-done.4.received_ref = f32[2,56,256]{2,1,0:T(8,128)S(1)} collective-permute-done((f32[2,56,256]{2,1,0:T(8,128)S(1)}, f32[2,56,256]{2,1,0:T(8,128)S(1)}, u32[]{:S(2)}, u32[]{:S(2)}) %collective-permute-start.4) | collective-permute-done | bytes 114720 | tf_op jit(solution)/shard_map/ppermute | solution.py:515
  57.3 0.9 %collective-permute-start.7 = (f32[80,256]{1,0:T(8,128)S(1)}, f32[80,256]{1,0:T(8,128)S(1)}, u32[]{:S(2)}, u32[]{:S(2)}) collective-permute-start(f32[80,256]{1,0:T(8,128)S(1)} %get-tuple-element.57), channel_id=1, source_target_pairs={{0,2},{1,3},{2,0},{3,1},{4,6},{5,7},{6,4},{7,5},{8,10},{9,11},{10,... | collective-permute-start | bytes 245768 | tf_op jit(solution)/shard_map/ppermute | solution.py:515
  58.2 3.2 %collective-permute-start.8 = (f32[24,256]{1,0:T(8,128)S(1)}, f32[24,256]{1,0:T(8,128)S(1)}, u32[]{:S(2)}, u32[]{:S(2)}) collective-permute-start(f32[24,256]{1,0:T(8,128)S(1)} %get-tuple-element.58), channel_id=1, source_target_pairs={{0,4},{1,5},{2,6},{3,7},{4,0},{5,1},{6,2},{7,3},{8,12},{9,13},{10,... | collective-permute-start | bytes 73736 | tf_op jit(solution)/shard_map/ppermute | solution.py:515
  61.5 0.3 collective-permute-start.9
  61.8 1.8 %collective-permute-done.8.refs_3_ = f32[24,256]{1,0:T(8,128)S(1)} collective-permute-done((f32[24,256]{1,0:T(8,128)S(1)}, f32[24,256]{1,0:T(8,128)S(1)}, u32[]{:S(2)}, u32[]{:S(2)}) %collective-permute-start.8) | collective-permute-done | bytes 24608 | tf_op jit(solution)/shard_map/ppermute | solution.py:515
  63.6 3.5 %collective-permute-done.9.refs_4_ = f32[24,256]{1,0:T(8,128)S(1)} collective-permute-done((f32[24,256]{1,0:T(8,128)S(1)}, f32[24,256]{1,0:T(8,128)S(1)}, u32[]{:S(2)}, u32[]{:S(2)}) %collective-permute-start.9) | collective-permute-done | bytes 24608 | tf_op jit(solution)/shard_map/ppermute | solution.py:515
  67.1 1.3 %stress_update.1 = (f32[6,8,225]{2,1,0:T(8,128)}, f32[2,3,1,256]{3,2,1,0:T(1,128)S(1)}) custom-call(f32[56,256]{1,0:T(8,128)S(1)} %get-tuple-element.55.refs_0_, f32[24,256]{1,0:T(8,128)S(1)} %get-tuple-element.56.refs_1_, f32[80,256]{1,0:T(8,128)S(1)} %collective-permute-done.7.refs_2_, f32[24,256]{1,0:T(8,128)S(1)} %collective-permute-done.8.refs_3_, ...), custom_call_target="tpu_custom_call" | custom-call | tf_op jit(solution)/shard_map/stress_update/pallas_call | solution.py:714
  68.4 3.4 %collective-permute-start.10 = (f32[3,1,256]{2,1,0:T(1,128)S(1)}, f32[3,1,256]{2,1,0:T(1,128)S(1)}, u32[]{:S(2)}, u32[]{:S(2)}) collective-permute-start(f32[3,1,256]{2,1,0:T(1,128)S(1)} %slice_bitcast_fusion), channel_id=1, source_target_pairs={{0,1},{1,2},{2,3},{3,4},{4,5},{5,6},{6,7},{8,9},{9,10},{10,11},{11... | collective-permute-start | bytes 9224 | tf_op jit(solution)/shard_map/ppermute | solution.py:50
  71.8 1.3 %collective-permute-done.10 = f32[3,1,256]{2,1,0:T(1,128)S(1)} collective-permute-done((f32[3,1,256]{2,1,0:T(1,128)S(1)}, f32[3,1,256]{2,1,0:T(1,128)S(1)}, u32[]{:S(2)}, u32[]{:S(2)}) %collective-permute-start.10) | collective-permute-done | bytes 3104 | tf_op jit(solution)/shard_map/ppermute | solution.py:50
  73.1 0.6 bitcast_add_fusion
  (20 shorter events, 0.1 us)
Async XLA Ops:
  0.6 0.8 %copy-start.1 = (f32[3,4096]{1,0:T(4,128)S(1)}, f32[3,4096]{1,0:T(4,128)}, u32[]{:S(2)}) copy-start(f32[3,4096]{1,0:T(4,128)} %euler_ref.1) | copy-start | bytes 147460
  2.4 1.5 %copy-start.7 = (s32[216,2048]{1,0:T(8,128)S(1)}, s32[216,2048]{1,0:T(8,128)}, u32[]{:S(2)}) copy-start(s32[216,2048]{1,0:T(8,128)} %ids_ref.1) | copy-start | bytes 5308420
  24.2 2.6 %collective-permute-start = (f32[16,56,256]{2,1,0:T(8,128)S(1)}, f32[16,56,256]{2,1,0:T(8,128)S(1)}, u32[]{:S(2)}, u32[]{:S(2)}) collective-permute-start(f32[16,56,256]{2,1,0:T(8,128)S(1)} %get-tuple-element.35), channel_id=1, source_target_pairs={{0,8},{8,0},{16,24},{24,16},{1,9},{9,1},{17,25},{25,17},{2,10},{10... | collective-permute-start | bytes 2752520 | tf_op jit(solution)/shard_map/ppermute | solution.py:317
  24.7 2.1 %copy-start.3 = (f32[3,1,256]{2,1,0:T(1,128)S(1)}, f32[3,1,256]{2,1,0:T(1,128)}, u32[]{:S(2)}) copy-start(f32[3,1,256]{2,1,0:T(1,128)} %refs_5_.1) | copy-start | bytes 9220
  26.9 13.7 %collective-permute-start.1 = (f32[2,4,56,256]{3,2,1,0:T(8,128)S(1)}, f32[2,4,56,256]{3,2,1,0:T(8,128)S(1)}, u32[]{:S(2)}, u32[]{:S(2)}) collective-permute-start(f32[2,4,56,256]{3,2,1,0:T(8,128)S(1)} %get-tuple-element.38), channel_id=1, source_target_pairs={{0,1},{1,0},{2,3},{3,2},{4,5},{5,4},{6,7},{7,6},{8,9},{9,8},{10,11... | collective-permute-start | bytes 1376264 | tf_op jit(solution)/shard_map/ppermute | solution.py:515
  40.7 26.4 %copy-start = (f32[12,8,225]{2,1,0:T(8,128)S(1)}, f32[12,8,225]{2,1,0:T(8,128)}, u32[]{:S(2)}) copy-start(f32[12,8,225]{2,1,0:T(8,128)} %refs_7_.1) | copy-start | bytes 259204
  40.7 26.4 %copy-start.2 = (f32[6,8,225]{2,1,0:T(8,128)S(1)}, f32[6,8,225]{2,1,0:T(8,128)}, u32[]{:S(2)}) copy-start(f32[6,8,225]{2,1,0:T(8,128)} %refs_6_.1) | copy-start | bytes 129604
  40.7 26.4 %copy-start.4 = (s32[8,225]{1,0:T(8,128)S(1)}, s32[8,225]{1,0:T(8,128)}, u32[]{:S(2)}) copy-start(s32[8,225]{1,0:T(8,128)} %refs_8_.1) | copy-start | bytes 21604
  40.7 26.4 %copy-start.5 = (bf16[16,144]{1,0:T(8,128)(2,1)S(1)}, bf16[16,144]{1,0:T(8,128)(2,1)}, u32[]{:S(2)}) copy-start(bf16[16,144]{1,0:T(8,128)(2,1)} %constant.11.clone.refs_10_) | copy-start | bytes 13828
  40.7 26.4 %copy-start.6 = (bf16[32,48]{1,0:T(8,128)(2,1)S(1)}, bf16[32,48]{1,0:T(8,128)(2,1)}, u32[]{:S(2)}) copy-start(bf16[32,48]{1,0:T(8,128)(2,1)} %constant.10.clone.refs_9_) | copy-start | bytes 9220
  40.8 1.9 %collective-permute-start.3 = (f32[16,24,256]{2,1,0:T(8,128)S(1)}, f32[16,24,256]{2,1,0:T(8,128)S(1)}, u32[]{:S(2)}, u32[]{:S(2)}) collective-permute-start(f32[16,24,256]{2,1,0:T(8,128)S(1)} %get-tuple-element.46), channel_id=1, source_target_pairs={{0,8},{8,0},{16,24},{24,16},{1,9},{9,1},{17,25},{25,17},{2,10},{10... | collective-permute-start | bytes 1179656 | tf_op jit(solution)/shard_map/ppermute | solution.py:317
  40.9 8.0 %collective-permute-start.2 = (f32[1,4,56,256]{3,2,1,0:T(8,128)S(1)}, f32[1,4,56,256]{3,2,1,0:T(8,128)S(1)}, u32[]{:S(2)}, u32[]{:S(2)}) collective-permute-start(f32[1,4,56,256]{3,2,1,0:T(8,128)S(1)} %get-tuple-element.44), channel_id=1, source_target_pairs={{0,16},{1,17},{2,18},{3,19},{4,20},{5,21},{6,22},{7,23},{8,24},{9,... | collective-permute-start | bytes 688136 | tf_op jit(solution)/shard_map/ppermute | solution.py:515
  42.8 9.1 %collective-permute-start.5 = (f32[2,4,24,256]{3,2,1,0:T(8,128)S(1)}, f32[2,4,24,256]{3,2,1,0:T(8,128)S(1)}, u32[]{:S(2)}, u32[]{:S(2)}) collective-permute-start(f32[2,4,24,256]{3,2,1,0:T(8,128)S(1)} %get-tuple-element.52), channel_id=1, source_target_pairs={{0,1},{1,0},{2,3},{3,2},{4,5},{5,4},{6,7},{7,6},{8,9},{9,8},{10,11... | collective-permute-start | bytes 589832 | tf_op jit(solution)/shard_map/ppermute | solution.py:515
  49.0 8.3 %collective-permute-start.4 = (f32[2,56,256]{2,1,0:T(8,128)S(1)}, f32[2,56,256]{2,1,0:T(8,128)S(1)}, u32[]{:S(2)}, u32[]{:S(2)}) collective-permute-start(f32[2,56,256]{2,1,0:T(8,128)S(1)} %get-tuple-element.50), channel_id=1, source_target_pairs={{0,4},{1,5},{2,6},{3,7},{4,0},{5,1},{6,2},{7,3},{8,12},{9,13},{10,... | collective-permute-start | bytes 344072 | tf_op jit(solution)/shard_map/ppermute | solution.py:515
  51.9 5.4 %collective-permute-start.6 = (f32[1,4,24,256]{3,2,1,0:T(8,128)S(1)}, f32[1,4,24,256]{3,2,1,0:T(8,128)S(1)}, u32[]{:S(2)}, u32[]{:S(2)}) collective-permute-start(f32[1,4,24,256]{3,2,1,0:T(8,128)S(1)} %get-tuple-element.54), channel_id=1, source_target_pairs={{0,16},{1,17},{2,18},{3,19},{4,20},{5,21},{6,22},{7,23},{8,24},{9,... | collective-permute-start | bytes 294920 | tf_op jit(solution)/shard_map/ppermute | solution.py:515
  57.3 9.8 %collective-permute-start.7 = (f32[80,256]{1,0:T(8,128)S(1)}, f32[80,256]{1,0:T(8,128)S(1)}, u32[]{:S(2)}, u32[]{:S(2)}) collective-permute-start(f32[80,256]{1,0:T(8,128)S(1)} %get-tuple-element.57), channel_id=1, source_target_pairs={{0,2},{1,3},{2,0},{3,1},{4,6},{5,7},{6,4},{7,5},{8,10},{9,11},{10,... | collective-permute-start | bytes 245768 | tf_op jit(solution)/shard_map/ppermute | solution.py:515
  58.2 5.4 %collective-permute-start.8 = (f32[24,256]{1,0:T(8,128)S(1)}, f32[24,256]{1,0:T(8,128)S(1)}, u32[]{:S(2)}, u32[]{:S(2)}) collective-permute-start(f32[24,256]{1,0:T(8,128)S(1)} %get-tuple-element.58), channel_id=1, source_target_pairs={{0,4},{1,5},{2,6},{3,7},{4,0},{5,1},{6,2},{7,3},{8,12},{9,13},{10,... | collective-permute-start | bytes 73736 | tf_op jit(solution)/shard_map/ppermute | solution.py:515
  61.5 5.6 %collective-permute-start.9 = (f32[24,256]{1,0:T(8,128)S(1)}, f32[24,256]{1,0:T(8,128)S(1)}, u32[]{:S(2)}, u32[]{:S(2)}) collective-permute-start(f32[24,256]{1,0:T(8,128)S(1)} %get-tuple-element.59), channel_id=1, source_target_pairs={{0,6},{1,7},{2,4},{3,5},{4,2},{5,3},{6,0},{7,1},{8,14},{9,15},{10,... | collective-permute-start | bytes 73736 | tf_op jit(solution)/shard_map/ppermute | solution.py:515
  68.4 4.7 %collective-permute-start.10 = (f32[3,1,256]{2,1,0:T(1,128)S(1)}, f32[3,1,256]{2,1,0:T(1,128)S(1)}, u32[]{:S(2)}, u32[]{:S(2)}) collective-permute-start(f32[3,1,256]{2,1,0:T(1,128)S(1)} %slice_bitcast_fusion), channel_id=1, source_target_pairs={{0,1},{1,2},{2,3},{3,4},{4,5},{5,6},{6,7},{8,9},{9,10},{10,11},{11... | collective-permute-start | bytes 9224 | tf_op jit(solution)/shard_map/ppermute | solution.py:50

commit v19 on v17

--- a/solution.py
+++ b/solution.py
@@ -279,7 +279,7 @@
         look_up(pair)
         return carry
 
-    lax.fori_loop(0, pairs, step, 0, unroll=2)
+    lax.fori_loop(0, pairs, step, 0, unroll=4 if first == 0 else 2)
     add_bricks(pairs - 2, True)
     fold_entries(pairs - 1)
     add_bricks(pairs - 1, True)
@@ -521,8 +521,13 @@
     ]
 
 
+def height_order(heights):
+    return [0] + list(range(2, heights)) + [1]
+
+
 def across_height(parts):
-    return [parts[0]] + [to_relative(parts[rest], 0, 0, 0, rest) for rest in range(1, len(parts))]
+    order = height_order(len(parts))
+    return [parts[0]] + [to_relative(parts[rest], 0, 0, 0, rest) for rest in order[1:]]
 
 
 def three_parts(value):
@@ -570,7 +575,7 @@
     elements = stress_ref.shape[2]
     rows, second_rows = first_ref.shape[0], second_refs[0].shape[0]
     gathered = [
-        first_ref[:, 0:elements] + second_refs[1][0:rows, 0:elements],
+        first_ref[:, 0:elements] + second_refs[-1][0:rows, 0:elements],
         sum(ref[ref.shape[0] - second_rows :, 0:elements] for ref in second_refs),
     ]
     counted = 9 * CHUNKS[1][1]
@@ -601,7 +606,7 @@
     height = lax.axis_index("fe") // 2
     above = height + (lax.axis_index("fe") & 1)
     upper = jnp.zeros((3, COLUMNS), jnp.float32)
-    for flip, ref in enumerate(second_refs):
+    for flip, ref in zip(height_order(heights), second_refs):
         wanted = (height ^ flip) == above
         upper = upper + jnp.where(wanted, ref[ref.shape[0] - 3 :, :], 0.0)
     values = jnp.where(

time: 68.5 us -> 68.8 us (level)
  no operation moved by 1% of the time
where the time goes in v19:
time: 68.8 us; the launch traced here: 68.5 us
  Pallas kernels  32 us (47%)
  starting transfers between devices  19.1 us (28%)
  waiting for transfers between devices  13 us (19%)
  local copies, waits for them, and re-layouts  2.35 us (3%)
  other arithmetic  1.32 us (2%)
  between operations  0.79 us (1%)
    pallas_call x2, Pallas kernels, cell_sums(): pl.pallas_call(functools.partial(cell_sum_kernel, octants, per_octant), o...  28.2 us
    ppermute x10, starting transfers between devices, to_relative(): lax.ppermute(block, ('ca', 'fe'), [(i, i ^ flip) for i in range(groups *...  15.1 us
    ppermute x10, waiting for transfers between devices, to_relative(): lax.ppermute(block, ('ca', 'fe'), [(i, i ^ flip) for i in range(groups *...  11.7 us
    ppermute x1, starting transfers between devices, passed_along(): return lax.ppermute(block, axis, route)  3.39 us
    unnamed x16, local copies, waits for them, and re-layouts  2.34 us
    pallas_call x1, Pallas kernels, brick_sums(): pl.pallas_call(brick_sum_kernel, out_shape=[jax.ShapeDtypeStruct((places,...  2.11 us
  transfers between devices with their start and end apart: 13, of which 8 were waited for; matrix products, arithmetic and copies ran while one was open for 0% of the time, Pallas kernels for 14%

profile of v19, /device:TPU:0, one launch (start us, length us, event | category | flops | bytes accessed | tf_op | source)
XLA Modules:
  0.0 68.5 jit_solution(13165442248791638553)
XLA Ops:
  0.6 0.8 %copy-done.1 = f32[3,4096]{1,0:T(4,128)S(1)} copy-done((f32[3,4096]{1,0:T(4,128)S(1)}, f32[3,4096]{1,0:T(4,128)}, u32[]{:S(2)}) %copy-start.1) | copy-done | bytes 49176
  1.5 0.2 rotation_table.1.table_ref
  1.6 0.7 %add_select_fusion = s32[2048]{0:T(1024)S(1)} fusion(s32[2048]{0:T(1024)} %param.15, s32[2048]{0:T(1024)} %bitcast.15, s32[2048]{0:T(1024)} %param.13), kind=kLoop, calls=%fused_computation | loop fusion | flops 8192 | bytes 32768 | tf_op jit(solution)/shard_map/jit(_where)/select_n | solution.py:746
  2.4 1.5 %copy-done.7 = s32[216,2048]{1,0:T(8,128)S(1)} copy-done((s32[216,2048]{1,0:T(8,128)S(1)}, s32[216,2048]{1,0:T(8,128)}, u32[]{:S(2)}) %copy-start.7) | copy-done | bytes 1769496
  3.9 20.6 %cell_sums.2 = (s32[1,2048]{1,0:T(1,128)S(1)}, f32[16,56,256]{2,1,0:T(8,128)S(1)}, bf16[112,2048]{1,0:T(8,128)(2,1)S(1)}, s32[56,2048]{1,0:T(8,128)S(1)}) custom-call(s32[216,2048]{1,0:T(8,128)S(1)} %copy-done.7, s32[1,2048]{1,0:T(1,128)S(1)} %bitcast.14, s32[48,8,128]{2,1,0:T(8,128)S(1)} %rotation_table.1.table_ref), custom_call_target="tpu_custom_call" | custom-call | flops 24000000000 | bytes 60000000 | tf_op jit(solution)/shard_map/cell_sums/pallas_call | solution.py:378
  24.4 0.5 collective-permute-start
  25.0 2.1 %brick_sums.1 = (f32[16,56,256]{2,1,0:T(8,128)S(1)}, s32[1,2048]{1,0:T(1,128)S(1)}) custom-call(bf16[112,2048]{1,0:T(8,128)(2,1)S(1)} %get-tuple-element.31.split_ref, s32[1,2048]{1,0:T(1,128)S(1)} %get-tuple-element.32.label_ref), custom_call_target="tpu_custom_call" | custom-call | flops 1680000000 | bytes 5600000 | tf_op jit(solution)/shard_map/brick_sums/pallas_call | solution.py:408
  27.1 0.1 core_sum_a.1
  27.2 3.8 %collective-permute-start.1 = (f32[4,56,256]{2,1,0:T(8,128)S(1)}, f32[4,56,256]{2,1,0:T(8,128)S(1)}, u32[]{:S(2)}, u32[]{:S(2)}) collective-permute-start(f32[4,56,256]{2,1,0:T(8,128)S(1)} %get-tuple-element.37), channel_id=1, source_target_pairs={{0,17},{1,16},{2,19},{3,18},{4,21},{5,20},{6,23},{7,22},{8,25},{9,... | collective-permute-start | bytes 688136 | tf_op jit(solution)/shard_map/ppermute | solution.py:514
  31.1 0.5 collective-permute-start.2
  31.6 0.1 collective-permute-start.3
  31.7 7.6 %cell_sums.3 = (f32[16,24,256]{2,1,0:T(8,128)S(1)}, f32[16,24,256]{2,1,0:T(8,128)S(1)}) custom-call(s32[56,2048]{1,0:T(8,128)S(1)} %get-tuple-element.41.ids_ref, s32[1,2048]{1,0:T(1,128)S(1)} %get-tuple-element.42.label_ref, s32[48,8,128]{2,1,0:T(8,128)S(1)} %rotation_table.1.table_ref), custom_call_target="tpu_custom_call" | custom-call | flops 8000000000 | bytes 20000000 | tf_op jit(solution)/shard_map/cell_sums/pallas_call | solution.py:378
  39.4 2.6 %collective-permute-done.2.refs_2_ = f32[4,56,256]{2,1,0:T(8,128)S(1)} collective-permute-done((f32[4,56,256]{2,1,0:T(8,128)S(1)}, f32[4,56,256]{2,1,0:T(8,128)S(1)}, u32[]{:S(2)}, u32[]{:S(2)}) %collective-permute-start.2) | collective-permute-done | bytes 229408 | tf_op jit(solution)/shard_map/ppermute | solution.py:514
  41.9 0.3 collective-permute-done.3.refs_3_
  42.2 0.1 plane_sum_a.1
  42.3 0.1 collective-permute-start.5
  42.4 2.7 %collective-permute-start.4 = (f32[2,56,256]{2,1,0:T(8,128)S(1)}, f32[2,56,256]{2,1,0:T(8,128)S(1)}, u32[]{:S(2)}, u32[]{:S(2)}) collective-permute-start(f32[2,56,256]{2,1,0:T(8,128)S(1)} %get-tuple-element.45), channel_id=1, source_target_pairs={{0,4},{1,5},{2,6},{3,7},{4,0},{5,1},{6,2},{7,3},{8,12},{9,13},{10,... | collective-permute-start | bytes 344072 | tf_op jit(solution)/shard_map/ppermute | solution.py:514
  45.1 1.7 %collective-permute-start.6 = (f32[4,24,256]{2,1,0:T(8,128)S(1)}, f32[4,24,256]{2,1,0:T(8,128)S(1)}, u32[]{:S(2)}, u32[]{:S(2)}) collective-permute-start(f32[4,24,256]{2,1,0:T(8,128)S(1)} %get-tuple-element.50), channel_id=1, source_target_pairs={{0,17},{1,16},{2,19},{3,18},{4,21},{5,20},{6,23},{7,22},{8,25},{9,... | collective-permute-start | bytes 294920 | tf_op jit(solution)/shard_map/ppermute | solution.py:514
  46.8 1.3 %collective-permute-start.7 = (f32[4,24,256]{2,1,0:T(8,128)S(1)}, f32[4,24,256]{2,1,0:T(8,128)S(1)}, u32[]{:S(2)}, u32[]{:S(2)}) collective-permute-start(f32[4,24,256]{2,1,0:T(8,128)S(1)} %get-tuple-element.51), channel_id=1, source_target_pairs={{0,16},{1,17},{2,18},{3,19},{4,20},{5,21},{6,22},{7,23},{8,24},{9,... | collective-permute-start | bytes 294920 | tf_op jit(solution)/shard_map/ppermute | solution.py:514
  48.1 0.5 collective-permute-start.8
  48.7 2.6 %collective-permute-done.4.received_ref = f32[2,56,256]{2,1,0:T(8,128)S(1)} collective-permute-done((f32[2,56,256]{2,1,0:T(8,128)S(1)}, f32[2,56,256]{2,1,0:T(8,128)S(1)}, u32[]{:S(2)}, u32[]{:S(2)}) %collective-permute-start.4) | collective-permute-done | bytes 114720 | tf_op jit(solution)/shard_map/ppermute | solution.py:514
  51.3 0.1 collective-permute-done.6.refs_1_
  51.4 1.6 %collective-permute-done.7.refs_2_ = f32[4,24,256]{2,1,0:T(8,128)S(1)} collective-permute-done((f32[4,24,256]{2,1,0:T(8,128)S(1)}, f32[4,24,256]{2,1,0:T(8,128)S(1)}, u32[]{:S(2)}, u32[]{:S(2)}) %collective-permute-start.7) | collective-permute-done | bytes 98336 | tf_op jit(solution)/shard_map/ppermute | solution.py:514
  53.1 1.6 %collective-permute-start.11 = (f32[80,256]{1,0:T(8,128)S(1)}, f32[80,256]{1,0:T(8,128)S(1)}, u32[]{:S(2)}, u32[]{:S(2)}) collective-permute-start(f32[80,256]{1,0:T(8,128)S(1)} %get-tuple-element.57), channel_id=1, source_target_pairs={{0,2},{1,3},{2,0},{3,1},{4,6},{5,7},{6,4},{7,5},{8,10},{9,11},{10,... | collective-permute-start | bytes 245768 | tf_op jit(solution)/shard_map/ppermute | solution.py:514
  54.7 1.6 %collective-permute-start.9 = (f32[24,256]{1,0:T(8,128)S(1)}, f32[24,256]{1,0:T(8,128)S(1)}, u32[]{:S(2)}, u32[]{:S(2)}) collective-permute-start(f32[24,256]{1,0:T(8,128)S(1)} %get-tuple-element.55), channel_id=1, source_target_pairs={{0,4},{1,5},{2,6},{3,7},{4,0},{5,1},{6,2},{7,3},{8,12},{9,13},{10,... | collective-permute-start | bytes 73736 | tf_op jit(solution)/shard_map/ppermute | solution.py:514
  56.3 1.2 %collective-permute-start.10 = (f32[24,256]{1,0:T(8,128)S(1)}, f32[24,256]{1,0:T(8,128)S(1)}, u32[]{:S(2)}, u32[]{:S(2)}) collective-permute-start(f32[24,256]{1,0:T(8,128)S(1)} %get-tuple-element.56), channel_id=1, source_target_pairs={{0,6},{1,7},{2,4},{3,5},{4,2},{5,3},{6,0},{7,1},{8,14},{9,15},{10,... | collective-permute-start | bytes 73736 | tf_op jit(solution)/shard_map/ppermute | solution.py:514
  57.5 2.1 %collective-permute-done.9.refs_2_ = f32[24,256]{1,0:T(8,128)S(1)} collective-permute-done((f32[24,256]{1,0:T(8,128)S(1)}, f32[24,256]{1,0:T(8,128)S(1)}, u32[]{:S(2)}, u32[]{:S(2)}) %collective-permute-start.9) | collective-permute-done | bytes 24608 | tf_op jit(solution)/shard_map/ppermute | solution.py:514
  59.6 2.4 %collective-permute-done.10.refs_3_ = f32[24,256]{1,0:T(8,128)S(1)} collective-permute-done((f32[24,256]{1,0:T(8,128)S(1)}, f32[24,256]{1,0:T(8,128)S(1)}, u32[]{:S(2)}, u32[]{:S(2)}) %collective-permute-start.10) | collective-permute-done | bytes 24608 | tf_op jit(solution)/shard_map/ppermute | solution.py:514
  62.0 1.3 %stress_update.1 = (f32[6,8,225]{2,1,0:T(8,128)}, f32[2,3,1,256]{3,2,1,0:T(1,128)S(1)}) custom-call(f32[56,256]{1,0:T(8,128)S(1)} %get-tuple-element.53.refs_0_, f32[24,256]{1,0:T(8,128)S(1)} %get-tuple-element.54.refs_1_, f32[24,256]{1,0:T(8,128)S(1)} %collective-permute-done.9.refs_2_, f32[24,256]{1,0:T(8,128)S(1)} %collective-permute-done.10.refs_3_, ...), custom_call_target="tpu_custom_call" | custom-call | tf_op jit(solution)/shard_map/stress_update/pallas_call | solution.py:721
  63.3 3.4 %collective-permute-start.12 = (f32[3,1,256]{2,1,0:T(1,128)S(1)}, f32[3,1,256]{2,1,0:T(1,128)S(1)}, u32[]{:S(2)}, u32[]{:S(2)}) collective-permute-start(f32[3,1,256]{2,1,0:T(1,128)S(1)} %slice_bitcast_fusion), channel_id=1, source_target_pairs={{0,1},{1,2},{2,3},{3,4},{4,5},{5,6},{6,7},{8,9},{9,10},{10,11},{11... | collective-permute-start | bytes 9224 | tf_op jit(solution)/shard_map/ppermute | solution.py:50
  66.7 1.3 %collective-permute-done.12 = f32[3,1,256]{2,1,0:T(1,128)S(1)} collective-permute-done((f32[3,1,256]{2,1,0:T(1,128)S(1)}, f32[3,1,256]{2,1,0:T(1,128)S(1)}, u32[]{:S(2)}, u32[]{:S(2)}) %collective-permute-start.12) | collective-permute-done | bytes 3104 | tf_op jit(solution)/shard_map/ppermute | solution.py:50
  68.0 0.6 bitcast_add_fusion
  (22 shorter events, 0.2 us)
Async XLA Ops:
  0.6 0.8 %copy-start.1 = (f32[3,4096]{1,0:T(4,128)S(1)}, f32[3,4096]{1,0:T(4,128)}, u32[]{:S(2)}) copy-start(f32[3,4096]{1,0:T(4,128)} %euler_ref.1) | copy-start | bytes 147460
  2.4 1.5 %copy-start.7 = (s32[216,2048]{1,0:T(8,128)S(1)}, s32[216,2048]{1,0:T(8,128)}, u32[]{:S(2)}) copy-start(s32[216,2048]{1,0:T(8,128)} %ids_ref.1) | copy-start | bytes 5308420
  24.4 2.6 %collective-permute-start = (f32[16,56,256]{2,1,0:T(8,128)S(1)}, f32[16,56,256]{2,1,0:T(8,128)S(1)}, u32[]{:S(2)}, u32[]{:S(2)}) collective-permute-start(f32[16,56,256]{2,1,0:T(8,128)S(1)} %get-tuple-element.34), channel_id=1, source_target_pairs={{0,8},{8,0},{16,24},{24,16},{1,9},{9,1},{17,25},{25,17},{2,10},{10... | collective-permute-start | bytes 2752520 | tf_op jit(solution)/shard_map/ppermute | solution.py:317
  25.0 2.1 %copy-start.3 = (f32[3,1,256]{2,1,0:T(1,128)S(1)}, f32[3,1,256]{2,1,0:T(1,128)}, u32[]{:S(2)}) copy-start(f32[3,1,256]{2,1,0:T(1,128)} %refs_5_.1) | copy-start | bytes 9220
  27.2 12.1 %collective-permute-start.1 = (f32[4,56,256]{2,1,0:T(8,128)S(1)}, f32[4,56,256]{2,1,0:T(8,128)S(1)}, u32[]{:S(2)}, u32[]{:S(2)}) collective-permute-start(f32[4,56,256]{2,1,0:T(8,128)S(1)} %get-tuple-element.37), channel_id=1, source_target_pairs={{0,17},{1,16},{2,19},{3,18},{4,21},{5,20},{6,23},{7,22},{8,25},{9,... | collective-permute-start | bytes 688136 | tf_op jit(solution)/shard_map/ppermute | solution.py:514
  31.1 10.9 %collective-permute-start.2 = (f32[4,56,256]{2,1,0:T(8,128)S(1)}, f32[4,56,256]{2,1,0:T(8,128)S(1)}, u32[]{:S(2)}, u32[]{:S(2)}) collective-permute-start(f32[4,56,256]{2,1,0:T(8,128)S(1)} %get-tuple-element.38), channel_id=1, source_target_pairs={{0,16},{1,17},{2,18},{3,19},{4,20},{5,21},{6,22},{7,23},{8,24},{9,... | collective-permute-start | bytes 688136 | tf_op jit(solution)/shard_map/ppermute | solution.py:514
  31.6 10.7 %collective-permute-start.3 = (f32[4,56,256]{2,1,0:T(8,128)S(1)}, f32[4,56,256]{2,1,0:T(8,128)S(1)}, u32[]{:S(2)}, u32[]{:S(2)}) collective-permute-start(f32[4,56,256]{2,1,0:T(8,128)S(1)} %get-tuple-element.39), channel_id=1, source_target_pairs={{0,1},{1,0},{2,3},{3,2},{4,5},{5,4},{6,7},{7,6},{8,9},{9,8},{10,11... | collective-permute-start | bytes 688136 | tf_op jit(solution)/shard_map/ppermute | solution.py:514
  39.3 22.7 %copy-start = (f32[12,8,225]{2,1,0:T(8,128)S(1)}, f32[12,8,225]{2,1,0:T(8,128)}, u32[]{:S(2)}) copy-start(f32[12,8,225]{2,1,0:T(8,128)} %refs_7_.1) | copy-start | bytes 259204
  39.3 22.7 %copy-start.2 = (f32[6,8,225]{2,1,0:T(8,128)S(1)}, f32[6,8,225]{2,1,0:T(8,128)}, u32[]{:S(2)}) copy-start(f32[6,8,225]{2,1,0:T(8,128)} %refs_6_.1) | copy-start | bytes 129604
  39.3 22.6 %copy-start.4 = (s32[8,225]{1,0:T(8,128)S(1)}, s32[8,225]{1,0:T(8,128)}, u32[]{:S(2)}) copy-start(s32[8,225]{1,0:T(8,128)} %refs_8_.1) | copy-start | bytes 21604
  39.3 22.6 %copy-start.5 = (bf16[16,144]{1,0:T(8,128)(2,1)S(1)}, bf16[16,144]{1,0:T(8,128)(2,1)}, u32[]{:S(2)}) copy-start(bf16[16,144]{1,0:T(8,128)(2,1)} %constant.11.clone.refs_10_) | copy-start | bytes 13828
  39.4 22.6 %copy-start.6 = (bf16[32,48]{1,0:T(8,128)(2,1)S(1)}, bf16[32,48]{1,0:T(8,128)(2,1)}, u32[]{:S(2)}) copy-start(bf16[32,48]{1,0:T(8,128)(2,1)} %constant.10.clone.refs_9_) | copy-start | bytes 9220
  42.3 2.7 %collective-permute-start.5 = (f32[16,24,256]{2,1,0:T(8,128)S(1)}, f32[16,24,256]{2,1,0:T(8,128)S(1)}, u32[]{:S(2)}, u32[]{:S(2)}) collective-permute-start(f32[16,24,256]{2,1,0:T(8,128)S(1)} %get-tuple-element.47), channel_id=1, source_target_pairs={{0,8},{8,0},{16,24},{24,16},{1,9},{9,1},{17,25},{25,17},{2,10},{10... | collective-permute-start | bytes 1179656 | tf_op jit(solution)/shard_map/ppermute | solution.py:317
  42.4 8.9 %collective-permute-start.4 = (f32[2,56,256]{2,1,0:T(8,128)S(1)}, f32[2,56,256]{2,1,0:T(8,128)S(1)}, u32[]{:S(2)}, u32[]{:S(2)}) collective-permute-start(f32[2,56,256]{2,1,0:T(8,128)S(1)} %get-tuple-element.45), channel_id=1, source_target_pairs={{0,4},{1,5},{2,6},{3,7},{4,0},{5,1},{6,2},{7,3},{8,12},{9,13},{10,... | collective-permute-start | bytes 344072 | tf_op jit(solution)/shard_map/ppermute | solution.py:514
  45.1 6.3 %collective-permute-start.6 = (f32[4,24,256]{2,1,0:T(8,128)S(1)}, f32[4,24,256]{2,1,0:T(8,128)S(1)}, u32[]{:S(2)}, u32[]{:S(2)}) collective-permute-start(f32[4,24,256]{2,1,0:T(8,128)S(1)} %get-tuple-element.50), channel_id=1, source_target_pairs={{0,17},{1,16},{2,19},{3,18},{4,21},{5,20},{6,23},{7,22},{8,25},{9,... | collective-permute-start | bytes 294920 | tf_op jit(solution)/shard_map/ppermute | solution.py:514
  46.8 6.2 %collective-permute-start.7 = (f32[4,24,256]{2,1,0:T(8,128)S(1)}, f32[4,24,256]{2,1,0:T(8,128)S(1)}, u32[]{:S(2)}, u32[]{:S(2)}) collective-permute-start(f32[4,24,256]{2,1,0:T(8,128)S(1)} %get-tuple-element.51), channel_id=1, source_target_pairs={{0,16},{1,17},{2,18},{3,19},{4,20},{5,21},{6,22},{7,23},{8,24},{9,... | collective-permute-start | bytes 294920 | tf_op jit(solution)/shard_map/ppermute | solution.py:514
  48.1 4.9 %collective-permute-start.8 = (f32[4,24,256]{2,1,0:T(8,128)S(1)}, f32[4,24,256]{2,1,0:T(8,128)S(1)}, u32[]{:S(2)}, u32[]{:S(2)}) collective-permute-start(f32[4,24,256]{2,1,0:T(8,128)S(1)} %get-tuple-element.52), channel_id=1, source_target_pairs={{0,1},{1,0},{2,3},{3,2},{4,5},{5,4},{6,7},{7,6},{8,9},{9,8},{10,11... | collective-permute-start | bytes 294920 | tf_op jit(solution)/shard_map/ppermute | solution.py:514
  53.1 8.9 %collective-permute-start.11 = (f32[80,256]{1,0:T(8,128)S(1)}, f32[80,256]{1,0:T(8,128)S(1)}, u32[]{:S(2)}, u32[]{:S(2)}) collective-permute-start(f32[80,256]{1,0:T(8,128)S(1)} %get-tuple-element.57), channel_id=1, source_target_pairs={{0,2},{1,3},{2,0},{3,1},{4,6},{5,7},{6,4},{7,5},{8,10},{9,11},{10,... | collective-permute-start | bytes 245768 | tf_op jit(solution)/shard_map/ppermute | solution.py:514
  54.7 4.9 %collective-permute-start.9 = (f32[24,256]{1,0:T(8,128)S(1)}, f32[24,256]{1,0:T(8,128)S(1)}, u32[]{:S(2)}, u32[]{:S(2)}) collective-permute-start(f32[24,256]{1,0:T(8,128)S(1)} %get-tuple-element.55), channel_id=1, source_target_pairs={{0,4},{1,5},{2,6},{3,7},{4,0},{5,1},{6,2},{7,3},{8,12},{9,13},{10,... | collective-permute-start | bytes 73736 | tf_op jit(solution)/shard_map/ppermute | solution.py:514
  56.3 5.6 %collective-permute-start.10 = (f32[24,256]{1,0:T(8,128)S(1)}, f32[24,256]{1,0:T(8,128)S(1)}, u32[]{:S(2)}, u32[]{:S(2)}) collective-permute-start(f32[24,256]{1,0:T(8,128)S(1)} %get-tuple-element.56), channel_id=1, source_target_pairs={{0,6},{1,7},{2,4},{3,5},{4,2},{5,3},{6,0},{7,1},{8,14},{9,15},{10,... | collective-permute-start | bytes 73736 | tf_op jit(solution)/shard_map/ppermute | solution.py:514
  63.3 4.7 %collective-permute-start.12 = (f32[3,1,256]{2,1,0:T(1,128)S(1)}, f32[3,1,256]{2,1,0:T(1,128)S(1)}, u32[]{:S(2)}, u32[]{:S(2)}) collective-permute-start(f32[3,1,256]{2,1,0:T(1,128)S(1)} %slice_bitcast_fusion), channel_id=1, source_target_pairs={{0,1},{1,2},{2,3},{3,4},{4,5},{5,6},{6,7},{8,9},{9,10},{10,11},{11... | collective-permute-start | bytes 9224 | tf_op jit(solution)/shard_map/ppermute | solution.py:50

commit v20 on v17

--- a/solution.py
+++ b/solution.py
@@ -517,7 +517,7 @@
 def across_plane(parts):
     return [parts[0]] + [
         to_relative(parts[index], 0, index // 2, index % 2, 0)
-        for index in range(len(parts) - 1, 0, -1)
+        for index in list(range(2, len(parts))) + [1]
     ]
 
 

time: 68.5 us -> 69.1 us (level)
  no operation moved by 1% of the time
where the time goes in v20:
time: 69.1 us; the launch traced here: 68.8 us
  Pallas kernels  31.7 us (46%)
  starting transfers between devices  19.2 us (28%)
  waiting for transfers between devices  13.4 us (19%)
  local copies, waits for them, and re-layouts  2.35 us (3%)
  other arithmetic  1.32 us (2%)
  between operations  0.78 us (1%)
    pallas_call x2, Pallas kernels, cell_sums(): pl.pallas_call(functools.partial(cell_sum_kernel, octants, per_octant), o...  27.9 us
    ppermute x10, starting transfers between devices, to_relative(): lax.ppermute(block, ('ca', 'fe'), [(i, i ^ flip) for i in range(groups *...  15.3 us
    ppermute x10, waiting for transfers between devices, to_relative(): lax.ppermute(block, ('ca', 'fe'), [(i, i ^ flip) for i in range(groups *...  12.1 us
    ppermute x1, starting transfers between devices, passed_along(): return lax.ppermute(block, axis, route)  3.36 us
    unnamed x16, local copies, waits for them, and re-layouts  2.34 us
    pallas_call x1, Pallas kernels, brick_sums(): pl.pallas_call(brick_sum_kernel, out_shape=[jax.ShapeDtypeStruct((places,...  2.11 us
  transfers between devices with their start and end apart: 13, of which 8 were waited for; matrix products, arithmetic and copies ran while one was open for 0% of the time, Pallas kernels for 14%

profile of v20, /device:TPU:0, one launch (start us, length us, event | category | flops | bytes accessed | tf_op | source)
XLA Modules:
  0.0 68.8 jit_solution(17131223993102359891)
XLA Ops:
  0.6 0.8 %copy-done.1 = f32[3,4096]{1,0:T(4,128)S(1)} copy-done((f32[3,4096]{1,0:T(4,128)S(1)}, f32[3,4096]{1,0:T(4,128)}, u32[]{:S(2)}) %copy-start.1) | copy-done | bytes 49176
  1.5 0.2 rotation_table.1.table_ref
  1.6 0.7 %add_select_fusion = s32[2048]{0:T(1024)S(1)} fusion(s32[2048]{0:T(1024)} %param.15, s32[2048]{0:T(1024)} %bitcast.15, s32[2048]{0:T(1024)} %param.13), kind=kLoop, calls=%fused_computation | loop fusion | flops 8192 | bytes 32768 | tf_op jit(solution)/shard_map/jit(_where)/select_n | solution.py:741
  2.4 1.5 %copy-done.7 = s32[216,2048]{1,0:T(8,128)S(1)} copy-done((s32[216,2048]{1,0:T(8,128)S(1)}, s32[216,2048]{1,0:T(8,128)}, u32[]{:S(2)}) %copy-start.7) | copy-done | bytes 1769496
  3.9 20.3 %cell_sums.2 = (s32[1,2048]{1,0:T(1,128)S(1)}, f32[16,56,256]{2,1,0:T(8,128)S(1)}, bf16[112,2048]{1,0:T(8,128)(2,1)S(1)}, s32[56,2048]{1,0:T(8,128)S(1)}) custom-call(s32[216,2048]{1,0:T(8,128)S(1)} %copy-done.7, s32[1,2048]{1,0:T(1,128)S(1)} %bitcast.14, s32[48,8,128]{2,1,0:T(8,128)S(1)} %rotation_table.1.table_ref), custom_call_target="tpu_custom_call" | custom-call | flops 24000000000 | bytes 60000000 | tf_op jit(solution)/shard_map/cell_sums/pallas_call | solution.py:378
  24.2 0.5 collective-permute-start
  24.7 2.1 %brick_sums.1 = (f32[16,56,256]{2,1,0:T(8,128)S(1)}, s32[1,2048]{1,0:T(1,128)S(1)}) custom-call(bf16[112,2048]{1,0:T(8,128)(2,1)S(1)} %get-tuple-element.31.split_ref, s32[1,2048]{1,0:T(1,128)S(1)} %get-tuple-element.32.label_ref), custom_call_target="tpu_custom_call" | custom-call | flops 1680000000 | bytes 5600000 | tf_op jit(solution)/shard_map/brick_sums/pallas_call | solution.py:408
  26.8 0.1 core_sum_a.1
  26.9 2.9 %collective-permute-start.1 = (f32[4,56,256]{2,1,0:T(8,128)S(1)}, f32[4,56,256]{2,1,0:T(8,128)S(1)}, u32[]{:S(2)}, u32[]{:S(2)}) collective-permute-start(f32[4,56,256]{2,1,0:T(8,128)S(1)} %get-tuple-element.37), channel_id=1, source_target_pairs={{0,16},{1,17},{2,18},{3,19},{4,20},{5,21},{6,22},{7,23},{8,24},{9,... | collective-permute-start | bytes 688136 | tf_op jit(solution)/shard_map/ppermute | solution.py:514
  29.9 1.4 %collective-permute-start.2 = (f32[4,56,256]{2,1,0:T(8,128)S(1)}, f32[4,56,256]{2,1,0:T(8,128)S(1)}, u32[]{:S(2)}, u32[]{:S(2)}) collective-permute-start(f32[4,56,256]{2,1,0:T(8,128)S(1)} %get-tuple-element.38), channel_id=1, source_target_pairs={{0,17},{1,16},{2,19},{3,18},{4,21},{5,20},{6,23},{7,22},{8,25},{9,... | collective-permute-start | bytes 688136 | tf_op jit(solution)/shard_map/ppermute | solution.py:514
  31.3 0.1 collective-permute-start.3
  31.4 7.6 %cell_sums.3 = (f32[16,24,256]{2,1,0:T(8,128)S(1)}, f32[16,24,256]{2,1,0:T(8,128)S(1)}) custom-call(s32[56,2048]{1,0:T(8,128)S(1)} %get-tuple-element.41.ids_ref, s32[1,2048]{1,0:T(1,128)S(1)} %get-tuple-element.42.label_ref, s32[48,8,128]{2,1,0:T(8,128)S(1)} %rotation_table.1.table_ref), custom_call_target="tpu_custom_call" | custom-call | flops 8000000000 | bytes 20000000 | tf_op jit(solution)/shard_map/cell_sums/pallas_call | solution.py:378
  39.0 1.7 %collective-permute-done.1.refs_1_ = f32[4,56,256]{2,1,0:T(8,128)S(1)} collective-permute-done((f32[4,56,256]{2,1,0:T(8,128)S(1)}, f32[4,56,256]{2,1,0:T(8,128)S(1)}, u32[]{:S(2)}, u32[]{:S(2)}) %collective-permute-start.1) | collective-permute-done | bytes 229408 | tf_op jit(solution)/shard_map/ppermute | solution.py:514
  40.7 1.3 %collective-permute-done.3.refs_3_ = f32[4,56,256]{2,1,0:T(8,128)S(1)} collective-permute-done((f32[4,56,256]{2,1,0:T(8,128)S(1)}, f32[4,56,256]{2,1,0:T(8,128)S(1)}, u32[]{:S(2)}, u32[]{:S(2)}) %collective-permute-start.3) | collective-permute-done | bytes 229408 | tf_op jit(solution)/shard_map/ppermute | solution.py:514
  42.0 0.1 plane_sum_a.1
  42.1 0.1 collective-permute-start.5
  42.2 2.8 %collective-permute-start.4 = (f32[2,56,256]{2,1,0:T(8,128)S(1)}, f32[2,56,256]{2,1,0:T(8,128)S(1)}, u32[]{:S(2)}, u32[]{:S(2)}) collective-permute-start(f32[2,56,256]{2,1,0:T(8,128)S(1)} %get-tuple-element.45), channel_id=1, source_target_pairs={{0,4},{1,5},{2,6},{3,7},{4,0},{5,1},{6,2},{7,3},{8,12},{9,13},{10,... | collective-permute-start | bytes 344072 | tf_op jit(solution)/shard_map/ppermute | solution.py:514
  45.1 1.6 %collective-permute-start.6 = (f32[4,24,256]{2,1,0:T(8,128)S(1)}, f32[4,24,256]{2,1,0:T(8,128)S(1)}, u32[]{:S(2)}, u32[]{:S(2)}) collective-permute-start(f32[4,24,256]{2,1,0:T(8,128)S(1)} %get-tuple-element.50), channel_id=1, source_target_pairs={{0,16},{1,17},{2,18},{3,19},{4,20},{5,21},{6,22},{7,23},{8,24},{9,... | collective-permute-start | bytes 294920 | tf_op jit(solution)/shard_map/ppermute | solution.py:514
  46.6 1.4 %collective-permute-start.7 = (f32[4,24,256]{2,1,0:T(8,128)S(1)}, f32[4,24,256]{2,1,0:T(8,128)S(1)}, u32[]{:S(2)}, u32[]{:S(2)}) collective-permute-start(f32[4,24,256]{2,1,0:T(8,128)S(1)} %get-tuple-element.51), channel_id=1, source_target_pairs={{0,17},{1,16},{2,19},{3,18},{4,21},{5,20},{6,23},{7,22},{8,25},{9,... | collective-permute-start | bytes 294920 | tf_op jit(solution)/shard_map/ppermute | solution.py:514
  48.1 0.5 collective-permute-start.8
  48.6 2.6 %collective-permute-done.4.received_ref = f32[2,56,256]{2,1,0:T(8,128)S(1)} collective-permute-done((f32[2,56,256]{2,1,0:T(8,128)S(1)}, f32[2,56,256]{2,1,0:T(8,128)S(1)}, u32[]{:S(2)}, u32[]{:S(2)}) %collective-permute-start.4) | collective-permute-done | bytes 114720 | tf_op jit(solution)/shard_map/ppermute | solution.py:514
  51.2 1.9 %collective-permute-done.7.refs_2_ = f32[4,24,256]{2,1,0:T(8,128)S(1)} collective-permute-done((f32[4,24,256]{2,1,0:T(8,128)S(1)}, f32[4,24,256]{2,1,0:T(8,128)S(1)}, u32[]{:S(2)}, u32[]{:S(2)}) %collective-permute-start.7) | collective-permute-done | bytes 98336 | tf_op jit(solution)/shard_map/ppermute | solution.py:514
  53.1 0.2 collective-permute-done.8.refs_3_
  53.4 1.6 %collective-permute-start.9 = (f32[80,256]{1,0:T(8,128)S(1)}, f32[80,256]{1,0:T(8,128)S(1)}, u32[]{:S(2)}, u32[]{:S(2)}) collective-permute-start(f32[80,256]{1,0:T(8,128)S(1)} %get-tuple-element.55), channel_id=1, source_target_pairs={{0,2},{1,3},{2,0},{3,1},{4,6},{5,7},{6,4},{7,5},{8,10},{9,11},{10,... | collective-permute-start | bytes 245768 | tf_op jit(solution)/shard_map/ppermute | solution.py:514
  55.0 1.6 %collective-permute-start.10 = (f32[24,256]{1,0:T(8,128)S(1)}, f32[24,256]{1,0:T(8,128)S(1)}, u32[]{:S(2)}, u32[]{:S(2)}) collective-permute-start(f32[24,256]{1,0:T(8,128)S(1)} %get-tuple-element.56), channel_id=1, source_target_pairs={{0,4},{1,5},{2,6},{3,7},{4,0},{5,1},{6,2},{7,3},{8,12},{9,13},{10,... | collective-permute-start | bytes 73736 | tf_op jit(solution)/shard_map/ppermute | solution.py:514
  56.6 1.2 %collective-permute-start.11 = (f32[24,256]{1,0:T(8,128)S(1)}, f32[24,256]{1,0:T(8,128)S(1)}, u32[]{:S(2)}, u32[]{:S(2)}) collective-permute-start(f32[24,256]{1,0:T(8,128)S(1)} %get-tuple-element.57), channel_id=1, source_target_pairs={{0,6},{1,7},{2,4},{3,5},{4,2},{5,3},{6,0},{7,1},{8,14},{9,15},{10,... | collective-permute-start | bytes 73736 | tf_op jit(solution)/shard_map/ppermute | solution.py:514
  57.8 2.3 %collective-permute-done.10.refs_3_ = f32[24,256]{1,0:T(8,128)S(1)} collective-permute-done((f32[24,256]{1,0:T(8,128)S(1)}, f32[24,256]{1,0:T(8,128)S(1)}, u32[]{:S(2)}, u32[]{:S(2)}) %collective-permute-start.10) | collective-permute-done | bytes 24608 | tf_op jit(solution)/shard_map/ppermute | solution.py:514
  60.1 2.1 %collective-permute-done.11.refs_4_ = f32[24,256]{1,0:T(8,128)S(1)} collective-permute-done((f32[24,256]{1,0:T(8,128)S(1)}, f32[24,256]{1,0:T(8,128)S(1)}, u32[]{:S(2)}, u32[]{:S(2)}) %collective-permute-start.11) | collective-permute-done | bytes 24608 | tf_op jit(solution)/shard_map/ppermute | solution.py:514
  62.3 1.3 %stress_update.1 = (f32[6,8,225]{2,1,0:T(8,128)}, f32[2,3,1,256]{3,2,1,0:T(1,128)S(1)}) custom-call(f32[56,256]{1,0:T(8,128)S(1)} %get-tuple-element.53.refs_0_, f32[24,256]{1,0:T(8,128)S(1)} %get-tuple-element.54.refs_1_, f32[80,256]{1,0:T(8,128)S(1)} %collective-permute-done.9.refs_2_, f32[24,256]{1,0:T(8,128)S(1)} %collective-permute-done.10.refs_3_, ...), custom_call_target="tpu_custom_call" | custom-call | tf_op jit(solution)/shard_map/stress_update/pallas_call | solution.py:716
  63.6 3.4 %collective-permute-start.12 = (f32[3,1,256]{2,1,0:T(1,128)S(1)}, f32[3,1,256]{2,1,0:T(1,128)S(1)}, u32[]{:S(2)}, u32[]{:S(2)}) collective-permute-start(f32[3,1,256]{2,1,0:T(1,128)S(1)} %slice_bitcast_fusion), channel_id=1, source_target_pairs={{0,1},{1,2},{2,3},{3,4},{4,5},{5,6},{6,7},{8,9},{9,10},{10,11},{11... | collective-permute-start | bytes 9224 | tf_op jit(solution)/shard_map/ppermute | solution.py:50
  66.9 1.3 %collective-permute-done.12 = f32[3,1,256]{2,1,0:T(1,128)S(1)} collective-permute-done((f32[3,1,256]{2,1,0:T(1,128)S(1)}, f32[3,1,256]{2,1,0:T(1,128)S(1)}, u32[]{:S(2)}, u32[]{:S(2)}) %collective-permute-start.12) | collective-permute-done | bytes 3104 | tf_op jit(solution)/shard_map/ppermute | solution.py:50
  68.2 0.6 bitcast_add_fusion
  (22 shorter events, 0.2 us)
Async XLA Ops:
  0.6 0.8 %copy-start.1 = (f32[3,4096]{1,0:T(4,128)S(1)}, f32[3,4096]{1,0:T(4,128)}, u32[]{:S(2)}) copy-start(f32[3,4096]{1,0:T(4,128)} %euler_ref.1) | copy-start | bytes 147460
  2.4 1.5 %copy-start.7 = (s32[216,2048]{1,0:T(8,128)S(1)}, s32[216,2048]{1,0:T(8,128)}, u32[]{:S(2)}) copy-start(s32[216,2048]{1,0:T(8,128)} %ids_ref.1) | copy-start | bytes 5308420
  24.2 2.6 %collective-permute-start = (f32[16,56,256]{2,1,0:T(8,128)S(1)}, f32[16,56,256]{2,1,0:T(8,128)S(1)}, u32[]{:S(2)}, u32[]{:S(2)}) collective-permute-start(f32[16,56,256]{2,1,0:T(8,128)S(1)} %get-tuple-element.34), channel_id=1, source_target_pairs={{0,8},{8,0},{16,24},{24,16},{1,9},{9,1},{17,25},{25,17},{2,10},{10... | collective-permute-start | bytes 2752520 | tf_op jit(solution)/shard_map/ppermute | solution.py:317
  24.7 2.1 %copy-start.3 = (f32[3,1,256]{2,1,0:T(1,128)S(1)}, f32[3,1,256]{2,1,0:T(1,128)}, u32[]{:S(2)}) copy-start(f32[3,1,256]{2,1,0:T(1,128)} %refs_5_.1) | copy-start | bytes 9220
  26.9 13.8 %collective-permute-start.1 = (f32[4,56,256]{2,1,0:T(8,128)S(1)}, f32[4,56,256]{2,1,0:T(8,128)S(1)}, u32[]{:S(2)}, u32[]{:S(2)}) collective-permute-start(f32[4,56,256]{2,1,0:T(8,128)S(1)} %get-tuple-element.37), channel_id=1, source_target_pairs={{0,16},{1,17},{2,18},{3,19},{4,20},{5,21},{6,22},{7,23},{8,24},{9,... | collective-permute-start | bytes 688136 | tf_op jit(solution)/shard_map/ppermute | solution.py:514
  29.9 10.9 %collective-permute-start.2 = (f32[4,56,256]{2,1,0:T(8,128)S(1)}, f32[4,56,256]{2,1,0:T(8,128)S(1)}, u32[]{:S(2)}, u32[]{:S(2)}) collective-permute-start(f32[4,56,256]{2,1,0:T(8,128)S(1)} %get-tuple-element.38), channel_id=1, source_target_pairs={{0,17},{1,16},{2,19},{3,18},{4,21},{5,20},{6,23},{7,22},{8,25},{9,... | collective-permute-start | bytes 688136 | tf_op jit(solution)/shard_map/ppermute | solution.py:514
  31.3 10.7 %collective-permute-start.3 = (f32[4,56,256]{2,1,0:T(8,128)S(1)}, f32[4,56,256]{2,1,0:T(8,128)S(1)}, u32[]{:S(2)}, u32[]{:S(2)}) collective-permute-start(f32[4,56,256]{2,1,0:T(8,128)S(1)} %get-tuple-element.39), channel_id=1, source_target_pairs={{0,1},{1,0},{2,3},{3,2},{4,5},{5,4},{6,7},{7,6},{8,9},{9,8},{10,11... | collective-permute-start | bytes 688136 | tf_op jit(solution)/shard_map/ppermute | solution.py:514
  39.0 23.3 %copy-start = (f32[12,8,225]{2,1,0:T(8,128)S(1)}, f32[12,8,225]{2,1,0:T(8,128)}, u32[]{:S(2)}) copy-start(f32[12,8,225]{2,1,0:T(8,128)} %refs_7_.1) | copy-start | bytes 259204
  39.0 23.3 %copy-start.2 = (f32[6,8,225]{2,1,0:T(8,128)S(1)}, f32[6,8,225]{2,1,0:T(8,128)}, u32[]{:S(2)}) copy-start(f32[6,8,225]{2,1,0:T(8,128)} %refs_6_.1) | copy-start | bytes 129604
  39.0 23.3 %copy-start.4 = (s32[8,225]{1,0:T(8,128)S(1)}, s32[8,225]{1,0:T(8,128)}, u32[]{:S(2)}) copy-start(s32[8,225]{1,0:T(8,128)} %refs_8_.1) | copy-start | bytes 21604
  39.0 23.3 %copy-start.5 = (bf16[16,144]{1,0:T(8,128)(2,1)S(1)}, bf16[16,144]{1,0:T(8,128)(2,1)}, u32[]{:S(2)}) copy-start(bf16[16,144]{1,0:T(8,128)(2,1)} %constant.11.clone.refs_10_) | copy-start | bytes 13828
  39.0 23.2 %copy-start.6 = (bf16[32,48]{1,0:T(8,128)(2,1)S(1)}, bf16[32,48]{1,0:T(8,128)(2,1)}, u32[]{:S(2)}) copy-start(bf16[32,48]{1,0:T(8,128)(2,1)} %constant.10.clone.refs_9_) | copy-start | bytes 9220
  42.1 2.9 %collective-permute-start.5 = (f32[16,24,256]{2,1,0:T(8,128)S(1)}, f32[16,24,256]{2,1,0:T(8,128)S(1)}, u32[]{:S(2)}, u32[]{:S(2)}) collective-permute-start(f32[16,24,256]{2,1,0:T(8,128)S(1)} %get-tuple-element.47), channel_id=1, source_target_pairs={{0,8},{8,0},{16,24},{24,16},{1,9},{9,1},{17,25},{25,17},{2,10},{10... | collective-permute-start | bytes 1179656 | tf_op jit(solution)/shard_map/ppermute | solution.py:317
  42.2 9.0 %collective-permute-start.4 = (f32[2,56,256]{2,1,0:T(8,128)S(1)}, f32[2,56,256]{2,1,0:T(8,128)S(1)}, u32[]{:S(2)}, u32[]{:S(2)}) collective-permute-start(f32[2,56,256]{2,1,0:T(8,128)S(1)} %get-tuple-element.45), channel_id=1, source_target_pairs={{0,4},{1,5},{2,6},{3,7},{4,0},{5,1},{6,2},{7,3},{8,12},{9,13},{10,... | collective-permute-start | bytes 344072 | tf_op jit(solution)/shard_map/ppermute | solution.py:514
  45.1 6.1 %collective-permute-start.6 = (f32[4,24,256]{2,1,0:T(8,128)S(1)}, f32[4,24,256]{2,1,0:T(8,128)S(1)}, u32[]{:S(2)}, u32[]{:S(2)}) collective-permute-start(f32[4,24,256]{2,1,0:T(8,128)S(1)} %get-tuple-element.50), channel_id=1, source_target_pairs={{0,16},{1,17},{2,18},{3,19},{4,20},{5,21},{6,22},{7,23},{8,24},{9,... | collective-permute-start | bytes 294920 | tf_op jit(solution)/shard_map/ppermute | solution.py:514
  46.6 6.4 %collective-permute-start.7 = (f32[4,24,256]{2,1,0:T(8,128)S(1)}, f32[4,24,256]{2,1,0:T(8,128)S(1)}, u32[]{:S(2)}, u32[]{:S(2)}) collective-permute-start(f32[4,24,256]{2,1,0:T(8,128)S(1)} %get-tuple-element.51), channel_id=1, source_target_pairs={{0,17},{1,16},{2,19},{3,18},{4,21},{5,20},{6,23},{7,22},{8,25},{9,... | collective-permute-start | bytes 294920 | tf_op jit(solution)/shard_map/ppermute | solution.py:514
  48.1 5.2 %collective-permute-start.8 = (f32[4,24,256]{2,1,0:T(8,128)S(1)}, f32[4,24,256]{2,1,0:T(8,128)S(1)}, u32[]{:S(2)}, u32[]{:S(2)}) collective-permute-start(f32[4,24,256]{2,1,0:T(8,128)S(1)} %get-tuple-element.52), channel_id=1, source_target_pairs={{0,1},{1,0},{2,3},{3,2},{4,5},{5,4},{6,7},{7,6},{8,9},{9,8},{10,11... | collective-permute-start | bytes 294920 | tf_op jit(solution)/shard_map/ppermute | solution.py:514
  53.4 8.9 %collective-permute-start.9 = (f32[80,256]{1,0:T(8,128)S(1)}, f32[80,256]{1,0:T(8,128)S(1)}, u32[]{:S(2)}, u32[]{:S(2)}) collective-permute-start(f32[80,256]{1,0:T(8,128)S(1)} %get-tuple-element.55), channel_id=1, source_target_pairs={{0,2},{1,3},{2,0},{3,1},{4,6},{5,7},{6,4},{7,5},{8,10},{9,11},{10,... | collective-permute-start | bytes 245768 | tf_op jit(solution)/shard_map/ppermute | solution.py:514
  55.0 5.1 %collective-permute-start.10 = (f32[24,256]{1,0:T(8,128)S(1)}, f32[24,256]{1,0:T(8,128)S(1)}, u32[]{:S(2)}, u32[]{:S(2)}) collective-permute-start(f32[24,256]{1,0:T(8,128)S(1)} %get-tuple-element.56), channel_id=1, source_target_pairs={{0,4},{1,5},{2,6},{3,7},{4,0},{5,1},{6,2},{7,3},{8,12},{9,13},{10,... | collective-permute-start | bytes 73736 | tf_op jit(solution)/shard_map/ppermute | solution.py:514
  56.6 5.6 %collective-permute-start.11 = (f32[24,256]{1,0:T(8,128)S(1)}, f32[24,256]{1,0:T(8,128)S(1)}, u32[]{:S(2)}, u32[]{:S(2)}) collective-permute-start(f32[24,256]{1,0:T(8,128)S(1)} %get-tuple-element.57), channel_id=1, source_target_pairs={{0,6},{1,7},{2,4},{3,5},{4,2},{5,3},{6,0},{7,1},{8,14},{9,15},{10,... | collective-permute-start | bytes 73736 | tf_op jit(solution)/shard_map/ppermute | solution.py:514
  63.6 4.7 %collective-permute-start.12 = (f32[3,1,256]{2,1,0:T(1,128)S(1)}, f32[3,1,256]{2,1,0:T(1,128)S(1)}, u32[]{:S(2)}, u32[]{:S(2)}) collective-permute-start(f32[3,1,256]{2,1,0:T(1,128)S(1)} %slice_bitcast_fusion), channel_id=1, source_target_pairs={{0,1},{1,2},{2,3},{3,4},{4,5},{5,6},{6,7},{8,9},{9,10},{10,11},{11... | collective-permute-start | bytes 9224 | tf_op jit(solution)/shard_map/ppermute | solution.py:50

commit v21 on v17

--- a/solution.py
+++ b/solution.py
@@ -188,12 +188,11 @@
     *refs,
 ):
     first, count = octants
-    start = ids_ref.shape[0] - (8 - first) * per_octant
+    start = first * per_octant % 8
     tile_ref, raw_ref, place_ref, masked_ref = refs[-4:]
     if first + count < 8:
-        label_out_ref, send_ref, split_ref, rest_ref = refs[:-4]
+        label_out_ref, send_ref, split_ref = refs[:-4]
         label_out_ref[...] = label_ref[...]
-        rest_ref[...] = ids_ref[pl.ds(ids_ref.shape[0] - rest_ref.shape[0], rest_ref.shape[0]), :]
         targets = [(send_ref.shape[0], send_ref)]
     else:
         send_ref, keep_ref, split_ref = refs[:-4]
@@ -360,6 +359,8 @@
 def cell_sums(octants, per_octant, ids, labels, table, places):
     first, count = octants
     bricks = ids.shape[1]
+    begin = first * per_octant // 8 * 8
+    ids = ids[begin : -(-(first + count) * per_octant // 8) * 8]
     rows = padded_rows(count)
     half = jax.ShapeDtypeStruct((places, rows, COLUMNS), jnp.float32)
     split = jax.ShapeDtypeStruct((2 * rows, bricks), jnp.bfloat16)
@@ -370,7 +371,6 @@
             jax.ShapeDtypeStruct(labels.shape, jnp.int32),
             half,
             split,
-            jax.ShapeDtypeStruct((-(-left * per_octant // 8) * 8, bricks), jnp.int32),
         ]
     else:
         out_shape = [half, half]
@@ -741,12 +741,12 @@
     labels = jnp.where(brick_active > 0, owner * COLUMNS + brick_element, -1).reshape(1, bricks)
     per_octant = grain_ids.shape[0] // 8
     table = rotation_table(euler_angles)
-    labels, send, split, ids = cell_sums(CHUNKS[0], per_octant, grain_ids, labels, table, half)
+    labels, send, split = cell_sums(CHUNKS[0], per_octant, grain_ids, labels, table, half)
     keep, labels = brick_sums(split, labels, half)
     core_a, labels, own = core_sum(
         keep, across_cores(send), [labels, displacement], "core_sum_a"
     )
-    send, keep = cell_sums(CHUNKS[1], per_octant, ids, labels, table, half)
+    send, keep = cell_sums(CHUNKS[1], per_octant, grain_ids, labels, table, half)
     flip = lax.axis_size("fe") // 4
     (kept, sent), own, send = plane_sum(
         across_plane(core_a), [own, send], [flip, flip], "plane_sum_a"

time: 68.5 us -> 68.9 us (level)
  local copies, waits for them, and re-layouts: 2.35 us -> 3.4 us
  other arithmetic: 1.32 us -> 0.59 us
    slice x0 -> x2, local copies, waits for them, and re-layouts: none -> 2.52 us  [cell_sums(): ids = ids[begin:-(-(first + count) * per_octant // 8) * 8]]
    unnamed x16 -> x20, local copies, waits for them, and re-layouts: 2.34 us -> 0.88 us
    select_n x1, other arithmetic: 0.74 us -> 0.01 us  [body(): jnp.where(brick_active > 0, owner * COLUMNS + brick_element, -1)]
  transfers between devices with their start and end apart: 13 -> 13, of which waited for: 8 -> 8; matrix products, arithmetic and copies ran while one was open for 0% -> 2% of each run, Pallas kernels for 14% -> 14%
where the time goes in v21:
time: 68.9 us; the launch traced here: 68.6 us
  Pallas kernels  31.7 us (46%)
  starting transfers between devices  18.8 us (27%)
  waiting for transfers between devices  13.3 us (19%)
  local copies, waits for them, and re-layouts  3.4 us (5%)
  between operations  0.84 us (1%)
    pallas_call x2, Pallas kernels, cell_sums(): pl.pallas_call(functools.partial(cell_sum_kernel, octants, per_octant), o...  27.8 us
    ppermute x10, starting transfers between devices, to_relative(): lax.ppermute(block, ('ca', 'fe'), [(i, i ^ flip) for i in range(groups *...  14.8 us
    ppermute x10, waiting for transfers between devices, to_relative(): lax.ppermute(block, ('ca', 'fe'), [(i, i ^ flip) for i in range(groups *...  12 us
    ppermute x1, starting transfers between devices, passed_along(): return lax.ppermute(block, axis, route)  3.4 us
    slice x2, local copies, waits for them, and re-layouts, cell_sums(): ids = ids[begin:-(-(first + count) * per_octant // 8) * 8]  2.52 us
    pallas_call x1, Pallas kernels, brick_sums(): pl.pallas_call(brick_sum_kernel, out_shape=[jax.ShapeDtypeStruct((places,...  2.11 us
  transfers between devices with their start and end apart: 13, of which 8 were waited for; matrix products, arithmetic and copies ran while one was open for 2% of the time, Pallas kernels for 14%

profile of v21, /device:TPU:0, one launch (start us, length us, event | category | flops | bytes accessed | tf_op | source)
XLA Modules:
  0.0 68.6 jit_solution(5560126617804303349)
XLA Ops:
  0.6 0.8 %copy-done.1 = f32[3,4096]{1,0:T(4,128)S(1)} copy-done((f32[3,4096]{1,0:T(4,128)S(1)}, f32[3,4096]{1,0:T(4,128)}, u32[]{:S(2)}) %copy-start.1) | copy-done | bytes 49176
  1.5 0.2 rotation_table.1.table_ref
  1.7 1.5 %slice.12.ids_ref = s32[168,2048]{1,0:T(8,128)S(1)} slice(s32[216,2048]{1,0:T(8,128)} %param.11), slice={[0:168], [0:2048]} | slice | bytes 2752512 | tf_op jit(solution)/shard_map/slice | solution.py:363
  3.2 20.3 %cell_sums.2 = (s32[1,2048]{1,0:T(1,128)S(1)}, f32[16,56,256]{2,1,0:T(8,128)S(1)}, bf16[112,2048]{1,0:T(8,128)(2,1)S(1)}) custom-call(s32[168,2048]{1,0:T(8,128)S(1)} %slice.12.ids_ref, s32[1,2048]{1,0:T(1,128)S(1)} %bitcast.14, s32[48,8,128]{2,1,0:T(8,128)S(1)} %rotation_table.1.table_ref), custom_call_target="tpu_custom_call" | custom-call | flops 24000000000 | bytes 60000000 | tf_op jit(solution)/shard_map/cell_sums/pallas_call | solution.py:378
  23.4 0.5 collective-permute-start
  24.0 1.0 %slice.13.ids_ref = s32[56,2048]{1,0:T(8,128)S(1)} slice(s32[216,2048]{1,0:T(8,128)} %param.11), slice={[160:216], [0:2048]} | slice | bytes 917504 | tf_op jit(solution)/shard_map/slice | solution.py:363
  25.0 2.1 %brick_sums.1 = (f32[16,56,256]{2,1,0:T(8,128)S(1)}, s32[1,2048]{1,0:T(1,128)S(1)}) custom-call(bf16[112,2048]{1,0:T(8,128)(2,1)S(1)} %get-tuple-element.30.split_ref, s32[1,2048]{1,0:T(1,128)S(1)} %get-tuple-element.31.label_ref), custom_call_target="tpu_custom_call" | custom-call | flops 1680000000 | bytes 5600000 | tf_op jit(solution)/shard_map/brick_sums/pallas_call | solution.py:408
  27.2 0.1 core_sum_a.1
  27.3 3.5 %collective-permute-start.1 = (f32[4,56,256]{2,1,0:T(8,128)S(1)}, f32[4,56,256]{2,1,0:T(8,128)S(1)}, u32[]{:S(2)}, u32[]{:S(2)}) collective-permute-start(f32[4,56,256]{2,1,0:T(8,128)S(1)} %get-tuple-element.36), channel_id=1, source_target_pairs={{0,17},{1,16},{2,19},{3,18},{4,21},{5,20},{6,23},{7,22},{8,25},{9,... | collective-permute-start | bytes 688136 | tf_op jit(solution)/shard_map/ppermute | solution.py:514
  30.8 0.5 collective-permute-start.2
  31.3 0.1 collective-permute-start.3
  31.5 7.6 %cell_sums.3 = (f32[16,24,256]{2,1,0:T(8,128)S(1)}, f32[16,24,256]{2,1,0:T(8,128)S(1)}) custom-call(s32[56,2048]{1,0:T(8,128)S(1)} %slice.13.ids_ref, s32[1,2048]{1,0:T(1,128)S(1)} %get-tuple-element.40.label_ref, s32[48,8,128]{2,1,0:T(8,128)S(1)} %rotation_table.1.table_ref), custom_call_target="tpu_custom_call" | custom-call | flops 8000000000 | bytes 20000000 | tf_op jit(solution)/shard_map/cell_sums/pallas_call | solution.py:378
  39.1 2.9 %collective-permute-done.2.refs_2_ = f32[4,56,256]{2,1,0:T(8,128)S(1)} collective-permute-done((f32[4,56,256]{2,1,0:T(8,128)S(1)}, f32[4,56,256]{2,1,0:T(8,128)S(1)}, u32[]{:S(2)}, u32[]{:S(2)}) %collective-permute-start.2) | collective-permute-done | bytes 229408 | tf_op jit(solution)/shard_map/ppermute | solution.py:514
  42.0 0.3 collective-permute-done.3.refs_3_
  42.3 0.1 plane_sum_a.1
  42.4 0.1 collective-permute-start.5
  42.4 2.6 %collective-permute-start.4 = (f32[2,56,256]{2,1,0:T(8,128)S(1)}, f32[2,56,256]{2,1,0:T(8,128)S(1)}, u32[]{:S(2)}, u32[]{:S(2)}) collective-permute-start(f32[2,56,256]{2,1,0:T(8,128)S(1)} %get-tuple-element.43), channel_id=1, source_target_pairs={{0,4},{1,5},{2,6},{3,7},{4,0},{5,1},{6,2},{7,3},{8,12},{9,13},{10,... | collective-permute-start | bytes 344072 | tf_op jit(solution)/shard_map/ppermute | solution.py:514
  45.2 1.7 %collective-permute-start.6 = (f32[4,24,256]{2,1,0:T(8,128)S(1)}, f32[4,24,256]{2,1,0:T(8,128)S(1)}, u32[]{:S(2)}, u32[]{:S(2)}) collective-permute-start(f32[4,24,256]{2,1,0:T(8,128)S(1)} %get-tuple-element.48), channel_id=1, source_target_pairs={{0,17},{1,16},{2,19},{3,18},{4,21},{5,20},{6,23},{7,22},{8,25},{9,... | collective-permute-start | bytes 294920 | tf_op jit(solution)/shard_map/ppermute | solution.py:514
  46.9 1.3 %collective-permute-start.7 = (f32[4,24,256]{2,1,0:T(8,128)S(1)}, f32[4,24,256]{2,1,0:T(8,128)S(1)}, u32[]{:S(2)}, u32[]{:S(2)}) collective-permute-start(f32[4,24,256]{2,1,0:T(8,128)S(1)} %get-tuple-element.49), channel_id=1, source_target_pairs={{0,16},{1,17},{2,18},{3,19},{4,20},{5,21},{6,22},{7,23},{8,24},{9,... | collective-permute-start | bytes 294920 | tf_op jit(solution)/shard_map/ppermute | solution.py:514
  48.2 0.5 collective-permute-start.8
  48.7 2.6 %collective-permute-done.4.received_ref = f32[2,56,256]{2,1,0:T(8,128)S(1)} collective-permute-done((f32[2,56,256]{2,1,0:T(8,128)S(1)}, f32[2,56,256]{2,1,0:T(8,128)S(1)}, u32[]{:S(2)}, u32[]{:S(2)}) %collective-permute-start.4) | collective-permute-done | bytes 114720 | tf_op jit(solution)/shard_map/ppermute | solution.py:514
  51.4 0.1 collective-permute-done.6.refs_1_
  51.5 1.6 %collective-permute-done.7.refs_2_ = f32[4,24,256]{2,1,0:T(8,128)S(1)} collective-permute-done((f32[4,24,256]{2,1,0:T(8,128)S(1)}, f32[4,24,256]{2,1,0:T(8,128)S(1)}, u32[]{:S(2)}, u32[]{:S(2)}) %collective-permute-start.7) | collective-permute-done | bytes 98336 | tf_op jit(solution)/shard_map/ppermute | solution.py:514
  53.1 1.6 %collective-permute-start.9 = (f32[80,256]{1,0:T(8,128)S(1)}, f32[80,256]{1,0:T(8,128)S(1)}, u32[]{:S(2)}, u32[]{:S(2)}) collective-permute-start(f32[80,256]{1,0:T(8,128)S(1)} %get-tuple-element.53), channel_id=1, source_target_pairs={{0,2},{1,3},{2,0},{3,1},{4,6},{5,7},{6,4},{7,5},{8,10},{9,11},{10,... | collective-permute-start | bytes 245768 | tf_op jit(solution)/shard_map/ppermute | solution.py:514
  54.8 1.6 %collective-permute-start.10 = (f32[24,256]{1,0:T(8,128)S(1)}, f32[24,256]{1,0:T(8,128)S(1)}, u32[]{:S(2)}, u32[]{:S(2)}) collective-permute-start(f32[24,256]{1,0:T(8,128)S(1)} %get-tuple-element.54), channel_id=1, source_target_pairs={{0,4},{1,5},{2,6},{3,7},{4,0},{5,1},{6,2},{7,3},{8,12},{9,13},{10,... | collective-permute-start | bytes 73736 | tf_op jit(solution)/shard_map/ppermute | solution.py:514
  56.4 1.2 %collective-permute-start.11 = (f32[24,256]{1,0:T(8,128)S(1)}, f32[24,256]{1,0:T(8,128)S(1)}, u32[]{:S(2)}, u32[]{:S(2)}) collective-permute-start(f32[24,256]{1,0:T(8,128)S(1)} %get-tuple-element.55), channel_id=1, source_target_pairs={{0,6},{1,7},{2,4},{3,5},{4,2},{5,3},{6,0},{7,1},{8,14},{9,15},{10,... | collective-permute-start | bytes 73736 | tf_op jit(solution)/shard_map/ppermute | solution.py:514
  57.6 2.1 %collective-permute-done.10.refs_3_ = f32[24,256]{1,0:T(8,128)S(1)} collective-permute-done((f32[24,256]{1,0:T(8,128)S(1)}, f32[24,256]{1,0:T(8,128)S(1)}, u32[]{:S(2)}, u32[]{:S(2)}) %collective-permute-start.10) | collective-permute-done | bytes 24608 | tf_op jit(solution)/shard_map/ppermute | solution.py:514
  59.7 2.4 %collective-permute-done.11.refs_4_ = f32[24,256]{1,0:T(8,128)S(1)} collective-permute-done((f32[24,256]{1,0:T(8,128)S(1)}, f32[24,256]{1,0:T(8,128)S(1)}, u32[]{:S(2)}, u32[]{:S(2)}) %collective-permute-start.11) | collective-permute-done | bytes 24608 | tf_op jit(solution)/shard_map/ppermute | solution.py:514
  62.1 1.3 %stress_update.1 = (f32[6,8,225]{2,1,0:T(8,128)}, f32[2,3,1,256]{3,2,1,0:T(1,128)S(1)}) custom-call(f32[56,256]{1,0:T(8,128)S(1)} %get-tuple-element.51.refs_0_, f32[24,256]{1,0:T(8,128)S(1)} %get-tuple-element.52.refs_1_, f32[80,256]{1,0:T(8,128)S(1)} %collective-permute-done.9.refs_2_, f32[24,256]{1,0:T(8,128)S(1)} %collective-permute-done.10.refs_3_, ...), custom_call_target="tpu_custom_call" | custom-call | tf_op jit(solution)/shard_map/stress_update/pallas_call | solution.py:716
  63.3 3.4 %collective-permute-start.12 = (f32[3,1,256]{2,1,0:T(1,128)S(1)}, f32[3,1,256]{2,1,0:T(1,128)S(1)}, u32[]{:S(2)}, u32[]{:S(2)}) collective-permute-start(f32[3,1,256]{2,1,0:T(1,128)S(1)} %slice_bitcast_fusion), channel_id=1, source_target_pairs={{0,1},{1,2},{2,3},{3,4},{4,5},{5,6},{6,7},{8,9},{9,10},{10,11},{11... | collective-permute-start | bytes 9224 | tf_op jit(solution)/shard_map/ppermute | solution.py:50
  66.7 1.3 %collective-permute-done.12 = f32[3,1,256]{2,1,0:T(1,128)S(1)} collective-permute-done((f32[3,1,256]{2,1,0:T(1,128)S(1)}, f32[3,1,256]{2,1,0:T(1,128)S(1)}, u32[]{:S(2)}, u32[]{:S(2)}) %collective-permute-start.12) | collective-permute-done | bytes 3104 | tf_op jit(solution)/shard_map/ppermute | solution.py:50
  68.0 0.6 bitcast_add_fusion
  (28 shorter events, 0.2 us)
Async XLA Ops:
  0.6 0.8 %copy-start.1 = (f32[3,4096]{1,0:T(4,128)S(1)}, f32[3,4096]{1,0:T(4,128)}, u32[]{:S(2)}) copy-start(f32[3,4096]{1,0:T(4,128)} %euler_ref.1) | copy-start | bytes 147460
  1.5 1.7 %copy-start.7 = (s32[2048]{0:T(1024)S(1)}, s32[2048]{0:T(1024)}, u32[]{:S(2)}) copy-start(s32[2048]{0:T(1024)} %param.15) | copy-start | bytes 24580
  1.5 1.7 %copy-start.8 = (s32[2048,1]{0,1:T(1,128)S(1)}, s32[2048,1]{0,1:T(1,128)}, u32[]{:S(2)}) copy-start(s32[2048,1]{0,1:T(1,128)} %param.14) | copy-start | bytes 24580
  1.5 1.7 %copy-start.9 = (s32[2048]{0:T(1024)S(1)}, s32[2048]{0:T(1024)}, u32[]{:S(2)}) copy-start(s32[2048]{0:T(1024)} %param.13) | copy-start | bytes 24580
  23.4 3.7 %collective-permute-start = (f32[16,56,256]{2,1,0:T(8,128)S(1)}, f32[16,56,256]{2,1,0:T(8,128)S(1)}, u32[]{:S(2)}, u32[]{:S(2)}) collective-permute-start(f32[16,56,256]{2,1,0:T(8,128)S(1)} %get-tuple-element.33), channel_id=1, source_target_pairs={{0,8},{8,0},{16,24},{24,16},{1,9},{9,1},{17,25},{25,17},{2,10},{10... | collective-permute-start | bytes 2752520 | tf_op jit(solution)/shard_map/ppermute | solution.py:316
  25.0 2.1 %copy-start.3 = (f32[3,1,256]{2,1,0:T(1,128)S(1)}, f32[3,1,256]{2,1,0:T(1,128)}, u32[]{:S(2)}) copy-start(f32[3,1,256]{2,1,0:T(1,128)} %refs_5_.1) | copy-start | bytes 9220
  27.3 11.8 %collective-permute-start.1 = (f32[4,56,256]{2,1,0:T(8,128)S(1)}, f32[4,56,256]{2,1,0:T(8,128)S(1)}, u32[]{:S(2)}, u32[]{:S(2)}) collective-permute-start(f32[4,56,256]{2,1,0:T(8,128)S(1)} %get-tuple-element.36), channel_id=1, source_target_pairs={{0,17},{1,16},{2,19},{3,18},{4,21},{5,20},{6,23},{7,22},{8,25},{9,... | collective-permute-start | bytes 688136 | tf_op jit(solution)/shard_map/ppermute | solution.py:514
  30.8 11.2 %collective-permute-start.2 = (f32[4,56,256]{2,1,0:T(8,128)S(1)}, f32[4,56,256]{2,1,0:T(8,128)S(1)}, u32[]{:S(2)}, u32[]{:S(2)}) collective-permute-start(f32[4,56,256]{2,1,0:T(8,128)S(1)} %get-tuple-element.37), channel_id=1, source_target_pairs={{0,16},{1,17},{2,18},{3,19},{4,20},{5,21},{6,22},{7,23},{8,24},{9,... | collective-permute-start | bytes 688136 | tf_op jit(solution)/shard_map/ppermute | solution.py:514
  31.3 11.0 %collective-permute-start.3 = (f32[4,56,256]{2,1,0:T(8,128)S(1)}, f32[4,56,256]{2,1,0:T(8,128)S(1)}, u32[]{:S(2)}, u32[]{:S(2)}) collective-permute-start(f32[4,56,256]{2,1,0:T(8,128)S(1)} %get-tuple-element.38), channel_id=1, source_target_pairs={{0,1},{1,0},{2,3},{3,2},{4,5},{5,4},{6,7},{7,6},{8,9},{9,8},{10,11... | collective-permute-start | bytes 688136 | tf_op jit(solution)/shard_map/ppermute | solution.py:514
  39.1 23.0 %copy-start = (f32[12,8,225]{2,1,0:T(8,128)S(1)}, f32[12,8,225]{2,1,0:T(8,128)}, u32[]{:S(2)}) copy-start(f32[12,8,225]{2,1,0:T(8,128)} %refs_7_.1) | copy-start | bytes 259204
  39.1 23.0 %copy-start.2 = (f32[6,8,225]{2,1,0:T(8,128)S(1)}, f32[6,8,225]{2,1,0:T(8,128)}, u32[]{:S(2)}) copy-start(f32[6,8,225]{2,1,0:T(8,128)} %refs_6_.1) | copy-start | bytes 129604
  39.1 23.0 %copy-start.4 = (s32[8,225]{1,0:T(8,128)S(1)}, s32[8,225]{1,0:T(8,128)}, u32[]{:S(2)}) copy-start(s32[8,225]{1,0:T(8,128)} %refs_8_.1) | copy-start | bytes 21604
  39.1 23.0 %copy-start.5 = (bf16[32,48]{1,0:T(8,128)(2,1)S(1)}, bf16[32,48]{1,0:T(8,128)(2,1)}, u32[]{:S(2)}) copy-start(bf16[32,48]{1,0:T(8,128)(2,1)} %constant.10.clone.refs_9_) | copy-start | bytes 9220
  39.1 22.9 %copy-start.6 = (bf16[16,144]{1,0:T(8,128)(2,1)S(1)}, bf16[16,144]{1,0:T(8,128)(2,1)}, u32[]{:S(2)}) copy-start(bf16[16,144]{1,0:T(8,128)(2,1)} %constant.11.clone.refs_10_) | copy-start | bytes 13828
  42.4 2.7 %collective-permute-start.5 = (f32[16,24,256]{2,1,0:T(8,128)S(1)}, f32[16,24,256]{2,1,0:T(8,128)S(1)}, u32[]{:S(2)}, u32[]{:S(2)}) collective-permute-start(f32[16,24,256]{2,1,0:T(8,128)S(1)} %get-tuple-element.45), channel_id=1, source_target_pairs={{0,8},{8,0},{16,24},{24,16},{1,9},{9,1},{17,25},{25,17},{2,10},{10... | collective-permute-start | bytes 1179656 | tf_op jit(solution)/shard_map/ppermute | solution.py:316
  42.4 8.9 %collective-permute-start.4 = (f32[2,56,256]{2,1,0:T(8,128)S(1)}, f32[2,56,256]{2,1,0:T(8,128)S(1)}, u32[]{:S(2)}, u32[]{:S(2)}) collective-permute-start(f32[2,56,256]{2,1,0:T(8,128)S(1)} %get-tuple-element.43), channel_id=1, source_target_pairs={{0,4},{1,5},{2,6},{3,7},{4,0},{5,1},{6,2},{7,3},{8,12},{9,13},{10,... | collective-permute-start | bytes 344072 | tf_op jit(solution)/shard_map/ppermute | solution.py:514
  45.2 6.3 %collective-permute-start.6 = (f32[4,24,256]{2,1,0:T(8,128)S(1)}, f32[4,24,256]{2,1,0:T(8,128)S(1)}, u32[]{:S(2)}, u32[]{:S(2)}) collective-permute-start(f32[4,24,256]{2,1,0:T(8,128)S(1)} %get-tuple-element.48), channel_id=1, source_target_pairs={{0,17},{1,16},{2,19},{3,18},{4,21},{5,20},{6,23},{7,22},{8,25},{9,... | collective-permute-start | bytes 294920 | tf_op jit(solution)/shard_map/ppermute | solution.py:514
  46.9 6.2 %collective-permute-start.7 = (f32[4,24,256]{2,1,0:T(8,128)S(1)}, f32[4,24,256]{2,1,0:T(8,128)S(1)}, u32[]{:S(2)}, u32[]{:S(2)}) collective-permute-start(f32[4,24,256]{2,1,0:T(8,128)S(1)} %get-tuple-element.49), channel_id=1, source_target_pairs={{0,16},{1,17},{2,18},{3,19},{4,20},{5,21},{6,22},{7,23},{8,24},{9,... | collective-permute-start | bytes 294920 | tf_op jit(solution)/shard_map/ppermute | solution.py:514
  48.2 4.9 %collective-permute-start.8 = (f32[4,24,256]{2,1,0:T(8,128)S(1)}, f32[4,24,256]{2,1,0:T(8,128)S(1)}, u32[]{:S(2)}, u32[]{:S(2)}) collective-permute-start(f32[4,24,256]{2,1,0:T(8,128)S(1)} %get-tuple-element.50), channel_id=1, source_target_pairs={{0,1},{1,0},{2,3},{3,2},{4,5},{5,4},{6,7},{7,6},{8,9},{9,8},{10,11... | collective-permute-start | bytes 294920 | tf_op jit(solution)/shard_map/ppermute | solution.py:514
  53.1 8.9 %collective-permute-start.9 = (f32[80,256]{1,0:T(8,128)S(1)}, f32[80,256]{1,0:T(8,128)S(1)}, u32[]{:S(2)}, u32[]{:S(2)}) collective-permute-start(f32[80,256]{1,0:T(8,128)S(1)} %get-tuple-element.53), channel_id=1, source_target_pairs={{0,2},{1,3},{2,0},{3,1},{4,6},{5,7},{6,4},{7,5},{8,10},{9,11},{10,... | collective-permute-start | bytes 245768 | tf_op jit(solution)/shard_map/ppermute | solution.py:514
  54.8 4.9 %collective-permute-start.10 = (f32[24,256]{1,0:T(8,128)S(1)}, f32[24,256]{1,0:T(8,128)S(1)}, u32[]{:S(2)}, u32[]{:S(2)}) collective-permute-start(f32[24,256]{1,0:T(8,128)S(1)} %get-tuple-element.54), channel_id=1, source_target_pairs={{0,4},{1,5},{2,6},{3,7},{4,0},{5,1},{6,2},{7,3},{8,12},{9,13},{10,... | collective-permute-start | bytes 73736 | tf_op jit(solution)/shard_map/ppermute | solution.py:514
  56.4 5.6 %collective-permute-start.11 = (f32[24,256]{1,0:T(8,128)S(1)}, f32[24,256]{1,0:T(8,128)S(1)}, u32[]{:S(2)}, u32[]{:S(2)}) collective-permute-start(f32[24,256]{1,0:T(8,128)S(1)} %get-tuple-element.55), channel_id=1, source_target_pairs={{0,6},{1,7},{2,4},{3,5},{4,2},{5,3},{6,0},{7,1},{8,14},{9,15},{10,... | collective-permute-start | bytes 73736 | tf_op jit(solution)/shard_map/ppermute | solution.py:514
  63.3 4.7 %collective-permute-start.12 = (f32[3,1,256]{2,1,0:T(1,128)S(1)}, f32[3,1,256]{2,1,0:T(1,128)S(1)}, u32[]{:S(2)}, u32[]{:S(2)}) collective-permute-start(f32[3,1,256]{2,1,0:T(1,128)S(1)} %slice_bitcast_fusion), channel_id=1, source_target_pairs={{0,1},{1,2},{2,3},{3,4},{4,5},{5,6},{6,7},{8,9},{9,10},{10,11},{11... | collective-permute-start | bytes 9224 | tf_op jit(solution)/shard_map/ppermute | solution.py:50
